TPU v7x, 32 devices: a whole 2x2x4 slice. The times are simulated.
32 devices in a mesh: section: 2 (over x), wide: 4 (over z), tp: 4 (over y, core).
Axes of the slice: x: 2, y: 2, z: 4, core: 2. Of those that a mesh axis runs over, the one named last changes fastest.
Arguments:
- inputs: bfloat16 [2, 4, 2048, 768], P(None, 'tp', 'wide'), may hold values from -6 to 6
- cotangent: bfloat16 [2, 4, 2048, 768], P(None, 'tp', 'wide'), may hold values from -6 to 6
- segment_ids: int32 [2, 4, 2048], replicated, may hold values from 0 to 3, as said below
- norm_gain: float32 [2, 2, 768], P('section'), may hold values from 0.5 to 1.5
- norm_shift: float32 [2, 2, 768], P('section'), may hold values from -1.75 to 1.75
- qkv_weight: bfloat16 [2, 768, 3, 768], P('section', 'wide', None, 'tp'), may hold values from -0.21875 to 0.21875
- qkv_bias: float32 [2, 3, 768], P('section', None, 'tp'), may hold values from -1.75 to 1.75
- out_weight: bfloat16 [2, 768, 768], P('section', 'tp', 'wide'), may hold values from -1.75 to 1.75
- out_bias: float32 [2, 768], P('section'), may hold values from -1.75 to 1.75
- up_weight: bfloat16 [2, 768, 3072], P('section', 'wide', 'tp'), may hold values from -0.21875 to 0.21875
- up_bias: float32 [2, 3072], P('section', 'tp'), may hold values from -1.75 to 1.75
- down_weight: bfloat16 [2, 3072, 768], P('section', 'tp', 'wide'), may hold values from -0.109375 to 0.109375
- down_bias: float32 [2, 768], P('section'), may hold values from -1.75 to 1.75
Outputs:
- section_outputs: bfloat16 [2, 2, 4, 2048, 768], P('section', None, 'tp', 'wide')
- input_grads: float32 [2, 2, 4, 2048, 768], P('section', None, 'tp', 'wide')
- norm_gain_grad: float32 [2, 2, 768], P('section')
- norm_shift_grad: float32 [2, 2, 768], P('section')
- qkv_weight_grad: float32 [2, 768, 3, 768], P('section', 'wide', None, 'tp')
- qkv_bias_grad: float32 [2, 3, 768], P('section', None, 'tp')
- out_weight_grad: float32 [2, 768, 768], P('section', 'tp', 'wide')
- out_bias_grad: float32 [2, 768], P('section')
- up_weight_grad: float32 [2, 768, 3072], P('section', 'wide', 'tp')
- up_bias_grad: float32 [2, 3072], P('section', 'tp')
- down_weight_grad: float32 [2, 3072, 768], P('section', 'tp', 'wide')
- down_bias_grad: float32 [2, 768], P('section')
Inputs may be any that keep to these rules, and one draw needn't show every extreme that they name: `segment_ids`: along each sequence the ids start at 0 and rise by one where a new document starts, never falling; in each micro-batch one sequence is a single document and another reaches the largest id.
All inputs are finite; a program needn't handle non-finite values.
Results may differ from a plain program's by a relative error of at most 0.025.
Values may be sent and summed in bfloat16 or wider, within the bound.
No kernel may reach another device: no remote copies, remote signals or barrier semaphores. Data moves between devices by JAX's collectives and lax.ppermute only.
A program may use at most 448 MiB of HBM per device.

v0:
```python
import jax
import jax.numpy as jnp
from jax import lax
from jax.sharding import PartitionSpec as P

HEAD_DIM = 64
ROTARY = 16


epsilon = 1e-05
rotary_base = 10000.0


def shifted(value, axis, steps):
    count = lax.axis_size(axis)
    first, last = (max(0, -steps), min(count, count - steps))
    return lax.ppermute(value, axis, [(source, source + steps) for source in range(first, last)])


def normalize_parts(values):
    centred = values - jnp.mean(values, -1, keepdims=True)
    inverse = lax.rsqrt(jnp.mean(centred * centred, -1, keepdims=True) + epsilon)
    return (centred * inverse, inverse)


def angle_tables(positions):
    freqs = rotary_base ** (-(2.0 * jnp.arange(ROTARY // 2, dtype=jnp.float32)) / ROTARY)
    turned = positions[:, None] * freqs[None, :]
    turned = jnp.concatenate([turned, turned], -1)
    return (jnp.cos(turned)[:, None, :], jnp.sin(turned)[:, None, :])


def rotate(values, cosine, sine):
    half = ROTARY // 2
    front = values[..., :ROTARY]
    turned = jnp.concatenate([-front[..., half:], front[..., :half]], -1)
    return jnp.concatenate([front * cosine + turned * sine, values[..., ROTARY:]], -1)


def rotate_back(grads, cosine, sine):
    half = ROTARY // 2
    front = grads[..., :ROTARY]
    scaled = front * sine
    turned = jnp.concatenate([scaled[..., half:], -scaled[..., :half]], -1)
    return jnp.concatenate([front * cosine + turned, grads[..., ROTARY:]], -1)


def gelu_exact(values):
    return jax.nn.gelu(values, approximate=False)


def in_groups(function, arrays):
    count = arrays[0].shape[0]
    group_size = 4
    grouped = jax.tree.map(
        lambda item: item.reshape((count // group_size, group_size) + item.shape[1:]), arrays
    )
    result = lax.map(function, grouped)
    return jax.tree.map(lambda item: item.reshape((count,) + item.shape[2:]), result)


def score_block(query, keys, query_segments, key_segments, query_places):
    raw = jnp.einsum("gqhd,gkhd->ghqk", query, keys, preferred_element_type=jnp.float32)
    key_places = jnp.arange(keys.shape[1])
    allowed = (query_segments[:, :, None] == key_segments[:, None, :]) & (
        query_places[None, :, None] >= key_places[None, None, :]
    )
    return jnp.where(allowed[:, None], raw * HEAD_DIM ** (-0.5), -jnp.inf)


def layer_forward(source, small, weights, query_segments, key_segments, query_places, cosine, sine):
    gain, shift, qkv_bias, out_bias, up_bias, down_bias = small
    qkv_full, out_full, up_full, down_full = weights
    normed, inverse = normalize_parts(source)
    first = (normed * gain[0] + shift[0]).astype(jnp.bfloat16)
    second = (normed * gain[1] + shift[1]).astype(jnp.bfloat16)
    first_all, second_all = (
        lax.all_gather(first, "tp", axis=0, tiled=True),
        lax.all_gather(second, "tp", axis=0, tiled=True),
    )
    mixed = (
        jnp.einsum("bcd,dte->bcte", first_all, qkv_full, preferred_element_type=jnp.float32)
        + qkv_bias
    )
    batch, span = (mixed.shape[0], mixed.shape[1])
    heads = mixed.reshape(batch, span, 3, -1, HEAD_DIM)
    query = rotate(heads[:, :, 0], cosine, sine).astype(jnp.bfloat16)
    keys = rotate(heads[:, :, 1], cosine, sine).astype(jnp.bfloat16)
    values = heads[:, :, 2].astype(jnp.bfloat16)
    keys_all, values_all = (
        lax.all_gather(keys, "wide", axis=1, tiled=True),
        lax.all_gather(values, "wide", axis=1, tiled=True),
    )

    def attend_group(item):
        block_query, block_keys, block_values, block_qseg, block_kseg = item
        scores = score_block(block_query, block_keys, block_qseg, block_kseg, query_places)
        highest = jnp.max(scores, -1, keepdims=True)
        probs = jax.nn.softmax(scores, -1)
        totals = jnp.log(jnp.sum(jnp.exp(scores - highest), -1)) + highest[..., 0]
        output = jnp.einsum(
            "ghqk,gkhd->gqhd",
            probs.astype(jnp.bfloat16),
            block_values,
            preferred_element_type=jnp.float32,
        )
        return (output, totals)

    attended, log_totals = in_groups(
        attend_group, (query, keys_all, values_all, query_segments, key_segments)
    )
    attended = attended.reshape(batch, span, -1).astype(jnp.bfloat16)
    hidden_in = (
        jnp.einsum("bcd,df->bcf", second_all, up_full, preferred_element_type=jnp.float32) + up_bias
    )
    hidden = gelu_exact(hidden_in).astype(jnp.bfloat16)
    partial_sum = jnp.einsum(
        "bce,ed->bcd", attended, out_full, preferred_element_type=jnp.float32
    ) + jnp.einsum("bcf,fd->bcd", hidden, down_full, preferred_element_type=jnp.float32)
    branch = lax.psum_scatter(
        partial_sum.astype(jnp.bfloat16), "tp", scatter_dimension=0, tiled=True
    ).astype(jnp.float32)
    output = source + branch + out_bias + down_bias
    kept = (
        normed,
        inverse,
        first_all,
        second_all,
        query,
        keys,
        values,
        keys_all,
        values_all,
        log_totals,
        attended,
        hidden_in,
    )
    return (output, kept)


def layer_backward(
    grad_out, kept, small, weights, query_segments, key_segments, query_places, cosine, sine
):
    (
        normed,
        inverse,
        first_all,
        second_all,
        query,
        keys,
        values,
        keys_all,
        values_all,
        log_totals,
        attended,
        hidden_in,
    ) = kept
    gain = small[0]
    qkv_full, out_full, up_full, down_full = weights
    bias_term = jnp.sum(grad_out, (0, 1))
    grad_all = lax.all_gather(grad_out.astype(jnp.bfloat16), "tp", axis=0, tiled=True)
    hidden_f, gelu_pull = jax.vjp(gelu_exact, hidden_in)
    hidden = hidden_f.astype(jnp.bfloat16)
    out_term = jnp.einsum("bcd,bce->de", grad_all, attended, preferred_element_type=jnp.float32)
    down_term = jnp.einsum("bcd,bcf->df", grad_all, hidden, preferred_element_type=jnp.float32)
    grad_attended = jnp.einsum(
        "bcd,ed->bce", grad_all, out_full, preferred_element_type=jnp.float32
    ).astype(jnp.bfloat16)
    grad_hidden = jnp.einsum("bcd,fd->bcf", grad_all, down_full, preferred_element_type=jnp.float32)
    grad_hidden_in = gelu_pull(grad_hidden)[0].astype(jnp.bfloat16)
    up_term = jnp.einsum(
        "bcd,bcf->df", second_all, grad_hidden_in, preferred_element_type=jnp.float32
    )
    up_bias_term = jnp.sum(grad_hidden_in.astype(jnp.float32), (0, 1))
    grad_second = jnp.einsum(
        "bcf,df->bcd", grad_hidden_in, up_full, preferred_element_type=jnp.float32
    )
    batch, span = (query.shape[0], query.shape[1])
    grad_heads = grad_attended.reshape(batch, span, -1, HEAD_DIM)
    scale = HEAD_DIM ** (-0.5)

    def back_group(item):
        block_query, block_keys, block_values, block_grad, block_qseg, block_kseg = item
        scores = score_block(block_query, block_keys, block_qseg, block_kseg, query_places)
        probs = jax.nn.softmax(scores, -1)
        grad_probs = jnp.einsum(
            "gqhd,gkhd->ghqk", block_grad, block_values, preferred_element_type=jnp.float32
        )
        centre = jnp.sum(probs * grad_probs, -1, keepdims=True)
        grad_scores = (probs * (grad_probs - centre) * scale).astype(jnp.bfloat16)
        grad_query = jnp.einsum(
            "ghqk,gkhd->gqhd", grad_scores, block_keys, preferred_element_type=jnp.float32
        )
        grad_keys = jnp.einsum(
            "ghqk,gqhd->gkhd", grad_scores, block_query, preferred_element_type=jnp.float32
        )
        grad_values = jnp.einsum(
            "ghqk,gqhd->gkhd",
            probs.astype(jnp.bfloat16),
            block_grad,
            preferred_element_type=jnp.float32,
        )
        return (grad_query, grad_keys, grad_values)

    grad_query, grad_keys_all, grad_values_all = in_groups(
        back_group, (query, keys_all, values_all, grad_heads, query_segments, key_segments)
    )
    grad_keys, grad_values = (
        lax.psum_scatter(
            grad_keys_all.astype(jnp.bfloat16), "wide", scatter_dimension=1, tiled=True
        ).astype(jnp.float32),
        lax.psum_scatter(
            grad_values_all.astype(jnp.bfloat16), "wide", scatter_dimension=1, tiled=True
        ).astype(jnp.float32),
    )
    grad_query_raw = rotate_back(grad_query, cosine, sine)
    grad_keys_raw = rotate_back(grad_keys, cosine, sine)
    grad_mixed = (
        jnp.stack([grad_query_raw, grad_keys_raw, grad_values], 2)
        .reshape(batch, span, 3, -1)
        .astype(jnp.bfloat16)
    )
    qkv_term = jnp.einsum(
        "bcd,bcte->dte", first_all, grad_mixed, preferred_element_type=jnp.float32
    )
    qkv_bias_term = jnp.sum(grad_mixed.astype(jnp.float32), (0, 1))
    grad_first = jnp.einsum(
        "bcte,dte->bcd", grad_mixed, qkv_full, preferred_element_type=jnp.float32
    )
    grad_one, grad_two = (
        lax.psum_scatter(
            grad_first.astype(jnp.bfloat16), "tp", scatter_dimension=0, tiled=True
        ).astype(jnp.float32),
        lax.psum_scatter(
            grad_second.astype(jnp.bfloat16), "tp", scatter_dimension=0, tiled=True
        ).astype(jnp.float32),
    )
    scaled = grad_one * gain[0] + grad_two * gain[1]
    grad_source = grad_out + inverse * (
        scaled
        - jnp.mean(scaled, -1, keepdims=True)
        - normed * jnp.mean(scaled * normed, -1, keepdims=True)
    )
    gain_term = jnp.stack([jnp.sum(grad_one * normed, (0, 1)), jnp.sum(grad_two * normed, (0, 1))])
    shift_term = jnp.stack([jnp.sum(grad_one, (0, 1)), jnp.sum(grad_two, (0, 1))])
    return (
        grad_source,
        (
            gain_term,
            shift_term,
            qkv_term,
            qkv_bias_term,
            out_term,
            bias_term,
            up_term,
            up_bias_term,
            down_term,
        ),
    )


def on_device(
    inputs,
    cotangent,
    segment_ids,
    norm_gain,
    norm_shift,
    qkv_weight,
    qkv_bias,
    out_weight,
    out_bias,
    up_weight,
    up_bias,
    down_weight,
    down_bias,
):
    sections = lax.axis_size("section")
    section_index = lax.axis_index("section")
    wide_index = lax.axis_index("wide")
    micro_count, span = (inputs.shape[0], inputs.shape[2])
    wide_start = wide_index * span
    query_places = wide_start + jnp.arange(span, dtype=jnp.int32)
    cosine, sine = angle_tables(query_places.astype(jnp.float32))
    weights = (
        lax.all_gather(qkv_weight[0], "wide", axis=0, tiled=True),
        lax.all_gather(out_weight[0], "wide", axis=1, tiled=True),
        lax.all_gather(up_weight[0], "wide", axis=0, tiled=True),
        lax.all_gather(down_weight[0], "wide", axis=1, tiled=True),
    )
    small = (norm_gain[0], norm_shift[0], qkv_bias[0], out_bias[0], up_bias[0], down_bias[0])
    ticks = micro_count + sections - 1
    micro_slots = jnp.arange(micro_count)
    received = jnp.zeros(inputs.shape[1:], jnp.bfloat16)
    outputs = jnp.zeros(inputs.shape, jnp.float32)
    kept_list = []
    for tick in range(ticks):
        micro = tick - section_index
        valid = (micro >= 0) & (micro < micro_count)
        picked = jnp.clip(micro, 0, micro_count - 1)
        source = jnp.where(
            section_index == 0, lax.dynamic_index_in_dim(inputs, picked, 0, False), received
        ).astype(jnp.float32)
        key_segments = lax.dynamic_index_in_dim(segment_ids, picked, 0, False)
        query_segments = lax.dynamic_slice_in_dim(key_segments, wide_start, span, 1)
        result, kept = layer_forward(
            source, small, weights, query_segments, key_segments, query_places, cosine, sine
        )
        selector = valid & (micro_slots == picked)
        outputs = jnp.where(selector[:, None, None, None], result[None], outputs)
        kept_list.append(kept)
        received = shifted(result.astype(jnp.bfloat16), "section", 1)
    stacked = jax.tree.map(lambda *items: jnp.stack(items), *kept_list)
    received = jnp.zeros(inputs.shape[1:], jnp.bfloat16)
    input_grads = jnp.zeros(inputs.shape, jnp.float32)
    totals = None
    for tick in range(ticks):
        micro = tick - (sections - 1 - section_index)
        valid = (micro >= 0) & (micro < micro_count)
        picked = jnp.clip(micro, 0, micro_count - 1)
        incoming = jnp.where(
            section_index == sections - 1,
            lax.dynamic_index_in_dim(cotangent, picked, 0, False),
            received,
        ).astype(jnp.float32)
        earlier = jnp.clip(picked + section_index, 0, ticks - 1)
        kept = jax.tree.map(lambda item: lax.dynamic_index_in_dim(item, earlier, 0, False), stacked)
        key_segments = lax.dynamic_index_in_dim(segment_ids, picked, 0, False)
        query_segments = lax.dynamic_slice_in_dim(key_segments, wide_start, span, 1)
        grad_source, terms = layer_backward(
            incoming, kept, small, weights, query_segments, key_segments, query_places, cosine, sine
        )
        weight_factor = valid.astype(jnp.float32)
        terms = jax.tree.map(lambda item: item * weight_factor, terms)
        totals = terms if totals is None else jax.tree.map(jnp.add, totals, terms)
        selector = valid & (micro_slots == picked)
        input_grads = jnp.where(selector[:, None, None, None], grad_source[None], input_grads)
        received = shifted(grad_source.astype(jnp.bfloat16), "section", -1)
    (
        gain_term,
        shift_term,
        qkv_term,
        qkv_bias_term,
        out_term,
        bias_term,
        up_term,
        up_bias_term,
        down_term,
    ) = totals
    qkv_grad, out_grad, up_grad, down_grad = (
        lax.psum_scatter(
            qkv_term.astype(jnp.bfloat16), "wide", scatter_dimension=0, tiled=True
        ).astype(jnp.float32),
        lax.psum_scatter(
            out_term.astype(jnp.bfloat16), "wide", scatter_dimension=0, tiled=True
        ).astype(jnp.float32),
        lax.psum_scatter(
            up_term.astype(jnp.bfloat16), "wide", scatter_dimension=0, tiled=True
        ).astype(jnp.float32),
        lax.psum_scatter(
            down_term.astype(jnp.bfloat16), "wide", scatter_dimension=0, tiled=True
        ).astype(jnp.float32),
    )
    qkv_bias_grad, up_bias_grad = lax.psum((qkv_bias_term, up_bias_term), "wide")
    gain_grad, shift_grad, bias_grad = lax.psum((gain_term, shift_term, bias_term), ("wide", "tp"))
    return (
        outputs.astype(jnp.bfloat16)[None],
        input_grads[None],
        gain_grad[None],
        shift_grad[None],
        qkv_grad[None],
        qkv_bias_grad[None],
        out_grad.T[None],
        bias_grad[None],
        up_grad[None],
        up_bias_grad[None],
        down_grad.T[None],
        bias_grad[None],
    )


def solution(mesh):
    return jax.shard_map(
        on_device,
        mesh=mesh,
        in_specs=(
            P(None, "tp", "wide", None),
            P(None, "tp", "wide", None),
            P(),
            P("section", None, None),
            P("section", None, None),
            P("section", "wide", None, "tp"),
            P("section", None, "tp"),
            P("section", "tp", "wide"),
            P("section", None),
            P("section", "wide", "tp"),
            P("section", "tp"),
            P("section", "tp", "wide"),
            P("section", None),
        ),
        out_specs=(
            P("section", None, "tp", "wide", None),
            P("section", None, "tp", "wide", None),
            P("section", None, None),
            P("section", None, None),
            P("section", "wide", None, "tp"),
            P("section", None, "tp"),
            P("section", "tp", "wide"),
            P("section", None),
            P("section", "wide", "tp"),
            P("section", "tp"),
            P("section", "tp", "wide"),
            P("section", None),
        ),
        check_vma=False,
    )
```

profile of v0, /device:TPU:4, one launch (start us, length us, event | category | flops | bytes accessed | tf_op | source)
XLA Modules:
  0.0 2125.9 jit_solution(8796076822643566047)
XLA Ops:
  17.9 30.0 %all-gather = bf16[1,768,3,192]{3,2,0,1:T(4,128)(2,1)S(1)} all-gather(bf16[1,192,3,192]{3,2,0,1:T(4,128)(2,1)S(1)} %copy.91), channel_id=2, replica_groups=mesh['section'=2,'wide'=4,'tp'=4] {'wide'}, dimensions={1}, use_global_device_ids=true | all-gather | bytes 1105920 | tf_op jit(solution)/shard_map/all_gather | solution.py:285
  50.3 29.4 %all-gather.2 = bf16[1,192,768]{1,0,2:T(2,128)(2,1)S(1)} all-gather(bf16[1,192,192]{1,0,2:T(2,128)(2,1)S(1)} %copy.96), channel_id=4, replica_groups=mesh['section'=2,'wide'=4,'tp'=4] {'wide'}, dimensions={2}, use_global_device_ids=true | all-gather | bytes 368640 | tf_op jit(solution)/shard_map/all_gather | solution.py:286
  89.7 19.1 compare_and_fusion
  111.5 11.3 reduce-scatter.20.cloned.1.call-start
  122.8 9.0 fusion.392
  131.8 17.4 all-gather.52.cloned.1.call-done
  149.2 19.9 fusion.274
  169.1 44.7 %all-gather.28.cloned.1.call-done = bf16[4,2048,3,64]{1,3,2,0:T(8,128)(2,1)} async-done(((bf16[4,512,3,64]{1,3,2,0:T(8,128)(2,1)}), bf16[4,2048,3,64]{1,3,2,0:T(8,128)(2,1)}) %all-gather.28.cloned.1.call-update) | async-done | bytes 3145744 | tf_op jit(solution)/shard_map/all_gather | solution.py:91
  213.8 24.2 %fusion.725 = (f32[4,3,512]{2,1,0:T(4,128)S(1)}, f32[4,3,512,2048]{3,2,1,0:T(8,128)}) fusion(pred[4,512,2048]{2,1,0:T(8,128)(4,1)} %get-tuple-element.294, bf16[4,2048,3,64]{1,3,2,0:T(8,128)(2,1)} %all-gather.28.cloned.1.call-done, bf16[4,512,3,48]{1,3,2,0:T(8,128)(2,1)S(1)} %slice.448, bf16[4,512,3,16]{1,3,2,0:T(8,128)(2,1)S(1)} %get-tuple-element.329), kind=kOutput, calls=%fused_computation.898 | convolution fusion | flops 1662519296 | bytes 58482688 | tf_op jit(solution)/shard_map/while/body/eval_jaxpr/sub | solution.py:99
  238.0 39.4 %all-gather.48.cloned.1.call-done = bf16[4,2048,1,3,64]{1,4,3,0,2:T(8,128)(2,1)} async-done(((bf16[4,512,1,3,64]{1,4,3,0,2:T(8,128)(2,1)}), bf16[4,2048,1,3,64]{1,4,3,0,2:T(8,128)(2,1)}) %all-gather.48.cloned.1.call-update) | async-done | bytes 3145744 | tf_op jit(solution)/shard_map/all_gather | solution.py:92
  277.4 19.7 fusion.419
  302.7 32.9 %reduce-scatter.20.cloned.1.call-done = bf16[1,512,768]{2,1,0:T(8,128)(2,1)} async-done(((bf16[4,512,768]{2,1,0:T(8,128)(2,1)}), bf16[1,512,768]{2,1,0:T(8,128)(2,1)}) %reduce-scatter.20.cloned.1.call-update) | async-done | bytes 786448 | tf_op jit(solution)/shard_map/reduce_scatter | solution.py:120
  341.0 16.5 collective-permute-done
  361.3 28.7 %all-gather.32.cloned.1.call-done = bf16[4,512,768]{2,1,0:T(8,128)(2,1)} async-done(((bf16[1,512,768]{2,1,0:T(8,128)(2,1)}), bf16[4,512,768]{2,1,0:T(8,128)(2,1)}) %all-gather.32.cloned.1.call-update) | async-done | bytes 3145744 | tf_op jit(solution)/shard_map/all_gather | solution.py:78
  402.7 18.0 all-gather.36.cloned.1.call-done
  429.8 18.6 fusion.272
  448.5 38.4 %all-gather.34.cloned.1.call-done = bf16[4,2048,3,64]{1,3,2,0:T(8,128)(2,1)} async-done(((bf16[4,512,3,64]{1,3,2,0:T(8,128)(2,1)}), bf16[4,2048,3,64]{1,3,2,0:T(8,128)(2,1)}) %all-gather.34.cloned.1.call-update) | async-done | bytes 3145744 | tf_op jit(solution)/shard_map/all_gather | solution.py:91
  486.9 24.9 %fusion.726 = (f32[4,3,512]{2,1,0:T(4,128)}, f32[4,3,512,2048]{3,2,1,0:T(8,128)}) fusion(pred[4,512,2048]{2,1,0:T(8,128)(4,1)} %get-tuple-element.290, bf16[4,2048,3,64]{1,3,2,0:T(8,128)(2,1)} %all-gather.34.cloned.1.call-done, bf16[4,512,3,48]{1,3,2,0:T(8,128)(2,1)S(1)} %slice.446, bf16[4,512,3,16]{1,3,2,0:T(8,128)(2,1)S(1)} %get-tuple-element.327), kind=kOutput, calls=%fused_computation.899 | convolution fusion | flops 1662519296 | bytes 58482688 | tf_op jit(solution)/shard_map/while/body/eval_jaxpr/sub | solution.py:99
  511.7 39.0 %all-gather.54.cloned.1.call-done = bf16[4,2048,1,3,64]{1,4,3,0,2:T(8,128)(2,1)} async-done(((bf16[4,512,1,3,64]{1,4,3,0,2:T(8,128)(2,1)}), bf16[4,2048,1,3,64]{1,4,3,0,2:T(8,128)(2,1)}) %all-gather.54.cloned.1.call-update) | async-done | bytes 3145744 | tf_op jit(solution)/shard_map/all_gather | solution.py:92
  550.7 19.1 fusion.416
  572.7 35.5 %reduce-scatter.22.cloned.1.call-done = bf16[1,512,768]{2,1,0:T(8,128)(2,1)} async-done(((bf16[4,512,768]{2,1,0:T(8,128)(2,1)}), bf16[1,512,768]{2,1,0:T(8,128)(2,1)}) %reduce-scatter.22.cloned.1.call-update) | async-done | bytes 786448 | tf_op jit(solution)/shard_map/reduce_scatter | solution.py:120
  613.3 16.7 collective-permute-done.1
  637.2 25.8 %all-gather.38.cloned.1.call-done = bf16[4,512,768]{2,1,0:T(8,128)(2,1)} async-done(((bf16[1,512,768]{2,1,0:T(8,128)(2,1)}), bf16[4,512,768]{2,1,0:T(8,128)(2,1)}) %all-gather.38.cloned.1.call-update) | async-done | bytes 3145744 | tf_op jit(solution)/shard_map/all_gather | solution.py:78
  675.0 17.9 all-gather.58.cloned.1.call-done
  699.9 23.0 %all-gather.42.cloned.1.call-done = bf16[4,512,768]{2,1,0:T(8,128)(2,1)} async-done(((bf16[1,512,768]{2,1,0:T(8,128)(2,1)}), bf16[4,512,768]{2,1,0:T(8,128)(2,1)}) %all-gather.42.cloned.1.call-update) | async-done | bytes 3145744 | tf_op jit(solution)/shard_map/all_gather | solution.py:79
  722.9 10.0 fusion.394
  732.9 56.6 %all-gather.40.cloned.1.call-done = bf16[4,2048,3,64]{1,3,2,0:T(8,128)(2,1)} async-done(((bf16[4,512,3,64]{1,3,2,0:T(8,128)(2,1)}), bf16[4,2048,3,64]{1,3,2,0:T(8,128)(2,1)}) %all-gather.40.cloned.1.call-update) | async-done | bytes 3145744 | tf_op jit(solution)/shard_map/all_gather | solution.py:91
  796.5 56.7 %all-gather.56.cloned.1.call-done = bf16[4,2048,1,3,64]{1,4,3,0,2:T(8,128)(2,1)} async-done(((bf16[4,512,1,3,64]{1,4,3,0,2:T(8,128)(2,1)}), bf16[4,2048,1,3,64]{1,4,3,0,2:T(8,128)(2,1)}) %all-gather.56.cloned.1.call-update) | async-done | bytes 3145744 | tf_op jit(solution)/shard_map/all_gather | solution.py:92
  853.2 8.5 pad_maximum_fusion.2
  861.7 21.4 %fusion.239 = f32[4,3,512,2048]{3,2,1,0:T(8,128)} fusion(bf16[4,512,3,64]{1,3,2,0:T(8,128)(2,1)S(1)} %bitcast.949, bf16[3,4,2048,3,64]{2,4,3,1,0:T(8,128)(2,1)} %pad_maximum_fusion.2, s32[]{:T(128)S(6)} %min.49), kind=kOutput, calls=%fused_computation.305 | convolution fusion | flops 1610612736 | bytes 54263812 | tf_op jit(solution)/shard_map/while/body/eval_jaxpr/gqhd,gkhd->ghqk/dot_general | solution.py:186
  883.1 23.9 %fusion.728 = (f32[4,3,512]{2,1,0:T(4,128)S(1)}, f32[4,3,512,2048]{3,2,1,0:T(8,128)}) fusion(pred[4,512,2048]{2,1,0:T(8,128)(4,1)} %get-tuple-element.292, bf16[3,4,2048,3,64]{2,4,3,1,0:T(8,128)(2,1)} %pad_maximum_fusion.1, s32[]{:T(128)S(6)} %min.49, bf16[3,4,512,3,64]{2,4,3,1,0:T(8,128)(2,1)S(1)} %copy-done.60), kind=kOutput, calls=%fused_computation.901 | convolution fusion | flops 1660946432 | bytes 58483712 | tf_op jit(solution)/shard_map/while/body/eval_jaxpr/sub | solution.py:185
  907.0 65.4 %fusion.276 = bf16[4,2048,3,64]{1,3,2,0:T(8,128)(2,1)} fusion(f32[4,3,512,2048]{3,2,1,0:T(8,128)} %fusion.239, bf16[3,4,512,3,64]{2,4,3,1,0:T(8,128)(2,1)S(1)} %copy-done.60, s32[]{:T(128)S(6)} %min.49, f32[4,3,512,2048]{3,2,1,0:T(8,128)} %get-tuple-element.364, f32[4,3,512]{2,1,0:T(4,128)S(1)} %get-tuple-element.363), kind=kOutput, calls=%fused_computation.337 | convolution fusion | flops 1700274176 | bytes 205324288 | tf_op jit(solution)/shard_map/while/body/eval_jaxpr/ghqk,gqhd->gkhd/dot_general | solution.py:194
  987.4 19.4 fusion.291
  1006.9 42.1 %fusion.86 = (f32[4,512,768]{2,1,0:T(8,128)}, f32[4,512,768]{2,1,0:T(8,128)S(1)}, f32[4,512,768]{2,1,0:T(8,128)}) fusion(f32[3,4,512,768]{3,2,1,0:T(8,128)} %pad_maximum_fusion, s32[]{:T(128)S(6)} %min.53, s32[]{:T(128)S(6)} %min.49, s32[]{:T(128)S(6)} %min.51), kind=kLoop, calls=%fused_computation.109 | loop fusion | flops 292552704 | bytes 37748748 | tf_op jit(solution)/shard_map/jvp()/erfc | solution.py:49
  1049.0 9.1 convert_reduce_fusion.2
  1064.0 65.7 %fusion.405 = f32[4,512,3,64]{1,3,2,0:T(8,128)S(1)} fusion(f32[4,3,512,2048]{3,2,1,0:T(8,128)} %fusion.239, bf16[3,4,2048,3,64]{2,4,3,1,0:T(8,128)(2,1)} %pad_maximum_fusion.1, s32[]{:T(128)S(6)} %min.49, f32[4,3,512,2048]{3,2,1,0:T(8,128)} %get-tuple-element.364, f32[4,3,512]{2,1,0:T(4,128)S(1)} %get-tuple-element.363), kind=kOutput, calls=%fused_computation.496 | convolution fusion | flops 1698701312 | bytes 206110720 | tf_op jit(solution)/shard_map/while/body/eval_jaxpr/ghqk,gkhd->gqhd/dot_general | solution.py:191
  1144.7 30.5 %reduce-scatter.30.cloned.1.call-done = bf16[1,512,768]{2,1,0:T(8,128)(2,1)} async-done(((bf16[4,512,768]{2,1,0:T(8,128)(2,1)}), bf16[1,512,768]{2,1,0:T(8,128)(2,1)}) %reduce-scatter.30.cloned.1.call-update) | async-done | bytes 786448 | tf_op jit(solution)/shard_map/reduce_scatter | solution.py:231
  1183.5 20.1 collective-permute-done.2
  1205.6 24.5 %fusion.737 = (f32[4,3,512]{2,1,0:T(4,128)S(1)}, f32[4,3,512,2048]{3,2,1,0:T(8,128)}) fusion(pred[4,512,2048]{2,1,0:T(8,128)(4,1)} %get-tuple-element.293, bf16[3,4,2048,3,64]{2,4,3,1,0:T(8,128)(2,1)} %pad_maximum_fusion.1, s32[]{:T(128)S(6)} %min.51, bf16[3,4,512,3,64]{2,4,3,1,0:T(8,128)(2,1)} %maximum_maximum_fusion), kind=kOutput, calls=%fused_computation.902 | convolution fusion | flops 1660946432 | bytes 58483712 | tf_op jit(solution)/shard_map/while/body/eval_jaxpr/sub | solution.py:185
  1236.0 21.5 %fusion.229 = f32[4,3,512,2048]{3,2,1,0:T(8,128)} fusion(bf16[4,512,3,64]{1,3,2,0:T(8,128)(2,1)S(1)} %bitcast.952, bf16[3,4,2048,3,64]{2,4,3,1,0:T(8,128)(2,1)} %pad_maximum_fusion.2, s32[]{:T(128)S(6)} %min.51), kind=kOutput, calls=%fused_computation.299 | convolution fusion | flops 1610612736 | bytes 54263812 | tf_op jit(solution)/shard_map/while/body/eval_jaxpr/gqhd,gkhd->ghqk/dot_general | solution.py:186
  1257.5 66.1 %fusion.279 = bf16[4,2048,3,64]{1,3,2,0:T(8,128)(2,1)} fusion(f32[4,3,512,2048]{3,2,1,0:T(8,128)} %fusion.229, bf16[3,4,512,3,64]{2,4,3,1,0:T(8,128)(2,1)} %maximum_maximum_fusion, s32[]{:T(128)S(6)} %min.51, f32[4,3,512,2048]{3,2,1,0:T(8,128)} %get-tuple-element.366, f32[4,3,512]{2,1,0:T(4,128)S(1)} %get-tuple-element.365), kind=kOutput, calls=%fused_computation.338 | convolution fusion | flops 1700274176 | bytes 205324288 | tf_op jit(solution)/shard_map/while/body/eval_jaxpr/ghqk,gqhd->gkhd/dot_general | solution.py:194
  1323.7 20.0 fusion.288
  1357.9 65.8 %fusion.400 = f32[4,512,3,64]{1,3,2,0:T(8,128)} fusion(f32[4,3,512,2048]{3,2,1,0:T(8,128)} %fusion.229, bf16[3,4,2048,3,64]{2,4,3,1,0:T(8,128)(2,1)} %pad_maximum_fusion.1, s32[]{:T(128)S(6)} %min.51, f32[4,3,512,2048]{3,2,1,0:T(8,128)} %get-tuple-element.366, f32[4,3,512]{2,1,0:T(4,128)S(1)} %get-tuple-element.365), kind=kOutput, calls=%fused_computation.495 | convolution fusion | flops 1698701312 | bytes 206110720 | tf_op jit(solution)/shard_map/while/body/eval_jaxpr/ghqk,gkhd->gqhd/dot_general | solution.py:191
  1427.9 20.4 reduce-scatter.36.cloned.1.call-done
  1453.9 33.8 %reduce-scatter.40.cloned.1.call-done = bf16[1,512,768]{2,1,0:T(8,128)(2,1)} async-done(((bf16[4,512,768]{2,1,0:T(8,128)(2,1)}), bf16[1,512,768]{2,1,0:T(8,128)(2,1)}) %reduce-scatter.40.cloned.1.call-update) | async-done | bytes 786448 | tf_op jit(solution)/shard_map/reduce_scatter | solution.py:234
  1487.6 41.1 %reduce-scatter.38.cloned.1.call-done = bf16[1,512,768]{2,1,0:T(8,128)(2,1)} async-done(((bf16[4,512,768]{2,1,0:T(8,128)(2,1)}), bf16[1,512,768]{2,1,0:T(8,128)(2,1)}) %reduce-scatter.38.cloned.1.call-update) | async-done | bytes 786448 | tf_op jit(solution)/shard_map/reduce_scatter | solution.py:231
  1537.0 20.0 collective-permute-done.3
  1559.0 24.5 %fusion.746 = (f32[4,3,512]{2,1,0:T(4,128)S(1)}, f32[4,3,512,2048]{3,2,1,0:T(8,128)}) fusion(pred[4,512,2048]{2,1,0:T(8,128)(4,1)} %get-tuple-element.289, bf16[3,4,2048,3,64]{2,4,3,1,0:T(8,128)(2,1)} %pad_maximum_fusion.1, s32[]{:T(128)S(6)} %min.53, bf16[3,4,512,3,64]{2,4,3,1,0:T(8,128)(2,1)} %maximum_maximum_fusion), kind=kOutput, calls=%fused_computation.903 | convolution fusion | flops 1660946432 | bytes 58483712 | tf_op jit(solution)/shard_map/while/body/eval_jaxpr/sub | solution.py:185
  1589.5 21.2 fusion.219
  1610.7 66.1 %fusion.282 = bf16[4,2048,3,64]{1,3,2,0:T(8,128)(2,1)} fusion(f32[4,3,512,2048]{3,2,1,0:T(8,128)} %fusion.219, bf16[3,4,512,3,64]{2,4,3,1,0:T(8,128)(2,1)} %maximum_maximum_fusion, s32[]{:T(128)S(6)} %min.53, f32[4,3,512,2048]{3,2,1,0:T(8,128)} %get-tuple-element.368, f32[4,3,512]{2,1,0:T(4,128)S(1)} %get-tuple-element.367), kind=kOutput, calls=%fused_computation.339 | convolution fusion | flops 1700274176 | bytes 205324288 | tf_op jit(solution)/shard_map/while/body/eval_jaxpr/ghqk,gqhd->gkhd/dot_general | solution.py:194
  1676.9 19.5 fusion.270
  1697.8 19.3 fusion.285
  1717.6 23.8 %fusion.727 = (f32[4,3,512]{2,1,0:T(4,128)S(1)}, f32[4,3,512,2048]{3,2,1,0:T(8,128)}) fusion(pred[4,512,2048]{2,1,0:T(8,128)(4,1)} %get-tuple-element.291, bf16[4,2048,3,64]{1,3,2,0:T(8,128)(2,1)} %all-gather.40.cloned.1.call-done, bf16[4,512,3,48]{1,3,2,0:T(8,128)(2,1)S(1)} %slice.444, bf16[4,512,3,16]{1,3,2,0:T(8,128)(2,1)S(1)} %copy-done.76), kind=kOutput, calls=%fused_computation.900 | convolution fusion | flops 1662519296 | bytes 58482688 | tf_op jit(solution)/shard_map/while/body/eval_jaxpr/sub | solution.py:99
  1741.5 20.5 fusion.413
  1764.9 8.4 fusion.195
  1793.5 10.4 convert_reduce_fusion
  1811.9 8.7 fusion.316
  1820.7 10.3 fusion.197
  1837.0 65.9 %fusion.395 = f32[4,512,3,64]{1,3,2,0:T(8,128)} fusion(f32[4,3,512,2048]{3,2,1,0:T(8,128)} %fusion.219, bf16[3,4,2048,3,64]{2,4,3,1,0:T(8,128)(2,1)} %pad_maximum_fusion.1, s32[]{:T(128)S(6)} %min.53, f32[4,3,512,2048]{3,2,1,0:T(8,128)} %get-tuple-element.368, f32[4,3,512]{2,1,0:T(4,128)S(1)} %get-tuple-element.367), kind=kOutput, calls=%fused_computation.494 | convolution fusion | flops 1698701312 | bytes 206110720 | tf_op jit(solution)/shard_map/while/body/eval_jaxpr/ghqk,gkhd->gqhd/dot_general | solution.py:191
  1904.3 10.0 fusion.313
  1956.1 13.2 all-reduce.1
  1977.3 36.2 %reduce-scatter.48.cloned.1.call-done = bf16[1,512,768]{2,1,0:T(8,128)(2,1)} async-done(((bf16[4,512,768]{2,1,0:T(8,128)(2,1)}), bf16[1,512,768]{2,1,0:T(8,128)(2,1)}) %reduce-scatter.48.cloned.1.call-update) | async-done | bytes 786448 | tf_op jit(solution)/shard_map/reduce_scatter | solution.py:234
  2013.5 40.6 %reduce-scatter.46.cloned.1.call-done = bf16[1,512,768]{2,1,0:T(8,128)(2,1)} async-done(((bf16[4,512,768]{2,1,0:T(8,128)(2,1)}), bf16[1,512,768]{2,1,0:T(8,128)(2,1)}) %reduce-scatter.46.cloned.1.call-update) | async-done | bytes 786448 | tf_op jit(solution)/shard_map/reduce_scatter | solution.py:231
  2057.0 57.0 %all-reduce = (f32[1,2,768]{2,1,0:T(2,128)}, f32[1,2,768]{2,1,0:T(2,128)}, f32[1,768]{1,0:T(1,128)S(1)}) all-reduce(f32[1,2,768]{2,1,0:T(2,128)S(1)} %fusion.576, f32[1,2,768]{2,1,0:T(2,128)S(1)} %fusion.579, f32[1,768]{1,0:T(1,128)S(1)} %broadcast_in_dim.360), channel_id=1, replica_groups=mesh['section'=2,'wide'=4,'tp'=4] {'wide','tp'}, use_global_device_ids=true, to_apply=%region_48.49 | all-reduce | flops 3840 | bytes 30720 | tf_op jit(solution)/shard_map/psum | solution.py:364
  (577 shorter events, 291.3 us)
Async XLA Ops:
  7.2 74.3 %all-gather.26.cloned.1.call-start = ((), (), s32[]{:S(2)}) async-start(), calls=%async_computation.19 | async-start | bytes 3932160 | tf_op jit(solution)/shard_map/all_gather | solution.py:78
  11.8 69.5 %copy-start.136 = (f32[1,768]{1,0:T(1,128)S(1)}, f32[1,768]{1,0:T(1,128)}, u32[]{:S(2)}) copy-start(f32[1,768]{1,0:T(1,128)} %param.23) | copy-start | bytes 9220
  14.7 108.1 %all-gather.50.cloned.1.call-start = ((), (), s32[]{:S(2)}) async-start(), calls=%async_computation.50 | async-start | bytes 1474560 | tf_op jit(solution)/shard_map/all_gather | solution.py:287
  15.4 107.4 %all-gather.30.cloned.1.call-start = ((), (), s32[]{:S(2)}) async-start(), calls=%async_computation.21 | async-start | bytes 3932160 | tf_op jit(solution)/shard_map/all_gather | solution.py:79
  16.2 133.0 %all-gather.52.cloned.1.call-start = ((), (), s32[]{:S(2)}) async-start(), calls=%async_computation.51 | async-start | bytes 1474560 | tf_op jit(solution)/shard_map/all_gather | solution.py:288
  16.7 197.0 %all-gather.28.cloned.1.call-start = ((), (), s32[]{:S(2)}) async-start(), calls=%async_computation.20 | async-start | bytes 3932160 | tf_op jit(solution)/shard_map/all_gather | solution.py:91
  17.6 68.0 %copy-start.130 = (f32[1,3,192]{2,1,0:T(4,128)}, f32[1,3,192]{2,1,0:T(4,128)S(1)}, u32[]{:S(2)}) copy-start(f32[1,3,192]{2,1,0:T(4,128)S(1)} %copy.181) | copy-start | bytes 6916
  81.3 67.8 %copy-start.122 = (f32[768]{0:T(1024)}, f32[768]{0:T(1024)S(1)}, u32[]{:S(2)}) copy-start(f32[768]{0:T(1024)S(1)} %reduce.18) | copy-start | bytes 9220
  88.6 125.2 %copy-start.77 = (bf16[4,512,3,16]{1,3,2,0:T(8,128)(2,1)}, bf16[4,512,3,16]{1,3,2,0:T(8,128)(2,1)S(1)}, u32[]{:S(2)}) copy-start(bf16[4,512,3,16]{1,3,2,0:T(8,128)(2,1)S(1)} %get-tuple-element.329) | copy-start | bytes 589828
  89.7 187.7 %all-gather.48.cloned.1.call-start = ((), (), s32[]{:S(2)}) async-start(), calls=%async_computation.49 | async-start | bytes 3932160 | tf_op jit(solution)/shard_map/all_gather | solution.py:92
  111.5 224.1 %reduce-scatter.20.cloned.1.call-start = ((), (), s32[]{:S(2)}) async-start(), calls=%async_computation.22 | async-start | bytes 3932160 | tf_op jit(solution)/shard_map/reduce_scatter | solution.py:120
  300.0 90.0 %copy-start.72 = (bf16[1,768,3,192]{1,3,2,0:T(8,128)(2,1)S(1)}, bf16[1,768,3,192]{1,3,2,0:T(8,128)(2,1)}, u32[]{:S(2)}) copy-start(bf16[1,768,3,192]{1,3,2,0:T(8,128)(2,1)} %copy.92) | copy-start | bytes 2654212
  300.0 90.0 %all-gather.32.cloned.1.call-start = ((), (), s32[]{:S(2)}) async-start(), calls=%async_computation.23 | async-start | bytes 3932160 | tf_op jit(solution)/shard_map/all_gather | solution.py:78
  337.1 20.4 collective-permute-start
  357.8 250.4 %copy-start.4 = (bf16[1,512,768]{2,1,0:T(8,128)(2,1)}, bf16[1,512,768]{2,1,0:T(8,128)(2,1)S(1)}, u32[]{:S(2)}) copy-start(bf16[1,512,768]{2,1,0:T(8,128)(2,1)S(1)} %get-tuple-element.265) | copy-start | bytes 2359300
  360.5 60.2 %all-gather.36.cloned.1.call-start = ((), (), s32[]{:S(2)}) async-start(), calls=%async_computation.25 | async-start | bytes 3932160 | tf_op jit(solution)/shard_map/all_gather | solution.py:79
  361.2 125.6 %all-gather.34.cloned.1.call-start = ((), (), s32[]{:S(2)}) async-start(), calls=%async_computation.24 | async-start | bytes 3932160 | tf_op jit(solution)/shard_map/all_gather | solution.py:91
  397.4 89.5 %copy-start.79 = (bf16[4,512,3,16]{1,3,2,0:T(8,128)(2,1)}, bf16[4,512,3,16]{1,3,2,0:T(8,128)(2,1)S(1)}, u32[]{:S(2)}) copy-start(bf16[4,512,3,16]{1,3,2,0:T(8,128)(2,1)S(1)} %get-tuple-element.327) | copy-start | bytes 589828
  398.4 152.3 %all-gather.54.cloned.1.call-start = ((), (), s32[]{:S(2)}) async-start(), calls=%async_computation.52 | async-start | bytes 3932160 | tf_op jit(solution)/shard_map/all_gather | solution.py:92
  402.7 205.6 %reduce-scatter.22.cloned.1.call-start = ((), (), s32[]{:S(2)}) async-start(), calls=%async_computation.26 | async-start | bytes 3932160 | tf_op jit(solution)/shard_map/reduce_scatter | solution.py:120
  572.6 90.3 %copy-start.131 = (f32[1,3,192]{2,1,0:T(4,128)S(1)}, f32[1,3,192]{2,1,0:T(4,128)}, u32[]{:S(2)}) copy-start(f32[1,3,192]{2,1,0:T(4,128)} %copy-done.130) | copy-start | bytes 6916
  572.6 90.3 %all-gather.38.cloned.1.call-start = ((), (), s32[]{:S(2)}) async-start(), calls=%async_computation.27 | async-start | bytes 3932160 | tf_op jit(solution)/shard_map/all_gather | solution.py:78
  609.7 20.4 collective-permute-start.1
  633.5 59.4 %all-gather.58.cloned.1.call-start = ((), (), s32[]{:S(2)}) async-start(), calls=%async_computation.54 | async-start | bytes 3932160 | tf_op jit(solution)/shard_map/all_gather | solution.py:161
  636.3 86.6 %all-gather.42.cloned.1.call-start = ((), (), s32[]{:S(2)}) async-start(), calls=%async_computation.29 | async-start | bytes 3932160 | tf_op jit(solution)/shard_map/all_gather | solution.py:79
  636.9 152.6 %all-gather.40.cloned.1.call-start = ((), (), s32[]{:S(2)}) async-start(), calls=%async_computation.28 | async-start | bytes 3932160 | tf_op jit(solution)/shard_map/all_gather | solution.py:91
  670.6 182.6 %all-gather.56.cloned.1.call-start = ((), (), s32[]{:S(2)}) async-start(), calls=%async_computation.53 | async-start | bytes 3932160 | tf_op jit(solution)/shard_map/all_gather | solution.py:92
  673.4 456.4 %reduce-scatter.26.cloned.1.call-start = ((), (), s32[]{:S(2)}) async-start(), calls=%async_computation.31 | async-start | bytes 3932160 | tf_op jit(solution)/shard_map/reduce_scatter | solution.py:209
  699.9 89.7 %copy-start.36 = (bf16[4,2048,3,64]{1,3,2,0:T(8,128)(2,1)S(1)}, bf16[4,2048,3,64]{1,3,2,0:T(8,128)(2,1)}, u32[]{:S(2)}) copy-start(bf16[4,2048,3,64]{1,3,2,0:T(8,128)(2,1)} %all-gather.28.cloned.1.call-done) | copy-start | bytes 9437188
  972.4 159.8 %reduce-scatter.28.cloned.1.call-start = ((), (), s32[]{:S(2)}) async-start(), calls=%async_computation.32 | async-start | bytes 3932160 | tf_op jit(solution)/shard_map/reduce_scatter | solution.py:212
  1006.9 137.9 %reduce-scatter.32.cloned.1.call-start = ((), (), s32[]{:S(2)}) async-start(), calls=%async_computation.34 | async-start | bytes 3932160 | tf_op jit(solution)/shard_map/reduce_scatter | solution.py:234
  1063.9 67.1 %copy-start.63 = (f32[512,16]{0,1:T(8,128)S(1)}, f32[512,16]{0,1:T(8,128)}, u32[]{:S(2)}) copy-start(f32[512,16]{0,1:T(8,128)} %copy-done.61) | copy-start | bytes 98308
  1063.9 111.4 %reduce-scatter.30.cloned.1.call-start = ((), (), s32[]{:S(2)}) async-start(), calls=%async_computation.33 | async-start | bytes 3932160 | tf_op jit(solution)/shard_map/reduce_scatter | solution.py:231
  1139.4 93.6 %all-gather.44.cloned.1.call-start = ((), (), s32[]{:S(2)}) async-start(), calls=%async_computation.35 | async-start | bytes 3932160 | tf_op jit(solution)/shard_map/all_gather | solution.py:161
  1182.3 21.3 %collective-permute-start.2 = (bf16[1,512,768]{2,1,0:T(8,128)(2,1)S(1)}, bf16[1,512,768]{2,1,0:T(8,128)(2,1)S(1)}, u32[]{:S(2)}, u32[]{:S(2)}) collective-permute-start(bf16[1,512,768]{2,1,0:T(8,128)(2,1)S(1)} %get-tuple-element.260), channel_id=1, source_target_pairs={{16,0},{17,1},{18,2},{19,3},{20,4},{21,5},{22,6},{23,7},{24,8},{25... | collective-permute-start | bytes 2359304 | tf_op jit(solution)/shard_map/ppermute | solution.py:17
  1205.3 219.9 %reduce-scatter.34.cloned.1.call-start = ((), (), s32[]{:S(2)}) async-start(), calls=%async_computation.36 | async-start | bytes 3932160 | tf_op jit(solution)/shard_map/reduce_scatter | solution.py:209
  1323.6 124.7 %reduce-scatter.36.cloned.1.call-start = ((), (), s32[]{:S(2)}) async-start(), calls=%async_computation.37 | async-start | bytes 3932160 | tf_op jit(solution)/shard_map/reduce_scatter | solution.py:212
  1343.6 144.0 %reduce-scatter.40.cloned.1.call-start = ((), (), s32[]{:S(2)}) async-start(), calls=%async_computation.39 | async-start | bytes 3932160 | tf_op jit(solution)/shard_map/reduce_scatter | solution.py:234
  1357.8 67.4 %copy-start.69 = (f32[512,16]{0,1:T(8,128)S(1)}, f32[512,16]{0,1:T(8,128)}, u32[]{:S(2)}) copy-start(f32[512,16]{0,1:T(8,128)} %copy-done.66) | copy-start | bytes 98308
  1357.8 68.7 %copy-start.64 = (f32[512,16]{0,1:T(8,128)S(1)}, f32[512,16]{0,1:T(8,128)}, u32[]{:S(2)}) copy-start(f32[512,16]{0,1:T(8,128)} %copy-done.61) | copy-start | bytes 98308
  1357.8 171.0 %reduce-scatter.38.cloned.1.call-start = ((), (), s32[]{:S(2)}) async-start(), calls=%async_computation.38 | async-start | bytes 3932160 | tf_op jit(solution)/shard_map/reduce_scatter | solution.py:231
  1448.3 80.5 %copy-start.89 = (f32[768]{0:T(1024)S(1)}, f32[768]{0:T(1024)}, u32[]{:S(2)}) copy-start(f32[768]{0:T(1024)} %copy-done.86) | copy-start | bytes 9220
  1448.3 80.5 %copy-start.94 = (f32[768]{0:T(1024)S(1)}, f32[768]{0:T(1024)}, u32[]{:S(2)}) copy-start(f32[768]{0:T(1024)} %copy-done.91) | copy-start | bytes 9220
  1453.8 78.4 %copy-start.14 = (bf16[1,512,768]{2,1,0:T(8,128)(2,1)S(1)}, bf16[1,512,768]{2,1,0:T(8,128)(2,1)}, u32[]{:S(2)}) copy-start(bf16[1,512,768]{2,1,0:T(8,128)(2,1)} %get-tuple-element.255) | copy-start | bytes 2359300
  1453.8 78.4 %copy-start.129 = (f32[1,1,512,1]{2,3,1,0:T(1,128)S(1)}, f32[1,1,512,1]{2,3,1,0:T(1,128)}, u32[]{:S(2)}) copy-start(f32[1,1,512,1]{2,3,1,0:T(1,128)} %get-tuple-element.349) | copy-start | bytes 6148
  1453.8 103.3 %copy-start.26 = (bf16[2,1,512,768]{3,2,1,0:T(8,128)(2,1)S(1)}, bf16[2,1,512,768]{3,2,1,0:T(8,128)(2,1)}, u32[]{:S(2)}) copy-start(bf16[2,1,512,768]{3,2,1,0:T(8,128)(2,1)} %param.14) | copy-start | bytes 4718596
  1453.8 132.6 %all-gather.46.cloned.1.call-start = ((), (), s32[]{:S(2)}) async-start(), calls=%async_computation.40 | async-start | bytes 3932160 | tf_op jit(solution)/shard_map/all_gather | solution.py:161
  1535.8 21.3 %collective-permute-start.3 = (bf16[1,512,768]{2,1,0:T(8,128)(2,1)S(1)}, bf16[1,512,768]{2,1,0:T(8,128)(2,1)S(1)}, u32[]{:S(2)}, u32[]{:S(2)}) collective-permute-start(bf16[1,512,768]{2,1,0:T(8,128)(2,1)S(1)} %get-tuple-element.258), channel_id=1, source_target_pairs={{16,0},{17,1},{18,2},{19,3},{20,4},{21,5},{22,6},{23,7},{24,8},{25... | collective-permute-start | bytes 2359304 | tf_op jit(solution)/shard_map/ppermute | solution.py:17
  1558.8 355.5 %reduce-scatter.42.cloned.1.call-start = ((), (), s32[]{:S(2)}) async-start(), calls=%async_computation.41 | async-start | bytes 3932160 | tf_op jit(solution)/shard_map/reduce_scatter | solution.py:209
  1610.7 66.2 %copy-start.147 = (u8[512,768]{1,0:T(8,128)(4,1)S(1)}, u8[512,768]{1,0:T(8,128)(4,1)}, u32[]{:S(2)}) copy-start(u8[512,768]{1,0:T(8,128)(4,1)} %get-tuple-element.208) | copy-start | bytes 1179652
  1610.7 66.2 %copy-start.148 = (u8[512,768]{1,0:T(8,128)(4,1)S(1)}, u8[512,768]{1,0:T(8,128)(4,1)}, u32[]{:S(2)}) copy-start(u8[512,768]{1,0:T(8,128)(4,1)} %get-tuple-element.209) | copy-start | bytes 1179652
  1676.8 240.3 %reduce-scatter.44.cloned.1.call-start = ((), (), s32[]{:S(2)}) async-start(), calls=%async_computation.42 | async-start | bytes 3932160 | tf_op jit(solution)/shard_map/reduce_scatter | solution.py:212
  1717.1 226.3 %reduce-scatter.24.cloned.1.call-start = ((), (), s32[]{:S(2)}) async-start(), calls=%async_computation.30 | async-start | bytes 3932160 | tf_op jit(solution)/shard_map/reduce_scatter | solution.py:120
  1764.8 184.1 %reduce-scatter.52.cloned.1.call-start = ((), (), s32[]{:S(2)}) async-start(), calls=%async_computation.46 | async-start | bytes 491520 | tf_op jit(solution)/shard_map/reduce_scatter | solution.py:353
  1811.8 138.8 %reduce-scatter.54.cloned.1.call-start = ((), (), s32[]{:S(2)}) async-start(), calls=%async_computation.47 | async-start | bytes 1474560 | tf_op jit(solution)/shard_map/reduce_scatter | solution.py:356
  1820.6 131.8 %reduce-scatter.56.cloned.1.call-start = ((), (), s32[]{:S(2)}) async-start(), calls=%async_computation.48 | async-start | bytes 1474560 | tf_op jit(solution)/shard_map/reduce_scatter | solution.py:359
  1914.3 61.2 %reduce-scatter.50.cloned.1.call-start = ((), (), s32[]{:S(2)}) async-start(), calls=%async_computation.45 | async-start | bytes 1474560 | tf_op jit(solution)/shard_map/reduce_scatter | solution.py:350
  1928.2 85.3 %reduce-scatter.48.cloned.1.call-start = ((), (), s32[]{:S(2)}) async-start(), calls=%async_computation.44 | async-start | bytes 3932160 | tf_op jit(solution)/shard_map/reduce_scatter | solution.py:234
  1934.7 119.3 %reduce-scatter.46.cloned.1.call-start = ((), (), s32[]{:S(2)}) async-start(), calls=%async_computation.43 | async-start | bytes 3932160 | tf_op jit(solution)/shard_map/reduce_scatter | solution.py:231
  1946.3 107.8 %copy-start.90 = (f32[768]{0:T(1024)S(1)}, f32[768]{0:T(1024)}, u32[]{:S(2)}) copy-start(f32[768]{0:T(1024)} %copy-done.86) | copy-start | bytes 9220
  1946.3 107.8 %copy-start.95 = (f32[768]{0:T(1024)S(1)}, f32[768]{0:T(1024)}, u32[]{:S(2)}) copy-start(f32[768]{0:T(1024)} %copy-done.91) | copy-start | bytes 9220
  1948.2 165.8 %copy-start.12 = (bf16[1,512,768]{2,1,0:T(8,128)(2,1)S(1)}, bf16[1,512,768]{2,1,0:T(8,128)(2,1)}, u32[]{:S(2)}) copy-start(bf16[1,512,768]{2,1,0:T(8,128)(2,1)} %get-tuple-element.257) | copy-start | bytes 2359300
  1948.2 165.8 %copy-start.128 = (f32[1,1,512,1]{2,3,1,0:T(1,128)S(1)}, f32[1,1,512,1]{2,3,1,0:T(1,128)}, u32[]{:S(2)}) copy-start(f32[1,1,512,1]{2,3,1,0:T(1,128)} %get-tuple-element.348) | copy-start | bytes 6148
  1952.4 164.2 %copy-start.19 = (f32[1,512,768]{2,1,0:T(8,128)S(1)}, f32[1,512,768]{2,1,0:T(8,128)}, u32[]{:S(2)}) copy-start(f32[1,512,768]{2,1,0:T(8,128)} %get-tuple-element.261) | copy-start | bytes 4718596
  (130 other events, 2011.9 us)
Sparse Core Ops, SparseCore 0:
  14.8 28.5 all-gather.25
  45.0 41.3 all-gather.49
  88.5 27.5 all-gather.29
  117.5 31.5 all-gather.51
  151.2 62.5 all-gather.27
  215.2 62.1 all-gather.47
  300.1 35.4 reduce-scatter.19
  360.6 29.2 all-gather.31
  392.1 28.5 all-gather.35
  422.2 64.6 all-gather.33
  488.5 62.1 all-gather.53
  572.7 35.4 reduce-scatter.21
  633.6 29.2 all-gather.37
  664.4 28.5 all-gather.57
  694.3 28.5 all-gather.41
  724.9 64.6 all-gather.39
  791.0 62.1 all-gather.55
  972.6 58.9 reduce-scatter.25
  1034.4 60.2 reduce-scatter.27
  1097.1 36.8 reduce-scatter.31
  1139.5 35.7 reduce-scatter.29
  1205.4 27.4 all-gather.43
  1323.7 61.3 reduce-scatter.33
  1387.9 60.3 reduce-scatter.35
  1450.8 36.8 reduce-scatter.39
  1490.8 37.9 reduce-scatter.37
  1558.9 27.4 all-gather.45
  1676.9 61.3 reduce-scatter.41
  1740.7 60.2 reduce-scatter.43
  1803.9 36.7 reduce-scatter.23
  1843.7 21.8 reduce-scatter.51
  1867.9 27.4 reduce-scatter.53
  1914.4 30.2 reduce-scatter.55
  1947.0 28.3 reduce-scatter.49
  1978.0 35.4 reduce-scatter.47
  2016.1 37.9 reduce-scatter.45
where the time goes:
time: 2140 us; the launch traced here: 2130 us
  matrix products  965 us (45%)
  waiting for transfers between devices  766 us (36%)
  other arithmetic  176 us (8%)
  blocking collectives  130 us (6%)
  local copies, waits for them, and re-layouts  48.3 us (2%)
  starting transfers between devices  24.3 us (1%)
    dot_general x3, matrix products, back_group(): jnp.einsum('ghqk,gqhd->gkhd', grad_scores, block_query, preferred_element...  198 us
    dot_general x3, matrix products, back_group(): jnp.einsum('ghqk,gkhd->gqhd', grad_scores, block_keys, preferred_element_...  197 us
    all_gather x3, waiting for transfers between devices, layer_forward(): lax.all_gather(keys, 'wide', axis=1, tiled=True)  140 us
    all_gather x3, waiting for transfers between devices, layer_forward(): lax.all_gather(values, 'wide', axis=1, tiled=True)  135 us
    reduce_scatter x3, waiting for transfers between devices, layer_backward(): lax.psum_scatter(grad_first.astype(jnp.bfloat16), 'tp', scatter_dimension...  112 us
    ppermute x4, waiting for transfers between devices, shifted(): lax.ppermute(value, axis, [(source, source + steps) for source in range(f...  73.4 us
    sub x3, matrix products, back_group(): probs = jax.nn.softmax(scores, -1)  73 us
    sub x3, matrix products, attend_group(): probs = jax.nn.softmax(scores, -1)  72.9 us
  transfers between devices with their start and end apart: 40, of which 27 were waited for; matrix products, arithmetic and copies ran while one was open for 37% of the time, Pallas kernels for 0%

commit v1 on v0

v1 whole, which is shorter than its diff:
```python
import functools

import jax
import jax.numpy as jnp
from jax import lax
from jax.experimental import pallas as pl
from jax.experimental.pallas import tpu as pltpu
from jax.sharding import PartitionSpec as P

HEAD_DIM = 64
ROTARY = 16
LANES = 256
CHUNKS = 2
QUERY_BLOCK = 256
KEY_BLOCK = 512
ROW_BLOCK = 256

epsilon = 1e-05
rotary_base = 10000.0
masked_out = -1e30
f32 = jnp.float32
bf16 = jnp.bfloat16
NT = (((1,), (1,)), ((), ()))


def params(size=44):
    return pltpu.CompilerParams(
        dimension_semantics=("arbitrary",), vmem_limit_bytes=size * 1024 * 1024
    )


def dot(left, right):
    return jnp.dot(left, right, preferred_element_type=f32)


def dot_nt(left, right):
    return lax.dot_general(left, right, NT, preferred_element_type=f32)


def rows_spec(rows, columns):
    return pl.BlockSpec((rows, columns), lambda i: (i, 0))


def whole_spec(array):
    return pl.BlockSpec(array.shape, lambda i: (0,) * array.ndim)


def smem_spec():
    return pl.BlockSpec(memory_space=pltpu.SMEM)


def standardize(values):
    centred = values - jnp.mean(values, -1, keepdims=True)
    inverse = lax.rsqrt(jnp.mean(centred * centred, -1, keepdims=True) + epsilon)
    return centred * inverse, inverse


def turn(values, cosine, low, high):
    half = ROTARY // 2
    ahead = pltpu.roll(values, LANES - half, 1)
    behind = pltpu.roll(values, half, 1)
    return values * cosine + ahead * low + behind * high


def turn_back(grads, cosine, low, high):
    half = ROTARY // 2
    ahead = pltpu.roll(grads * high, LANES - half, 1)
    behind = pltpu.roll(grads * low, half, 1)
    return grads * cosine + ahead + behind


def enter_kernel(
    heads,
    x_ref, gs_ref, wq_ref, bq_ref, wu_ref, bu_ref, c_ref, lo_ref, hi_ref, seg_ref,
    a0_ref, a1_ref, q_ref, k_ref, v_ref, h_ref, d_ref,
):
    normed, _ = standardize(x_ref[...].astype(f32))
    first = (normed * gs_ref[0:1] + gs_ref[2:3]).astype(bf16)
    second = (normed * gs_ref[1:2] + gs_ref[3:4]).astype(bf16)
    a0_ref[...] = first
    a1_ref[...] = second
    mixed = dot(first, wq_ref[...]) + bq_ref[...]
    cosine, low, high = c_ref[...], lo_ref[...], hi_ref[...]
    query = turn(mixed[:, :LANES], cosine, low, high)
    keys = turn(mixed[:, LANES : 2 * LANES], cosine, low, high)
    lane = lax.broadcasted_iota(jnp.int32, query.shape, 1)
    used = heads * HEAD_DIM
    mine = (lane - used) == seg_ref[...]
    spare = lane >= used
    q_ref[...] = jnp.where(
        spare, jnp.where(mine, 1.0, 0.0), query * HEAD_DIM ** (-0.5)
    ).astype(bf16)
    k_ref[...] = jnp.where(spare, jnp.where(mine, 0.0, masked_out), keys).astype(bf16)
    v_ref[...] = mixed[:, 2 * LANES :].astype(bf16)
    before = dot(second, wu_ref[...]) + bu_ref[...]
    phi = 0.5 + 0.5 * lax.erf(before * (0.5**0.5))
    density = jnp.exp(before * before * (-0.5)) * 0.3989422804014327
    h_ref[...] = (before * phi).astype(bf16)
    d_ref[...] = (phi + before * density).astype(bf16)


def enter(x, gs, wq, bq, wu, bu, tables, seg, heads):
    tokens, width = x.shape
    rows = min(ROW_BLOCK, tokens)
    hidden = wu.shape[1]
    columns = (width, width, LANES, LANES, LANES, hidden, hidden)
    return pl.pallas_call(
        functools.partial(enter_kernel, heads),
        grid=(tokens // rows,),
        in_specs=[rows_spec(rows, width)]
        + [whole_spec(item) for item in (gs, wq, bq, wu, bu)]
        + [rows_spec(rows, LANES)] * 3
        + [rows_spec(rows, 1)],
        out_specs=[rows_spec(rows, item) for item in columns],
        out_shape=[jax.ShapeDtypeStruct((tokens, item), bf16) for item in columns],
        compiler_params=params(),
        cost_estimate=pl.CostEstimate(
            flops=2 * tokens * width * (wq.shape[1] + hidden),
            bytes_accessed=20 * tokens * width,
            transcendentals=2 * tokens * hidden,
        ),
        name="enter",
    )(x, gs, wq, bq, wu, bu, *tables, seg)


def head_lanes(array, heads, spare):
    lane = lax.broadcasted_iota(jnp.int32, array.shape, 1)
    zero = jnp.zeros_like(array)
    result = []
    for head in range(heads):
        keep = (lane >= head * HEAD_DIM) & (lane < (head + 1) * HEAD_DIM)
        if spare:
            keep = keep | (lane >= heads * HEAD_DIM)
        result.append(jnp.where(keep, array, zero))
    return result


def attend_kernel(
    heads, key_block, start_ref, q_ref, k_ref, v_ref, h_ref, wo_ref, wd_ref,
    o_ref, lse_ref, part_ref, top_ref, sum_ref, acc_ref,
):
    rows = q_ref.shape[0]
    queries = head_lanes(q_ref[...], heads, True)
    first_row = start_ref[0] + pl.program_id(0) * rows
    full = first_row // key_block
    top_ref[...] = jnp.full(top_ref.shape, masked_out, f32)
    sum_ref[...] = jnp.zeros(sum_ref.shape, f32)
    acc_ref[...] = jnp.zeros(acc_ref.shape, f32)

    def step(block, diagonal):
        place = pl.ds(pl.multiple_of(block * key_block, key_block), key_block)
        keys = k_ref[place, :]
        for head in range(heads):
            half = head * HEAD_DIM // 128 * 128
            scores = dot_nt(queries[head], keys)
            if diagonal:
                row = lax.broadcasted_iota(jnp.int32, scores.shape, 0) + first_row
                column = lax.broadcasted_iota(jnp.int32, scores.shape, 1) + block * key_block
                scores = jnp.where(column <= row, scores, masked_out)
            before = top_ref[head]
            top = jnp.maximum(before, jnp.max(scores, -1, keepdims=True))
            fade = jnp.exp(before - top)
            probs = jnp.exp(scores - top[:, :1])
            top_ref[head] = top
            sum_ref[head] = sum_ref[head] * fade + jnp.sum(probs, -1, keepdims=True)
            acc_ref[head] = acc_ref[head] * fade + dot(
                probs.astype(bf16), v_ref[place, half : half + 128]
            )

    @pl.loop(0, full)
    def _(block):
        step(block, False)

    step(full, True)
    lane = lax.broadcasted_iota(jnp.int32, (rows, 128), 1)
    parts = []
    for half in range(LANES // 128):
        part = jnp.zeros((rows, 128), f32)
        for head in range(heads):
            offset = head * HEAD_DIM - half * 128
            if 0 <= offset < 128:
                keep = (lane >= offset) & (lane < offset + HEAD_DIM)
                part = jnp.where(keep, acc_ref[head] / sum_ref[head], part)
        parts.append(part)
    attended = jnp.concatenate(parts, 1).astype(bf16)
    o_ref[...] = attended
    totals = jnp.zeros((rows, 128), f32)
    for head in range(heads):
        totals = jnp.where(lane == head, top_ref[head] + jnp.log(sum_ref[head]), totals)
    lse_ref[...] = totals.T[: lse_ref.shape[0]]
    part_ref[...] = (
        dot_nt(attended, wo_ref[...]) + dot_nt(h_ref[...], wd_ref[...])
    ).astype(bf16)


def attend(start, q, k, v, h, wo, wd, heads):
    tokens = q.shape[0]
    rows = min(QUERY_BLOCK, tokens)
    key_block = min(KEY_BLOCK, k.shape[0])
    hidden, width = h.shape[1], wo.shape[0]
    return pl.pallas_call(
        functools.partial(attend_kernel, heads, key_block),
        grid=(tokens // rows,),
        in_specs=[smem_spec(), rows_spec(rows, LANES), whole_spec(k), whole_spec(v)]
        + [rows_spec(rows, hidden), whole_spec(wo), whole_spec(wd)],
        out_specs=[
            rows_spec(rows, LANES),
            pl.BlockSpec((8, rows), lambda i: (0, i)),
            rows_spec(rows, width),
        ],
        out_shape=[
            jax.ShapeDtypeStruct((tokens, LANES), bf16),
            jax.ShapeDtypeStruct((8, tokens), f32),
            jax.ShapeDtypeStruct((tokens, width), bf16),
        ],
        scratch_shapes=[pltpu.VMEM((heads, rows, 128), f32)] * 3,
        compiler_params=params(),
        cost_estimate=pl.CostEstimate(
            flops=3 * tokens * k.shape[0] * heads * 512 + 2 * tokens * width * (hidden + LANES),
            bytes_accessed=8 * tokens * width,
            transcendentals=tokens * k.shape[0] * heads,
        ),
        name="attend",
    )(start, q, k, v, h, wo, wd)


def attend_back_kernel(
    heads, key_block, carried, start_ref, gb_ref, wo_ref, wd_ref, d_ref, q_ref, o_ref, lse_ref,
    k_ref, v_ref, kt_ref, *rest,
):
    if carried:
        dk_in_ref, dv_in_ref, *rest = rest
    gu_ref, dq_ref, dk_ref, dv_ref, dqt_ref = rest
    rows = q_ref.shape[0]
    first_row = start_ref[0] + pl.program_id(0) * rows
    full = first_row // key_block

    @pl.when(pl.program_id(0) == 0)
    def _():
        dk_ref[...] = jnp.zeros(dk_ref.shape, f32)
        dv_ref[...] = jnp.zeros(dv_ref.shape, f32)
        if carried:
            dk_ref[...] = dk_in_ref[...]
            dv_ref[...] = dv_in_ref[...]

    grad = gb_ref[...]
    gu_ref[...] = (dot(grad, wd_ref[...]) * d_ref[...].astype(f32)).astype(bf16)
    grad_out = dot(grad, wo_ref[...]).astype(bf16)
    product = (grad_out.astype(f32) * o_ref[...].astype(f32)).T
    centres = [
        jnp.sum(product[head * HEAD_DIM : (head + 1) * HEAD_DIM], 0, keepdims=True)
        for head in range(heads)
    ]
    queries = head_lanes(q_ref[...], heads, True)
    grads = head_lanes(grad_out, heads, False)
    dqt_ref[...] = jnp.zeros(dqt_ref.shape, f32)

    def step(block, diagonal):
        place = pl.ds(pl.multiple_of(block * key_block, key_block), key_block)
        keys = k_ref[place, :]
        values = v_ref[place, :]
        grad_keys = dk_ref[place, :]
        grad_values = dv_ref[place, :]
        for head in range(heads):
            here = slice(head * HEAD_DIM, (head + 1) * HEAD_DIM)
            scores = dot_nt(keys, queries[head])
            probs = jnp.exp(scores - lse_ref[head : head + 1, :])
            if diagonal:
                column = lax.broadcasted_iota(jnp.int32, scores.shape, 0) + block * key_block
                row = lax.broadcasted_iota(jnp.int32, scores.shape, 1) + first_row
                probs = jnp.where(column <= row, probs, 0.0)
            grad_probs = dot_nt(values, grads[head])
            grad_scores = (probs * (grad_probs - centres[head])).astype(bf16)
            grad_values += dot(probs.astype(bf16), grads[head])
            grad_keys += dot(grad_scores, queries[head])
            dqt_ref[here, :] += dot(kt_ref[here, place], grad_scores)
        dk_ref[place, :] = grad_keys
        dv_ref[place, :] = grad_values

    @pl.loop(0, full)
    def _(block):
        step(block, False)

    step(full, True)
    dq_ref[...] = dqt_ref[...].T * HEAD_DIM ** (-0.5)


def attend_back(start, gb, wo, wd, d, q, o, lse, k, v, carried, heads):
    tokens, width = gb.shape
    rows = min(QUERY_BLOCK, tokens)
    span = k.shape[0]
    key_block = min(KEY_BLOCK, span)
    hidden = wd.shape[1]
    kt = k.T
    carried = list(carried)
    whole = pl.BlockSpec((span, LANES), lambda i: (0, 0))
    return pl.pallas_call(
        functools.partial(attend_back_kernel, heads, key_block, bool(carried)),
        grid=(tokens // rows,),
        in_specs=[smem_spec(), rows_spec(rows, width), whole_spec(wo), whole_spec(wd)]
        + [rows_spec(rows, hidden), rows_spec(rows, LANES), rows_spec(rows, LANES)]
        + [pl.BlockSpec((8, rows), lambda i: (0, i)), whole, whole, whole_spec(kt)]
        + [whole] * len(carried),
        out_specs=[rows_spec(rows, hidden), rows_spec(rows, LANES), whole, whole],
        out_shape=[
            jax.ShapeDtypeStruct((tokens, hidden), bf16),
            jax.ShapeDtypeStruct((tokens, LANES), f32),
            jax.ShapeDtypeStruct((span, LANES), f32),
            jax.ShapeDtypeStruct((span, LANES), f32),
        ],
        scratch_shapes=[pltpu.VMEM((LANES, rows), f32)],
        compiler_params=params(),
        cost_estimate=pl.CostEstimate(
            flops=7 * tokens * span * heads * 512 + 2 * tokens * width * (hidden + LANES),
            bytes_accessed=8 * tokens * width,
            transcendentals=tokens * span * heads,
        ),
        name="attend_back",
    )(start, gb, wo, wd, d, q, o, lse, k, v, kt, *carried)


def leave_kernel(
    x_ref, gs_ref, dq_ref, dk_ref, dv_ref, gu_ref, wq_ref, wu_ref, c_ref, lo_ref, hi_ref,
    gm_ref, e_ref, norm_ref, mixed_ref, up_ref,
):
    @pl.when(pl.program_id(0) == 0)
    def _():
        norm_ref[...] = jnp.zeros(norm_ref.shape, f32)
        mixed_ref[...] = jnp.zeros(mixed_ref.shape, f32)
        up_ref[...] = jnp.zeros(up_ref.shape, f32)

    cosine, low, high = c_ref[...], lo_ref[...], hi_ref[...]
    grads = jnp.concatenate(
        [
            turn_back(dq_ref[...], cosine, low, high),
            turn_back(dk_ref[...], cosine, low, high),
            dv_ref[...],
        ],
        1,
    ).astype(bf16)
    gm_ref[...] = grads
    grad_up = gu_ref[...]
    mixed_ref[...] += jnp.sum(grads.astype(f32), 0, keepdims=True)
    up_ref[...] += jnp.sum(grad_up.astype(f32), 0, keepdims=True)
    grad_first = dot_nt(grads, wq_ref[...])
    grad_second = dot_nt(grad_up, wu_ref[...])
    normed, _ = standardize(x_ref[...].astype(f32))
    norm_ref[0:1] += jnp.sum(grad_first * normed, 0, keepdims=True)
    norm_ref[1:2] += jnp.sum(grad_second * normed, 0, keepdims=True)
    norm_ref[2:3] += jnp.sum(grad_first, 0, keepdims=True)
    norm_ref[3:4] += jnp.sum(grad_second, 0, keepdims=True)
    e_ref[...] = (grad_first * gs_ref[0:1] + grad_second * gs_ref[1:2]).astype(bf16)


def leave(x, gs, dq, dk, dv, gu, wq, wu, tables):
    tokens, width = x.shape
    rows = min(ROW_BLOCK, tokens)
    hidden, mixed = wu.shape[1], wq.shape[1]
    sums = [(4, width), (1, mixed), (1, hidden)]
    return pl.pallas_call(
        leave_kernel,
        grid=(tokens // rows,),
        in_specs=[rows_spec(rows, width), whole_spec(gs)]
        + [rows_spec(rows, LANES)] * 3
        + [rows_spec(rows, hidden), whole_spec(wq), whole_spec(wu)]
        + [rows_spec(rows, LANES)] * 3,
        out_specs=[rows_spec(rows, mixed), rows_spec(rows, width)]
        + [pl.BlockSpec(item, lambda i: (0, 0)) for item in sums],
        out_shape=[
            jax.ShapeDtypeStruct((tokens, mixed), bf16),
            jax.ShapeDtypeStruct((tokens, width), bf16),
        ]
        + [jax.ShapeDtypeStruct(item, f32) for item in sums],
        compiler_params=params(),
        cost_estimate=pl.CostEstimate(
            flops=2 * tokens * width * (mixed + hidden),
            bytes_accessed=16 * tokens * width,
            transcendentals=tokens,
        ),
        name="leave",
    )(x, gs, dq, dk, dv, gu, wq, wu, *tables)


def pick(bit, zero, one):
    return jnp.where(bit == 0, zero, one)


def reverse_bits(index, bits):
    result = 0
    for bit in range(bits):
        result = result * 2 + ((index >> bit) & 1)
    return result


class Plan:
    def __init__(self, batch, length):
        self.wide, self.tp = lax.axis_size("wide"), lax.axis_size("tp")
        self.batch, self.length = batch, length
        self.bits = self.tp.bit_length() - 1
        self.group = self.wide // batch
        self.chunks = CHUNKS if self.group == 1 else 1
        self.unit = length // (self.wide * self.chunks)
        self.section = lax.axis_index("section")
        self.wide_index = lax.axis_index("wide")
        self.tp_index = lax.axis_index("tp")
        self.part = sum(
            ((self.tp_index >> bit) & 1) << (self.bits - 1 - bit) for bit in range(self.bits)
        )

    def units(self):
        for unit in range(self.wide * self.chunks):
            owner, half = divmod(unit, self.chunks)
            rest, part = divmod(unit, self.tp)
            sub, chunk = divmod(rest, self.chunks)
            for sequence in range(self.batch):
                worker = (sequence * self.group + sub) * self.tp + reverse_bits(part, self.bits)
                yield owner * self.tp + sequence, worker, half, chunk, part

    def to_work(self, block):
        chunks = []
        for chunk in range(self.chunks):
            result = None
            for half in range(self.chunks):
                pairs = [u[:2] for u in self.units() if u[2] == half and u[3] == chunk]
                piece = block[half * self.unit : (half + 1) * self.unit]
                piece = lax.ppermute(piece, ("wide", "tp"), pairs)
                if result is None:
                    result = piece
                else:
                    result = jnp.where(self.part % self.chunks == half, piece, result)
            chunks.append(result)
        return chunks

    def to_owner(self, chunks, cross):
        devices = self.wide * self.tp
        received = []
        for turn_index in range(self.chunks):
            piece = chunks[0]
            for chunk in range(1, self.chunks):
                here = (self.part + turn_index) % self.chunks == chunk
                piece = jnp.where(here, chunks[chunk], piece)
            pairs = []
            for owner, worker, _, chunk, part in self.units():
                if (part + turn_index) % self.chunks == chunk:
                    for section in range(2):
                        target = section ^ int(cross)
                        pairs.append((section * devices + worker, target * devices + owner))
            received.append(lax.ppermute(piece, ("section", "wide", "tp"), pairs))
        if self.chunks == 1:
            return received[0]
        chunk = (self.wide_index * self.chunks // self.tp) % self.chunks
        ordered = []
        for half in range(self.chunks):
            piece = received[0]
            for turn_index in range(1, self.chunks):
                piece = jnp.where(
                    (chunk - half) % self.chunks == turn_index, received[turn_index], piece
                )
            ordered.append(piece)
        return jnp.concatenate(ordered, 0)

    def exchange(self, first, second):
        mine = [pick(self.section, a, b) for a, b in zip(first, second)]
        other = [pick(self.section, b, a) for a, b in zip(first, second)]
        same, cross = self.to_owner(mine, False), self.to_owner(other, True)
        return jnp.stack([pick(self.section, same, cross), pick(self.section, cross, same)])

    def swap(self, value):
        return lax.ppermute(value, "section", [(0, 1), (1, 0)])

    def gather(self, block):
        for bit in reversed(range(self.bits)):
            other = lax.ppermute(
                block, "tp", [(index, index ^ (1 << bit)) for index in range(self.tp)]
            )
            here = (self.tp_index >> bit) & 1
            block = jnp.concatenate([pick(here, block, other), pick(here, other, block)], 0)
        return block

    def scatter(self, block):
        for bit in range(self.bits):
            half = block.shape[0] // 2
            here = (self.tp_index >> bit) & 1
            sent = pick(here, block[half:], block[:half]).astype(bf16)
            kept = pick(here, block[:half], block[half:]).astype(f32)
            other = lax.ppermute(
                sent, "tp", [(index, index ^ (1 << bit)) for index in range(self.tp)]
            )
            block = kept + other.astype(f32)
        return block

    def groups(self):
        return [
            [sequence * self.group + sub for sub in range(self.group)]
            for sequence in range(self.batch)
        ]

    def all_places(self, block):
        if self.group == 1:
            return block
        return lax.all_gather(block, "wide", axis=0, tiled=True, axis_index_groups=self.groups())

    def own_places(self, block):
        if self.group == 1:
            return block
        return lax.psum_scatter(
            block.astype(bf16), "wide", scatter_dimension=0, tiled=True,
            axis_index_groups=self.groups(),
        ).astype(f32)


def angle_tables(places, heads):
    half = ROTARY // 2
    freqs = rotary_base ** (-(2.0 * jnp.arange(half, dtype=f32)) / ROTARY)
    turned = places[:, None].astype(f32) * freqs[None, :]
    cosine, sine = jnp.cos(turned), jnp.sin(turned)
    none = jnp.zeros_like(sine)
    rest = jnp.zeros((places.shape[0], HEAD_DIM - ROTARY), f32)
    tail = jnp.zeros((places.shape[0], LANES - heads * HEAD_DIM), f32)
    return (
        jnp.concatenate([cosine, cosine, rest + 1.0] * heads + [tail + 1.0], 1),
        jnp.concatenate([-sine, none, rest] * heads + [tail], 1),
        jnp.concatenate([none, sine, rest] * heads + [tail], 1),
    )


def on_device(
    inputs, cotangent, segment_ids, norm_gain, norm_shift, qkv_weight, qkv_bias, out_weight,
    out_bias, up_weight, up_bias, down_weight, down_bias,
):
    batch, length = segment_ids.shape[1], segment_ids.shape[2]
    plan = Plan(batch, length)
    width = inputs.shape[-1]
    local = qkv_weight.shape[-1]
    hidden = up_weight.shape[-1]
    heads = local // HEAD_DIM
    section = plan.section

    source = plan.to_work(jnp.where(section == 0, inputs[0, 0], inputs[1, 0]))
    entry = jnp.concatenate([qkv_weight[0].reshape(-1, 3 * local), up_weight[0]], 1)
    exit_ = jnp.concatenate([out_weight[0].T, down_weight[0].T], 1)
    small = jnp.concatenate(
        [
            norm_gain[0].reshape(-1), norm_shift[0].reshape(-1), out_bias[0] + down_bias[0],
            qkv_bias[0].reshape(-1), up_bias[0],
        ]
    )
    entry_other, small_other = plan.swap(entry), plan.swap(small)
    exit_other = plan.swap(exit_)
    layers = []
    for layer in range(2):
        mine = section == layer
        entry_all = lax.all_gather(
            jnp.where(mine, entry, entry_other), "wide", axis=0, tiled=True
        )
        exit_all = lax.all_gather(jnp.where(mine, exit_, exit_other), "wide", axis=0, tiled=True)
        values = jnp.where(mine, small, small_other)
        gain_shift = values[: 4 * width].reshape(4, width)
        after_bias = values[4 * width : 5 * width]
        qkv_row = values[5 * width : 5 * width + 3 * local].reshape(1, 3, local)
        up_row = values[5 * width + 3 * local :].reshape(1, hidden)
        space = ((0, 0), (0, 0), (0, LANES - local))
        wq = jnp.pad(entry_all[:, : 3 * local].reshape(width, 3, local), space)
        bq = jnp.pad(qkv_row, space)
        layers.append(
            dict(
                gs=gain_shift,
                after=after_bias,
                wq=wq.reshape(width, 3 * LANES),
                bq=bq.reshape(1, 3 * LANES),
                wu=entry_all[:, 3 * local :],
                bu=up_row,
                wo=jnp.pad(exit_all[:, :local], ((0, 0), (0, LANES - local))),
                wd=exit_all[:, local:],
            )
        )

    segments = lax.dynamic_index_in_dim(segment_ids, section, 0, False)
    segments = lax.dynamic_index_in_dim(segments, plan.wide_index // plan.group, 0, False)
    sub_length = length // plan.group
    first_place = (plan.wide_index % plan.group) * sub_length
    segments = lax.dynamic_slice_in_dim(segments, first_place, sub_length, 0)
    tables = angle_tables(first_place + jnp.arange(sub_length, dtype=jnp.int32), heads)
    size = plan.unit * plan.tp
    starts = [(first_place + index * size).reshape(1) for index in range(plan.chunks)]
    spans = [slice(index * size, (index + 1) * size) for index in range(plan.chunks)]
    chunk_tables = [[table[span] for table in tables] for span in spans]
    chunk_segments = [segments[span].reshape(-1, 1) for span in spans]

    outputs, kept = [], []
    blocks = source
    for layer in range(2):
        w = layers[layer]
        state, after = [], []
        keys = values = None
        for index in range(plan.chunks):
            x = plan.gather(blocks[index])
            a0, a1, q, k, v, h, d = enter(
                x, w["gs"], w["wq"], w["bq"], w["wu"], w["bu"], chunk_tables[index],
                chunk_segments[index], heads,
            )
            k, v = plan.all_places(k), plan.all_places(v)
            keys = k if keys is None else jnp.concatenate([keys, k], 0)
            values = v if values is None else jnp.concatenate([values, v], 0)
            o, lse, part = attend(
                starts[index], q, keys, values, h, w["wo"], w["wd"], heads
            )
            branch = plan.scatter(part)
            result = blocks[index].astype(f32) + branch + w["after"]
            after.append(result.astype(bf16))
            state.append(
                dict(x=x, a0=a0, a1=a1, q=q, h=h, d=d, o=o, lse=lse, k=keys, v=values)
            )
        kept.append((blocks, state))
        outputs.append(after)
        blocks = after
    section_outputs = plan.exchange(outputs[0], outputs[1])

    grads = plan.to_work(jnp.where(section == 0, cotangent[0, 0], cotangent[1, 0]))
    input_grads, weight_grads, norm_grads, bias_grads = {}, {}, {}, {}
    for layer in reversed(range(2)):
        w = layers[layer]
        blocks, state = kept[layer]
        carried = ()
        gathered, grad_up, grad_mixed, after = {}, {}, {}, {}
        norm_sum = mixed_sum = up_sum = 0.0
        for index in reversed(range(plan.chunks)):
            s = state[index]
            gb = plan.gather(grads[index])
            gu, dq, dk, dv = attend_back(
                starts[index], gb, w["wo"], w["wd"], s["d"], s["q"], s["o"], s["lse"],
                s["k"], s["v"], carried, heads,
            )
            if plan.chunks > 1:
                carried = (dk[: index * size], dv[: index * size])
                dk, dv = dk[index * size :], dv[index * size :]
            dk, dv = plan.own_places(dk), plan.own_places(dv)
            gm, e, norm_part, mixed_part, up_part = leave(
                s["x"], w["gs"], dq, dk, dv, gu, w["wq"], w["wu"], chunk_tables[index]
            )
            norm_sum += norm_part
            mixed_sum += mixed_part
            up_sum += up_part
            scaled = plan.scatter(e)
            normed, inverse = standardize(blocks[index].astype(f32))
            after[index] = grads[index].astype(f32) + inverse * (
                scaled
                - jnp.mean(scaled, -1, keepdims=True)
                - normed * jnp.mean(scaled * normed, -1, keepdims=True)
            )
            gathered[index], grad_up[index], grad_mixed[index] = gb, gu, gm

        def join(items):
            return jnp.concatenate([items[index] for index in range(plan.chunks)], 0)

        def over_tokens(left, right):
            return lax.dot_general(
                left, right, (((0,), (0,)), ((), ())), preferred_element_type=f32
            )

        def saved(name):
            return join([s[name] for s in state])

        gb = join(gathered)
        out_term = over_tokens(gb, saved("o"))[:, :local]
        down_term = over_tokens(gb, saved("h"))
        up_term = over_tokens(saved("a1"), join(grad_up))
        qkv_term = over_tokens(saved("a0"), join(grad_mixed))
        qkv_term = qkv_term.reshape(width, 3, LANES)[:, :, :local].reshape(width, 3 * local)
        early = jnp.concatenate([out_term, down_term, up_term], 1).astype(bf16)
        weight_grads[layer] = [
            lax.psum_scatter(item, "wide", scatter_dimension=0, tiled=True)
            for item in (early, qkv_term.astype(bf16))
        ]
        bias = sum(jnp.sum(item.astype(f32), 0) for item in grads)
        norm_grads[layer] = jnp.concatenate([norm_sum.reshape(-1), bias])
        mixed_sum = mixed_sum.reshape(3, LANES)[:, :local].reshape(-1)
        bias_grads[layer] = jnp.concatenate([mixed_sum, up_sum.reshape(-1)])
        input_grads[layer] = [after[index].astype(bf16) for index in range(plan.chunks)]
        grads = input_grads[layer]

    all_grads = plan.exchange(input_grads[0], input_grads[1]).astype(f32)
    totals = []
    for first, second in zip(weight_grads[0], weight_grads[1]):
        mine, other = pick(section, first, second), pick(section, second, first)
        totals.append(mine.astype(f32) + plan.swap(other).astype(f32))
    early, qkv_grad = totals
    out_grad, down_grad = early[:, :local], early[:, local : local + hidden]
    up_grad = early[:, local + hidden :]
    norm_total = lax.psum(
        jnp.stack([norm_grads[0], norm_grads[1]]), ("section", "wide", "tp")
    )
    bias_total = lax.psum(jnp.stack([bias_grads[0], bias_grads[1]]), ("section", "wide"))
    norm_total = pick(section, norm_total[0], norm_total[1])
    bias_total = pick(section, bias_total[0], bias_total[1])
    bias_grad = norm_total[4 * width :]
    return (
        section_outputs[None, :, None],
        all_grads[None, :, None],
        norm_total[: 2 * width].reshape(1, 2, width),
        norm_total[2 * width : 4 * width].reshape(1, 2, width),
        qkv_grad.reshape(1, -1, 3, local),
        bias_total[: 3 * local].reshape(1, 3, local),
        out_grad.T[None],
        bias_grad[None],
        up_grad[None],
        bias_total[3 * local :][None],
        down_grad.T[None],
        bias_grad[None],
    )


def solution(mesh):
    return jax.shard_map(
        on_device,
        mesh=mesh,
        in_specs=(
            P(None, "tp", "wide", None),
            P(None, "tp", "wide", None),
            P(),
            P("section", None, None),
            P("section", None, None),
            P("section", "wide", None, "tp"),
            P("section", None, "tp"),
            P("section", "tp", "wide"),
            P("section", None),
            P("section", "wide", "tp"),
            P("section", "tp"),
            P("section", "tp", "wide"),
            P("section", None),
        ),
        out_specs=(
            P("section", None, "tp", "wide", None),
            P("section", None, "tp", "wide", None),
            P("section", None, None),
            P("section", None, None),
            P("section", "wide", None, "tp"),
            P("section", None, "tp"),
            P("section", "tp", "wide"),
            P("section", None),
            P("section", "wide", "tp"),
            P("section", "tp"),
            P("section", "tp", "wide"),
            P("section", None),
        ),
        check_vma=False,
    )
```

time: 2140 us -> 927 us (0.43)
  matrix products: 965 us -> 28.4 us
  waiting for transfers between devices: 766 us -> 256 us
  Pallas kernels: 0 us -> 201 us
  local copies, waits for them, and re-layouts: 48.3 us -> 177 us
  other arithmetic: 176 us -> 96.6 us
  blocking collectives: 130 us -> 75.8 us
  starting transfers between devices: 24.3 us -> 59.8 us
    dot_general x51 -> x8, matrix products: 819 us -> 28.4 us  [over_tokens(): lax.dot_general(left, right, (((0,), (0,)), ((), ())), preferred_element_...]
    all_gather x17 -> x4, waiting for transfers between devices: 411 us -> 27.2 us  [the longest x2 27.2 us: on_device(): lax.all_gather(jnp.where(mine, entry, entry_other), 'wide', axis=0, tiled...]
    reduce_scatter x19 -> x0, waiting for transfers between devices: 277 us -> none  [the longest x3 112 us: layer_backward(): lax.psum_scatter(grad_first.astype(jnp.bfloat16), 'tp', scatter_dimension...]
    pallas_call x0 -> x16, Pallas kernels: none -> 201 us  [the longest x4 73.9 us: attend_back(): pl.pallas_call(functools.partial(attend_back_kernel, heads, key_block, bo...]
    ppermute x4 -> x53, waiting for transfers between devices: 73.4 us -> 228 us  [the longest x8 94.5 us: to_owner(): received.append(lax.ppermute(piece, ('section', 'wide', 'tp'), pairs))]
    sub x6 -> x0, matrix products: 146 us -> none  [the longest x3 73 us: back_group(): probs = jax.nn.softmax(scores, -1)]
    another operation x19 -> x3, other arithmetic: 92.9 us -> 1.69 us  [the longest x1 1.64 us: exchange(): jnp.stack([pick(self.section, same, cross), pick(self.section, cross, sam...]
    unnamed x314 -> x496, local copies, waits for them, and re-layouts: 26.6 us -> 94.2 us
  transfers between devices with their start and end apart: 40 -> 61, of which waited for: 27 -> 23; matrix products, arithmetic and copies ran while one was open for 37% -> 23% of each run, Pallas kernels for 0% -> 20%
where the time goes in v1:
time: 927 us; the launch traced here: 912 us
  waiting for transfers between devices  256 us (28%)
  Pallas kernels  201 us (22%)
  local copies, waits for them, and re-layouts  177 us (19%)
  other arithmetic  96.6 us (10%)
  blocking collectives  75.8 us (8%)
  starting transfers between devices  59.8 us (6%)
  matrix products  28.4 us (3%)
  between operations  17.1 us (2%)
    ppermute x8, waiting for transfers between devices, to_owner(): received.append(lax.ppermute(piece, ('section', 'wide', 'tp'), pairs))  94.5 us
    unnamed x496, local copies, waits for them, and re-layouts  94.2 us
    pallas_call x4, Pallas kernels, attend_back(): pl.pallas_call(functools.partial(attend_back_kernel, heads, key_block, bo...  73.9 us
    pallas_call x4, Pallas kernels, attend(): pl.pallas_call(functools.partial(attend_kernel, heads, key_block), grid=(...  71.8 us
    ppermute x8, waiting for transfers between devices, to_work(): piece = lax.ppermute(piece, ('wide', 'tp'), pairs)  51.6 us
    psum x1, blocking collectives, on_device(): lax.psum(jnp.stack([norm_grads[0], norm_grads[1]]), ('section', 'wide', '...  38.9 us
    psum x1, blocking collectives, on_device(): lax.psum(jnp.stack([bias_grads[0], bias_grads[1]]), ('section', 'wide'))  36.9 us
    ppermute x16, waiting for transfers between devices, scatter(): lax.ppermute(sent, 'tp', [(index, index ^ 1 << bit) for index in range(se...  33.5 us
  transfers between devices with their start and end apart: 61, of which 23 were waited for; matrix products, arithmetic and copies ran while one was open for 23% of the time, Pallas kernels for 20%

profile of v1, /device:TPU:4, one launch (start us, length us, event | category | flops | bytes accessed | tf_op | source)
XLA Modules:
  0.0 912.2 jit_solution(1366249509387053677)
XLA Ops:
  11.0 9.4 %collective-permute-done.10 = bf16[192,960]{1,0:T(8,128)(2,1)S(1)} collective-permute-done((bf16[192,960]{1,0:T(8,128)(2,1)S(1)}, bf16[192,960]{1,0:T(8,128)(2,1)S(1)}, u32[]{:S(2)}, u32[]{:S(2)}) %collective-permute-start.10) | collective-permute-done | bytes 368672 | tf_op jit(solution)/shard_map/ppermute | solution.py:469
  24.4 5.2 collective-permute-start.7
  37.7 5.5 multiply_sine_fusion
  44.4 8.1 concatenate.263
  52.5 8.0 concatenate.262
  60.7 7.3 concatenate.261
  76.8 3.6 fusion.141
  83.4 7.1 collective-permute-start.38
  93.2 3.1 collective-permute-start.37
  102.2 16.6 %collective-permute-done.37 = bf16[256,768]{1,0:T(8,128)(2,1)S(1)} collective-permute-done((bf16[256,768]{1,0:T(8,128)(2,1)}, bf16[256,768]{1,0:T(8,128)(2,1)S(1)}, u32[]{:S(2)}, u32[]{:S(2)}) %collective-permute-start.37) | collective-permute-done | bytes 393248 | tf_op jit(solution)/shard_map/ppermute | solution.py:426
  119.0 33.5 %collective-permute-done.27 = bf16[256,768]{1,0:T(8,128)(2,1)S(1)} collective-permute-done((bf16[256,768]{1,0:T(8,128)(2,1)S(1)}, bf16[256,768]{1,0:T(8,128)(2,1)S(1)}, u32[]{:S(2)}, u32[]{:S(2)}) %collective-permute-start.27) | collective-permute-done | bytes 393248 | tf_op jit(solution)/shard_map/ppermute | solution.py:426
  165.9 2.9 slice.439.wd_ref
  170.8 27.2 %all-gather.5.cloned.1.call-done = bf16[768,1344]{1,0:T(8,128)(2,1)} async-done(((bf16[192,1344]{1,0:T(8,128)(2,1)}), bf16[768,1344]{1,0:T(8,128)(2,1)}) %all-gather.5.cloned.1.call-update) | async-done | bytes 2064400 | tf_op jit(solution)/shard_map/all_gather | solution.py:553
  205.9 7.1 enter.5
  225.8 11.9 %attend.5 = (bf16[1024,256]{1,0:T(8,128)(2,1)S(1)}, f32[8,1024]{1,0:T(8,128)S(1)}, bf16[1024,768]{1,0:T(8,128)(2,1)S(1)}) custom-call(s32[1]{0:T(128)} %constant.186.clone.1.start_ref, bf16[1024,256]{1,0:T(8,128)(2,1)S(1)} %copy-done.122, bf16[1024,256]{1,0:T(8,128)(2,1)S(1)} %copy-done.63, bf16[1024,256]{1,0:T(8,128)(2,1)S(1)} %copy-done.66, ...), custom_call_target="tpu_custom_call" | custom-call | flops 6442450944 | bytes 6291456 | tf_op jit(solution)/shard_map/attend/pallas_call | solution.py:201
  240.3 7.1 enter.4
  251.2 2.6 fusion.124
  264.0 24.0 %attend.4 = (bf16[1024,256]{1,0:T(8,128)(2,1)S(1)}, f32[8,1024]{1,0:T(8,128)S(1)}, bf16[1024,768]{1,0:T(8,128)(2,1)S(1)}) custom-call(s32[1]{0:T(128)} %constant.177.clone.1.start_ref, bf16[1024,256]{1,0:T(8,128)(2,1)S(1)} %copy-done.125, bf16[2048,256]{1,0:T(8,128)(2,1)S(1)} %copy-done.58, bf16[2048,256]{1,0:T(8,128)(2,1)S(1)} %copy-done.87, ...), custom_call_target="tpu_custom_call" | custom-call | flops 11274289152 | bytes 6291456 | tf_op jit(solution)/shard_map/attend/pallas_call | solution.py:201
  312.9 2.6 collective-permute-done.12
  315.6 2.9 convert_reduce_fusion
  321.4 9.2 %collective-permute-done.13 = bf16[256,768]{1,0:T(8,128)(2,1)S(1)} collective-permute-done((bf16[256,768]{1,0:T(8,128)(2,1)S(1)}, bf16[256,768]{1,0:T(8,128)(2,1)S(1)}, u32[]{:S(2)}, u32[]{:S(2)}) %collective-permute-start.13) | collective-permute-done | bytes 393248 | tf_op jit(solution)/shard_map/ppermute | solution.py:473
  331.7 5.7 collective-permute-done.17
  341.8 7.1 enter.6
  358.6 7.1 enter.7
  380.0 12.1 %attend.7 = (bf16[1024,256]{1,0:T(8,128)(2,1)S(1)}, f32[8,1024]{1,0:T(8,128)S(1)}, bf16[1024,768]{1,0:T(8,128)(2,1)S(1)}) custom-call(s32[1]{0:T(128)} %constant.186.clone.1.start_ref, bf16[1024,256]{1,0:T(8,128)(2,1)S(1)} %copy-done.130, bf16[1024,256]{1,0:T(8,128)(2,1)S(1)} %copy-done.73, bf16[1024,256]{1,0:T(8,128)(2,1)S(1)} %copy-done.76, ...), custom_call_target="tpu_custom_call" | custom-call | flops 6442450944 | bytes 6291456 | tf_op jit(solution)/shard_map/attend/pallas_call | solution.py:201
  407.1 23.8 %attend.6 = (bf16[1024,256]{1,0:T(8,128)(2,1)S(1)}, f32[8,1024]{1,0:T(8,128)S(1)}, bf16[1024,768]{1,0:T(8,128)(2,1)S(1)}) custom-call(s32[1]{0:T(128)} %constant.177.clone.1.start_ref, bf16[1024,256]{1,0:T(8,128)(2,1)S(1)} %copy-done.128, bf16[2048,256]{1,0:T(8,128)(2,1)S(1)} %copy-done.60, bf16[2048,256]{1,0:T(8,128)(2,1)S(1)} %copy-done.89, ...), custom_call_target="tpu_custom_call" | custom-call | flops 11274289152 | bytes 6291456 | tf_op jit(solution)/shard_map/attend/pallas_call | solution.py:201
  433.5 23.9 %attend_back.4 = (bf16[1024,768]{1,0:T(8,128)(2,1)S(1)}, f32[1024,256]{1,0:T(8,128)S(1)}, f32[2048,256]{1,0:T(8,128)}, f32[2048,256]{1,0:T(8,128)}) custom-call(s32[1]{0:T(128)} %constant.177.clone.1.start_ref, bf16[1024,768]{1,0:T(8,128)(2,1)S(1)} %copy-done.41, bf16[768,256]{1,0:T(8,128)(2,1)S(1)} %copy-done.85, bf16[768,768]{1,0:T(8,128)(2,1)S(1)} %copy-done.46, ...), custom_call_target="tpu_custom_call" | custom-call | flops 24159191040 | bytes 6291456 | tf_op jit(solution)/shard_map/attend_back/pallas_call | solution.py:297
  457.5 2.7 fusion.140
  462.8 13.3 %attend_back.6 = (bf16[1024,768]{1,0:T(8,128)(2,1)}, f32[1024,256]{1,0:T(8,128)S(1)}, f32[1024,256]{1,0:T(8,128)S(1)}, f32[1024,256]{1,0:T(8,128)S(1)}) custom-call(s32[1]{0:T(128)} %constant.186.clone.1.start_ref, bf16[1024,768]{1,0:T(8,128)(2,1)} %pad_maximum_fusion.10.gb_ref, bf16[768,256]{1,0:T(8,128)(2,1)S(1)} %copy-done.86, ...), custom_call_target="tpu_custom_call" | custom-call | flops 12884901888 | bytes 6291456 | tf_op jit(solution)/shard_map/attend_back/pallas_call | solution.py:297
  482.7 6.7 leave.6
  493.1 6.6 leave.4
  499.8 2.5 broadcast_select_fusion.10
  502.8 5.6 fusion.36
  508.5 2.7 fusion.52
  518.6 8.4 collective-permute-done.32
  528.5 6.9 collective-permute-done.42
  536.9 6.9 collective-permute-done.33
  544.1 3.8 fusion.42
  547.9 3.5 collective-permute-done.43
  554.7 23.9 %attend_back.5 = (bf16[1024,768]{1,0:T(8,128)(2,1)S(1)}, f32[1024,256]{1,0:T(8,128)S(1)}, f32[2048,256]{1,0:T(8,128)}, f32[2048,256]{1,0:T(8,128)}) custom-call(s32[1]{0:T(128)} %constant.177.clone.1.start_ref, bf16[1024,768]{1,0:T(8,128)(2,1)S(1)} %pad_maximum_fusion.9.gb_ref, bf16[768,256]{1,0:T(8,128)(2,1)S(1)} %copy-done.83, ...), custom_call_target="tpu_custom_call" | custom-call | flops 24159191040 | bytes 6291456 | tf_op jit(solution)/shard_map/attend_back/pallas_call | solution.py:297
  585.5 6.7 leave.5
  592.3 12.8 %attend_back.7 = (bf16[1024,768]{1,0:T(8,128)(2,1)}, f32[1024,256]{1,0:T(8,128)S(1)}, f32[1024,256]{1,0:T(8,128)S(1)}, f32[1024,256]{1,0:T(8,128)S(1)}) custom-call(s32[1]{0:T(128)} %constant.186.clone.1.start_ref, bf16[1024,768]{1,0:T(8,128)(2,1)} %pad_maximum_fusion.11.gb_ref, bf16[768,256]{1,0:T(8,128)(2,1)S(1)} %copy-done.83, ...), custom_call_target="tpu_custom_call" | custom-call | flops 12884901888 | bytes 6291456 | tf_op jit(solution)/shard_map/attend_back/pallas_call | solution.py:297
  605.1 6.7 leave.7
  611.8 2.7 fusion.57
  616.4 3.0 fusion.66
  629.1 4.5 copy.144
  634.1 7.6 collective-permute-done.20
  641.7 2.8 broadcast_select_fusion.52
  644.6 2.8 collective-permute-start.24
  648.3 4.0 collective-permute-start.26
  653.7 42.4 %collective-permute-done.24 = bf16[256,768]{1,0:T(8,128)(2,1)S(1)} collective-permute-done((bf16[256,768]{1,0:T(8,128)(2,1)}, bf16[256,768]{1,0:T(8,128)(2,1)S(1)}, u32[]{:S(2)}, u32[]{:S(2)}) %collective-permute-start.24) | collective-permute-done | bytes 393248 | tf_op jit(solution)/shard_map/ppermute | solution.py:448
  696.2 27.2 %collective-permute-done.26 = bf16[256,768]{1,0:T(8,128)(2,1)S(1)} collective-permute-done((bf16[256,768]{1,0:T(8,128)(2,1)S(1)}, bf16[256,768]{1,0:T(8,128)(2,1)S(1)}, u32[]{:S(2)}, u32[]{:S(2)}) %collective-permute-start.26) | collective-permute-done | bytes 393248 | tf_op jit(solution)/shard_map/ppermute | solution.py:448
  728.2 2.8 fusion.62
  731.3 5.2 fusion.47
  736.5 2.8 fusion.39
  739.5 4.4 copy.142
  747.9 38.9 %psum.14 = f32[2,3840]{1,0:T(2,128)S(1)} all-reduce(f32[2,3840]{1,0:T(2,128)S(1)} %pad_maximum_fusion.32), channel_id=1, replica_groups=mesh['section'=2,'wide'=4,'tp'=4] {'section','wide','tp'}, use_global_device_ids=true, to_apply=%region_20.21 | all-reduce | flops 7680 | bytes 61440 | tf_op jit(solution)/shard_map/psum | solution.py:690
  786.9 36.9 %psum.15 = f32[2,1344]{1,0:T(2,128)S(1)} all-reduce(f32[2,1344]{1,0:T(2,128)S(1)} %pad_maximum_fusion.35), channel_id=1, replica_groups=mesh['section'=2,'wide'=4,'tp'=4] {'section','wide'}, use_global_device_ids=true, to_apply=%region_23.24 | all-reduce | flops 2688 | bytes 21504 | tf_op jit(solution)/shard_map/psum | solution.py:693
  828.9 4.2 collective-permute-done.36
  833.6 3.8 collective-permute-done.46
  848.9 13.7 %collective-permute-done.50 = bf16[256,768]{1,0:T(8,128)(2,1)S(1)} collective-permute-done((bf16[256,768]{1,0:T(8,128)(2,1)S(1)}, bf16[256,768]{1,0:T(8,128)(2,1)S(1)}, u32[]{:S(2)}, u32[]{:S(2)}) %collective-permute-start.50) | collective-permute-done | bytes 393248 | tf_op jit(solution)/shard_map/ppermute | solution.py:448
  862.6 2.9 collective-permute-done.49
  866.5 6.9 collective-permute-done.47
  885.6 13.2 %collective-permute-done.51 = bf16[192,576]{0,1:T(8,128)(2,1)S(1)} collective-permute-done((bf16[192,576]{0,1:T(8,128)(2,1)S(1)}, bf16[192,576]{0,1:T(8,128)(2,1)S(1)}, u32[]{:S(2)}, u32[]{:S(2)}) %collective-permute-start.51) | collective-permute-done | bytes 221216 | tf_op jit(solution)/shard_map/ppermute | solution.py:469
  (807 shorter events, 258.4 us)
Async XLA Ops:
  7.2 158.7 %all-gather.7.cloned.1.call-start = ((), (), s32[]{:S(2)}) async-start(), calls=%async_computation.5 | async-start | bytes 1966080 | tf_op jit(solution)/shard_map/all_gather | solution.py:556
  9.5 10.9 %collective-permute-start.10 = (bf16[192,960]{1,0:T(8,128)(2,1)S(1)}, bf16[192,960]{1,0:T(8,128)(2,1)S(1)}, u32[]{:S(2)}, u32[]{:S(2)}) collective-permute-start(bf16[192,960]{1,0:T(8,128)(2,1)S(1)} %pad_maximum_fusion.31), channel_id=1, source_target_pairs={{0,16},{16,0},{1,17},{17,1},{2,18},{18,2},{3,19},{19,3},{4,20},{20... | collective-permute-start | bytes 1105928 | tf_op jit(solution)/shard_map/ppermute | solution.py:469
  22.6 146.2 %all-gather.11.cloned.1.call-start = ((), (), s32[]{:S(2)}) async-start(), calls=%async_computation.7 | async-start | bytes 1966080 | tf_op jit(solution)/shard_map/all_gather | solution.py:556
  23.4 174.6 %all-gather.5.cloned.1.call-start = ((), (), s32[]{:S(2)}) async-start(), calls=%async_computation.4 | async-start | bytes 2703360 | tf_op jit(solution)/shard_map/all_gather | solution.py:553
  24.4 68.1 %collective-permute-start.7 = (bf16[256,768]{1,0:T(8,128)(2,1)}, bf16[256,768]{1,0:T(8,128)(2,1)}, u32[]{:S(2)}, u32[]{:S(2)}) collective-permute-start(bf16[256,768]{1,0:T(8,128)(2,1)} %get-tuple-element.324), channel_id=1, source_target_pairs={{0,0},{1,4},{2,8},{3,12},{4,1},{5,5},{6,9},{7,13},{16,16},{17,20},... | collective-permute-start | bytes 1179656 | tf_op jit(solution)/shard_map/ppermute | solution.py:426
  29.5 68.0 %collective-permute-start.1 = (bf16[256,768]{1,0:T(8,128)(2,1)}, bf16[256,768]{1,0:T(8,128)(2,1)}, u32[]{:S(2)}, u32[]{:S(2)}) collective-permute-start(bf16[256,768]{1,0:T(8,128)(2,1)} %get-tuple-element.324), channel_id=1, source_target_pairs={{8,0},{9,4},{10,8},{11,12},{12,1},{13,5},{14,9},{15,13},{24,16},{2... | collective-permute-start | bytes 1179656 | tf_op jit(solution)/shard_map/ppermute | solution.py:426
  31.0 62.2 %collective-permute-start.6 = (bf16[256,768]{1,0:T(8,128)(2,1)}, bf16[256,768]{1,0:T(8,128)(2,1)}, u32[]{:S(2)}, u32[]{:S(2)}) collective-permute-start(bf16[256,768]{1,0:T(8,128)(2,1)} %get-tuple-element.325), channel_id=1, source_target_pairs={{0,2},{1,6},{2,10},{3,14},{4,3},{5,7},{6,11},{7,15},{16,18},{17,22... | collective-permute-start | bytes 1179656 | tf_op jit(solution)/shard_map/ppermute | solution.py:426
  33.3 65.5 %collective-permute-start = (bf16[256,768]{1,0:T(8,128)(2,1)}, bf16[256,768]{1,0:T(8,128)(2,1)}, u32[]{:S(2)}, u32[]{:S(2)}) collective-permute-start(bf16[256,768]{1,0:T(8,128)(2,1)} %get-tuple-element.325), channel_id=1, source_target_pairs={{8,2},{9,6},{10,10},{11,14},{12,3},{13,7},{14,11},{15,15},{24,18},... | collective-permute-start | bytes 1179656 | tf_op jit(solution)/shard_map/ppermute | solution.py:426
  36.0 35.7 %collective-permute-start.5 = (bf16[192,1344]{1,0:T(8,128)(2,1)}, bf16[192,1344]{1,0:T(8,128)(2,1)}, u32[]{:S(2)}, u32[]{:S(2)}) collective-permute-start(bf16[192,1344]{1,0:T(8,128)(2,1)} %pad_maximum_fusion.26), channel_id=1, source_target_pairs={{0,16},{16,0},{1,17},{17,1},{2,18},{18,2},{3,19},{19,3},{4,20},{20... | collective-permute-start | bytes 1548296 | tf_op jit(solution)/shard_map/ppermute | solution.py:469
  71.6 133.2 %copy-start.3 = (f32[1024,256]{1,0:T(8,128)}, f32[1024,256]{1,0:T(8,128)S(1)}, u32[]{:S(2)}) copy-start(f32[1024,256]{1,0:T(8,128)S(1)} %get-tuple-element.260.c_ref) | copy-start | bytes 3145732
  71.6 11.7 %collective-permute-start.4 = (f32[5184]{0:T(1024)S(1)}, f32[5184]{0:T(1024)S(1)}, u32[]{:S(2)}, u32[]{:S(2)}) collective-permute-start(f32[5184]{0:T(1024)S(1)} %concatenate.259), channel_id=1, source_target_pairs={{0,16},{16,0},{1,17},{17,1},{2,18},{18,2},{3,19},{19,3},{4,20},{20... | collective-permute-start | bytes 62216 | tf_op jit(solution)/shard_map/ppermute | solution.py:469
  74.6 229.9 %all-gather.9.cloned.1.call-start = ((), (), s32[]{:S(2)}) async-start(), calls=%async_computation.6 | async-start | bytes 2703360 | tf_op jit(solution)/shard_map/all_gather | solution.py:553
  83.4 18.6 %collective-permute-start.38 = (bf16[256,768]{1,0:T(8,128)(2,1)}, bf16[256,768]{1,0:T(8,128)(2,1)S(1)}, u32[]{:S(2)}, u32[]{:S(2)}) collective-permute-start(bf16[256,768]{1,0:T(8,128)(2,1)} %get-tuple-element.308), channel_id=1, source_target_pairs={{0,0},{1,4},{2,8},{3,12},{4,1},{5,5},{6,9},{7,13},{16,16},{17,20},... | collective-permute-start | bytes 1179656 | tf_op jit(solution)/shard_map/ppermute | solution.py:426
  91.9 148.0 %copy-start.91 = (f32[4,768]{1,0:T(4,128)}, f32[4,768]{1,0:T(4,128)S(1)}, u32[]{:S(2)}) copy-start(f32[4,768]{1,0:T(4,128)S(1)} %reshape.572.gs_ref) | copy-start | bytes 36868
  92.5 26.5 %collective-permute-start.28 = (bf16[256,768]{1,0:T(8,128)(2,1)}, bf16[256,768]{1,0:T(8,128)(2,1)S(1)}, u32[]{:S(2)}, u32[]{:S(2)}) collective-permute-start(bf16[256,768]{1,0:T(8,128)(2,1)} %get-tuple-element.308), channel_id=1, source_target_pairs={{8,0},{9,4},{10,8},{11,12},{12,1},{13,5},{14,9},{15,13},{24,16},{2... | collective-permute-start | bytes 1179656 | tf_op jit(solution)/shard_map/ppermute | solution.py:426
  93.2 25.6 %collective-permute-start.37 = (bf16[256,768]{1,0:T(8,128)(2,1)}, bf16[256,768]{1,0:T(8,128)(2,1)S(1)}, u32[]{:S(2)}, u32[]{:S(2)}) collective-permute-start(bf16[256,768]{1,0:T(8,128)(2,1)} %get-tuple-element.309), channel_id=1, source_target_pairs={{0,2},{1,6},{2,10},{3,14},{4,3},{5,7},{6,11},{7,15},{16,18},{17,22... | collective-permute-start | bytes 1179656 | tf_op jit(solution)/shard_map/ppermute | solution.py:426
  97.5 55.0 %collective-permute-start.27 = (bf16[256,768]{1,0:T(8,128)(2,1)S(1)}, bf16[256,768]{1,0:T(8,128)(2,1)S(1)}, u32[]{:S(2)}, u32[]{:S(2)}) collective-permute-start(bf16[256,768]{1,0:T(8,128)(2,1)S(1)} %copy-done.213), channel_id=1, source_target_pairs={{8,2},{9,6},{10,10},{11,14},{12,3},{13,7},{14,11},{15,15},{24,18},... | collective-permute-start | bytes 1179656 | tf_op jit(solution)/shard_map/ppermute | solution.py:426
  98.8 57.9 %collective-permute-start.8 = (bf16[256,768]{1,0:T(8,128)(2,1)S(1)}, bf16[256,768]{1,0:T(8,128)(2,1)}, u32[]{:S(2)}, u32[]{:S(2)}) collective-permute-start(bf16[256,768]{1,0:T(8,128)(2,1)S(1)} %get-tuple-element.235), channel_id=1, source_target_pairs={{0,2},{1,3},{2,0},{3,1},{4,6},{5,7},{6,4},{7,5},{8,10},{9,11},{10,... | collective-permute-start | bytes 1179656 | tf_op jit(solution)/shard_map/ppermute | solution.py:473
  102.0 56.6 %collective-permute-start.2 = (bf16[256,768]{1,0:T(8,128)(2,1)S(1)}, bf16[256,768]{1,0:T(8,128)(2,1)}, u32[]{:S(2)}, u32[]{:S(2)}) collective-permute-start(bf16[256,768]{1,0:T(8,128)(2,1)S(1)} %get-tuple-element.241), channel_id=1, source_target_pairs={{0,2},{1,3},{2,0},{3,1},{4,6},{5,7},{6,4},{7,5},{8,10},{9,11},{10,... | collective-permute-start | bytes 1179656 | tf_op jit(solution)/shard_map/ppermute | solution.py:473
  118.9 35.7 %collective-permute-start.39 = (bf16[256,768]{1,0:T(8,128)(2,1)S(1)}, bf16[256,768]{1,0:T(8,128)(2,1)}, u32[]{:S(2)}, u32[]{:S(2)}) collective-permute-start(bf16[256,768]{1,0:T(8,128)(2,1)S(1)} %get-tuple-element.229), channel_id=1, source_target_pairs={{0,2},{1,3},{2,0},{3,1},{4,6},{5,7},{6,4},{7,5},{8,10},{9,11},{10,... | collective-permute-start | bytes 1179656 | tf_op jit(solution)/shard_map/ppermute | solution.py:473
  152.6 7.9 collective-permute-start.29
  154.6 571.8 %reduce-scatter.15.cloned.1.call-start = ((), (), s32[]{:S(2)}) async-start(), calls=%async_computation.9 | async-start | bytes 1228800
  156.8 142.1 %collective-permute-start.40 = (bf16[512,768]{1,0:T(8,128)(2,1)}, bf16[512,768]{1,0:T(8,128)(2,1)}, u32[]{:S(2)}, u32[]{:S(2)}) collective-permute-start(bf16[512,768]{1,0:T(8,128)(2,1)} %pad_maximum_fusion.22), channel_id=1, source_target_pairs={{0,1},{1,0},{2,3},{3,2},{4,5},{5,4},{6,7},{7,6},{8,9},{9,8},{10,11... | collective-permute-start | bytes 2359304 | tf_op jit(solution)/shard_map/ppermute | solution.py:473
  157.9 4.7 collective-permute-start.9
  159.6 4.6 collective-permute-start.3
  162.7 125.6 %collective-permute-start.30 = (bf16[512,768]{1,0:T(8,128)(2,1)}, bf16[512,768]{1,0:T(8,128)(2,1)}, u32[]{:S(2)}, u32[]{:S(2)}) collective-permute-start(bf16[512,768]{1,0:T(8,128)(2,1)} %pad_maximum_fusion.20), channel_id=1, source_target_pairs={{0,1},{1,0},{2,3},{3,2},{4,5},{5,4},{6,7},{7,6},{8,9},{9,8},{10,11... | collective-permute-start | bytes 2359304 | tf_op jit(solution)/shard_map/ppermute | solution.py:473
  239.9 52.5 %collective-permute-start.15 = (bf16[512,768]{1,0:T(8,128)(2,1)}, bf16[512,768]{1,0:T(8,128)(2,1)}, u32[]{:S(2)}, u32[]{:S(2)}) collective-permute-start(bf16[512,768]{1,0:T(8,128)(2,1)} %broadcast_select_fusion.17), channel_id=1, source_target_pairs={{0,1},{1,0},{2,3},{3,2},{4,5},{5,4},{6,7},{7,6},{8,9},{9,8},{10,11... | collective-permute-start | bytes 2359304 | tf_op jit(solution)/shard_map/ppermute | solution.py:486
  288.1 8.1 collective-permute-start.11
  295.6 17.3 %collective-permute-start.16 = (bf16[256,768]{1,0:T(8,128)(2,1)}, bf16[256,768]{1,0:T(8,128)(2,1)}, u32[]{:S(2)}, u32[]{:S(2)}) collective-permute-start(bf16[256,768]{1,0:T(8,128)(2,1)} %select_convert_fusion.6), channel_id=1, source_target_pairs={{0,2},{1,3},{2,0},{3,1},{4,6},{5,7},{6,4},{7,5},{8,10},{9,11},{10,... | collective-permute-start | bytes 1179656 | tf_op jit(solution)/shard_map/ppermute | solution.py:486
  297.4 18.2 %collective-permute-start.12 = (bf16[256,768]{1,0:T(8,128)(2,1)}, bf16[256,768]{1,0:T(8,128)(2,1)}, u32[]{:S(2)}, u32[]{:S(2)}) collective-permute-start(bf16[256,768]{1,0:T(8,128)(2,1)} %select_convert_fusion.7), channel_id=1, source_target_pairs={{0,2},{1,3},{2,0},{3,1},{4,6},{5,7},{6,4},{7,5},{8,10},{9,11},{10,... | collective-permute-start | bytes 1179656 | tf_op jit(solution)/shard_map/ppermute | solution.py:486
  318.5 12.1 %collective-permute-start.13 = (bf16[256,768]{1,0:T(8,128)(2,1)S(1)}, bf16[256,768]{1,0:T(8,128)(2,1)S(1)}, u32[]{:S(2)}, u32[]{:S(2)}) collective-permute-start(bf16[256,768]{1,0:T(8,128)(2,1)S(1)} %get-tuple-element.341), channel_id=1, source_target_pairs={{0,2},{1,3},{2,0},{3,1},{4,6},{5,7},{6,4},{7,5},{8,10},{9,11},{10,... | collective-permute-start | bytes 1179656 | tf_op jit(solution)/shard_map/ppermute | solution.py:473
  319.1 18.2 %collective-permute-start.17 = (bf16[256,768]{1,0:T(8,128)(2,1)S(1)}, bf16[256,768]{1,0:T(8,128)(2,1)S(1)}, u32[]{:S(2)}, u32[]{:S(2)}) collective-permute-start(bf16[256,768]{1,0:T(8,128)(2,1)S(1)} %get-tuple-element.238), channel_id=1, source_target_pairs={{0,2},{1,3},{2,0},{3,1},{4,6},{5,7},{6,4},{7,5},{8,10},{9,11},{10,... | collective-permute-start | bytes 1179656 | tf_op jit(solution)/shard_map/ppermute | solution.py:473
  330.8 8.2 collective-permute-start.14
  338.4 16.1 %collective-permute-start.18 = (bf16[512,768]{1,0:T(8,128)(2,1)}, bf16[512,768]{1,0:T(8,128)(2,1)}, u32[]{:S(2)}, u32[]{:S(2)}) collective-permute-start(bf16[512,768]{1,0:T(8,128)(2,1)} %pad_maximum_fusion.17), channel_id=1, source_target_pairs={{0,1},{1,0},{2,3},{3,2},{4,5},{5,4},{6,7},{7,6},{8,9},{9,8},{10,11... | collective-permute-start | bytes 2359304 | tf_op jit(solution)/shard_map/ppermute | solution.py:473
  393.2 226.2 %collective-permute-start.21 = (bf16[512,768]{1,0:T(8,128)(2,1)}, bf16[512,768]{1,0:T(8,128)(2,1)}, u32[]{:S(2)}, u32[]{:S(2)}) collective-permute-start(bf16[512,768]{1,0:T(8,128)(2,1)} %broadcast_select_fusion.13), channel_id=1, source_target_pairs={{0,1},{1,0},{2,3},{3,2},{4,5},{5,4},{6,7},{7,6},{8,9},{9,8},{10,11... | collective-permute-start | bytes 2359304 | tf_op jit(solution)/shard_map/ppermute | solution.py:486
  433.0 189.4 %collective-permute-start.19 = (bf16[512,768]{1,0:T(8,128)(2,1)}, bf16[512,768]{1,0:T(8,128)(2,1)}, u32[]{:S(2)}, u32[]{:S(2)}) collective-permute-start(bf16[512,768]{1,0:T(8,128)(2,1)} %broadcast_select_fusion.14), channel_id=1, source_target_pairs={{0,1},{1,0},{2,3},{3,2},{4,5},{5,4},{6,7},{7,6},{8,9},{9,8},{10,11... | collective-permute-start | bytes 2359304 | tf_op jit(solution)/shard_map/ppermute | solution.py:486
  502.3 10.5 %collective-permute-start.31 = (bf16[512,768]{1,0:T(8,128)(2,1)}, bf16[512,768]{1,0:T(8,128)(2,1)}, u32[]{:S(2)}, u32[]{:S(2)}) collective-permute-start(bf16[512,768]{1,0:T(8,128)(2,1)} %broadcast_select_fusion.10), channel_id=1, source_target_pairs={{0,1},{1,0},{2,3},{3,2},{4,5},{5,4},{6,7},{7,6},{8,9},{9,8},{10,11... | collective-permute-start | bytes 2359304 | tf_op jit(solution)/shard_map/ppermute | solution.py:486
  502.4 13.2 %collective-permute-start.41 = (bf16[512,768]{1,0:T(8,128)(2,1)}, bf16[512,768]{1,0:T(8,128)(2,1)}, u32[]{:S(2)}, u32[]{:S(2)}) collective-permute-start(bf16[512,768]{1,0:T(8,128)(2,1)} %broadcast_select_fusion.4), channel_id=1, source_target_pairs={{0,1},{1,0},{2,3},{3,2},{4,5},{5,4},{6,7},{7,6},{8,9},{9,8},{10,11... | collective-permute-start | bytes 2359304 | tf_op jit(solution)/shard_map/ppermute | solution.py:486
  512.6 361.7 %reduce-scatter.13.cloned.1.call-start = ((), (), s32[]{:S(2)}) async-start(), calls=%async_computation.8 | async-start | bytes 1228800
  514.9 12.0 %collective-permute-start.32 = (bf16[256,768]{1,0:T(8,128)(2,1)S(1)}, bf16[256,768]{1,0:T(8,128)(2,1)S(1)}, u32[]{:S(2)}, u32[]{:S(2)}) collective-permute-start(bf16[256,768]{1,0:T(8,128)(2,1)S(1)} %select_convert_fusion.3), channel_id=1, source_target_pairs={{0,2},{1,3},{2,0},{3,1},{4,6},{5,7},{6,4},{7,5},{8,10},{9,11},{10,... | collective-permute-start | bytes 1179656 | tf_op jit(solution)/shard_map/ppermute | solution.py:486
  517.1 18.3 %collective-permute-start.42 = (bf16[256,768]{1,0:T(8,128)(2,1)S(1)}, bf16[256,768]{1,0:T(8,128)(2,1)S(1)}, u32[]{:S(2)}, u32[]{:S(2)}) collective-permute-start(bf16[256,768]{1,0:T(8,128)(2,1)S(1)} %select_convert_fusion.1), channel_id=1, source_target_pairs={{0,2},{1,3},{2,0},{3,1},{4,6},{5,7},{6,4},{7,5},{8,10},{9,11},{10,... | collective-permute-start | bytes 1179656 | tf_op jit(solution)/shard_map/ppermute | solution.py:486
  527.8 16.0 %collective-permute-start.33 = (bf16[256,768]{1,0:T(8,128)(2,1)S(1)}, bf16[256,768]{1,0:T(8,128)(2,1)S(1)}, u32[]{:S(2)}, u32[]{:S(2)}) collective-permute-start(bf16[256,768]{1,0:T(8,128)(2,1)S(1)} %get-tuple-element.223), channel_id=1, source_target_pairs={{0,2},{1,3},{2,0},{3,1},{4,6},{5,7},{6,4},{7,5},{8,10},{9,11},{10,... | collective-permute-start | bytes 1179656 | tf_op jit(solution)/shard_map/ppermute | solution.py:473
  536.3 15.1 %collective-permute-start.43 = (bf16[256,768]{1,0:T(8,128)(2,1)S(1)}, bf16[256,768]{1,0:T(8,128)(2,1)S(1)}, u32[]{:S(2)}, u32[]{:S(2)}) collective-permute-start(bf16[256,768]{1,0:T(8,128)(2,1)S(1)} %get-tuple-element.225), channel_id=1, source_target_pairs={{0,2},{1,3},{2,0},{3,1},{4,6},{5,7},{6,4},{7,5},{8,10},{9,11},{10,... | collective-permute-start | bytes 1179656 | tf_op jit(solution)/shard_map/ppermute | solution.py:473
  544.0 7.7 collective-permute-start.34
  551.5 30.6 %collective-permute-start.44 = (bf16[512,768]{1,0:T(8,128)(2,1)S(1)}, bf16[512,768]{1,0:T(8,128)(2,1)S(1)}, u32[]{:S(2)}, u32[]{:S(2)}) collective-permute-start(bf16[512,768]{1,0:T(8,128)(2,1)S(1)} %pad_maximum_fusion.23), channel_id=1, source_target_pairs={{0,1},{1,0},{2,3},{3,2},{4,5},{5,4},{6,7},{7,6},{8,9},{9,8},{10,11... | collective-permute-start | bytes 2359304 | tf_op jit(solution)/shard_map/ppermute | solution.py:473
  616.3 259.1 %reduce-scatter.19.cloned.1.call-start = ((), (), s32[]{:S(2)}) async-start(), calls=%async_computation.11 | async-start | bytes 3440640
  621.8 12.3 %collective-permute-start.22 = (bf16[256,768]{1,0:T(8,128)(2,1)}, bf16[256,768]{1,0:T(8,128)(2,1)}, u32[]{:S(2)}, u32[]{:S(2)}) collective-permute-start(bf16[256,768]{1,0:T(8,128)(2,1)} %select_convert_fusion.4), channel_id=1, source_target_pairs={{0,2},{1,3},{2,0},{3,1},{4,6},{5,7},{6,4},{7,5},{8,10},{9,11},{10,... | collective-permute-start | bytes 1179656 | tf_op jit(solution)/shard_map/ppermute | solution.py:486
  625.9 15.8 %collective-permute-start.20 = (bf16[256,768]{1,0:T(8,128)(2,1)}, bf16[256,768]{1,0:T(8,128)(2,1)}, u32[]{:S(2)}, u32[]{:S(2)}) collective-permute-start(bf16[256,768]{1,0:T(8,128)(2,1)} %select_convert_fusion.5), channel_id=1, source_target_pairs={{0,2},{1,3},{2,0},{3,1},{4,6},{5,7},{6,4},{7,5},{8,10},{9,11},{10,... | collective-permute-start | bytes 1179656 | tf_op jit(solution)/shard_map/ppermute | solution.py:486
  633.6 243.3 %reduce-scatter.17.cloned.1.call-start = ((), (), s32[]{:S(2)}) async-start(), calls=%async_computation.10 | async-start | bytes 3440640
  644.6 51.6 %collective-permute-start.24 = (bf16[256,768]{1,0:T(8,128)(2,1)}, bf16[256,768]{1,0:T(8,128)(2,1)S(1)}, u32[]{:S(2)}, u32[]{:S(2)}) collective-permute-start(bf16[256,768]{1,0:T(8,128)(2,1)} %get-tuple-element.245), channel_id=1, source_target_pairs={{0,0},{16,16},{4,1},{20,17},{8,2},{24,18},{12,3},{28,19},{1,4},{17... | collective-permute-start | bytes 1179656 | tf_op jit(solution)/shard_map/ppermute | solution.py:448
  648.2 47.9 %collective-permute-start.23 = (bf16[256,768]{1,0:T(8,128)(2,1)}, bf16[256,768]{1,0:T(8,128)(2,1)S(1)}, u32[]{:S(2)}, u32[]{:S(2)}) collective-permute-start(bf16[256,768]{1,0:T(8,128)(2,1)} %get-tuple-element.279), channel_id=1, source_target_pairs={{2,0},{18,16},{6,1},{22,17},{10,2},{26,18},{14,3},{30,19},{3,4},{1... | collective-permute-start | bytes 1179656 | tf_op jit(solution)/shard_map/ppermute | solution.py:448
  648.3 75.1 %collective-permute-start.26 = (bf16[256,768]{1,0:T(8,128)(2,1)S(1)}, bf16[256,768]{1,0:T(8,128)(2,1)S(1)}, u32[]{:S(2)}, u32[]{:S(2)}) collective-permute-start(bf16[256,768]{1,0:T(8,128)(2,1)S(1)} %get-tuple-element.280), channel_id=1, source_target_pairs={{0,16},{16,0},{4,17},{20,1},{8,18},{24,2},{12,19},{28,3},{1,20},{1... | collective-permute-start | bytes 1179656 | tf_op jit(solution)/shard_map/ppermute | solution.py:448
  652.4 72.3 %collective-permute-start.25 = (bf16[256,768]{1,0:T(8,128)(2,1)S(1)}, bf16[256,768]{1,0:T(8,128)(2,1)S(1)}, u32[]{:S(2)}, u32[]{:S(2)}) collective-permute-start(bf16[256,768]{1,0:T(8,128)(2,1)S(1)} %get-tuple-element.281), channel_id=1, source_target_pairs={{2,16},{18,0},{6,17},{22,1},{10,18},{26,2},{14,19},{30,3},{3,20},{... | collective-permute-start | bytes 1179656 | tf_op jit(solution)/shard_map/ppermute | solution.py:448
  746.3 77.4 %collective-permute-start.35 = (bf16[512,768]{1,0:T(8,128)(2,1)}, bf16[512,768]{1,0:T(8,128)(2,1)}, u32[]{:S(2)}, u32[]{:S(2)}) collective-permute-start(bf16[512,768]{1,0:T(8,128)(2,1)} %broadcast_select_fusion.7), channel_id=1, source_target_pairs={{0,1},{1,0},{2,3},{3,2},{4,5},{5,4},{6,7},{7,6},{8,9},{9,8},{10,11... | collective-permute-start | bytes 2359304 | tf_op jit(solution)/shard_map/ppermute | solution.py:486
  747.3 76.4 %copy-start.165 = (bf16[1024,768]{1,0:T(8,128)(2,1)S(1)}, bf16[1024,768]{1,0:T(8,128)(2,1)}, u32[]{:S(2)}) copy-start(bf16[1024,768]{1,0:T(8,128)(2,1)} %get-tuple-element.123) | copy-start | bytes 4718596
  747.3 79.4 %collective-permute-start.45 = (bf16[512,768]{1,0:T(8,128)(2,1)}, bf16[512,768]{1,0:T(8,128)(2,1)}, u32[]{:S(2)}, u32[]{:S(2)}) collective-permute-start(bf16[512,768]{1,0:T(8,128)(2,1)} %broadcast_select_fusion.1), channel_id=1, source_target_pairs={{0,1},{1,0},{2,3},{3,2},{4,5},{5,4},{6,7},{7,6},{8,9},{9,8},{10,11... | collective-permute-start | bytes 2359304 | tf_op jit(solution)/shard_map/ppermute | solution.py:486
  825.3 7.8 collective-permute-start.36
  828.2 9.1 collective-permute-start.46
  839.0 23.6 %collective-permute-start.50 = (bf16[256,768]{1,0:T(8,128)(2,1)S(1)}, bf16[256,768]{1,0:T(8,128)(2,1)S(1)}, u32[]{:S(2)}, u32[]{:S(2)}) collective-permute-start(bf16[256,768]{1,0:T(8,128)(2,1)S(1)} %get-tuple-element.267), channel_id=1, source_target_pairs={{0,16},{16,0},{4,17},{20,1},{8,18},{24,2},{12,19},{28,3},{1,20},{1... | collective-permute-start | bytes 1179656 | tf_op jit(solution)/shard_map/ppermute | solution.py:448
  839.6 26.0 %collective-permute-start.49 = (bf16[256,768]{1,0:T(8,128)(2,1)S(1)}, bf16[256,768]{1,0:T(8,128)(2,1)S(1)}, u32[]{:S(2)}, u32[]{:S(2)}) collective-permute-start(bf16[256,768]{1,0:T(8,128)(2,1)S(1)} %get-tuple-element.268), channel_id=1, source_target_pairs={{2,16},{18,0},{6,17},{22,1},{10,18},{26,2},{14,19},{30,3},{3,20},{... | collective-permute-start | bytes 1179656 | tf_op jit(solution)/shard_map/ppermute | solution.py:448
  841.9 31.5 %collective-permute-start.47 = (bf16[256,768]{1,0:T(8,128)(2,1)S(1)}, bf16[256,768]{1,0:T(8,128)(2,1)S(1)}, u32[]{:S(2)}, u32[]{:S(2)}) collective-permute-start(bf16[256,768]{1,0:T(8,128)(2,1)S(1)} %get-tuple-element.266), channel_id=1, source_target_pairs={{2,0},{18,16},{6,1},{22,17},{10,2},{26,18},{14,3},{30,19},{3,4},{1... | collective-permute-start | bytes 1179656 | tf_op jit(solution)/shard_map/ppermute | solution.py:448
  844.4 29.0 %collective-permute-start.48 = (bf16[256,768]{1,0:T(8,128)(2,1)S(1)}, bf16[256,768]{1,0:T(8,128)(2,1)S(1)}, u32[]{:S(2)}, u32[]{:S(2)}) collective-permute-start(bf16[256,768]{1,0:T(8,128)(2,1)S(1)} %get-tuple-element.230), channel_id=1, source_target_pairs={{0,0},{16,16},{4,1},{20,17},{8,2},{24,18},{12,3},{28,19},{1,4},{17... | collective-permute-start | bytes 1179656 | tf_op jit(solution)/shard_map/ppermute | solution.py:448
  879.5 20.5 %collective-permute-start.52 = (bf16[192,1728]{1,0:T(8,128)(2,1)}, bf16[192,1728]{1,0:T(8,128)(2,1)}, u32[]{:S(2)}, u32[]{:S(2)}) collective-permute-start(bf16[192,1728]{1,0:T(8,128)(2,1)} %copy.132), channel_id=1, source_target_pairs={{0,16},{16,0},{1,17},{17,1},{2,18},{18,2},{3,19},{19,3},{4,20},{20... | collective-permute-start | bytes 1990664 | tf_op jit(solution)/shard_map/ppermute | solution.py:469
  882.0 16.8 %collective-permute-start.51 = (bf16[192,576]{0,1:T(8,128)(2,1)S(1)}, bf16[192,576]{0,1:T(8,128)(2,1)S(1)}, u32[]{:S(2)}, u32[]{:S(2)}) collective-permute-start(bf16[192,576]{0,1:T(8,128)(2,1)S(1)} %broadcast_select_fusion.67), channel_id=1, source_target_pairs={{0,16},{16,0},{1,17},{17,1},{2,18},{18,2},{3,19},{19,3},{4,20},{20... | collective-permute-start | bytes 663560 | tf_op jit(solution)/shard_map/ppermute | solution.py:469
  (238 other events, 1396.4 us)
Sparse Core Ops, SparseCore 0:
  22.7 52.9 all-gather.6
  77.3 58.6 all-gather.10
  138.2 59.7 all-gather.4
  200.0 46.1 all-gather.8
  512.7 24.9 reduce-scatter.14
  616.5 24.9 reduce-scatter.12
  644.4 80.6 reduce-scatter.18
  786.9 57.6 reduce-scatter.16

commit v2 on v1

v2 whole, which is shorter than its diff:
```python
import functools

import jax
import jax.numpy as jnp
import numpy as np
from jax import lax
from jax.experimental import pallas as pl
from jax.experimental.pallas import tpu as pltpu
from jax.sharding import PartitionSpec as P

HEAD_DIM = 64
ROTARY = 16
LANES = 256
CHUNKS = 2
QUERY_BLOCK = 256
KEY_BLOCK = 512
ROW_BLOCK = 256

epsilon = 1e-05
rotary_base = 10000.0
masked_out = -1e30
f32 = jnp.float32
bf16 = jnp.bfloat16
NT = (((1,), (1,)), ((), ()))


def params(size=44):
    return pltpu.CompilerParams(
        dimension_semantics=("arbitrary",), vmem_limit_bytes=size * 1024 * 1024
    )


def dot(left, right):
    return jnp.dot(left, right, preferred_element_type=f32)


def dot_nt(left, right):
    return lax.dot_general(left, right, NT, preferred_element_type=f32)


def rows_spec(rows, columns):
    return pl.BlockSpec((rows, columns), lambda i: (i, 0))


def whole_spec(array):
    return pl.BlockSpec(array.shape, lambda i: (0,) * array.ndim)


def smem_spec():
    return pl.BlockSpec(memory_space=pltpu.SMEM)


def standardize(values):
    centred = values - jnp.mean(values, -1, keepdims=True)
    inverse = lax.rsqrt(jnp.mean(centred * centred, -1, keepdims=True) + epsilon)
    return centred * inverse, inverse


def wide_table(ref):
    return jnp.concatenate([ref[...]] * (LANES // ref.shape[1]), 1)


def halves(signed):
    place = lax.broadcasted_iota(jnp.int32, signed.shape, 1) % HEAD_DIM
    zero = jnp.zeros_like(signed)
    half = ROTARY // 2
    return jnp.where(place < half, signed, zero), jnp.where(place < half, zero, signed)


def turn(values, cosine, signed):
    half = ROTARY // 2
    low, high = halves(signed)
    ahead = pltpu.roll(values, LANES - half, 1)
    behind = pltpu.roll(values, half, 1)
    return values * cosine + ahead * low + behind * high


def turn_back(grads, cosine, signed):
    half = ROTARY // 2
    low, high = halves(signed)
    ahead = pltpu.roll(grads * high, LANES - half, 1)
    behind = pltpu.roll(grads * low, half, 1)
    return grads * cosine + ahead + behind


def any_specs(arrays):
    return [pl.BlockSpec(memory_space=pl.ANY)] * len(arrays)


def cost(micros, transfers):
    return pl.CostEstimate(
        flops=int(micros * 1.15e9), bytes_accessed=int(transfers), transcendentals=0
    )


class View:
    def __init__(self, array, first, width):
        if first % width:
            array, first = array[:, first : first + width], 0
        self.array, self.block, self.shape = array, first // width, (array.shape[0], width)

    def spec(self):
        block = self.block
        return pl.BlockSpec(self.shape, lambda i: (0, block))


def project_kernel(heads, x_ref, gs_ref, w_ref, b_ref, c_ref, s_ref, seg_ref, *rest):
    a0_ref, a1_ref, q_ref, k_ref, v_ref = rest[-5:]
    normed, _ = standardize(x_ref[...].astype(f32))
    first = (normed * gs_ref[0:1] + gs_ref[2:3]).astype(bf16)
    a0_ref[...] = first
    a1_ref[...] = (normed * gs_ref[1:2] + gs_ref[3:4]).astype(bf16)
    mixed = dot(first, w_ref[...]) + b_ref[...]
    cosine, signed = wide_table(c_ref), wide_table(s_ref)
    query = turn(mixed[:, :LANES], cosine, signed)
    keys = turn(mixed[:, LANES : 2 * LANES], cosine, signed)
    lane = lax.broadcasted_iota(jnp.int32, query.shape, 1)
    used = heads * HEAD_DIM
    mine = (lane - used) == seg_ref[...]
    spare = lane >= used
    q_ref[...] = jnp.where(
        spare, jnp.where(mine, 1.0, 0.0), query * HEAD_DIM ** (-0.5)
    ).astype(bf16)
    k_ref[...] = jnp.where(spare, jnp.where(mine, 0.0, masked_out), keys).astype(bf16)
    v_ref[...] = mixed[:, 2 * LANES :].astype(bf16)


def project(x, w, tables, seg, heads, after=()):
    tokens, width = x.shape
    rows = min(ROW_BLOCK, tokens)
    columns = (width, width, LANES, LANES, LANES)
    return pl.pallas_call(
        functools.partial(project_kernel, heads),
        grid=(tokens // rows,),
        in_specs=[rows_spec(rows, width), whole_spec(w["gs"]), w["wq"].spec()]
        + [whole_spec(w["bq"])]
        + [rows_spec(rows, item.shape[1]) for item in tables]
        + [rows_spec(rows, 1)]
        + any_specs(after),
        out_specs=[rows_spec(rows, item) for item in columns],
        out_shape=[jax.ShapeDtypeStruct((tokens, item), bf16) for item in columns],
        compiler_params=params(),
        cost_estimate=cost(4.0 * tokens / 1024, 6 * tokens * width),
        name="project",
    )(x, w["gs"], w["wq"].array, w["bq"], *tables, seg, *after)


def feed_kernel(a_ref, o_ref, wu_ref, bu_ref, wd_ref, wo_ref, *rest):
    h_ref, d_ref, part_ref = rest[-3:]
    before = dot(a_ref[...], wu_ref[...]) + bu_ref[...]
    phi = 0.5 + 0.5 * lax.erf(before * (0.5**0.5))
    density = jnp.exp(before * before * (-0.5)) * 0.3989422804014327
    hidden = (before * phi).astype(bf16)
    h_ref[...] = hidden
    d_ref[...] = (phi + before * density).astype(bf16)
    part_ref[...] = (dot_nt(hidden, wd_ref[...]) + dot_nt(o_ref[...], wo_ref[...])).astype(bf16)


def feed(a1, o, w, after=()):
    tokens, width = a1.shape
    rows = min(ROW_BLOCK, tokens)
    hidden = w["bu"].shape[1]
    columns = (hidden, hidden, width)
    return pl.pallas_call(
        feed_kernel,
        grid=(tokens // rows,),
        in_specs=[rows_spec(rows, width), rows_spec(rows, LANES), w["wu"].spec()]
        + [whole_spec(w["bu"]), w["wd"].spec(), w["wo"].spec()]
        + any_specs(after),
        out_specs=[rows_spec(rows, item) for item in columns],
        out_shape=[jax.ShapeDtypeStruct((tokens, item), bf16) for item in columns],
        compiler_params=params(),
        cost_estimate=cost(5.0 * tokens / 1024, 6 * tokens * width),
        name="feed",
    )(a1, o, w["wu"].array, w["bu"], w["wd"].array, w["wo"].array, *after)


def feed_back_kernel(gb_ref, wd_ref, d_ref, *rest):
    rest[-1][...] = (dot(gb_ref[...], wd_ref[...]) * d_ref[...].astype(f32)).astype(bf16)


def feed_back(gb, w, d, after=()):
    tokens, width = gb.shape
    rows = min(ROW_BLOCK, tokens)
    hidden = d.shape[1]
    return pl.pallas_call(
        feed_back_kernel,
        grid=(tokens // rows,),
        in_specs=[rows_spec(rows, width), w["wd"].spec(), rows_spec(rows, hidden)]
        + any_specs(after),
        out_specs=rows_spec(rows, hidden),
        out_shape=jax.ShapeDtypeStruct((tokens, hidden), bf16),
        compiler_params=params(),
        cost_estimate=cost(2.0 * tokens / 1024, 6 * tokens * width),
        name="feed_back",
    )(gb, w["wd"].array, d, *after)


def head_lanes(array, heads, spare):
    lane = lax.broadcasted_iota(jnp.int32, array.shape, 1)
    zero = jnp.zeros_like(array)
    result = []
    for head in range(heads):
        keep = (lane >= head * HEAD_DIM) & (lane < (head + 1) * HEAD_DIM)
        if spare:
            keep = keep | (lane >= heads * HEAD_DIM)
        result.append(jnp.where(keep, array, zero))
    return result


def join_once(parts, target):
    @pl.when(pl.program_id(0) == 0)
    def _():
        first = 0
        for part in parts:
            target[first : first + part.shape[0], :] = part[...]
            first += part.shape[0]


def attend_kernel(heads, key_block, pieces, start_ref, q_ref, *rest):
    k_refs, v_refs = rest[:pieces], rest[pieces : 2 * pieces]
    o_ref, lse_ref, top_ref, sum_ref, acc_ref, k_ref, vt_ref = rest[-7:]
    join_once(k_refs, k_ref)

    @pl.when(pl.program_id(0) == 0)
    def _():
        acc_ref[...] = jnp.zeros(acc_ref.shape, f32)
        first = 0
        for ref in v_refs:
            block = min(key_block, ref.shape[0])
            for at in range(0, ref.shape[0], block):
                vt_ref[:, first + at : first + at + block] = ref[at : at + block, :].T
            first += ref.shape[0]

    rows = q_ref.shape[0]
    queries = head_lanes(q_ref[...], heads, True)
    first_row = start_ref[0] + pl.program_id(0) * rows
    full = first_row // key_block

    def step(block, diagonal, fresh):
        place = pl.ds(pl.multiple_of(block * key_block, key_block), key_block)
        keys = k_ref[place, :]
        for head in range(heads):
            here = slice(head * HEAD_DIM, (head + 1) * HEAD_DIM)
            line = slice(head, head + 1)
            scores = dot_nt(keys, queries[head])
            if diagonal:
                column = lax.broadcasted_iota(jnp.int32, scores.shape, 0) + block * key_block
                row = lax.broadcasted_iota(jnp.int32, scores.shape, 1) + first_row
                scores = jnp.where(column <= row, scores, masked_out)
            top = jnp.max(scores, 0, keepdims=True)
            if not fresh:
                before = top_ref[line, :]
                top = jnp.maximum(before, top)
                fade = jnp.exp(before - top)
            probs = jnp.exp(scores - top)
            total = jnp.sum(probs, 0, keepdims=True)
            value = dot(vt_ref[here, place], probs.astype(bf16))
            if not fresh:
                total += sum_ref[line, :] * fade
                value += acc_ref[here, :] * fade
            top_ref[line, :] = top
            sum_ref[line, :] = total
            acc_ref[here, :] = value

    step(full, True, True)

    @pl.loop(0, full)
    def _(block):
        step(block, False, False)

    for head in range(heads):
        here = slice(head * HEAD_DIM, (head + 1) * HEAD_DIM)
        acc_ref[here, :] = acc_ref[here, :] / sum_ref[head : head + 1, :]
    o_ref[...] = acc_ref[...].T.astype(bf16)
    lse_ref[...] = jnp.zeros(lse_ref.shape, f32)
    lse_ref[:heads, :] = top_ref[:heads, :] + jnp.log(sum_ref[:heads, :])


def attend(start, q, keys, values, heads, after=()):
    tokens = q.shape[0]
    rows = min(QUERY_BLOCK, tokens)
    span = sum(item.shape[0] for item in keys)
    key_block = min(KEY_BLOCK, span)
    return pl.pallas_call(
        functools.partial(attend_kernel, heads, key_block, len(keys)),
        grid=(tokens // rows,),
        in_specs=[smem_spec(), rows_spec(rows, LANES)]
        + [whole_spec(item) for item in (*keys, *values)]
        + any_specs(after),
        out_specs=[rows_spec(rows, LANES), pl.BlockSpec((8, rows), lambda i: (0, i))],
        out_shape=[
            jax.ShapeDtypeStruct((tokens, LANES), bf16),
            jax.ShapeDtypeStruct((8, tokens), f32),
        ],
        scratch_shapes=[pltpu.VMEM((8, rows), f32)] * 2
        + [pltpu.VMEM((LANES, rows), f32)]
        + [pltpu.VMEM((span, LANES), bf16), pltpu.VMEM((LANES, span), bf16)],
        compiler_params=params(),
        cost_estimate=cost(7.0 * tokens * span / 1024 / 1024, 6 * tokens * LANES),
        name="attend",
    )(start, q, *keys, *values, *after)


def attend_back_kernel(
    heads, key_block, pieces, carried, start_ref, gb_ref, w_ref, q_ref, o_ref, *rest,
):
    lse_ref, rest = rest[0], rest[1:]
    k_refs, v_refs, rest = rest[:pieces], rest[pieces : 2 * pieces], rest[2 * pieces :]
    carry_refs = rest[: 2 * carried]
    dq_ref, rest = rest[-(2 * pieces + 7)], rest[-(2 * pieces + 6) :]
    dk_refs, dv_refs, rest = rest[:pieces], rest[pieces : 2 * pieces], rest[2 * pieces :]
    k_ref, v_ref, kt_ref, dk_ref, dv_ref, dqt_ref = rest
    rows = q_ref.shape[0]
    first_row = start_ref[0] + pl.program_id(0) * rows
    full = first_row // key_block
    join_once(k_refs, k_ref)
    join_once(v_refs, v_ref)

    @pl.when(pl.program_id(0) == 0)
    def _():
        dk_ref[...] = jnp.zeros(dk_ref.shape, f32)
        dv_ref[...] = jnp.zeros(dv_ref.shape, f32)
        for refs, target in ((carry_refs[:carried], dk_ref), (carry_refs[carried:], dv_ref)):
            first = 0
            for ref in refs:
                target[first : first + ref.shape[0], :] = ref[...]
                first += ref.shape[0]
        for first in range(0, k_ref.shape[0], key_block):
            kt_ref[:, first : first + key_block] = k_ref[first : first + key_block, :].T

    grad = gb_ref[...]
    grad_out = dot(grad, w_ref[...]).astype(bf16)
    product = (grad_out.astype(f32) * o_ref[...].astype(f32)).T
    centres = [
        jnp.sum(product[head * HEAD_DIM : (head + 1) * HEAD_DIM], 0, keepdims=True)
        for head in range(heads)
    ]
    queries = head_lanes(q_ref[...], heads, True)
    grads = head_lanes(grad_out, heads, False)
    dqt_ref[...] = jnp.zeros(dqt_ref.shape, f32)

    def step(block, diagonal):
        place = pl.ds(pl.multiple_of(block * key_block, key_block), key_block)
        keys = k_ref[place, :]
        values = v_ref[place, :]
        grad_keys = dk_ref[place, :]
        grad_values = dv_ref[place, :]
        for head in range(heads):
            here = slice(head * HEAD_DIM, (head + 1) * HEAD_DIM)
            scores = dot_nt(keys, queries[head])
            probs = jnp.exp(scores - lse_ref[head : head + 1, :])
            if diagonal:
                column = lax.broadcasted_iota(jnp.int32, scores.shape, 0) + block * key_block
                row = lax.broadcasted_iota(jnp.int32, scores.shape, 1) + first_row
                probs = jnp.where(column <= row, probs, 0.0)
            grad_probs = dot_nt(values, grads[head])
            grad_scores = (probs * (grad_probs - centres[head])).astype(bf16)
            grad_values += dot(probs.astype(bf16), grads[head])
            grad_keys += dot(grad_scores, queries[head])
            dqt_ref[here, :] += dot(kt_ref[here, place], grad_scores)
        dk_ref[place, :] = grad_keys
        dv_ref[place, :] = grad_values

    @pl.loop(0, full)
    def _(block):
        step(block, False)

    step(full, True)
    dq_ref[...] = dqt_ref[...].T * HEAD_DIM ** (-0.5)

    @pl.when(pl.program_id(0) == pl.num_programs(0) - 1)
    def _():
        for refs, source in ((dk_refs, dk_ref), (dv_refs, dv_ref)):
            first = 0
            for ref in refs:
                ref[...] = source[first : first + ref.shape[0], :]
                first += ref.shape[0]


def attend_back(start, gb, w, q, o, lse, keys, values, carried, heads, after=()):
    tokens, width = gb.shape
    rows = min(QUERY_BLOCK, tokens)
    sizes = [item.shape[0] for item in keys]
    span = sum(sizes)
    key_block = min(KEY_BLOCK, span)
    carry_keys, carry_values = carried
    whole = [pl.BlockSpec((size, LANES), lambda i: (0, 0)) for size in sizes]
    result = pl.pallas_call(
        functools.partial(attend_back_kernel, heads, key_block, len(keys), len(carry_keys)),
        grid=(tokens // rows,),
        in_specs=[smem_spec(), rows_spec(rows, width), w["wo"].spec()]
        + [rows_spec(rows, LANES), rows_spec(rows, LANES)]
        + [pl.BlockSpec((8, rows), lambda i: (0, i))]
        + [whole_spec(item) for item in (*keys, *values, *carry_keys, *carry_values)]
        + any_specs(after),
        out_specs=[rows_spec(rows, LANES)] + whole + whole,
        out_shape=[jax.ShapeDtypeStruct((tokens, LANES), f32)]
        + [jax.ShapeDtypeStruct((size, LANES), f32) for size in sizes] * 2,
        scratch_shapes=[pltpu.VMEM((span, LANES), bf16)] * 2
        + [pltpu.VMEM((LANES, span), bf16)]
        + [pltpu.VMEM((span, LANES), f32)] * 2
        + [pltpu.VMEM((LANES, rows), f32)],
        compiler_params=params(),
        cost_estimate=cost(12.5 * tokens * span / 1024 / 1024, 4 * tokens * width),
        name="attend_back",
    )(start, gb, w["wo"].array, q, o, lse, *keys, *values, *carry_keys, *carry_values, *after)
    pieces = len(keys)
    return result[0], result[1 : 1 + pieces], result[1 + pieces :]


def leave_kernel(
    x_ref, gs_ref, dq_ref, dk_ref, dv_ref, gu_ref, wq_ref, wu_ref, c_ref, s_ref, *rest,
):
    gm_ref, e_ref, norm_ref, mixed_ref, up_ref = rest[-5:]

    @pl.when(pl.program_id(0) == 0)
    def _():
        norm_ref[...] = jnp.zeros(norm_ref.shape, f32)
        mixed_ref[...] = jnp.zeros(mixed_ref.shape, f32)
        up_ref[...] = jnp.zeros(up_ref.shape, f32)

    cosine, signed = wide_table(c_ref), wide_table(s_ref)
    grads = jnp.concatenate(
        [
            turn_back(dq_ref[...], cosine, signed),
            turn_back(dk_ref[...], cosine, signed),
            dv_ref[...],
        ],
        1,
    ).astype(bf16)
    gm_ref[...] = grads
    grad_up = gu_ref[...]
    mixed_ref[...] += jnp.sum(grads.astype(f32), 0, keepdims=True)
    up_ref[...] += jnp.sum(grad_up.astype(f32), 0, keepdims=True)
    grad_first = dot_nt(grads, wq_ref[...])
    grad_second = dot_nt(grad_up, wu_ref[...])
    normed, _ = standardize(x_ref[...].astype(f32))
    norm_ref[0:1] += jnp.sum(grad_first * normed, 0, keepdims=True)
    norm_ref[1:2] += jnp.sum(grad_second * normed, 0, keepdims=True)
    norm_ref[2:3] += jnp.sum(grad_first, 0, keepdims=True)
    norm_ref[3:4] += jnp.sum(grad_second, 0, keepdims=True)
    e_ref[...] = (grad_first * gs_ref[0:1] + grad_second * gs_ref[1:2]).astype(bf16)


def leave(x, dq, dk, dv, gu, w, tables, after=()):
    tokens, width = x.shape
    rows = min(ROW_BLOCK, tokens)
    mixed = 3 * LANES
    hidden = gu.shape[1]
    sums = [(4, width), (1, mixed), (1, hidden)]
    return pl.pallas_call(
        leave_kernel,
        grid=(tokens // rows,),
        in_specs=[rows_spec(rows, width), whole_spec(w["gs"])]
        + [rows_spec(rows, LANES)] * 3
        + [rows_spec(rows, hidden), w["wq"].spec(), w["wu"].spec()]
        + [rows_spec(rows, item.shape[1]) for item in tables]
        + any_specs(after),
        out_specs=[rows_spec(rows, mixed), rows_spec(rows, width)]
        + [pl.BlockSpec(item, lambda i: (0, 0)) for item in sums],
        out_shape=[
            jax.ShapeDtypeStruct((tokens, mixed), bf16),
            jax.ShapeDtypeStruct((tokens, width), bf16),
        ]
        + [jax.ShapeDtypeStruct(item, f32) for item in sums],
        compiler_params=params(),
        cost_estimate=cost(6.7 * tokens / 1024, 6 * tokens * width),
        name="leave",
    )(x, w["gs"], dq, dk, dv, gu, w["wq"].array, w["wu"].array, *tables, *after)


def hold(value, token):
    first = token[(slice(0, 1),) * token.ndim].reshape((1,) * value.ndim)
    return jnp.where(first == jnp.inf, jnp.zeros_like(value), value)


def pick(bit, zero, one):
    return jnp.where(bit == 0, zero, one)


def mirrored(index, bits):
    return sum(((index >> bit) & 1) << (bits - 1 - bit) for bit in range(bits))


class Plan:
    def __init__(self, batch, length):
        self.wide, self.tp = lax.axis_size("wide"), lax.axis_size("tp")
        self.batch, self.length = batch, length
        self.bits = self.tp.bit_length() - 1
        self.group = self.wide // batch
        self.sequence_bits = batch.bit_length() - 1
        self.chunks = CHUNKS if self.group == 1 else 1
        self.unit = length // (self.wide * self.chunks)
        self.section = lax.axis_index("section")
        self.wide_index = lax.axis_index("wide")
        self.tp_index = lax.axis_index("tp")
        self.sequence = mirrored(self.wide_index // self.group, self.sequence_bits)
        self.part = mirrored(self.tp_index, self.bits)

    def units(self):
        for unit in range(self.wide * self.chunks):
            owner, half = divmod(unit, self.chunks)
            rest, part = divmod(unit, self.tp)
            sub, chunk = divmod(rest, self.chunks)
            for sequence in range(self.batch):
                place = mirrored(sequence, self.sequence_bits) * self.group + sub
                worker = place * self.tp + mirrored(part, self.bits)
                yield owner * self.tp + sequence, worker, half, chunk, part

    def to_work(self, block):
        chunks = []
        for chunk in range(self.chunks):
            result = None
            for half in range(self.chunks):
                pairs = [u[:2] for u in self.units() if u[2] == half and u[3] == chunk]
                piece = block[half * self.unit : (half + 1) * self.unit]
                piece = lax.ppermute(piece, ("wide", "tp"), pairs)
                if result is None:
                    result = piece
                else:
                    result = jnp.where(self.part % self.chunks == half, piece, result)
            chunks.append(result)
        return chunks

    def to_work_whole(self, block):
        received = []
        own = (self.wide_index * self.chunks // self.tp) % self.chunks
        for turn_index in range(self.chunks):
            piece = block[: self.unit]
            for half in range(1, self.chunks):
                here = (own - turn_index) % self.chunks == half
                piece = jnp.where(here, block[half * self.unit : (half + 1) * self.unit], piece)
            pairs = [u[:2] for u in self.units() if (u[4] + turn_index) % self.chunks == u[3]]
            received.append(lax.ppermute(piece, ("wide", "tp"), pairs))
        chunks = []
        for chunk in range(self.chunks):
            piece = received[0]
            for turn_index in range(1, self.chunks):
                here = (self.part + turn_index) % self.chunks == chunk
                piece = jnp.where(here, received[turn_index], piece)
            chunks.append(piece)
        return chunks

    def to_owner(self, chunks, layer, micro, only=None, both=False):
        devices = self.wide * self.tp
        received = {}
        for turn_index in range(self.chunks):
            for chunk in range(self.chunks) if only is None else [only]:
                pairs = []
                for owner, worker, _, held, part in self.units():
                    moved = held if only is None else only
                    if held == moved and (part + turn_index) % self.chunks == held:
                        pairs.append((micro * devices + worker, layer * devices + owner))
                        if both:
                            pairs.append(
                                ((1 - micro) * devices + worker, (1 - layer) * devices + owner)
                            )
                if only is None:
                    piece = chunks[0]
                    for other in range(1, self.chunks):
                        here = (self.part + turn_index) % self.chunks == other
                        piece = jnp.where(here, chunks[other], piece)
                else:
                    piece = chunks[only]
                received[turn_index] = lax.ppermute(piece, ("section", "wide", "tp"), pairs)
                if only is None:
                    break
        if self.chunks == 1:
            return received[0]
        chunk = (self.wide_index * self.chunks // self.tp) % self.chunks
        ordered = []
        for half in range(self.chunks):
            piece = received[0]
            for turn_index in range(1, self.chunks):
                piece = jnp.where(
                    (chunk - half) % self.chunks == turn_index, received[turn_index], piece
                )
            ordered.append(piece)
        return jnp.concatenate(ordered, 0)

    def exchange(self, first, second):
        mine = [pick(self.section, a, b) for a, b in zip(first, second)]
        other = [pick(self.section, b, a) for a, b in zip(first, second)]
        same, cross = self.to_owner(mine, 0, 0, both=True), self.to_owner(other, 1, 0, both=True)
        return jnp.stack([pick(self.section, same, cross), pick(self.section, cross, same)])

    def owned(self, chunks, layer):
        return jnp.stack([self.to_owner(chunks, layer, micro) for micro in range(2)])

    def owned_late(self, chunks, layer):
        own = (self.wide_index * self.chunks // self.tp) % self.chunks
        result = None
        for chunk in reversed(range(self.chunks)):
            part = jnp.stack([self.to_owner(chunks, layer, micro, chunk) for micro in range(2)])
            result = part if result is None else jnp.where(own == chunk, part, result)
        return result

    def wide_steps(self, value_at):
        return [
            lax.ppermute(
                value_at(step), "wide", [(index, index ^ step) for index in range(self.wide)]
            )
            for step in range(1, self.wide)
        ]

    def wide_gather(self, block):
        if self.wide > 4:
            return lax.all_gather(block, "wide", axis=0, tiled=True)
        pieces = [block] + self.wide_steps(lambda step: block)
        step = 1
        while len(pieces) > 1:
            here = (self.wide_index // step) % 2
            pieces = [
                pick(here, jnp.concatenate([a, b], 0), jnp.concatenate([b, a], 0))
                for a, b in zip(pieces[::2], pieces[1::2])
            ]
            step *= 2
        return pieces[0]

    def wide_scatter(self, block):
        if self.wide > 4:
            return lax.psum_scatter(
                block, "wide", scatter_dimension=0, tiled=True
            ).astype(f32)
        return sum(item.astype(f32) for item in self.wide_steps_of(block))

    def wide_steps_of(self, block):
        if self.wide > 4:
            return [self.wide_scatter(block)]
        rows = block.shape[0] // self.wide

        def share(step):
            first = (self.wide_index ^ step) * rows
            return lax.dynamic_slice_in_dim(block, first, rows, 0)

        return [share(0)] + self.wide_steps(share)

    def send(self, value, source):
        return lax.ppermute(value, "section", [(source, 1 - source)])

    def gather(self, block):
        for bit in reversed(range(self.bits)):
            other = lax.ppermute(
                block, "tp", [(index, index ^ (1 << bit)) for index in range(self.tp)]
            )
            here = (self.tp_index >> bit) & 1
            block = jnp.concatenate([pick(here, block, other), pick(here, other, block)], 0)
        return block

    def scatter_first(self, pieces):
        here = self.tp_index & 1
        if len(pieces) == 1:
            half = pieces[0].shape[0] // 2
            pieces = [pieces[0][:half], pieces[0][half:]]
        other = lax.ppermute(
            pick(here, pieces[1], pieces[0]), "tp", [(i, i ^ 1) for i in range(self.tp)]
        )
        return pick(here, pieces[0], pieces[1]).astype(f32) + other.astype(f32)

    def scatter_rest(self, block):
        for bit in range(1, self.bits):
            half = block.shape[0] // 2
            here = (self.tp_index >> bit) & 1
            sent = pick(here, block[half:], block[:half]).astype(bf16)
            kept = pick(here, block[:half], block[half:])
            other = lax.ppermute(
                sent, "tp", [(index, index ^ (1 << bit)) for index in range(self.tp)]
            )
            block = kept + other.astype(f32)
        return block

    def groups(self):
        return [
            [sequence * self.group + sub for sub in range(self.group)]
            for sequence in range(self.batch)
        ]

    def all_places(self, block):
        if self.group == 1:
            return block
        return lax.all_gather(block, "wide", axis=0, tiled=True, axis_index_groups=self.groups())

    def own_places(self, block):
        if self.group == 1:
            return block
        return lax.psum_scatter(
            block.astype(bf16), "wide", scatter_dimension=0, tiled=True,
            axis_index_groups=self.groups(),
        ).astype(f32)


def angle_tables(length):
    half = ROTARY // 2
    freqs = np.float32(rotary_base) ** (-(2.0 * np.arange(half, dtype=np.float32)) / ROTARY)
    turned = np.arange(length, dtype=np.float32)[:, None] * freqs[None, :].astype(np.float32)
    cosine, sine = np.cos(turned), np.sin(turned)
    rest = np.zeros((length, HEAD_DIM - ROTARY), np.float32)
    return (
        np.concatenate([cosine, cosine, rest + 1.0] * 2, 1).astype(np.float32),
        np.concatenate([-sine, sine, rest] * 2, 1).astype(np.float32),
    )


def on_device(
    inputs, cotangent, segment_ids, norm_gain, norm_shift, qkv_weight, qkv_bias, out_weight,
    out_bias, up_weight, up_bias, down_weight, down_bias,
):
    batch, length = segment_ids.shape[1], segment_ids.shape[2]
    plan = Plan(batch, length)
    width = inputs.shape[-1]
    local = qkv_weight.shape[-1]
    hidden = up_weight.shape[-1]
    heads = local // HEAD_DIM
    section = plan.section
    space = LANES - local

    fill = ((0, 0), (0, 0), (0, space))
    qkv = qkv_weight[0].reshape(-1, 3 * local)
    up = up_weight[0]
    leaving = jnp.concatenate(
        [down_weight[0].T, jnp.pad(out_weight[0].T, ((0, 0), (0, space)))], 1
    )
    small = jnp.concatenate(
        [
            norm_gain[0].reshape(-1), norm_shift[0].reshape(-1), out_bias[0] + down_bias[0],
            jnp.pad(qkv_bias[0], ((0, 0), (0, space))).reshape(-1), up_bias[0],
        ]
    )
    qkv_there = plan.send(qkv, 0)
    source = plan.to_work(jnp.where(section == 0, inputs[0, 0], inputs[1, 0]))
    small_there = lax.ppermute(small, "section", [(0, 1), (1, 0)])
    rest = jnp.concatenate([up, leaving], 1)
    share = rest.shape[0] // 2
    first = section == 0
    halves_there = [plan.send(rest[share:], 0), plan.send(rest[:share], 1)]
    half_rests = [
        jnp.where(first, rest[:share], halves_there[0]),
        jnp.where(first, halves_there[1], rest[share:]),
    ]

    def gather_rest(half):
        return lax.all_gather(half, ("wide", "section"), axis=0, tiled=True)

    def gather_qkv(value):
        value = plan.wide_gather(value).reshape(width, 3, local)
        return jnp.pad(value, fill).reshape(width, 3 * LANES)

    wq = gather_qkv(jnp.where(first, qkv, qkv_there))
    rests = [gather_rest(half_rests[0])]
    mixed = 3 * LANES
    layers = [dict(wq=View(wq, 0, mixed)), {}]

    def views(array):
        return dict(
            wu=View(array, 0, hidden), wd=View(array, hidden, hidden),
            wo=View(array, 2 * hidden, LANES),
        )

    layers[0].update(views(rests[0]))
    for layer, w in enumerate(layers):
        values = jnp.where(section == layer, small, small_there)
        at = 5 * width
        w["gs"] = values[: 4 * width].reshape(4, width)
        w["after"] = values[4 * width : at]
        w["bq"] = values[at : at + mixed].reshape(1, mixed)
        w["bu"] = values[at + mixed :].reshape(1, hidden)

    segments = lax.dynamic_index_in_dim(segment_ids, section, 0, False)
    segments = lax.dynamic_index_in_dim(segments, plan.sequence, 0, False)
    sub_length = length // plan.group
    first_place = (plan.wide_index % plan.group) * sub_length
    tables = angle_tables(length)
    if plan.group > 1:
        segments = lax.dynamic_slice_in_dim(segments, first_place, sub_length, 0)
        tables = [lax.dynamic_slice_in_dim(t, first_place, sub_length, 0) for t in tables]
    size = plan.unit * plan.tp
    starts = [(first_place + index * size).reshape(1) for index in range(plan.chunks)]
    spans = [slice(index * size, (index + 1) * size) for index in range(plan.chunks)]
    chunk_tables = [[jnp.asarray(table[span]) for table in tables] for span in spans]
    chunk_segments = [segments[span].reshape(-1, 1) for span in spans]
    last = plan.chunks - 1

    outputs, kept = [], []
    blocks = source

    def finished(index, pending, blocks, w):
        done = plan.scatter_rest(pending)
        return (blocks[index].astype(f32) + done + w["after"]).astype(bf16)

    for layer in range(2):
        w = layers[layer]
        state, after, pending = [], [], []
        keys, values = [], []
        for index in range(plan.chunks):
            x = plan.gather(blocks[index])
            a0, a1, q, k, v = project(x, w, chunk_tables[index], chunk_segments[index], heads)
            keys, values = keys + [plan.all_places(k)], values + [plan.all_places(v)]
            tied = ()
            if layer > 0 and pending:
                tied = (pending[-1],)
            o, lse = attend(starts[index], q, keys, values, heads, tied)
            state.append(dict(x=x, a0=a0, a1=a1, q=q, o=o, lse=lse, k=keys, v=values))
            if layer == 0 and index == 0:
                there = plan.send(hold(qkv, q), 1)
                there = gather_qkv(jnp.where(first, there, qkv))
                layers[1]["wq"] = View(there, 0, mixed)
                layers[1].update(views(gather_rest(hold(half_rests[1], rests[0]))))
            if layer > 0:
                if pending:
                    after.append(finished(index - 1, pending[-1], blocks, w))
                s = state[index]
                s["h"], s["d"], part = feed(a1, o, w, tuple(after))
                pending.append(plan.scatter_first([part]))
        if layer == 0:
            for index, s in enumerate(state):
                s["h"], s["d"], part = feed(s["a1"], s["o"], w)
                pending.append(plan.scatter_first([part]))
        while len(after) < plan.chunks:
            after.append(finished(len(after), pending[len(after)], blocks, w))
        kept.append((blocks, state))
        outputs.append(after)
        blocks = after

    grads = jnp.where(section == 0, cotangent[0, 0], cotangent[1, 0])
    grads = plan.to_work_whole(hold(grads, kept[1][1][0]["q"]))
    gathered = {index: plan.gather(grads[index]) for index in reversed(range(plan.chunks))}
    held = [hold(item, gathered[0]) for item in outputs[0]]
    section_outputs = plan.exchange(held, outputs[1])
    input_grads, weight_grads, small_grads = {}, {}, {}

    def over_tokens(left, right):
        left, right = jnp.concatenate(left, 0), jnp.concatenate(right, 0)
        return lax.dot_general(left, right, (((0,), (0,)), ((), ())), preferred_element_type=f32)

    for layer in reversed(range(2)):
        w = layers[layer]
        blocks, state = kept[layer]
        carried = ((), ())
        after, pending = {}, {}
        if layer == 0:
            gathered = {
                index: plan.gather(grads[index]) for index in reversed(range(plan.chunks))
            }
        every_grad = [gathered[index] for index in range(plan.chunks)]
        grad_up, grad_mixed, sums = {}, {}, 0.0
        for index in reversed(range(plan.chunks)):
            s = state[index]
            dq, dk, dv = attend_back(
                starts[index], gathered[index], w, s["q"], s["o"], s["lse"],
                s["k"], s["v"], carried, heads,
            )
            carried = (dk[:-1], dv[:-1])
            dk, dv = plan.own_places(dk[-1]), plan.own_places(dv[-1])
            if index == last:
                for other in reversed(range(plan.chunks)):
                    grad_up[other] = feed_back(gathered[other], w, state[other]["d"])
                ups = [grad_up[other] for other in range(plan.chunks)]
                early = [
                    over_tokens(every_grad, [s["o"] for s in state])[:, :local].astype(bf16),
                    over_tokens(every_grad, [s["h"] for s in state]).astype(bf16),
                    over_tokens([s["a1"] for s in state], ups).astype(bf16),
                ]
                if layer == 0:
                    early = jnp.concatenate(early, 1)
            tied = ()
            if index < last:
                tied = (pending[index + 1],)
            gm, e, norm_part, mixed_part, up_part = leave(
                s["x"], dq, dk, dv, grad_up[index], w, chunk_tables[index], tied
            )
            mixed_part = mixed_part.reshape(3, LANES)[:, :local].reshape(-1)
            sums += jnp.concatenate([norm_part.reshape(-1), mixed_part, up_part.reshape(-1)])
            pending[index] = plan.scatter_first([e])
            if layer == 0 and index == last:
                early = plan.wide_steps_of(early)
            if layer == 0 and index == last:
                held = [hold(item, dq) for item in input_grads[1]]
                owned_second = plan.owned(held, 1)
            grad_mixed[index] = gm
        for index in reversed(range(plan.chunks)):
            scaled = plan.scatter_rest(pending[index])
            normed, inverse = standardize(blocks[index].astype(f32))
            after[index] = grads[index].astype(f32) + inverse * (
                scaled
                - jnp.mean(scaled, -1, keepdims=True)
                - normed * jnp.mean(scaled * normed, -1, keepdims=True)
            )
        qkv_term = over_tokens(
            [s["a0"] for s in state], [grad_mixed[index] for index in range(plan.chunks)]
        )
        qkv_term = qkv_term.reshape(width, 3, LANES)[:, :, :local].reshape(width, 3 * local)
        if layer == 0:
            early = sum(hold(item, gm).astype(f32) for item in early)
            weight_grads[0] = [early, plan.wide_scatter(qkv_term.astype(bf16))]
        else:
            weight_grads[1] = lax.psum_scatter(
                jnp.concatenate(early + [qkv_term.astype(bf16)], 1),
                ("wide", "section"), scatter_dimension=0, tiled=True,
            )
        bias = sum(jnp.sum(item.astype(f32), 0) for item in grads)
        small_grads[layer] = jnp.concatenate([sums, bias])
        input_grads[layer] = [after[index].astype(bf16) for index in range(plan.chunks)]
        grads = input_grads[layer]

    owned_grads = [plan.owned_late(input_grads[0], 0), owned_second]
    all_grads = pick(section, *owned_grads).astype(f32)
    early, qkv_grad = [
        item + plan.send(item.astype(bf16), 1).astype(f32) for item in weight_grads[0]
    ]
    half = weight_grads[1]
    whole = jnp.concatenate([plan.send(half, 0), half], 0).astype(f32)
    split = local + 2 * hidden
    early, qkv_grad = pick(section, early, whole[:, :split]), pick(section, qkv_grad, whole[:, split:])
    out_grad, down_grad = early[:, :local], early[:, local : local + hidden]
    up_grad = early[:, local + hidden :]
    total = jnp.stack([small_grads[0], small_grads[1]])
    total = lax.all_gather(total, ("section", "wide", "tp"), axis=0)
    total = pick(section, total[:, 0], total[:, 1]).reshape(2 * plan.wide, plan.tp, -1)
    total = jnp.sum(total, 0)
    at = 4 * width + 3 * local
    own = lax.dynamic_index_in_dim(total, plan.tp_index, 0, False)[4 * width : at + hidden]
    shared = jnp.sum(total, 0)
    shared = jnp.concatenate([shared[: 4 * width], shared[at + hidden :]])
    bias_grad = shared[4 * width :]
    return (
        section_outputs[None, :, None],
        all_grads[None, :, None],
        shared[: 2 * width].reshape(1, 2, width),
        shared[2 * width : 4 * width].reshape(1, 2, width),
        qkv_grad.reshape(1, -1, 3, local),
        own[: 3 * local].reshape(1, 3, local),
        out_grad.T[None],
        bias_grad[None],
        up_grad[None],
        own[3 * local :][None],
        down_grad.T[None],
        bias_grad[None],
    )


def solution(mesh):
    return jax.shard_map(
        on_device,
        mesh=mesh,
        in_specs=(
            P(None, "tp", "wide", None),
            P(None, "tp", "wide", None),
            P(),
            P("section", None, None),
            P("section", None, None),
            P("section", "wide", None, "tp"),
            P("section", None, "tp"),
            P("section", "tp", "wide"),
            P("section", None),
            P("section", "wide", "tp"),
            P("section", "tp"),
            P("section", "tp", "wide"),
            P("section", None),
        ),
        out_specs=(
            P("section", None, "tp", "wide", None),
            P("section", None, "tp", "wide", None),
            P("section", None, None),
            P("section", None, None),
            P("section", "wide", None, "tp"),
            P("section", None, "tp"),
            P("section", "tp", "wide"),
            P("section", None),
            P("section", "wide", "tp"),
            P("section", "tp"),
            P("section", "tp", "wide"),
            P("section", None),
        ),
        check_vma=False,
    )
```

time: 927 us -> 799 us (0.86)
  starting transfers between devices: 59.8 us -> 156 us
  blocking collectives: 75.8 us -> 0 us
  local copies, waits for them, and re-layouts: 177 us -> 104 us
  waiting for transfers between devices: 256 us -> 204 us
  Pallas kernels: 201 us -> 182 us
    psum x2 -> x0, blocking collectives: 75.8 us -> none  [the longest x1 38.9 us: on_device(): lax.psum(jnp.stack([norm_grads[0], norm_grads[1]]), ('section', 'wide', '...]
    ppermute x29 -> x54, starting transfers between devices: 32 us -> 98.2 us  [the longest x16 53.5 us: to_owner(): received[turn_index] = lax.ppermute(piece, ('section', 'wide', 'tp'), pairs)]
    ppermute x16, starting transfers between devices: 4.98 us -> 49.6 us  [gather(): lax.ppermute(block, 'tp', [(index, index ^ 1 << bit) for index in range(s...]
    ppermute x8 -> x4, waiting for transfers between devices: 51.6 us -> 12.3 us  [to_work(): piece = lax.ppermute(piece, ('wide', 'tp'), pairs)]
    unnamed x496 -> x475, local copies, waits for them, and re-layouts: 94.2 us -> 57.1 us
    concatenate x7 -> x4, local copies, waits for them, and re-layouts: 31.8 us -> 1.62 us  [on_device(): jnp.concatenate([norm_part.reshape(-1), mixed_part, up_part.reshape(-1)])]
    all_gather x4 -> x3, waiting for transfers between devices: 27.2 us -> 0.04 us  [the longest x2 0.02 us: gather_rest(): return lax.all_gather(half, ('wide', 'section'), axis=0, tiled=True)]
    slice x29 -> x21, local copies, waits for them, and re-layouts: 25.3 us -> 7.05 us  [the longest x6 3.9 us: hold(): first = token[(slice(0, 1),) * token.ndim].reshape((1,) * value.ndim)]
  transfers between devices with their start and end apart: 61 -> 78, of which waited for: 23 -> 23; matrix products, arithmetic and copies ran while one was open for 23% -> 21% of each run, Pallas kernels for 20% -> 21%
where the time goes in v2:
time: 799 us; the launch traced here: 790 us
  waiting for transfers between devices  204 us (26%)
  Pallas kernels  182 us (23%)
  starting transfers between devices  156 us (20%)
  local copies, waits for them, and re-layouts  104 us (13%)
  other arithmetic  99.3 us (12%)
  matrix products  22 us (3%)
  between operations  22 us (3%)
    pallas_call x4, Pallas kernels, attend_back(): pl.pallas_call(functools.partial(attend_back_kernel, heads, key_block, le...  65.7 us
    ppermute x12, waiting for transfers between devices, wide_steps(): lax.ppermute(value_at(step), 'wide', [(index, index ^ step) for index in...  64.7 us
    unnamed x475, local copies, waits for them, and re-layouts  57.1 us
    ppermute x16, starting transfers between devices, to_owner(): received[turn_index] = lax.ppermute(piece, ('section', 'wide', 'tp'), pairs)  53.5 us
    ppermute x16, starting transfers between devices, gather(): lax.ppermute(block, 'tp', [(index, index ^ 1 << bit) for index in range(s...  49.6 us
    pallas_call x4, Pallas kernels, attend(): pl.pallas_call(functools.partial(attend_kernel, heads, key_block, len(key...  48.7 us
    ppermute x16, waiting for transfers between devices, gather(): lax.ppermute(block, 'tp', [(index, index ^ 1 << bit) for index in range(s...  43.5 us
    ppermute x8, waiting for transfers between devices, scatter_rest(): lax.ppermute(sent, 'tp', [(index, index ^ 1 << bit) for index in range(se...  35 us
  transfers between devices with their start and end apart: 78, of which 23 were waited for; matrix products, arithmetic and copies ran while one was open for 21% of the time, Pallas kernels for 21%

profile of v2, /device:TPU:4, one launch (start us, length us, event | category | flops | bytes accessed | tf_op | source)
XLA Modules:
  0.0 790.2 jit_solution(2145461190305174462)
XLA Ops:
  10.5 4.1 collective-permute-start.1
  28.2 4.0 collective-permute-done.9
  35.7 7.3 collective-permute-done
  44.2 6.1 collective-permute-start.2
  50.3 5.0 collective-permute-done.22
  57.7 17.3 %collective-permute-start.3 = (bf16[512,768]{1,0:T(8,128)(2,1)}, bf16[512,768]{1,0:T(8,128)(2,1)}, u32[]{:S(2)}, u32[]{:S(2)}) collective-permute-start(bf16[512,768]{1,0:T(8,128)(2,1)} %pad_maximum_fusion.13), channel_id=1, source_target_pairs={{0,1},{1,0},{2,3},{3,2},{4,5},{5,4},{6,7},{7,6},{8,9},{9,8},{10,11... | collective-permute-start | bytes 2359304 | tf_op jit(solution)/shard_map/ppermute | solution.py:644
  85.4 3.6 project.4
  93.5 3.6 project.6
  99.5 16.7 %attend.5 = (bf16[1024,256]{1,0:T(8,128)(2,1)S(1)}, f32[8,1024]{1,0:T(8,128)S(1)}) custom-call(s32[1]{0:T(128)} %constant.263.clone.1.start_ref, bf16[1024,256]{1,0:T(8,128)(2,1)S(1)} %get-tuple-element.96.q_ref, bf16[1024,256]{1,0:T(8,128)(2,1)S(1)} %get-tuple-element.90.rest_0_.rest_1_, bf16[1024,256]{1,0:T(8,128)(2,1)S(1)} %get-tuple-element.97.rest_1_.rest_2_, ...), custom_call_target="tpu_custom_call" | custom-call | flops 16099999744 | bytes 1572864 | tf_op jit(solution)/shard_map/attend/pallas_call | solution.py:285
  116.3 10.9 %collective-permute-start.17 = (bf16[192,576]{0,1:T(8,128)(2,1)S(1)}, bf16[192,576]{0,1:T(8,128)(2,1)S(1)}, u32[]{:S(2)}, u32[]{:S(2)}) collective-permute-start(bf16[192,576]{0,1:T(8,128)(2,1)S(1)} %broadcast_select_fusion.75), channel_id=1, source_target_pairs={{0,12},{4,8},{8,4},{12,0},{1,13},{5,9},{9,5},{13,1},{2,14},{6,10},... | collective-permute-start | bytes 663560 | tf_op jit(solution)/shard_map/ppermute | solution.py:601
  127.2 7.6 attend.4
  136.9 14.3 %collective-permute-done.16 = bf16[192,576]{0,1:T(8,128)(2,1)S(1)} collective-permute-done((bf16[192,576]{0,1:T(8,128)(2,1)S(1)}, bf16[192,576]{0,1:T(8,128)(2,1)S(1)}, u32[]{:S(2)}, u32[]{:S(2)}) %collective-permute-start.16) | collective-permute-done | bytes 221216 | tf_op jit(solution)/shard_map/ppermute | solution.py:601
  155.2 5.3 feed.5
  164.0 5.3 feed.4
  185.9 6.4 collective-permute-done.27
  192.3 7.4 collective-permute-done.11
  204.8 9.4 %collective-permute-done.12 = bf16[256,768]{1,0:T(8,128)(2,1)S(1)} collective-permute-done((bf16[256,768]{1,0:T(8,128)(2,1)S(1)}, bf16[256,768]{1,0:T(8,128)(2,1)S(1)}, u32[]{:S(2)}, u32[]{:S(2)}) %collective-permute-start.12) | collective-permute-done | bytes 393248 | tf_op jit(solution)/shard_map/ppermute | solution.py:644
  215.9 5.1 collective-permute-done.28
  223.3 3.5 project.5
  230.6 7.6 attend.6
  238.2 9.4 %collective-permute-done.19 = bf16[256,768]{1,0:T(8,128)(2,1)S(1)} collective-permute-done((bf16[256,768]{1,0:T(8,128)(2,1)S(1)}, bf16[256,768]{1,0:T(8,128)(2,1)S(1)}, u32[]{:S(2)}, u32[]{:S(2)}) %collective-permute-start.19) | collective-permute-done | bytes 393248 | tf_op jit(solution)/shard_map/ppermute | solution.py:535
  247.6 6.9 collective-permute-done.18
  257.3 9.5 %collective-permute-done.20 = bf16[256,768]{1,0:T(8,128)(2,1)S(1)} collective-permute-done((bf16[256,768]{1,0:T(8,128)(2,1)S(1)}, bf16[256,768]{1,0:T(8,128)(2,1)S(1)}, u32[]{:S(2)}, u32[]{:S(2)}) %collective-permute-start.20) | collective-permute-done | bytes 393248 | tf_op jit(solution)/shard_map/ppermute | solution.py:644
  266.9 8.3 %collective-permute-start.21 = (bf16[512,768]{1,0:T(8,128)(2,1)S(1)}, bf16[512,768]{1,0:T(8,128)(2,1)S(1)}, u32[]{:S(2)}, u32[]{:S(2)}) collective-permute-start(bf16[512,768]{1,0:T(8,128)(2,1)S(1)} %pad_maximum_fusion.15), channel_id=1, source_target_pairs={{0,1},{1,0},{2,3},{3,2},{4,5},{5,4},{6,7},{7,6},{8,9},{9,8},{10,11... | collective-permute-start | bytes 2359304 | tf_op jit(solution)/shard_map/ppermute | solution.py:644
  275.2 3.5 project.7
  289.7 5.3 feed.6
  306.2 16.7 %attend.7 = (bf16[1024,256]{1,0:T(8,128)(2,1)S(1)}, f32[8,1024]{1,0:T(8,128)S(1)}) custom-call(s32[1]{0:T(128)} %constant.263.clone.1.start_ref, bf16[1024,256]{1,0:T(8,128)(2,1)S(1)} %copy-done.118, bf16[1024,256]{1,0:T(8,128)(2,1)S(1)} %get-tuple-element.103.rest_0_.rest_1_, bf16[1024,256]{1,0:T(8,128)(2,1)S(1)} %copy-done.120, ...), custom_call_target="tpu_custom_call" | custom-call | flops 16099999744 | bytes 1572864 | tf_op jit(solution)/shard_map/attend/pallas_call | solution.py:285
  322.9 21.7 %attend_back.4 = (f32[1024,256]{1,0:T(8,128)S(1)}, f32[1024,256]{1,0:T(8,128)S(1)}, f32[1024,256]{1,0:T(8,128)S(1)}, f32[1024,256]{1,0:T(8,128)S(1)}, f32[1024,256]{1,0:T(8,128)S(1)}) custom-call(s32[1]{0:T(128)} %constant.263.clone.1.start_ref, bf16[1024,768]{1,0:T(8,128)(2,1)S(1)} %pad_maximum_fusion.9.gb_ref, ...), custom_call_target="tpu_custom_call" | custom-call | flops 28750000128 | bytes 3145728 | tf_op jit(solution)/shard_map/attend_back/pallas_call | solution.py:389
  346.5 11.4 %attend_back.5 = (f32[1024,256]{1,0:T(8,128)S(1)}, f32[1024,256]{1,0:T(8,128)S(1)}, f32[1024,256]{1,0:T(8,128)S(1)}) custom-call(s32[1]{0:T(128)} %constant.261.clone.1.start_ref, bf16[1024,768]{1,0:T(8,128)(2,1)S(1)} %pad_maximum_fusion.8.gb_ref, bf16[768,1792]{1,0:T(8,128)(2,1)} %all-gather.8.cloned.1.call-done.wu_ref.wd_ref.wo_ref.w_ref, ...), custom_call_target="tpu_custom_call" | custom-call | flops 14375000064 | bytes 3145728 | tf_op jit(solution)/shard_map/attend_back/pallas_call | solution.py:389
  362.5 5.3 feed.7
  372.4 6.1 leave.4
  382.0 3.7 fusion.41
  385.8 3.8 fusion.54
  403.6 2.5 convert_add_fusion.4.rest_0_
  406.2 6.1 leave.5
  412.3 2.7 fusion.49
  418.5 5.8 copy.97
  432.0 3.5 collective-permute-start.38
  435.5 4.0 collective-permute-done.46
  441.6 19.5 %collective-permute-done.47 = bf16[256,768]{1,0:T(8,128)(2,1)S(1)} collective-permute-done((bf16[256,768]{1,0:T(8,128)(2,1)S(1)}, bf16[256,768]{1,0:T(8,128)(2,1)S(1)}, u32[]{:S(2)}, u32[]{:S(2)}) %collective-permute-start.47) | collective-permute-done | bytes 393248 | tf_op jit(solution)/shard_map/ppermute | solution.py:644
  464.6 9.2 %collective-permute-done.43 = bf16[256,768]{1,0:T(8,128)(2,1)S(1)} collective-permute-done((bf16[256,768]{1,0:T(8,128)(2,1)S(1)}, bf16[256,768]{1,0:T(8,128)(2,1)S(1)}, u32[]{:S(2)}, u32[]{:S(2)}) %collective-permute-start.43) | collective-permute-done | bytes 393248 | tf_op jit(solution)/shard_map/ppermute | solution.py:667
  474.6 10.8 %collective-permute-start.44 = (bf16[256,768]{1,0:T(8,128)(2,1)S(1)}, bf16[256,768]{1,0:T(8,128)(2,1)S(1)}, u32[]{:S(2)}, u32[]{:S(2)}) collective-permute-start(bf16[256,768]{1,0:T(8,128)(2,1)S(1)} %get-tuple-element.213), channel_id=1, source_target_pairs={{0,2},{1,3},{2,0},{3,1},{4,6},{5,7},{6,4},{7,5},{8,10},{9,11},{10,... | collective-permute-start | bytes 1179656 | tf_op jit(solution)/shard_map/ppermute | solution.py:644
  488.2 21.5 %attend_back.6 = (f32[1024,256]{1,0:T(8,128)S(1)}, f32[1024,256]{1,0:T(8,128)S(1)}, f32[1024,256]{1,0:T(8,128)S(1)}, f32[1024,256]{1,0:T(8,128)S(1)}, f32[1024,256]{1,0:T(8,128)S(1)}) custom-call(s32[1]{0:T(128)} %constant.263.clone.1.start_ref, bf16[1024,768]{1,0:T(8,128)(2,1)S(1)} %pad_maximum_fusion.11.gb_ref, ...), custom_call_target="tpu_custom_call" | custom-call | flops 28750000128 | bytes 3145728 | tf_op jit(solution)/shard_map/attend_back/pallas_call | solution.py:389
  514.4 21.6 %collective-permute-start.62 = (bf16[256,768]{1,0:T(8,128)(2,1)}, bf16[256,768]{1,0:T(8,128)(2,1)}, u32[]{:S(2)}, u32[]{:S(2)}) collective-permute-start(bf16[256,768]{1,0:T(8,128)(2,1)} %get-tuple-element.265), channel_id=1, source_target_pairs={{0,16},{8,17},{4,18},{12,19},{1,20},{9,21},{5,22},{13,23},{2,24},{... | collective-permute-start | bytes 1179656 | tf_op jit(solution)/shard_map/ppermute | solution.py:566
  546.1 5.9 leave.6
  555.8 2.8 collective-permute-done.61
  570.8 11.1 %attend_back.7 = (f32[1024,256]{1,0:T(8,128)S(1)}, f32[1024,256]{1,0:T(8,128)S(1)}, f32[1024,256]{1,0:T(8,128)S(1)}) custom-call(s32[1]{0:T(128)} %constant.261.clone.1.start_ref, bf16[1024,768]{1,0:T(8,128)(2,1)S(1)} %pad_maximum_fusion.10.gb_ref, bf16[768,1792]{1,0:T(8,128)(2,1)} %all-gather.6.cloned.1.call-done.wu_ref.wd_ref.wo_ref.w_ref, ...), custom_call_target="tpu_custom_call" | custom-call | flops 14375000064 | bytes 3145728 | tf_op jit(solution)/shard_map/attend_back/pallas_call | solution.py:389
  582.0 6.4 leave.7
  589.5 2.7 fusion.59
  600.9 4.2 fusion.44
  605.2 2.9 fusion.38
  610.5 4.5 constant_dynamic-slice_fusion.2
  621.5 3.5 collective-permute-start.72
  624.9 32.9 %collective-permute-done.66 = bf16[192,576]{0,1:T(8,128)(2,1)} collective-permute-done((bf16[192,576]{0,1:T(8,128)(2,1)}, bf16[192,576]{0,1:T(8,128)(2,1)}, u32[]{:S(2)}, u32[]{:S(2)}) %collective-permute-start.66) | collective-permute-done | bytes 221216 | tf_op jit(solution)/shard_map/ppermute | solution.py:601
  664.2 8.7 %collective-permute-done.71 = bf16[192,1728]{1,0:T(8,128)(2,1)S(1)} collective-permute-done((bf16[192,1728]{1,0:T(8,128)(2,1)}, bf16[192,1728]{1,0:T(8,128)(2,1)S(1)}, u32[]{:S(2)}, u32[]{:S(2)}) %collective-permute-start.71) | collective-permute-done | bytes 663584 | tf_op jit(solution)/shard_map/ppermute | solution.py:601
  679.4 8.8 %collective-permute-done.70 = bf16[192,1728]{1,0:T(8,128)(2,1)} collective-permute-done((bf16[192,1728]{1,0:T(8,128)(2,1)}, bf16[192,1728]{1,0:T(8,128)(2,1)}, u32[]{:S(2)}, u32[]{:S(2)}) %collective-permute-start.70) | collective-permute-done | bytes 663584 | tf_op jit(solution)/shard_map/ppermute | solution.py:601
  688.2 7.3 collective-permute-start.58
  697.8 3.4 fusion.119
  709.0 7.9 %collective-permute-done.51 = bf16[256,768]{1,0:T(8,128)(2,1)S(1)} collective-permute-done((bf16[256,768]{1,0:T(8,128)(2,1)S(1)}, bf16[256,768]{1,0:T(8,128)(2,1)S(1)}, u32[]{:S(2)}, u32[]{:S(2)}) %collective-permute-start.51) | collective-permute-done | bytes 393248 | tf_op jit(solution)/shard_map/ppermute | solution.py:667
  724.7 5.1 collective-permute-start.52
  732.1 13.8 %collective-permute-done.55 = bf16[256,768]{1,0:T(8,128)(2,1)} collective-permute-done((bf16[256,768]{1,0:T(8,128)(2,1)}, bf16[256,768]{1,0:T(8,128)(2,1)}, u32[]{:S(2)}, u32[]{:S(2)}) %collective-permute-start.55) | collective-permute-done | bytes 393248 | tf_op jit(solution)/shard_map/ppermute | solution.py:566
  747.1 9.9 %collective-permute-done.52 = bf16[256,768]{1,0:T(8,128)(2,1)} collective-permute-done((bf16[256,768]{1,0:T(8,128)(2,1)}, bf16[256,768]{1,0:T(8,128)(2,1)}, u32[]{:S(2)}, u32[]{:S(2)}) %collective-permute-start.52) | collective-permute-done | bytes 393248 | tf_op jit(solution)/shard_map/ppermute | solution.py:566
  762.8 4.2 fusion.132
  773.5 3.0 add_select_fusion
  (824 shorter events, 249.7 us)
Async XLA Ops:
  7.2 145.2 %all-gather.6.cloned.1.call-start = ((), (), s32[]{:S(2)}) async-start(), calls=%async_computation.1 | async-start | bytes 3096576 | tf_op jit(solution)/shard_map/all_gather | solution.py:743
  9.8 34.5 %collective-permute-start.23 = (bf16[256,768]{1,0:T(8,128)(2,1)}, bf16[256,768]{1,0:T(8,128)(2,1)S(1)}, u32[]{:S(2)}, u32[]{:S(2)}) collective-permute-start(bf16[256,768]{1,0:T(8,128)(2,1)} %get-tuple-element.299), channel_id=1, source_target_pairs={{8,0},{9,8},{10,4},{11,12},{12,1},{13,9},{14,5},{15,13},{24,16},{2... | collective-permute-start | bytes 1179656 | tf_op jit(solution)/shard_map/ppermute | solution.py:518
  10.5 24.6 %collective-permute-start.1 = (bf16[256,768]{1,0:T(8,128)(2,1)}, bf16[256,768]{1,0:T(8,128)(2,1)S(1)}, u32[]{:S(2)}, u32[]{:S(2)}) collective-permute-start(bf16[256,768]{1,0:T(8,128)(2,1)} %get-tuple-element.299), channel_id=1, source_target_pairs={{0,0},{1,8},{2,4},{3,12},{4,1},{5,9},{6,5},{7,13},{16,16},{17,24},... | collective-permute-start | bytes 1179656 | tf_op jit(solution)/shard_map/ppermute | solution.py:518
  23.4 31.9 %collective-permute-start.22 = (bf16[256,768]{1,0:T(8,128)(2,1)}, bf16[256,768]{1,0:T(8,128)(2,1)}, u32[]{:S(2)}, u32[]{:S(2)}) collective-permute-start(bf16[256,768]{1,0:T(8,128)(2,1)} %get-tuple-element.300), channel_id=1, source_target_pairs={{8,2},{9,10},{10,6},{11,14},{12,3},{13,11},{14,7},{15,15},{24,18},... | collective-permute-start | bytes 1179656 | tf_op jit(solution)/shard_map/ppermute | solution.py:518
  26.2 16.8 %collective-permute-start = (bf16[256,768]{1,0:T(8,128)(2,1)}, bf16[256,768]{1,0:T(8,128)(2,1)}, u32[]{:S(2)}, u32[]{:S(2)}) collective-permute-start(bf16[256,768]{1,0:T(8,128)(2,1)} %get-tuple-element.300), channel_id=1, source_target_pairs={{0,2},{1,10},{2,6},{3,14},{4,3},{5,11},{6,7},{7,15},{16,18},{17,26... | collective-permute-start | bytes 1179656 | tf_op jit(solution)/shard_map/ppermute | solution.py:518
  32.2 42.8 %collective-permute-start.8 = (bf16[192,576]{0,1:T(8,128)(2,1)S(1)}, bf16[192,576]{0,1:T(8,128)(2,1)}, u32[]{:S(2)}, u32[]{:S(2)}) collective-permute-start(bf16[192,576]{0,1:T(8,128)(2,1)S(1)} %broadcast_select_fusion.76), channel_id=1, source_target_pairs={{0,12},{4,8},{8,4},{12,0},{1,13},{5,9},{9,5},{13,1},{2,14},{6,10},... | collective-permute-start | bytes 663560 | tf_op jit(solution)/shard_map/ppermute | solution.py:601
  35.0 251.4 %all-gather.8.cloned.1.call-start = ((), (), s32[]{:S(2)}) async-start(), calls=%async_computation.2 | async-start | bytes 3096576 | tf_op jit(solution)/shard_map/all_gather | solution.py:743
  35.1 41.2 %collective-permute-start.7 = (bf16[192,576]{0,1:T(8,128)(2,1)S(1)}, bf16[192,576]{0,1:T(8,128)(2,1)S(1)}, u32[]{:S(2)}, u32[]{:S(2)}) collective-permute-start(bf16[192,576]{0,1:T(8,128)(2,1)S(1)} %broadcast_select_fusion.76), channel_id=1, source_target_pairs={{0,8},{4,12},{8,0},{12,4},{1,9},{5,13},{9,1},{13,5},{2,10},{6,14},... | collective-permute-start | bytes 663560 | tf_op jit(solution)/shard_map/ppermute | solution.py:601
  43.0 34.8 %collective-permute-start.6 = (bf16[192,576]{0,1:T(8,128)(2,1)S(1)}, bf16[192,576]{0,1:T(8,128)(2,1)S(1)}, u32[]{:S(2)}, u32[]{:S(2)}) collective-permute-start(bf16[192,576]{0,1:T(8,128)(2,1)S(1)} %broadcast_select_fusion.76), channel_id=1, source_target_pairs={{0,4},{4,0},{8,12},{12,8},{1,5},{5,1},{9,13},{13,9},{2,6},{6,2},{1... | collective-permute-start | bytes 663560 | tf_op jit(solution)/shard_map/ppermute | solution.py:601
  56.5 24.5 %collective-permute-start.24 = (bf16[256,768]{1,0:T(8,128)(2,1)S(1)}, bf16[256,768]{1,0:T(8,128)(2,1)}, u32[]{:S(2)}, u32[]{:S(2)}) collective-permute-start(bf16[256,768]{1,0:T(8,128)(2,1)S(1)} %get-tuple-element.220), channel_id=1, source_target_pairs={{0,2},{1,3},{2,0},{3,1},{4,6},{5,7},{6,4},{7,5},{8,10},{9,11},{10,... | collective-permute-start | bytes 1179656 | tf_op jit(solution)/shard_map/ppermute | solution.py:644
  57.7 25.0 %collective-permute-start.3 = (bf16[512,768]{1,0:T(8,128)(2,1)}, bf16[512,768]{1,0:T(8,128)(2,1)}, u32[]{:S(2)}, u32[]{:S(2)}) collective-permute-start(bf16[512,768]{1,0:T(8,128)(2,1)} %pad_maximum_fusion.13), channel_id=1, source_target_pairs={{0,1},{1,0},{2,3},{3,2},{4,5},{5,4},{6,7},{7,6},{8,9},{9,8},{10,11... | collective-permute-start | bytes 2359304 | tf_op jit(solution)/shard_map/ppermute | solution.py:644
  75.0 108.6 %collective-permute-start.30 = (bf16[96,1792]{1,0:T(8,128)(2,1)}, bf16[96,1792]{1,0:T(8,128)(2,1)}, u32[]{:S(2)}, u32[]{:S(2)}) collective-permute-start(bf16[96,1792]{1,0:T(8,128)(2,1)} %get-tuple-element.301), channel_id=1, source_target_pairs={{16,0},{17,1},{18,2},{19,3},{20,4},{21,5},{22,6},{23,7},{24,8},{25... | collective-permute-start | bytes 1032200 | tf_op jit(solution)/shard_map/ppermute | solution.py:640
  90.5 25.8 %collective-permute-start.14 = (bf16[192,576]{0,1:T(8,128)(2,1)S(1)}, bf16[192,576]{0,1:T(8,128)(2,1)S(1)}, u32[]{:S(2)}, u32[]{:S(2)}) collective-permute-start(bf16[192,576]{0,1:T(8,128)(2,1)S(1)} %broadcast_select_fusion.74), channel_id=1, source_target_pairs={{16,0},{17,1},{18,2},{19,3},{20,4},{21,5},{22,6},{23,7},{24,8},{25... | collective-permute-start | bytes 663560 | tf_op jit(solution)/shard_map/ppermute | solution.py:640
  116.3 20.6 %collective-permute-start.17 = (bf16[192,576]{0,1:T(8,128)(2,1)S(1)}, bf16[192,576]{0,1:T(8,128)(2,1)S(1)}, u32[]{:S(2)}, u32[]{:S(2)}) collective-permute-start(bf16[192,576]{0,1:T(8,128)(2,1)S(1)} %broadcast_select_fusion.75), channel_id=1, source_target_pairs={{0,12},{4,8},{8,4},{12,0},{1,13},{5,9},{9,5},{13,1},{2,14},{6,10},... | collective-permute-start | bytes 663560 | tf_op jit(solution)/shard_map/ppermute | solution.py:601
  127.2 24.0 %collective-permute-start.16 = (bf16[192,576]{0,1:T(8,128)(2,1)S(1)}, bf16[192,576]{0,1:T(8,128)(2,1)S(1)}, u32[]{:S(2)}, u32[]{:S(2)}) collective-permute-start(bf16[192,576]{0,1:T(8,128)(2,1)S(1)} %broadcast_select_fusion.75), channel_id=1, source_target_pairs={{0,8},{4,12},{8,0},{12,4},{1,9},{5,13},{9,1},{13,5},{2,10},{6,14},... | collective-permute-start | bytes 663560 | tf_op jit(solution)/shard_map/ppermute | solution.py:601
  136.3 34.0 %collective-permute-start.15 = (bf16[192,576]{0,1:T(8,128)(2,1)S(1)}, bf16[192,576]{0,1:T(8,128)(2,1)}, u32[]{:S(2)}, u32[]{:S(2)}) collective-permute-start(bf16[192,576]{0,1:T(8,128)(2,1)S(1)} %broadcast_select_fusion.75), channel_id=1, source_target_pairs={{0,4},{4,0},{8,12},{12,8},{1,5},{5,1},{9,13},{13,9},{2,6},{6,2},{1... | collective-permute-start | bytes 663560 | tf_op jit(solution)/shard_map/ppermute | solution.py:601
  162.6 15.1 %collective-permute-start.26 = (bf16[512,768]{1,0:T(8,128)(2,1)}, bf16[512,768]{1,0:T(8,128)(2,1)}, u32[]{:S(2)}, u32[]{:S(2)}) collective-permute-start(bf16[512,768]{1,0:T(8,128)(2,1)} %broadcast_select_fusion.7), channel_id=1, source_target_pairs={{0,1},{1,0},{2,3},{3,2},{4,5},{5,4},{6,7},{7,6},{8,9},{9,8},{10,11... | collective-permute-start | bytes 2359304 | tf_op jit(solution)/shard_map/ppermute | solution.py:656
  181.7 18.0 %collective-permute-start.11 = (bf16[256,768]{1,0:T(8,128)(2,1)S(1)}, bf16[256,768]{1,0:T(8,128)(2,1)S(1)}, u32[]{:S(2)}, u32[]{:S(2)}) collective-permute-start(bf16[256,768]{1,0:T(8,128)(2,1)S(1)} %select_convert_fusion.7), channel_id=1, source_target_pairs={{0,2},{1,3},{2,0},{3,1},{4,6},{5,7},{6,4},{7,5},{8,10},{9,11},{10,... | collective-permute-start | bytes 1179656 | tf_op jit(solution)/shard_map/ppermute | solution.py:667
  185.5 575.0 %reduce-scatter.4.cloned.1.call-start = ((), (), s32[]{:S(2)}) async-start(), calls=%async_computation.4 | async-start | bytes 3981312 | tf_op jit(solution)/shard_map/reduce_scatter | solution.py:897
  202.5 18.5 %collective-permute-start.28 = (bf16[256,768]{1,0:T(8,128)(2,1)S(1)}, bf16[256,768]{1,0:T(8,128)(2,1)S(1)}, u32[]{:S(2)}, u32[]{:S(2)}) collective-permute-start(bf16[256,768]{1,0:T(8,128)(2,1)S(1)} %get-tuple-element.323), channel_id=1, source_target_pairs={{0,2},{1,3},{2,0},{3,1},{4,6},{5,7},{6,4},{7,5},{8,10},{9,11},{10,... | collective-permute-start | bytes 1179656 | tf_op jit(solution)/shard_map/ppermute | solution.py:644
  221.1 35.4 %collective-permute-start.29 = (bf16[512,768]{1,0:T(8,128)(2,1)S(1)}, bf16[512,768]{1,0:T(8,128)(2,1)S(1)}, u32[]{:S(2)}, u32[]{:S(2)}) collective-permute-start(bf16[512,768]{1,0:T(8,128)(2,1)S(1)} %pad_maximum_fusion.17), channel_id=1, source_target_pairs={{0,1},{1,0},{2,3},{3,2},{4,5},{5,4},{6,7},{7,6},{8,9},{9,8},{10,11... | collective-permute-start | bytes 2359304 | tf_op jit(solution)/shard_map/ppermute | solution.py:644
  228.6 19.1 %collective-permute-start.19 = (bf16[256,768]{1,0:T(8,128)(2,1)S(1)}, bf16[256,768]{1,0:T(8,128)(2,1)S(1)}, u32[]{:S(2)}, u32[]{:S(2)}) collective-permute-start(bf16[256,768]{1,0:T(8,128)(2,1)S(1)} %get-tuple-element.291), channel_id=1, source_target_pairs={{0,0},{1,8},{2,4},{3,12},{4,1},{5,9},{6,5},{7,13},{8,2},{9,10},{10... | collective-permute-start | bytes 1179656 | tf_op jit(solution)/shard_map/ppermute | solution.py:535
  230.5 24.0 %collective-permute-start.18 = (bf16[256,768]{1,0:T(8,128)(2,1)S(1)}, bf16[256,768]{1,0:T(8,128)(2,1)S(1)}, u32[]{:S(2)}, u32[]{:S(2)}) collective-permute-start(bf16[256,768]{1,0:T(8,128)(2,1)S(1)} %get-tuple-element.292), channel_id=1, source_target_pairs={{0,2},{1,10},{2,6},{3,14},{4,3},{5,11},{6,7},{7,15},{8,0},{9,8},{1... | collective-permute-start | bytes 1179656 | tf_op jit(solution)/shard_map/ppermute | solution.py:535
  257.0 24.8 %collective-permute-start.39 = (bf16[256,768]{1,0:T(8,128)(2,1)S(1)}, bf16[256,768]{1,0:T(8,128)(2,1)S(1)}, u32[]{:S(2)}, u32[]{:S(2)}) collective-permute-start(bf16[256,768]{1,0:T(8,128)(2,1)S(1)} %get-tuple-element.215), channel_id=1, source_target_pairs={{0,2},{1,3},{2,0},{3,1},{4,6},{5,7},{6,4},{7,5},{8,10},{9,11},{10,... | collective-permute-start | bytes 1179656 | tf_op jit(solution)/shard_map/ppermute | solution.py:644
  266.9 16.3 %collective-permute-start.21 = (bf16[512,768]{1,0:T(8,128)(2,1)S(1)}, bf16[512,768]{1,0:T(8,128)(2,1)S(1)}, u32[]{:S(2)}, u32[]{:S(2)}) collective-permute-start(bf16[512,768]{1,0:T(8,128)(2,1)S(1)} %pad_maximum_fusion.15), channel_id=1, source_target_pairs={{0,1},{1,0},{2,3},{3,2},{4,5},{5,4},{6,7},{7,6},{8,9},{9,8},{10,11... | collective-permute-start | bytes 2359304 | tf_op jit(solution)/shard_map/ppermute | solution.py:644
  283.2 13.8 %collective-permute-start.40 = (bf16[512,768]{1,0:T(8,128)(2,1)}, bf16[512,768]{1,0:T(8,128)(2,1)}, u32[]{:S(2)}, u32[]{:S(2)}) collective-permute-start(bf16[512,768]{1,0:T(8,128)(2,1)} %pad_maximum_fusion.20), channel_id=1, source_target_pairs={{0,1},{1,0},{2,3},{3,2},{4,5},{5,4},{6,7},{7,6},{8,9},{9,8},{10,11... | collective-permute-start | bytes 2359304 | tf_op jit(solution)/shard_map/ppermute | solution.py:644
  306.0 54.4 %collective-permute-start.32 = (bf16[256,768]{1,0:T(8,128)(2,1)S(1)}, bf16[256,768]{1,0:T(8,128)(2,1)}, u32[]{:S(2)}, u32[]{:S(2)}) collective-permute-start(bf16[256,768]{1,0:T(8,128)(2,1)S(1)} %select_convert_fusion.5), channel_id=1, source_target_pairs={{0,2},{1,3},{2,0},{3,1},{4,6},{5,7},{6,4},{7,5},{8,10},{9,11},{10,... | collective-permute-start | bytes 1179656 | tf_op jit(solution)/shard_map/ppermute | solution.py:667
  380.5 17.5 %collective-permute-start.33 = (bf16[512,768]{1,0:T(8,128)(2,1)}, bf16[512,768]{1,0:T(8,128)(2,1)}, u32[]{:S(2)}, u32[]{:S(2)}) collective-permute-start(bf16[512,768]{1,0:T(8,128)(2,1)} %broadcast_select_fusion.5), channel_id=1, source_target_pairs={{0,1},{1,0},{2,3},{3,2},{4,5},{5,4},{6,7},{7,6},{8,9},{9,8},{10,11... | collective-permute-start | bytes 2359304 | tf_op jit(solution)/shard_map/ppermute | solution.py:656
  381.0 22.5 %collective-permute-start.41 = (bf16[512,768]{1,0:T(8,128)(2,1)}, bf16[512,768]{1,0:T(8,128)(2,1)}, u32[]{:S(2)}, u32[]{:S(2)}) collective-permute-start(bf16[512,768]{1,0:T(8,128)(2,1)} %broadcast_select_fusion.4), channel_id=1, source_target_pairs={{0,1},{1,0},{2,3},{3,2},{4,5},{5,4},{6,7},{7,6},{8,9},{9,8},{10,11... | collective-permute-start | bytes 2359304 | tf_op jit(solution)/shard_map/ppermute | solution.py:656
  401.6 25.7 %collective-permute-start.34 = (bf16[256,768]{1,0:T(8,128)(2,1)}, bf16[256,768]{1,0:T(8,128)(2,1)}, u32[]{:S(2)}, u32[]{:S(2)}) collective-permute-start(bf16[256,768]{1,0:T(8,128)(2,1)} %select_convert_fusion.4), channel_id=1, source_target_pairs={{0,2},{1,3},{2,0},{3,1},{4,6},{5,7},{6,4},{7,5},{8,10},{9,11},{10,... | collective-permute-start | bytes 1179656 | tf_op jit(solution)/shard_map/ppermute | solution.py:667
  424.3 338.5 %all-gather.10.cloned.1.call-start = ((), (), s32[]{:S(2)}) async-start(), calls=%async_computation.3 | async-start | bytes 1385472 | tf_op jit(solution)/shard_map/all_gather | solution.py:918
  427.2 13.7 %collective-permute-start.42 = (bf16[512,768]{1,0:T(8,128)(2,1)S(1)}, bf16[512,768]{1,0:T(8,128)(2,1)S(1)}, u32[]{:S(2)}, u32[]{:S(2)}) collective-permute-start(bf16[512,768]{1,0:T(8,128)(2,1)S(1)} %broadcast_select_fusion.3), channel_id=1, source_target_pairs={{0,1},{1,0},{2,3},{3,2},{4,5},{5,4},{6,7},{7,6},{8,9},{9,8},{10,11... | collective-permute-start | bytes 2359304 | tf_op jit(solution)/shard_map/ppermute | solution.py:656
  428.7 32.5 %collective-permute-start.36 = (bf16[256,768]{1,0:T(8,128)(2,1)S(1)}, bf16[256,768]{1,0:T(8,128)(2,1)S(1)}, u32[]{:S(2)}, u32[]{:S(2)}) collective-permute-start(bf16[256,768]{1,0:T(8,128)(2,1)S(1)} %get-tuple-element.230), channel_id=1, source_target_pairs={{0,0},{16,16},{8,1},{24,17},{4,2},{20,18},{12,3},{28,19},{1,4},{17... | collective-permute-start | bytes 1179656 | tf_op jit(solution)/shard_map/ppermute | solution.py:566
  431.4 30.2 %collective-permute-start.35 = (bf16[256,768]{1,0:T(8,128)(2,1)S(1)}, bf16[256,768]{1,0:T(8,128)(2,1)S(1)}, u32[]{:S(2)}, u32[]{:S(2)}) collective-permute-start(bf16[256,768]{1,0:T(8,128)(2,1)S(1)} %get-tuple-element.247), channel_id=1, source_target_pairs={{2,0},{18,16},{10,1},{26,17},{6,2},{22,18},{14,3},{30,19},{3,4},{1... | collective-permute-start | bytes 1179656 | tf_op jit(solution)/shard_map/ppermute | solution.py:566
  432.0 31.0 %collective-permute-start.38 = (bf16[256,768]{1,0:T(8,128)(2,1)S(1)}, bf16[256,768]{1,0:T(8,128)(2,1)S(1)}, u32[]{:S(2)}, u32[]{:S(2)}) collective-permute-start(bf16[256,768]{1,0:T(8,128)(2,1)S(1)} %get-tuple-element.248), channel_id=1, source_target_pairs={{0,16},{16,0},{8,17},{24,1},{4,18},{20,2},{12,19},{28,3},{1,20},{1... | collective-permute-start | bytes 1179656 | tf_op jit(solution)/shard_map/ppermute | solution.py:566
  439.5 23.5 %collective-permute-start.37 = (bf16[256,768]{1,0:T(8,128)(2,1)S(1)}, bf16[256,768]{1,0:T(8,128)(2,1)S(1)}, u32[]{:S(2)}, u32[]{:S(2)}) collective-permute-start(bf16[256,768]{1,0:T(8,128)(2,1)S(1)} %get-tuple-element.249), channel_id=1, source_target_pairs={{2,16},{18,0},{10,17},{26,1},{6,18},{22,2},{14,19},{30,3},{3,20},{... | collective-permute-start | bytes 1179656 | tf_op jit(solution)/shard_map/ppermute | solution.py:566
  440.9 20.2 %collective-permute-start.47 = (bf16[256,768]{1,0:T(8,128)(2,1)S(1)}, bf16[256,768]{1,0:T(8,128)(2,1)S(1)}, u32[]{:S(2)}, u32[]{:S(2)}) collective-permute-start(bf16[256,768]{1,0:T(8,128)(2,1)S(1)} %get-tuple-element.211), channel_id=1, source_target_pairs={{0,2},{1,3},{2,0},{3,1},{4,6},{5,7},{6,4},{7,5},{8,10},{9,11},{10,... | collective-permute-start | bytes 1179656 | tf_op jit(solution)/shard_map/ppermute | solution.py:644
  461.1 12.8 %collective-permute-start.43 = (bf16[256,768]{1,0:T(8,128)(2,1)S(1)}, bf16[256,768]{1,0:T(8,128)(2,1)S(1)}, u32[]{:S(2)}, u32[]{:S(2)}) collective-permute-start(bf16[256,768]{1,0:T(8,128)(2,1)S(1)} %select_convert_fusion.3), channel_id=1, source_target_pairs={{0,2},{1,3},{2,0},{3,1},{4,6},{5,7},{6,4},{7,5},{8,10},{9,11},{10,... | collective-permute-start | bytes 1179656 | tf_op jit(solution)/shard_map/ppermute | solution.py:667
  461.2 24.3 %collective-permute-start.48 = (bf16[512,768]{1,0:T(8,128)(2,1)S(1)}, bf16[512,768]{1,0:T(8,128)(2,1)S(1)}, u32[]{:S(2)}, u32[]{:S(2)}) collective-permute-start(bf16[512,768]{1,0:T(8,128)(2,1)S(1)} %pad_maximum_fusion.22), channel_id=1, source_target_pairs={{0,1},{1,0},{2,3},{3,2},{4,5},{5,4},{6,7},{7,6},{8,9},{9,8},{10,11... | collective-permute-start | bytes 2359304 | tf_op jit(solution)/shard_map/ppermute | solution.py:644
  474.6 37.2 %collective-permute-start.44 = (bf16[256,768]{1,0:T(8,128)(2,1)S(1)}, bf16[256,768]{1,0:T(8,128)(2,1)S(1)}, u32[]{:S(2)}, u32[]{:S(2)}) collective-permute-start(bf16[256,768]{1,0:T(8,128)(2,1)S(1)} %get-tuple-element.213), channel_id=1, source_target_pairs={{0,2},{1,3},{2,0},{3,1},{4,6},{5,7},{6,4},{7,5},{8,10},{9,11},{10,... | collective-permute-start | bytes 1179656 | tf_op jit(solution)/shard_map/ppermute | solution.py:644
  512.9 40.6 %collective-permute-start.64 = (bf16[256,768]{1,0:T(8,128)(2,1)}, bf16[256,768]{1,0:T(8,128)(2,1)}, u32[]{:S(2)}, u32[]{:S(2)}) collective-permute-start(bf16[256,768]{1,0:T(8,128)(2,1)} %get-tuple-element.265), channel_id=1, source_target_pairs={{16,16},{24,17},{20,18},{28,19},{17,20},{25,21},{21,22},{29,23},{1... | collective-permute-start | bytes 1179656 | tf_op jit(solution)/shard_map/ppermute | solution.py:566
  514.4 41.3 %collective-permute-start.62 = (bf16[256,768]{1,0:T(8,128)(2,1)}, bf16[256,768]{1,0:T(8,128)(2,1)}, u32[]{:S(2)}, u32[]{:S(2)}) collective-permute-start(bf16[256,768]{1,0:T(8,128)(2,1)} %get-tuple-element.265), channel_id=1, source_target_pairs={{0,16},{8,17},{4,18},{12,19},{1,20},{9,21},{5,22},{13,23},{2,24},{... | collective-permute-start | bytes 1179656 | tf_op jit(solution)/shard_map/ppermute | solution.py:566
  536.1 17.6 %collective-permute-start.63 = (bf16[256,768]{1,0:T(8,128)(2,1)}, bf16[256,768]{1,0:T(8,128)(2,1)}, u32[]{:S(2)}, u32[]{:S(2)}) collective-permute-start(bf16[256,768]{1,0:T(8,128)(2,1)} %get-tuple-element.266), channel_id=1, source_target_pairs={{18,16},{26,17},{22,18},{30,19},{19,20},{27,21},{23,22},{31,23},{1... | collective-permute-start | bytes 1179656 | tf_op jit(solution)/shard_map/ppermute | solution.py:566
  537.5 21.1 %collective-permute-start.61 = (bf16[256,768]{1,0:T(8,128)(2,1)}, bf16[256,768]{1,0:T(8,128)(2,1)}, u32[]{:S(2)}, u32[]{:S(2)}) collective-permute-start(bf16[256,768]{1,0:T(8,128)(2,1)} %get-tuple-element.266), channel_id=1, source_target_pairs={{2,16},{10,17},{6,18},{14,19},{3,20},{11,21},{7,22},{15,23},{0,24}... | collective-permute-start | bytes 1179656 | tf_op jit(solution)/shard_map/ppermute | solution.py:566
  540.9 19.8 %collective-permute-start.45 = (bf16[512,768]{1,0:T(8,128)(2,1)}, bf16[512,768]{1,0:T(8,128)(2,1)}, u32[]{:S(2)}, u32[]{:S(2)}) collective-permute-start(bf16[512,768]{1,0:T(8,128)(2,1)} %pad_maximum_fusion.21), channel_id=1, source_target_pairs={{0,1},{1,0},{2,3},{3,2},{4,5},{5,4},{6,7},{7,6},{8,9},{9,8},{10,11... | collective-permute-start | bytes 2359304 | tf_op jit(solution)/shard_map/ppermute | solution.py:644
  553.5 14.1 %collective-permute-start.49 = (bf16[512,768]{1,0:T(8,128)(2,1)S(1)}, bf16[512,768]{1,0:T(8,128)(2,1)S(1)}, u32[]{:S(2)}, u32[]{:S(2)}) collective-permute-start(bf16[512,768]{1,0:T(8,128)(2,1)S(1)} %broadcast_select_fusion.2), channel_id=1, source_target_pairs={{0,1},{1,0},{2,3},{3,2},{4,5},{5,4},{6,7},{7,6},{8,9},{9,8},{10,11... | collective-permute-start | bytes 2359304 | tf_op jit(solution)/shard_map/ppermute | solution.py:656
  595.0 65.3 %collective-permute-start.56 = (bf16[256,768]{1,0:T(8,128)(2,1)}, bf16[256,768]{1,0:T(8,128)(2,1)}, u32[]{:S(2)}, u32[]{:S(2)}) collective-permute-start(bf16[256,768]{1,0:T(8,128)(2,1)} %select_convert_fusion), channel_id=1, source_target_pairs={{0,2},{1,3},{2,0},{3,1},{4,6},{5,7},{6,4},{7,5},{8,10},{9,11},{10,... | collective-permute-start | bytes 1179656 | tf_op jit(solution)/shard_map/ppermute | solution.py:667
  596.0 107.6 %collective-permute-start.50 = (bf16[512,768]{1,0:T(8,128)(2,1)}, bf16[512,768]{1,0:T(8,128)(2,1)}, u32[]{:S(2)}, u32[]{:S(2)}) collective-permute-start(bf16[512,768]{1,0:T(8,128)(2,1)} %broadcast_select_fusion.1), channel_id=1, source_target_pairs={{0,1},{1,0},{2,3},{3,2},{4,5},{5,4},{6,7},{7,6},{8,9},{9,8},{10,11... | collective-permute-start | bytes 2359304 | tf_op jit(solution)/shard_map/ppermute | solution.py:656
  597.3 22.6 %collective-permute-start.65 = (bf16[192,576]{0,1:T(8,128)(2,1)}, bf16[192,576]{0,1:T(8,128)(2,1)}, u32[]{:S(2)}, u32[]{:S(2)}) collective-permute-start(bf16[192,576]{0,1:T(8,128)(2,1)} %get-tuple-element.258), channel_id=1, source_target_pairs={{0,4},{4,0},{8,12},{12,8},{1,5},{5,1},{9,13},{13,9},{2,6},{6,2},{1... | collective-permute-start | bytes 663560 | tf_op jit(solution)/shard_map/ppermute | solution.py:601
  599.0 22.5 %collective-permute-start.67 = (bf16[192,576]{0,1:T(8,128)(2,1)}, bf16[192,576]{0,1:T(8,128)(2,1)}, u32[]{:S(2)}, u32[]{:S(2)}) collective-permute-start(bf16[192,576]{0,1:T(8,128)(2,1)} %get-tuple-element.259), channel_id=1, source_target_pairs={{0,12},{4,8},{8,4},{12,0},{1,13},{5,9},{9,5},{13,1},{2,14},{6,10},... | collective-permute-start | bytes 663560 | tf_op jit(solution)/shard_map/ppermute | solution.py:601
  599.0 58.8 %collective-permute-start.66 = (bf16[192,576]{0,1:T(8,128)(2,1)}, bf16[192,576]{0,1:T(8,128)(2,1)}, u32[]{:S(2)}, u32[]{:S(2)}) collective-permute-start(bf16[192,576]{0,1:T(8,128)(2,1)} %get-tuple-element.260), channel_id=1, source_target_pairs={{0,8},{4,12},{8,0},{12,4},{1,9},{5,13},{9,1},{13,5},{2,10},{6,14},... | collective-permute-start | bytes 663560 | tf_op jit(solution)/shard_map/ppermute | solution.py:601
  619.9 53.0 %collective-permute-start.71 = (bf16[192,1728]{1,0:T(8,128)(2,1)}, bf16[192,1728]{1,0:T(8,128)(2,1)S(1)}, u32[]{:S(2)}, u32[]{:S(2)}) collective-permute-start(bf16[192,1728]{1,0:T(8,128)(2,1)} %copy.87), channel_id=1, source_target_pairs={{0,8},{4,12},{8,0},{12,4},{1,9},{5,13},{9,1},{13,5},{2,10},{6,14},... | collective-permute-start | bytes 1990664 | tf_op jit(solution)/shard_map/ppermute | solution.py:601
  621.5 55.1 %collective-permute-start.72 = (bf16[192,1728]{1,0:T(8,128)(2,1)}, bf16[192,1728]{1,0:T(8,128)(2,1)}, u32[]{:S(2)}, u32[]{:S(2)}) collective-permute-start(bf16[192,1728]{1,0:T(8,128)(2,1)} %copy.89), channel_id=1, source_target_pairs={{0,12},{4,8},{8,4},{12,0},{1,13},{5,9},{9,5},{13,1},{2,14},{6,10},... | collective-permute-start | bytes 1990664 | tf_op jit(solution)/shard_map/ppermute | solution.py:601
  657.9 30.3 %collective-permute-start.70 = (bf16[192,1728]{1,0:T(8,128)(2,1)}, bf16[192,1728]{1,0:T(8,128)(2,1)}, u32[]{:S(2)}, u32[]{:S(2)}) collective-permute-start(bf16[192,1728]{1,0:T(8,128)(2,1)} %copy.85), channel_id=1, source_target_pairs={{0,4},{4,0},{8,12},{12,8},{1,5},{5,1},{9,13},{13,9},{2,6},{6,2},{1... | collective-permute-start | bytes 1990664 | tf_op jit(solution)/shard_map/ppermute | solution.py:601
  660.3 117.0 %collective-permute-start.68 = (bf16[192,576]{0,1:T(8,128)(2,1)}, bf16[192,576]{0,1:T(8,128)(2,1)}, u32[]{:S(2)}, u32[]{:S(2)}) collective-permute-start(bf16[192,576]{0,1:T(8,128)(2,1)} %fusion.118), channel_id=1, source_target_pairs={{16,0},{17,1},{18,2},{19,3},{20,4},{21,5},{22,6},{23,7},{24,8},{25... | collective-permute-start | bytes 663560 | tf_op jit(solution)/shard_map/ppermute | solution.py:640
  673.8 32.2 %collective-permute-start.60 = (bf16[256,768]{1,0:T(8,128)(2,1)}, bf16[256,768]{1,0:T(8,128)(2,1)}, u32[]{:S(2)}, u32[]{:S(2)}) collective-permute-start(bf16[256,768]{1,0:T(8,128)(2,1)} %fusion.108), channel_id=1, source_target_pairs={{18,8},{26,9},{22,10},{30,11},{19,12},{27,13},{23,14},{31,15}} | collective-permute-start | bytes 1179656 | tf_op jit(solution)/shard_map/ppermute | solution.py:566
  676.6 30.8 %collective-permute-start.59 = (bf16[256,768]{1,0:T(8,128)(2,1)}, bf16[256,768]{1,0:T(8,128)(2,1)}, u32[]{:S(2)}, u32[]{:S(2)}) collective-permute-start(bf16[256,768]{1,0:T(8,128)(2,1)} %fusion.108), channel_id=1, source_target_pairs={{16,8},{24,9},{20,10},{28,11},{17,12},{25,13},{21,14},{29,15}} | collective-permute-start | bytes 1179656 | tf_op jit(solution)/shard_map/ppermute | solution.py:566
  688.2 31.6 %collective-permute-start.58 = (bf16[256,768]{1,0:T(8,128)(2,1)}, bf16[256,768]{1,0:T(8,128)(2,1)}, u32[]{:S(2)}, u32[]{:S(2)}) collective-permute-start(bf16[256,768]{1,0:T(8,128)(2,1)} %fusion.108), channel_id=1, source_target_pairs={{2,8},{10,9},{6,10},{14,11},{3,12},{11,13},{7,14},{15,15}} | collective-permute-start | bytes 1179656 | tf_op jit(solution)/shard_map/ppermute | solution.py:566
  703.6 17.4 %collective-permute-start.57 = (bf16[256,768]{1,0:T(8,128)(2,1)}, bf16[256,768]{1,0:T(8,128)(2,1)S(1)}, u32[]{:S(2)}, u32[]{:S(2)}) collective-permute-start(bf16[256,768]{1,0:T(8,128)(2,1)} %fusion.108), channel_id=1, source_target_pairs={{0,8},{8,9},{4,10},{12,11},{1,12},{9,13},{5,14},{13,15}} | collective-permute-start | bytes 1179656 | tf_op jit(solution)/shard_map/ppermute | solution.py:566
  705.9 17.9 %collective-permute-start.73 = (bf16[192,1728]{1,0:T(8,128)(2,1)S(1)}, bf16[192,1728]{1,0:T(8,128)(2,1)S(1)}, u32[]{:S(2)}, u32[]{:S(2)}) collective-permute-start(bf16[192,1728]{1,0:T(8,128)(2,1)S(1)} %copy-done.200), channel_id=1, source_target_pairs={{16,0},{17,1},{18,2},{19,3},{20,4},{21,5},{22,6},{23,7},{24,8},{25... | collective-permute-start | bytes 1990664 | tf_op jit(solution)/shard_map/ppermute | solution.py:640
  718.4 27.4 %collective-permute-start.55 = (bf16[256,768]{1,0:T(8,128)(2,1)}, bf16[256,768]{1,0:T(8,128)(2,1)}, u32[]{:S(2)}, u32[]{:S(2)}) collective-permute-start(bf16[256,768]{1,0:T(8,128)(2,1)} %fusion.106), channel_id=1, source_target_pairs={{16,0},{24,1},{20,2},{28,3},{17,4},{25,5},{21,6},{29,7}} | collective-permute-start | bytes 1179656 | tf_op jit(solution)/shard_map/ppermute | solution.py:566
  719.7 26.2 %collective-permute-start.54 = (bf16[256,768]{1,0:T(8,128)(2,1)}, bf16[256,768]{1,0:T(8,128)(2,1)}, u32[]{:S(2)}, u32[]{:S(2)}) collective-permute-start(bf16[256,768]{1,0:T(8,128)(2,1)} %fusion.106), channel_id=1, source_target_pairs={{18,0},{26,1},{22,2},{30,3},{19,4},{27,5},{23,6},{31,7}} | collective-permute-start | bytes 1179656 | tf_op jit(solution)/shard_map/ppermute | solution.py:566
  722.2 24.9 %collective-permute-start.53 = (bf16[256,768]{1,0:T(8,128)(2,1)}, bf16[256,768]{1,0:T(8,128)(2,1)}, u32[]{:S(2)}, u32[]{:S(2)}) collective-permute-start(bf16[256,768]{1,0:T(8,128)(2,1)} %fusion.106), channel_id=1, source_target_pairs={{0,0},{8,1},{4,2},{12,3},{1,4},{9,5},{5,6},{13,7}} | collective-permute-start | bytes 1179656 | tf_op jit(solution)/shard_map/ppermute | solution.py:566
  724.7 32.4 %collective-permute-start.52 = (bf16[256,768]{1,0:T(8,128)(2,1)}, bf16[256,768]{1,0:T(8,128)(2,1)}, u32[]{:S(2)}, u32[]{:S(2)}) collective-permute-start(bf16[256,768]{1,0:T(8,128)(2,1)} %fusion.106), channel_id=1, source_target_pairs={{2,0},{10,1},{6,2},{14,3},{3,4},{11,5},{7,6},{15,7}} | collective-permute-start | bytes 1179656 | tf_op jit(solution)/shard_map/ppermute | solution.py:566
  (247 other events, 2536.3 us)
Sparse Core Ops, SparseCore 0:
  35.2 75.0 all-gather.5
  185.6 65.8 all-gather.7
  424.5 110.3 reduce-scatter.3
  620.0 99.8 all-gather.9

commit v3 on v2

--- a/solution.py
+++ b/solution.py
@@ -11,7 +11,7 @@
 HEAD_DIM = 64
 ROTARY = 16
 LANES = 256
-CHUNKS = 2
+CHUNKS = 1
 QUERY_BLOCK = 256
 KEY_BLOCK = 512
 ROW_BLOCK = 256
@@ -94,14 +94,15 @@
 
 
 class View:
-    def __init__(self, array, first, width):
+    def __init__(self, array, first, width, part=0, parts=1):
         if first % width:
             array, first = array[:, first : first + width], 0
-        self.array, self.block, self.shape = array, first // width, (array.shape[0], width)
+        self.array, self.block = array, (part, first // width)
+        self.shape = (array.shape[0] // parts, width)
 
     def spec(self):
         block = self.block
-        return pl.BlockSpec(self.shape, lambda i: (0, block))
+        return pl.BlockSpec(self.shape, lambda i: block)
 
 
 def project_kernel(heads, x_ref, gs_ref, w_ref, b_ref, c_ref, s_ref, seg_ref, *rest):
@@ -470,9 +471,11 @@
     )(x, w["gs"], dq, dk, dv, gu, w["wq"].array, w["wu"].array, *tables, *after)
 
 
-def hold(value, token):
-    first = token[(slice(0, 1),) * token.ndim].reshape((1,) * value.ndim)
-    return jnp.where(first == jnp.inf, jnp.zeros_like(value), value)
+def hold(value, *tokens):
+    for token in tokens:
+        first = token[(slice(0, 1),) * token.ndim].reshape((1,) * value.ndim)
+        value = jnp.where(first == jnp.inf, jnp.zeros_like(value), value)
+    return value
 
 
 def pick(bit, zero, one):
@@ -515,6 +518,8 @@
             for half in range(self.chunks):
                 pairs = [u[:2] for u in self.units() if u[2] == half and u[3] == chunk]
                 piece = block[half * self.unit : (half + 1) * self.unit]
+                if chunks:
+                    piece = hold(piece, chunks[0])
                 piece = lax.ppermute(piece, ("wide", "tp"), pairs)
                 if result is None:
                     result = piece
@@ -542,30 +547,22 @@
             chunks.append(piece)
         return chunks
 
-    def to_owner(self, chunks, layer, micro, only=None, both=False):
+    def to_owner(self, chunks, cross, tokens):
         devices = self.wide * self.tp
-        received = {}
+        received = []
         for turn_index in range(self.chunks):
-            for chunk in range(self.chunks) if only is None else [only]:
-                pairs = []
-                for owner, worker, _, held, part in self.units():
-                    moved = held if only is None else only
-                    if held == moved and (part + turn_index) % self.chunks == held:
-                        pairs.append((micro * devices + worker, layer * devices + owner))
-                        if both:
-                            pairs.append(
-                                ((1 - micro) * devices + worker, (1 - layer) * devices + owner)
-                            )
-                if only is None:
-                    piece = chunks[0]
-                    for other in range(1, self.chunks):
-                        here = (self.part + turn_index) % self.chunks == other
-                        piece = jnp.where(here, chunks[other], piece)
-                else:
-                    piece = chunks[only]
-                received[turn_index] = lax.ppermute(piece, ("section", "wide", "tp"), pairs)
-                if only is None:
-                    break
+            piece = chunks[0]
+            for chunk in range(1, self.chunks):
+                here = (self.part + turn_index) % self.chunks == chunk
+                piece = jnp.where(here, chunks[chunk], piece)
+            pairs = []
+            for owner, worker, _, chunk, part in self.units():
+                if (part + turn_index) % self.chunks == chunk:
+                    for plane in range(2):
+                        target = plane ^ cross
+                        pairs.append((plane * devices + worker, target * devices + owner))
+            piece = lax.ppermute(piece, ("section", "wide", "tp"), pairs)
+            received.append(hold(piece, *tokens))
         if self.chunks == 1:
             return received[0]
         chunk = (self.wide_index * self.chunks // self.tp) % self.chunks
@@ -579,22 +576,11 @@
             ordered.append(piece)
         return jnp.concatenate(ordered, 0)
 
-    def exchange(self, first, second):
+    def exchange(self, first, second, *tokens):
         mine = [pick(self.section, a, b) for a, b in zip(first, second)]
         other = [pick(self.section, b, a) for a, b in zip(first, second)]
-        same, cross = self.to_owner(mine, 0, 0, both=True), self.to_owner(other, 1, 0, both=True)
+        same, cross = self.to_owner(mine, 0, tokens), self.to_owner(other, 1, tokens)
         return jnp.stack([pick(self.section, same, cross), pick(self.section, cross, same)])
-
-    def owned(self, chunks, layer):
-        return jnp.stack([self.to_owner(chunks, layer, micro) for micro in range(2)])
-
-    def owned_late(self, chunks, layer):
-        own = (self.wide_index * self.chunks // self.tp) % self.chunks
-        result = None
-        for chunk in reversed(range(self.chunks)):
-            part = jnp.stack([self.to_owner(chunks, layer, micro, chunk) for micro in range(2)])
-            result = part if result is None else jnp.where(own == chunk, part, result)
-        return result
 
     def wide_steps(self, value_at):
         return [
@@ -607,7 +593,14 @@
     def wide_gather(self, block):
         if self.wide > 4:
             return lax.all_gather(block, "wide", axis=0, tiled=True)
-        pieces = [block] + self.wide_steps(lambda step: block)
+        return self.wide_join(self.wide_pieces(block))
+
+    def wide_pieces(self, block):
+        if self.wide > 4:
+            return [lax.all_gather(block, "wide", axis=0, tiled=True)]
+        return [block] + self.wide_steps(lambda step: block)
+
+    def wide_join(self, pieces):
         step = 1
         while len(pieces) > 1:
             here = (self.wide_index // step) % 2
@@ -636,11 +629,33 @@
 
         return [share(0)] + self.wide_steps(share)
 
+    def sum_all(self, value, axes):
+        for axis in axes:
+            count = lax.axis_size(axis)
+            step = 1
+            while step < count:
+                pairs = [(index, index ^ step) for index in range(count)]
+                value = value + lax.ppermute(value, axis, pairs)
+                step *= 2
+        return value
+
+    def swap(self, value):
+        return lax.ppermute(value, "section", [(0, 1), (1, 0)])
+
     def send(self, value, source):
         return lax.ppermute(value, "section", [(source, 1 - source)])
 
     def gather(self, block):
-        for bit in reversed(range(self.bits)):
+        return self.gather_rest(self.gather_first(block))
+
+    def gather_first(self, block):
+        return self.gather_bits(block, range(self.bits - 1, 0, -1))
+
+    def gather_rest(self, block):
+        return self.gather_bits(block, [0])
+
+    def gather_bits(self, block, bits):
+        for bit in bits:
             other = lax.ppermute(
                 block, "tp", [(index, index ^ (1 << bit)) for index in range(self.tp)]
             )
@@ -658,7 +673,7 @@
         )
         return pick(here, pieces[0], pieces[1]).astype(f32) + other.astype(f32)
 
-    def scatter_rest(self, block):
+    def scatter_rest(self, block, *tokens):
         for bit in range(1, self.bits):
             half = block.shape[0] // 2
             here = (self.tp_index >> bit) & 1
@@ -667,7 +682,7 @@
             other = lax.ppermute(
                 sent, "tp", [(index, index ^ (1 << bit)) for index in range(self.tp)]
             )
-            block = kept + other.astype(f32)
+            block = kept + hold(other, *tokens).astype(f32)
         return block
 
     def groups(self):
@@ -727,37 +742,29 @@
             jnp.pad(qkv_bias[0], ((0, 0), (0, space))).reshape(-1), up_bias[0],
         ]
     )
-    qkv_there = plan.send(qkv, 0)
-    source = plan.to_work(jnp.where(section == 0, inputs[0, 0], inputs[1, 0]))
-    small_there = lax.ppermute(small, "section", [(0, 1), (1, 0)])
-    rest = jnp.concatenate([up, leaving], 1)
-    share = rest.shape[0] // 2
     first = section == 0
-    halves_there = [plan.send(rest[share:], 0), plan.send(rest[:share], 1)]
-    half_rests = [
-        jnp.where(first, rest[:share], halves_there[0]),
-        jnp.where(first, halves_there[1], rest[share:]),
-    ]
-
-    def gather_rest(half):
-        return lax.all_gather(half, ("wide", "section"), axis=0, tiled=True)
-
-    def gather_qkv(value):
-        value = plan.wide_gather(value).reshape(width, 3, local)
-        return jnp.pad(value, fill).reshape(width, 3 * LANES)
-
-    wq = gather_qkv(jnp.where(first, qkv, qkv_there))
-    rests = [gather_rest(half_rests[0])]
     mixed = 3 * LANES
-    layers = [dict(wq=View(wq, 0, mixed)), {}]
-
-    def views(array):
-        return dict(
-            wu=View(array, 0, hidden), wd=View(array, hidden, hidden),
-            wo=View(array, 2 * hidden, LANES),
+    small_there = plan.swap(small)
+    padded = jnp.pad(qkv_weight[0], fill).reshape(-1, mixed)
+    weights = jnp.concatenate([padded, up, leaving], 1)
+    share = weights.shape[0] // 2
+    half_there = plan.swap(jnp.where(first, weights[share:], weights[:share]))
+
+    def gather_halves(plane_zero, plane_one):
+        half = jnp.where(first, plane_zero, plane_one)
+        array = lax.all_gather(half, ("wide", "section"), axis=0, tiled=True)
+        at = mixed + hidden
+        return array, dict(
+            wq=View(array, 0, mixed), wu=View(array, mixed, hidden),
+            wd=View(array, at, hidden), wo=View(array, at + hidden, LANES),
         )
 
-    layers[0].update(views(rests[0]))
+    source = plan.to_work(jnp.where(first, inputs[0, 0], inputs[1, 0]))
+    weights_first, views_first = gather_halves(weights[:share], half_there)
+    weights_second, views_second = gather_halves(
+        half_there, hold(weights[share:], weights_first)
+    )
+    layers = [views_first, views_second]
     for layer, w in enumerate(layers):
         values = jnp.where(section == layer, small, small_there)
         at = 5 * width
@@ -784,148 +791,215 @@
     outputs, kept = [], []
     blocks = source
 
-    def finished(index, pending, blocks, w):
-        done = plan.scatter_rest(pending)
+    def finished(index, pending, blocks, w, *tokens):
+        done = plan.scatter_rest(pending, *tokens)
         return (blocks[index].astype(f32) + done + w["after"]).astype(bf16)
 
-    for layer in range(2):
+    def step_in(layer, index, x, keys, values, tied):
         w = layers[layer]
-        state, after, pending = [], [], []
-        keys, values = [], []
-        for index in range(plan.chunks):
-            x = plan.gather(blocks[index])
-            a0, a1, q, k, v = project(x, w, chunk_tables[index], chunk_segments[index], heads)
-            keys, values = keys + [plan.all_places(k)], values + [plan.all_places(v)]
-            tied = ()
-            if layer > 0 and pending:
-                tied = (pending[-1],)
-            o, lse = attend(starts[index], q, keys, values, heads, tied)
-            state.append(dict(x=x, a0=a0, a1=a1, q=q, o=o, lse=lse, k=keys, v=values))
-            if layer == 0 and index == 0:
-                there = plan.send(hold(qkv, q), 1)
-                there = gather_qkv(jnp.where(first, there, qkv))
-                layers[1]["wq"] = View(there, 0, mixed)
-                layers[1].update(views(gather_rest(hold(half_rests[1], rests[0]))))
-            if layer > 0:
-                if pending:
-                    after.append(finished(index - 1, pending[-1], blocks, w))
-                s = state[index]
-                s["h"], s["d"], part = feed(a1, o, w, tuple(after))
-                pending.append(plan.scatter_first([part]))
-        if layer == 0:
-            for index, s in enumerate(state):
-                s["h"], s["d"], part = feed(s["a1"], s["o"], w)
-                pending.append(plan.scatter_first([part]))
-        while len(after) < plan.chunks:
-            after.append(finished(len(after), pending[len(after)], blocks, w))
-        kept.append((blocks, state))
-        outputs.append(after)
-        blocks = after
-
-    grads = jnp.where(section == 0, cotangent[0, 0], cotangent[1, 0])
-    grads = plan.to_work_whole(hold(grads, kept[1][1][0]["q"]))
-    gathered = {index: plan.gather(grads[index]) for index in reversed(range(plan.chunks))}
-    held = [hold(item, gathered[0]) for item in outputs[0]]
-    section_outputs = plan.exchange(held, outputs[1])
-    input_grads, weight_grads, small_grads = {}, {}, {}
+        a0, a1, q, k, v = project(x, w, chunk_tables[index], chunk_segments[index], heads, tied)
+        keys.append(plan.all_places(k))
+        values.append(plan.all_places(v))
+        return dict(x=x, a0=a0, a1=a1, q=q, k=list(keys), v=list(values))
+
+    def step_attend(index, s, tied):
+        s["o"], s["lse"] = attend(starts[index], s["q"], s["k"], s["v"], heads, tied)
+
+    def step_out(layer, s, tied):
+        s["h"], s["d"], part = feed(s["a1"], s["o"], layers[layer], tied)
+        return part
+
+    keys, values, state, parts, pending = [], [], [], [], []
+    for index in range(plan.chunks):
+        x = blocks[index]
+        if index == 0:
+            x = hold(x, small_there, half_there)
+        state.append(step_in(0, index, plan.gather(x), keys, values, ()))
+        if index == 0:
+            grads = jnp.where(section == 0, cotangent[0, 0], cotangent[1, 0])
+            grads = plan.to_work_whole(hold(grads, state[0]["q"]))
+        step_attend(index, state[index], ())
+    for index in range(plan.chunks):
+        parts.append(step_out(0, state[index], tuple(grads) if index == last else ()))
+        pending.append(plan.scatter_first([parts[index]]))
+    after = []
+    for index in range(plan.chunks):
+        if after:
+            pending[index] = hold(pending[index], after[-1])
+        after.append(finished(index, pending[index], blocks, layers[0]))
+    kept.append((blocks, state))
+    outputs.append(after)
+
+    blocks = after
+    keys, values, state, pending, after = [], [], [], [], []
+    for index in range(plan.chunks):
+        s = step_in(1, index, plan.gather(blocks[index]), keys, values, ())
+        state.append(s)
+        if index == last:
+            coming = plan.gather_first(hold(grads[last], s["q"]))
+            step_attend(index, s, (parts[0], coming) if last else ())
+        else:
+            step_attend(index, s, ())
+        parts[index] = step_out(1, s, (coming,) if index == last else ())
+        pending.append(plan.scatter_first([parts[index]]))
+    kept.append((blocks, state))
+    pending_out = pending
+    gathered = {last: plan.gather_rest(coming)}
+    for index in range(last):
+        gathered[index] = plan.gather(hold(grads[index], parts[index]))
 
     def over_tokens(left, right):
         left, right = jnp.concatenate(left, 0), jnp.concatenate(right, 0)
         return lax.dot_general(left, right, (((0,), (0,)), ((), ())), preferred_element_type=f32)
 
-    for layer in reversed(range(2)):
-        w = layers[layer]
-        blocks, state = kept[layer]
-        carried = ((), ())
-        after, pending = {}, {}
-        if layer == 0:
-            gathered = {
-                index: plan.gather(grads[index]) for index in reversed(range(plan.chunks))
-            }
-        every_grad = [gathered[index] for index in range(plan.chunks)]
-        grad_up, grad_mixed, sums = {}, {}, 0.0
-        for index in reversed(range(plan.chunks)):
-            s = state[index]
-            dq, dk, dv = attend_back(
-                starts[index], gathered[index], w, s["q"], s["o"], s["lse"],
-                s["k"], s["v"], carried, heads,
+    def step_back(layer, index, gb, carried, tied):
+        s = kept[layer][1][index]
+        dq, dk, dv = attend_back(
+            starts[index], gb, layers[layer], s["q"], s["o"], s["lse"], s["k"], s["v"], carried,
+            heads, tied,
+        )
+        carried = (dk[:-1], dv[:-1])
+        return dq, plan.own_places(dk[-1]), plan.own_places(dv[-1]), carried
+
+    def step_leave(layer, index, s, gu, tied):
+        dq, dk, dv, _ = s
+        x = kept[layer][1][index]["x"]
+        gm, e, norm_part, mixed_part, up_part = leave(
+            x, dq, dk, dv, gu, layers[layer], chunk_tables[index], tied
+        )
+        mixed_part = mixed_part.reshape(3, LANES)[:, :local].reshape(-1)
+        return gm, e, jnp.concatenate([norm_part.reshape(-1), mixed_part, up_part.reshape(-1)])
+
+    def step_grad(layer, index, pending):
+        scaled = plan.scatter_rest(pending)
+        normed, inverse = standardize(kept[layer][0][index].astype(f32))
+        grad = grads[index].astype(f32) + inverse * (
+            scaled
+            - jnp.mean(scaled, -1, keepdims=True)
+            - normed * jnp.mean(scaled * normed, -1, keepdims=True)
+        )
+        return grad.astype(bf16)
+
+    def early_terms(layer, gathered, grad_up):
+        state = kept[layer][1]
+        every = [gathered[index] for index in range(plan.chunks)]
+        ups = [grad_up[index] for index in range(plan.chunks)]
+        return [
+            over_tokens(every, [s["h"] for s in state]).astype(bf16),
+            over_tokens([s["a1"] for s in state], ups).astype(bf16),
+            over_tokens(every, [s["o"] for s in state]).astype(bf16),
+        ]
+
+    def qkv_terms(layer, grad_mixed):
+        term = over_tokens(
+            [s["a0"] for s in kept[layer][1]], [grad_mixed[index] for index in range(plan.chunks)]
+        )
+        return term.astype(bf16)
+
+    def without_fill(array):
+        return array.reshape(-1, 3, LANES)[:, :, :local].reshape(-1, 3 * local)
+
+    def bias_sum(grads):
+        return sum(jnp.sum(item.astype(f32), 0) for item in grads)
+
+    order = list(reversed(range(plan.chunks)))
+    second_grads = grads
+    results, grad_mixed, pending, sums, carried = {}, {}, {}, 0.0, ((), ())
+    grad_up, waiting = {}, tuple(parts)
+    for index in order:
+        results[index] = step_back(1, index, gathered[index], carried, waiting)
+        carried = results[index][-1]
+        grad_up[index] = feed_back(gathered[index], layers[1], kept[1][1][index]["d"])
+        if index == last:
+            token = results[last][0]
+            second_outputs = [
+                finished(other, pending_out[other], blocks, layers[1], token)
+                for other in range(plan.chunks)
+            ]
+            tied = tuple(second_outputs)
+        else:
+            tied = (pending[index + 1],)
+        grad_mixed[index], e, part = step_leave(1, index, results[index], grad_up[index], tied)
+        sums += part
+        pending[index] = plan.scatter_first([e])
+        waiting = (e,)
+    early = jnp.concatenate(early_terms(1, gathered, grad_up), 1)
+    early_second = lax.psum_scatter(
+        early, ("wide", "section"), scatter_dimension=0, tiled=True
+    )
+    after = {}
+    for index in order:
+        if after:
+            pending[index] = hold(pending[index], after[index + 1])
+        after[index] = hold(step_grad(1, index, pending[index]), early)
+    small_second = jnp.concatenate([sums, bias_sum(grads)])
+    second_qkv = qkv_terms(1, grad_mixed)
+    input_second = [after[index] for index in range(plan.chunks)]
+    grads = input_second
+    gathered = {index: plan.gather(grads[index]) for index in order}
+    results, grad_mixed, pending, sums, carried = {}, {}, {}, 0.0, ((), ())
+    grad_up, waiting = {}, ()
+    for index in order:
+        results[index] = step_back(0, index, gathered[index], carried, waiting)
+        carried = results[index][-1]
+        if index == last:
+            for other in order:
+                grad_up[other] = feed_back(
+                    gathered[other], layers[0], kept[0][1][other]["d"]
+                )
+            early = jnp.concatenate(early_terms(0, gathered, grad_up) + [second_qkv], 1)
+            early_sum = lax.psum_scatter(
+                early, ("wide", "section"), scatter_dimension=0, tiled=True
             )
-            carried = (dk[:-1], dv[:-1])
-            dk, dv = plan.own_places(dk[-1]), plan.own_places(dv[-1])
-            if index == last:
-                for other in reversed(range(plan.chunks)):
-                    grad_up[other] = feed_back(gathered[other], w, state[other]["d"])
-                ups = [grad_up[other] for other in range(plan.chunks)]
-                early = [
-                    over_tokens(every_grad, [s["o"] for s in state])[:, :local].astype(bf16),
-                    over_tokens(every_grad, [s["h"] for s in state]).astype(bf16),
-                    over_tokens([s["a1"] for s in state], ups).astype(bf16),
-                ]
-                if layer == 0:
-                    early = jnp.concatenate(early, 1)
-            tied = ()
-            if index < last:
-                tied = (pending[index + 1],)
-            gm, e, norm_part, mixed_part, up_part = leave(
-                s["x"], dq, dk, dv, grad_up[index], w, chunk_tables[index], tied
-            )
-            mixed_part = mixed_part.reshape(3, LANES)[:, :local].reshape(-1)
-            sums += jnp.concatenate([norm_part.reshape(-1), mixed_part, up_part.reshape(-1)])
-            pending[index] = plan.scatter_first([e])
-            if layer == 0 and index == last:
-                early = plan.wide_steps_of(early)
-            if layer == 0 and index == last:
-                held = [hold(item, dq) for item in input_grads[1]]
-                owned_second = plan.owned(held, 1)
-            grad_mixed[index] = gm
-        for index in reversed(range(plan.chunks)):
-            scaled = plan.scatter_rest(pending[index])
-            normed, inverse = standardize(blocks[index].astype(f32))
-            after[index] = grads[index].astype(f32) + inverse * (
-                scaled
-                - jnp.mean(scaled, -1, keepdims=True)
-                - normed * jnp.mean(scaled * normed, -1, keepdims=True)
-            )
-        qkv_term = over_tokens(
-            [s["a0"] for s in state], [grad_mixed[index] for index in range(plan.chunks)]
-        )
-        qkv_term = qkv_term.reshape(width, 3, LANES)[:, :, :local].reshape(width, 3 * local)
-        if layer == 0:
-            early = sum(hold(item, gm).astype(f32) for item in early)
-            weight_grads[0] = [early, plan.wide_scatter(qkv_term.astype(bf16))]
+            token = results[last][0]
+            tied = (early,)
         else:
-            weight_grads[1] = lax.psum_scatter(
-                jnp.concatenate(early + [qkv_term.astype(bf16)], 1),
-                ("wide", "section"), scatter_dimension=0, tiled=True,
-            )
-        bias = sum(jnp.sum(item.astype(f32), 0) for item in grads)
-        small_grads[layer] = jnp.concatenate([sums, bias])
-        input_grads[layer] = [after[index].astype(bf16) for index in range(plan.chunks)]
-        grads = input_grads[layer]
-
-    owned_grads = [plan.owned_late(input_grads[0], 0), owned_second]
-    all_grads = pick(section, *owned_grads).astype(f32)
-    early, qkv_grad = [
-        item + plan.send(item.astype(bf16), 1).astype(f32) for item in weight_grads[0]
-    ]
-    half = weight_grads[1]
-    whole = jnp.concatenate([plan.send(half, 0), half], 0).astype(f32)
-    split = local + 2 * hidden
-    early, qkv_grad = pick(section, early, whole[:, :split]), pick(section, qkv_grad, whole[:, split:])
-    out_grad, down_grad = early[:, :local], early[:, local : local + hidden]
-    up_grad = early[:, local + hidden :]
-    total = jnp.stack([small_grads[0], small_grads[1]])
-    total = lax.all_gather(total, ("section", "wide", "tp"), axis=0)
-    total = pick(section, total[:, 0], total[:, 1]).reshape(2 * plan.wide, plan.tp, -1)
-    total = jnp.sum(total, 0)
+            tied = (pending[index + 1],)
+        grad_mixed[index], e, part = step_leave(0, index, results[index], grad_up[index], tied)
+        sums += part
+        pending[index] = plan.scatter_first([e])
+        waiting = (e,)
+    after = {index: step_grad(0, index, pending[index]) for index in order}
+    input_first = [after[index] for index in range(plan.chunks)]
+    all_grads = plan.exchange(input_first, input_second)
+    held = [hold(item, gathered[last]) for item in second_outputs]
+    section_outputs = plan.exchange(outputs[0], held, all_grads)
+    qkv_shares = plan.wide_steps_of(
+        hold(without_fill(qkv_terms(0, grad_mixed)), after[0])
+    )
+    total = jnp.stack([jnp.concatenate([sums, bias_sum(grads)]), small_second])
     at = 4 * width + 3 * local
-    own = lax.dynamic_index_in_dim(total, plan.tp_index, 0, False)[4 * width : at + hidden]
-    shared = jnp.sum(total, 0)
-    shared = jnp.concatenate([shared[: 4 * width], shared[at + hidden :]])
+    shared = jnp.concatenate([total[:, : 4 * width], total[:, at + hidden :]], 1)
+    shared = plan.sum_all(shared, ("tp",))
+    total = hold(jnp.concatenate([shared, total[:, 4 * width : at + hidden]], 1), after[0])
+    if plan.wide > 4:
+        total = lax.psum(total, "wide")
+    else:
+        terms = [total] + plan.wide_steps(lambda step: total)
+        while len(terms) > 1:
+            terms = [one + two for one, two in zip(terms[::2], terms[1::2])]
+        total = terms[0]
+    first_qkv_sum = sum(item.astype(f32) for item in qkv_shares)
+    split = 2 * hidden + LANES
+    here = plan.send(early_second, 0)
+    there, here_qkv = plan.send(early_sum[:, :split], 1), plan.send(early_sum[:, split:], 0)
+    early = pick(
+        section,
+        jnp.concatenate([early_sum[:, :split], there], 0),
+        jnp.concatenate([here, early_second], 0),
+    ).astype(f32)
+    qkv_grad = first_qkv_sum + plan.send(first_qkv_sum.astype(bf16), 1).astype(f32)
+    second_qkv = without_fill(jnp.concatenate([here_qkv, early_sum[:, split:]], 0)).astype(f32)
+    qkv_grad = pick(section, qkv_grad, second_qkv)
+    down_grad, up_grad = early[:, :hidden], early[:, hidden : 2 * hidden]
+    out_grad = early[:, 2 * hidden : 2 * hidden + local]
+    total = total + plan.swap(total)
+    total = pick(section, total[0], total[1])
+    shared, own = total[: 5 * width], total[5 * width :]
     bias_grad = shared[4 * width :]
     return (
         section_outputs[None, :, None],
-        all_grads[None, :, None],
+        all_grads.astype(f32)[None, :, None],
         shared[: 2 * width].reshape(1, 2, width),
         shared[2 * width : 4 * width].reshape(1, 2, width),
         qkv_grad.reshape(1, -1, 3, local),

time: 799 us -> 714 us (0.89)
  starting transfers between devices: 156 us -> 42.2 us
  waiting for transfers between devices: 204 us -> 314 us
  local copies, waits for them, and re-layouts: 104 us -> 47.9 us
  other arithmetic: 99.3 us -> 63.4 us
  Pallas kernels: 182 us -> 195 us
    ppermute x33 -> x17, starting transfers between devices: 105 us -> 15.7 us  [the longest x4 7.63 us: to_owner(): piece = lax.ppermute(piece, ('section', 'wide', 'tp'), pairs)]
    ppermute x33 -> x17, waiting for transfers between devices: 71.4 us -> 149 us  [the longest x4 63.2 us: to_owner(): piece = lax.ppermute(piece, ('section', 'wide', 'tp'), pairs)]
    ppermute x4 -> x1, waiting for transfers between devices: 12.3 us -> 37.4 us  [to_work(): piece = lax.ppermute(piece, ('wide', 'tp'), pairs)]
    unnamed x475 -> x181, local copies, waits for them, and re-layouts: 57.1 us -> 35 us
    all_gather x3 -> x2, waiting for transfers between devices: 0.04 us -> 15.8 us  [gather_halves(): array = lax.all_gather(half, ('wide', 'section'), axis=0, tiled=True)]
    ppermute x12 -> x6, starting transfers between devices: 22.5 us -> 8.83 us  [wide_steps(): lax.ppermute(value_at(step), 'wide', [(index, index ^ step) for index in...]
    ppermute x12 -> x6, waiting for transfers between devices: 64.7 us -> 52.9 us  [wide_steps(): lax.ppermute(value_at(step), 'wide', [(index, index ^ step) for index in...]
    dynamic_slice x5 -> x1, local copies, waits for them, and re-layouts: 10.7 us -> 1.08 us  [share(): return lax.dynamic_slice_in_dim(block, first, rows, 0)]
  transfers between devices with their start and end apart: 78 -> 41, of which waited for: 23 -> 24; matrix products, arithmetic and copies ran while one was open for 21% -> 12% of each run, Pallas kernels for 21% -> 21%
where the time goes in v3:
time: 714 us; the launch traced here: 708 us
  waiting for transfers between devices  314 us (44%)
  Pallas kernels  195 us (27%)
  other arithmetic  63.4 us (9%)
  local copies, waits for them, and re-layouts  47.9 us (7%)
  starting transfers between devices  42.2 us (6%)
  matrix products  23.3 us (3%)
  between operations  22.6 us (3%)
    pallas_call x2, Pallas kernels, attend_back(): pl.pallas_call(functools.partial(attend_back_kernel, heads, key_block, le...  65.3 us
    ppermute x4, waiting for transfers between devices, to_owner(): piece = lax.ppermute(piece, ('section', 'wide', 'tp'), pairs)  63.2 us
    ppermute x8, waiting for transfers between devices, gather_bits(): lax.ppermute(block, 'tp', [(index, index ^ 1 << bit) for index in range(s...  55.4 us
    ppermute x6, waiting for transfers between devices, wide_steps(): lax.ppermute(value_at(step), 'wide', [(index, index ^ step) for index in...  52.9 us
    pallas_call x2, Pallas kernels, attend(): pl.pallas_call(functools.partial(attend_kernel, heads, key_block, len(key...  48.2 us
    ppermute x1, waiting for transfers between devices, to_work(): piece = lax.ppermute(piece, ('wide', 'tp'), pairs)  37.4 us
    unnamed x181, local copies, waits for them, and re-layouts  35 us
    ppermute x4, waiting for transfers between devices, scatter_rest(): lax.ppermute(sent, 'tp', [(index, index ^ 1 << bit) for index in range(se...  33.1 us
  transfers between devices with their start and end apart: 41, of which 24 were waited for; matrix products, arithmetic and copies ran while one was open for 12% of the time, Pallas kernels for 21%

profile of v3, /device:TPU:4, one launch (start us, length us, event | category | flops | bytes accessed | tf_op | source)
XLA Modules:
  0.0 708.2 jit_solution(2052342768950489938)
XLA Ops:
  10.7 11.5 %collective-permute-done.1 = bf16[96,2560]{1,0:T(8,128)(2,1)S(1)} collective-permute-done((bf16[96,2560]{1,0:T(8,128)(2,1)S(1)}, bf16[96,2560]{1,0:T(8,128)(2,1)S(1)}, u32[]{:S(2)}, u32[]{:S(2)}) %collective-permute-start.1) | collective-permute-done | bytes 491552 | tf_op jit(solution)/shard_map/ppermute | solution.py:643
  24.2 3.4 collective-permute-start
  29.4 2.3 collective-permute-done.2
  34.1 37.4 %collective-permute-done = bf16[512,768]{1,0:T(8,128)(2,1)S(1)} collective-permute-done((bf16[512,768]{1,0:T(8,128)(2,1)}, bf16[512,768]{1,0:T(8,128)(2,1)S(1)}, u32[]{:S(2)}, u32[]{:S(2)}) %collective-permute-start) | collective-permute-done | bytes 786464 | tf_op jit(solution)/shard_map/ppermute | solution.py:523
  71.7 14.9 %collective-permute-done.3 = bf16[512,768]{1,0:T(8,128)(2,1)S(1)} collective-permute-done((bf16[512,768]{1,0:T(8,128)(2,1)S(1)}, bf16[512,768]{1,0:T(8,128)(2,1)S(1)}, u32[]{:S(2)}, u32[]{:S(2)}) %collective-permute-start.3) | collective-permute-done | bytes 786464 | tf_op jit(solution)/shard_map/ppermute | solution.py:659
  88.5 3.3 collective-permute-done.4
  91.7 2.0 broadcast_select_fusion.11
  93.7 1.9 pad_maximum_fusion.1.x_ref
  95.6 15.8 %all-gather.3.cloned.1.call-done.w_ref.wu_ref.wd_ref.wo_ref.wq_ref = bf16[768,2560]{1,0:T(8,128)(2,1)} async-done(((bf16[96,2560]{1,0:T(8,128)(2,1)}), bf16[768,2560]{1,0:T(8,128)(2,1)}) %all-gather.3.cloned.1.call-update) | async-done | bytes 3932176 | tf_op jit(solution)/shard_map/all_gather | solution.py:755
  113.9 9.9 %project.2 = (bf16[2048,768]{1,0:T(8,128)(2,1)S(1)}, bf16[2048,768]{1,0:T(8,128)(2,1)}, bf16[2048,256]{1,0:T(8,128)(2,1)S(1)}, bf16[2048,256]{1,0:T(8,128)(2,1)S(1)}, bf16[2048,256]{1,0:T(8,128)(2,1)S(1)}) custom-call(bf16[2048,768]{1,0:T(8,128)(2,1)} %pad_maximum_fusion.1.x_ref, f32[4,768]{1,0:T(4,128)S(1)} %slice.230.gs_ref, ...), custom_call_target="tpu_custom_call" | custom-call | flops 9200000000 | bytes 9437184 | tf_op jit(solution)/shard_map/project/pallas_call | solution.py:133
  129.9 2.9 collective-permute-start.5
  138.2 24.1 %attend.2 = (bf16[2048,256]{1,0:T(8,128)(2,1)S(1)}, f32[8,2048]{1,0:T(8,128)S(1)}) custom-call(s32[1]{0:T(128)} %constant.98.clone.1.start_ref, bf16[2048,256]{1,0:T(8,128)(2,1)S(1)} %get-tuple-element.49.q_ref, bf16[2048,256]{1,0:T(8,128)(2,1)S(1)} %copy-done.34, bf16[2048,256]{1,0:T(8,128)(2,1)S(1)} %copy-done.37), custom_call_target="tpu_custom_call" | custom-call | flops 32199999488 | bytes 3145728 | tf_op jit(solution)/shard_map/attend/pallas_call | solution.py:286
  162.3 14.0 %collective-permute-done.5.rest_0_ = bf16[512,768]{1,0:T(8,128)(2,1)S(1)} collective-permute-done((bf16[512,768]{1,0:T(8,128)(2,1)}, bf16[512,768]{1,0:T(8,128)(2,1)S(1)}, u32[]{:S(2)}, u32[]{:S(2)}) %collective-permute-start.5) | collective-permute-done | bytes 786464 | tf_op jit(solution)/shard_map/ppermute | solution.py:540
  176.3 13.4 %feed.2 = (bf16[2048,768]{1,0:T(8,128)(2,1)S(1)}, bf16[2048,768]{1,0:T(8,128)(2,1)S(1)}, bf16[2048,768]{1,0:T(8,128)(2,1)}) custom-call(bf16[2048,768]{1,0:T(8,128)(2,1)} %get-tuple-element.48.a_ref, bf16[2048,256]{1,0:T(8,128)(2,1)S(1)} %get-tuple-element.52.o_ref, bf16[768,2560]{1,0:T(8,128)(2,1)} %all-gather.3.cloned.1.call-done.w_ref.wu_ref.wd_ref.wo_ref.wq_ref, ...), custom_call_target="tpu_custom_call" | custom-call | flops 11500000256 | bytes 9437184 | tf_op jit(solution)/shard_map/feed/pallas_call | solution.py:165
  191.3 3.2 broadcast_select_fusion.3
  194.6 3.4 collective-permute-done.6
  199.9 18.5 %collective-permute-done.7 = bf16[512,768]{1,0:T(8,128)(2,1)S(1)} collective-permute-done((bf16[512,768]{1,0:T(8,128)(2,1)S(1)}, bf16[512,768]{1,0:T(8,128)(2,1)S(1)}, u32[]{:S(2)}, u32[]{:S(2)}) %collective-permute-start.7) | collective-permute-done | bytes 786464 | tf_op jit(solution)/shard_map/ppermute | solution.py:682
  220.0 18.5 %collective-permute-done.8 = bf16[512,768]{1,0:T(8,128)(2,1)S(1)} collective-permute-done((bf16[512,768]{1,0:T(8,128)(2,1)S(1)}, bf16[512,768]{1,0:T(8,128)(2,1)S(1)}, u32[]{:S(2)}, u32[]{:S(2)}) %collective-permute-start.8) | collective-permute-done | bytes 786464 | tf_op jit(solution)/shard_map/ppermute | solution.py:659
  240.1 3.7 collective-permute-done.9
  243.8 2.2 broadcast_select_fusion.9
  246.0 1.9 pad_maximum_fusion.2.x_ref
  249.2 9.8 %project.3 = (bf16[2048,768]{1,0:T(8,128)(2,1)S(1)}, bf16[2048,768]{1,0:T(8,128)(2,1)}, bf16[2048,256]{1,0:T(8,128)(2,1)S(1)}, bf16[2048,256]{1,0:T(8,128)(2,1)S(1)}, bf16[2048,256]{1,0:T(8,128)(2,1)S(1)}) custom-call(bf16[2048,768]{1,0:T(8,128)(2,1)} %pad_maximum_fusion.2.x_ref, f32[4,768]{1,0:T(4,128)S(1)} %slice.242.gs_ref, ...), custom_call_target="tpu_custom_call" | custom-call | flops 9200000000 | bytes 9437184 | tf_op jit(solution)/shard_map/project/pallas_call | solution.py:133
  262.5 24.1 %attend.3 = (bf16[2048,256]{1,0:T(8,128)(2,1)S(1)}, f32[8,2048]{1,0:T(8,128)S(1)}) custom-call(s32[1]{0:T(128)} %constant.98.clone.1.start_ref, bf16[2048,256]{1,0:T(8,128)(2,1)S(1)} %get-tuple-element.54.q_ref, bf16[2048,256]{1,0:T(8,128)(2,1)S(1)} %get-tuple-element.56.rest_0_.rest_1_, bf16[2048,256]{1,0:T(8,128)(2,1)S(1)} %get-tuple-element.57.rest_1_.rest_2_), custom_call_target="tpu_custom_call" | custom-call | flops 32199999488 | bytes 3145728 | tf_op jit(solution)/shard_map/attend/pallas_call | solution.py:286
  286.9 13.2 %feed.3 = (bf16[2048,768]{1,0:T(8,128)(2,1)S(1)}, bf16[2048,768]{1,0:T(8,128)(2,1)S(1)}, bf16[2048,768]{1,0:T(8,128)(2,1)}) custom-call(bf16[2048,768]{1,0:T(8,128)(2,1)} %get-tuple-element.55.a_ref, bf16[2048,256]{1,0:T(8,128)(2,1)S(1)} %get-tuple-element.58.o_ref, bf16[768,2560]{1,0:T(8,128)(2,1)} %all-gather.5.cloned.1.call-done.w_ref.wu_ref.wd_ref.wo_ref.wq_ref, ...), custom_call_target="tpu_custom_call" | custom-call | flops 11500000256 | bytes 9437184 | tf_op jit(solution)/shard_map/feed/pallas_call | solution.py:165
  300.1 3.2 broadcast_select_fusion.2
  303.9 2.9 collective-permute-done.12
  310.6 2.0 pad_maximum_fusion.3.gb_ref
  313.3 32.6 %attend_back.2 = (f32[2048,256]{1,0:T(8,128)S(1)}, f32[2048,256]{1,0:T(8,128)S(1)}, f32[2048,256]{1,0:T(8,128)}) custom-call(s32[1]{0:T(128)} %constant.98.clone.1.start_ref, bf16[2048,768]{1,0:T(8,128)(2,1)} %pad_maximum_fusion.3.gb_ref, bf16[768,2560]{1,0:T(8,128)(2,1)} %all-gather.5.cloned.1.call-done.w_ref.wu_ref.wd_ref.wo_ref.wq_ref, ...), custom_call_target="tpu_custom_call" | custom-call | flops 57500000256 | bytes 6291456 | tf_op jit(solution)/shard_map/attend_back/pallas_call | solution.py:390
  348.5 1.9 copy-done.27
  350.3 5.2 feed_back.2.gu_ref
  355.6 4.2 fusion.15
  360.6 12.2 %leave.2 = (bf16[2048,768]{1,0:T(8,128)(2,1)}, bf16[2048,768]{1,0:T(8,128)(2,1)}, f32[4,768]{1,0:T(4,128)S(1)}, f32[1,768]{1,0:T(1,128)S(1)}, f32[1,768]{1,0:T(1,128)S(1)}) custom-call(bf16[2048,768]{1,0:T(8,128)(2,1)} %pad_maximum_fusion.2.x_ref, f32[4,768]{1,0:T(4,128)S(1)} %slice.242.gs_ref, f32[2048,256]{1,0:T(8,128)S(1)} %get-tuple-element.62.dq_ref, ...), custom_call_target="tpu_custom_call" | custom-call | flops 15409999872 | bytes 9437184 | tf_op jit(solution)/shard_map/leave/pallas_call | solution.py:453
  372.9 2.2 broadcast_select_fusion.1
  375.7 2.7 convolution_convert_fusion.5
  382.4 2.7 convolution_convert_fusion
  385.2 14.6 %collective-permute-done.15 = bf16[512,768]{1,0:T(8,128)(2,1)S(1)} collective-permute-done((bf16[512,768]{1,0:T(8,128)(2,1)S(1)}, bf16[512,768]{1,0:T(8,128)(2,1)S(1)}, u32[]{:S(2)}, u32[]{:S(2)}) %collective-permute-start.15) | collective-permute-done | bytes 786464 | tf_op jit(solution)/shard_map/ppermute | solution.py:682
  404.9 15.1 %collective-permute-done.16 = bf16[512,768]{1,0:T(8,128)(2,1)S(1)} collective-permute-done((bf16[512,768]{1,0:T(8,128)(2,1)S(1)}, bf16[512,768]{1,0:T(8,128)(2,1)S(1)}, u32[]{:S(2)}, u32[]{:S(2)}) %collective-permute-start.16) | collective-permute-done | bytes 786464 | tf_op jit(solution)/shard_map/ppermute | solution.py:659
  423.5 5.8 convolution_convert_fusion.2
  429.4 2.5 broadcast_select_fusion.4
  436.7 5.6 feed_back.3.gu_ref
  442.3 2.7 convolution_convert_fusion.4
  445.3 2.7 convolution_convert_fusion.3
  448.0 2.1 pad_maximum_fusion.rest_0_
  453.0 32.7 %attend_back.3 = (f32[2048,256]{1,0:T(8,128)S(1)}, f32[2048,256]{1,0:T(8,128)S(1)}, f32[2048,256]{1,0:T(8,128)}) custom-call(s32[1]{0:T(128)} %constant.98.clone.1.start_ref, bf16[2048,768]{1,0:T(8,128)(2,1)} %copy-done.2, bf16[768,2560]{1,0:T(8,128)(2,1)} %all-gather.3.cloned.1.call-done.w_ref.wu_ref.wd_ref.wo_ref.wq_ref, bf16[2048,256]{1,0:T(8,128)(2,1)S(1)} %copy-done.9, ...), custom_call_target="tpu_custom_call" | custom-call | flops 57500000256 | bytes 6291456 | tf_op jit(solution)/shard_map/attend_back/pallas_call | solution.py:390
  487.2 12.3 %leave.3 = (bf16[2048,768]{1,0:T(8,128)(2,1)}, bf16[2048,768]{1,0:T(8,128)(2,1)}, f32[4,768]{1,0:T(4,128)S(1)}, f32[1,768]{1,0:T(1,128)S(1)}, f32[1,768]{1,0:T(1,128)S(1)}) custom-call(bf16[2048,768]{1,0:T(8,128)(2,1)} %pad_maximum_fusion.1.x_ref, f32[4,768]{1,0:T(4,128)S(1)} %copy-done.7, f32[2048,256]{1,0:T(8,128)S(1)} %get-tuple-element.68.dq_ref, ...), custom_call_target="tpu_custom_call" | custom-call | flops 15409999872 | bytes 9437184 | tf_op jit(solution)/shard_map/leave/pallas_call | solution.py:453
  499.6 3.4 broadcast_select_fusion
  504.6 4.7 convolution_convert_fusion.1
  509.4 1.9 convert_add_fusion
  514.9 16.7 %collective-permute-done.25 = f32[2,3840]{1,0:T(2,128)S(1)} collective-permute-done((f32[2,3840]{1,0:T(2,128)S(1)}, f32[2,3840]{1,0:T(2,128)S(1)}, u32[]{:S(2)}, u32[]{:S(2)}) %collective-permute-start.25) | collective-permute-done | bytes 30752 | tf_op jit(solution)/shard_map/ppermute | solution.py:638
  536.2 3.3 collective-permute-start.28
  543.9 3.2 collective-permute-start.31
  548.3 1.9 collective-permute-start.20
  550.2 3.8 collective-permute-start.21
  554.7 15.7 %collective-permute-done.30 = bf16[192,576]{0,1:T(8,128)(2,1)S(1)} collective-permute-done((bf16[192,576]{0,1:T(8,128)(2,1)S(1)}, bf16[192,576]{0,1:T(8,128)(2,1)S(1)}, u32[]{:S(2)}, u32[]{:S(2)}) %collective-permute-start.30) | collective-permute-done | bytes 221216 | tf_op jit(solution)/shard_map/ppermute | solution.py:587
  570.4 1.9 collective-permute-start.22
  572.3 34.9 %collective-permute-done.31 = bf16[192,576]{0,1:T(8,128)(2,1)S(1)} collective-permute-done((bf16[192,576]{0,1:T(8,128)(2,1)S(1)}, bf16[192,576]{0,1:T(8,128)(2,1)S(1)}, u32[]{:S(2)}, u32[]{:S(2)}) %collective-permute-start.31) | collective-permute-done | bytes 221216 | tf_op jit(solution)/shard_map/ppermute | solution.py:587
  609.1 2.0 collective-permute-start.36
  612.0 42.8 %collective-permute-done.20 = bf16[512,768]{1,0:T(8,128)(2,1)} collective-permute-done((bf16[512,768]{1,0:T(8,128)(2,1)S(1)}, bf16[512,768]{1,0:T(8,128)(2,1)}, u32[]{:S(2)}, u32[]{:S(2)}) %collective-permute-start.20) | collective-permute-done | bytes 786464 | tf_op jit(solution)/shard_map/ppermute | solution.py:564
  656.2 8.9 %collective-permute-done.21 = bf16[512,768]{1,0:T(8,128)(2,1)} collective-permute-done((bf16[512,768]{1,0:T(8,128)(2,1)S(1)}, bf16[512,768]{1,0:T(8,128)(2,1)}, u32[]{:S(2)}, u32[]{:S(2)}) %collective-permute-start.21) | collective-permute-done | bytes 786464 | tf_op jit(solution)/shard_map/ppermute | solution.py:564
  667.8 1.9 maximum_convert_fusion
  669.6 3.0 collective-permute-done.22
  672.6 8.5 %collective-permute-done.23 = bf16[512,768]{1,0:T(8,128)(2,1)} collective-permute-done((bf16[512,768]{1,0:T(8,128)(2,1)}, bf16[512,768]{1,0:T(8,128)(2,1)}, u32[]{:S(2)}, u32[]{:S(2)}) %collective-permute-start.23) | collective-permute-done | bytes 786464 | tf_op jit(solution)/shard_map/ppermute | solution.py:564
  683.5 3.3 collective-permute-start.34
  692.3 5.1 collective-permute-done.35
  (355 shorter events, 95.8 us)
Async XLA Ops:
  7.2 80.8 %copy-start = (s32[2,4,2048]{2,1,0:T(4,128)S(1)}, s32[2,4,2048]{2,1,0:T(4,128)}, u32[]{:S(2)}) copy-start(s32[2,4,2048]{2,1,0:T(4,128)} %param.17) | copy-start | bytes 196612
  7.2 104.2 %all-gather.3.cloned.1.call-start = ((), (), s32[]{:S(2)}) async-start(), calls=%async_computation.2 | async-start | bytes 4423680 | tf_op jit(solution)/shard_map/all_gather | solution.py:755
  9.0 13.1 %copy-start.55 = (bf16[192,2560]{1,0:T(8,128)(2,1)}, bf16[192,2560]{1,0:T(8,128)(2,1)S(1)}, u32[]{:S(2)}) copy-start(bf16[192,2560]{1,0:T(8,128)(2,1)S(1)} %fusion.23) | copy-start | bytes 2949124
  9.1 14.2 %copy-start.66 = (bf16[2,1,512,768]{3,2,1,0:T(8,128)(2,1)S(1)}, bf16[2,1,512,768]{3,2,1,0:T(8,128)(2,1)}, u32[]{:S(2)}) copy-start(bf16[2,1,512,768]{3,2,1,0:T(8,128)(2,1)} %param.15) | copy-start | bytes 4718596
  9.1 13.0 %collective-permute-start.1 = (bf16[96,2560]{1,0:T(8,128)(2,1)S(1)}, bf16[96,2560]{1,0:T(8,128)(2,1)S(1)}, u32[]{:S(2)}, u32[]{:S(2)}) collective-permute-start(bf16[96,2560]{1,0:T(8,128)(2,1)S(1)} %broadcast_select_fusion.30), channel_id=1, source_target_pairs={{0,16},{16,0},{1,17},{17,1},{2,18},{18,2},{3,19},{19,3},{4,20},{20... | collective-permute-start | bytes 1474568 | tf_op jit(solution)/shard_map/ppermute | solution.py:643
  22.2 10.8 %copy-start.64 = (bf16[96,2560]{1,0:T(8,128)(2,1)}, bf16[96,2560]{1,0:T(8,128)(2,1)S(1)}, u32[]{:S(2)}) copy-start(bf16[96,2560]{1,0:T(8,128)(2,1)S(1)} %collective-permute-done.1) | copy-start | bytes 1474564
  23.2 224.8 %all-gather.5.cloned.1.call-start = ((), (), s32[]{:S(2)}) async-start(), calls=%async_computation.3 | async-start | bytes 4423680 | tf_op jit(solution)/shard_map/all_gather | solution.py:755
  24.2 47.4 %collective-permute-start = (bf16[512,768]{1,0:T(8,128)(2,1)}, bf16[512,768]{1,0:T(8,128)(2,1)S(1)}, u32[]{:S(2)}, u32[]{:S(2)}) collective-permute-start(bf16[512,768]{1,0:T(8,128)(2,1)} %select_bitcast_fusion.4), channel_id=1, source_target_pairs={{0,0},{1,8},{2,4},{3,12},{4,2},{5,10},{6,6},{7,14},{8,1},{9,9},{10... | collective-permute-start | bytes 2359304 | tf_op jit(solution)/shard_map/ppermute | solution.py:523
  27.9 3.9 collective-permute-start.2
  71.5 15.2 %copy-start.42 = (bf16[512,768]{1,0:T(8,128)(2,1)}, bf16[512,768]{1,0:T(8,128)(2,1)S(1)}, u32[]{:S(2)}) copy-start(bf16[512,768]{1,0:T(8,128)(2,1)S(1)} %collective-permute-done) | copy-start | bytes 2359300
  71.6 15.0 %collective-permute-start.3 = (bf16[512,768]{1,0:T(8,128)(2,1)S(1)}, bf16[512,768]{1,0:T(8,128)(2,1)S(1)}, u32[]{:S(2)}, u32[]{:S(2)}) collective-permute-start(bf16[512,768]{1,0:T(8,128)(2,1)S(1)} %select_select_fusion), channel_id=1, source_target_pairs={{0,2},{1,3},{2,0},{3,1},{4,6},{5,7},{6,4},{7,5},{8,10},{9,11},{10,... | collective-permute-start | bytes 2359304 | tf_op jit(solution)/shard_map/ppermute | solution.py:659
  88.0 3.8 collective-permute-start.4
  88.4 23.0 %copy-start.6 = (f32[4,768]{1,0:T(4,128)}, f32[4,768]{1,0:T(4,128)S(1)}, u32[]{:S(2)}) copy-start(f32[4,768]{1,0:T(4,128)S(1)} %slice.230.gs_ref) | copy-start | bytes 36868
  113.9 15.0 %copy-start.67 = (bf16[2,1,512,768]{3,2,1,0:T(8,128)(2,1)S(1)}, bf16[2,1,512,768]{3,2,1,0:T(8,128)(2,1)}, u32[]{:S(2)}) copy-start(bf16[2,1,512,768]{3,2,1,0:T(8,128)(2,1)} %param.16) | copy-start | bytes 4718596
  127.4 8.3 %copy-start.8 = (bf16[2048,256]{1,0:T(8,128)(2,1)}, bf16[2048,256]{1,0:T(8,128)(2,1)S(1)}, u32[]{:S(2)}) copy-start(bf16[2048,256]{1,0:T(8,128)(2,1)S(1)} %get-tuple-element.49.q_ref) | copy-start | bytes 3145732
  127.4 7.2 %copy-start.56 = (bf16[192,2560]{1,0:T(8,128)(2,1)S(1)}, bf16[192,2560]{1,0:T(8,128)(2,1)}, u32[]{:S(2)}) copy-start(bf16[192,2560]{1,0:T(8,128)(2,1)} %copy-done.55) | copy-start | bytes 2949124
  127.4 7.2 %copy-start.65 = (bf16[96,2560]{1,0:T(8,128)(2,1)S(1)}, bf16[96,2560]{1,0:T(8,128)(2,1)}, u32[]{:S(2)}) copy-start(bf16[96,2560]{1,0:T(8,128)(2,1)} %copy-done.64) | copy-start | bytes 1474564
  129.9 46.4 %collective-permute-start.5 = (bf16[512,768]{1,0:T(8,128)(2,1)}, bf16[512,768]{1,0:T(8,128)(2,1)S(1)}, u32[]{:S(2)}, u32[]{:S(2)}) collective-permute-start(bf16[512,768]{1,0:T(8,128)(2,1)} %select_bitcast_fusion.3), channel_id=1, source_target_pairs={{0,0},{1,8},{2,4},{3,12},{4,2},{5,10},{6,6},{7,14},{8,1},{9,9},{10... | collective-permute-start | bytes 2359304 | tf_op jit(solution)/shard_map/ppermute | solution.py:540
  135.5 473.6 %reduce-scatter.5.cloned.1.call-start = ((), (), s32[]{:S(2)}) async-start(), calls=%async_computation.5 | async-start | bytes 3096576 | tf_op jit(solution)/shard_map/reduce_scatter | solution.py:927
  162.3 27.3 %copy-start.30 = (bf16[2048,256]{1,0:T(8,128)(2,1)}, bf16[2048,256]{1,0:T(8,128)(2,1)S(1)}, u32[]{:S(2)}) copy-start(bf16[2048,256]{1,0:T(8,128)(2,1)S(1)} %get-tuple-element.52.o_ref) | copy-start | bytes 3145732
  194.5 3.5 collective-permute-start.6
  198.7 19.6 %collective-permute-start.7 = (bf16[512,768]{1,0:T(8,128)(2,1)S(1)}, bf16[512,768]{1,0:T(8,128)(2,1)S(1)}, u32[]{:S(2)}, u32[]{:S(2)}) collective-permute-start(bf16[512,768]{1,0:T(8,128)(2,1)S(1)} %select_convert_fusion.3), channel_id=1, source_target_pairs={{0,2},{1,3},{2,0},{3,1},{4,6},{5,7},{6,4},{7,5},{8,10},{9,11},{10,... | collective-permute-start | bytes 2359304 | tf_op jit(solution)/shard_map/ppermute | solution.py:682
  199.8 19.9 %copy-start.73 = (f32[512]{0:T(512)}, f32[512]{0:T(512)S(1)}, u32[]{:S(2)}) copy-start(f32[512]{0:T(512)S(1)} %broadcast_multiply_fusion.2) | copy-start | bytes 6148
  219.7 20.4 %copy-start.45 = (bf16[512,768]{1,0:T(8,128)(2,1)}, bf16[512,768]{1,0:T(8,128)(2,1)S(1)}, u32[]{:S(2)}) copy-start(bf16[512,768]{1,0:T(8,128)(2,1)S(1)} %get-tuple-element.133) | copy-start | bytes 2359300
  219.7 18.8 %collective-permute-start.8 = (bf16[512,768]{1,0:T(8,128)(2,1)S(1)}, bf16[512,768]{1,0:T(8,128)(2,1)S(1)}, u32[]{:S(2)}, u32[]{:S(2)}) collective-permute-start(bf16[512,768]{1,0:T(8,128)(2,1)S(1)} %get-tuple-element.133), channel_id=1, source_target_pairs={{0,2},{1,3},{2,0},{3,1},{4,6},{5,7},{6,4},{7,5},{8,10},{9,11},{10,... | collective-permute-start | bytes 2359304 | tf_op jit(solution)/shard_map/ppermute | solution.py:659
  240.1 3.8 collective-permute-start.9
  261.9 24.8 %collective-permute-start.10 = (bf16[512,768]{1,0:T(8,128)(2,1)S(1)}, bf16[512,768]{1,0:T(8,128)(2,1)S(1)}, u32[]{:S(2)}, u32[]{:S(2)}) collective-permute-start(bf16[512,768]{1,0:T(8,128)(2,1)S(1)} %broadcast_select_fusion.15), channel_id=1, source_target_pairs={{0,2},{1,3},{2,0},{3,1},{4,6},{5,7},{6,4},{7,5},{8,10},{9,11},{10,... | collective-permute-start | bytes 2359304 | tf_op jit(solution)/shard_map/ppermute | solution.py:659
  303.3 3.5 collective-permute-start.12
  303.4 6.7 collective-permute-start.11
  308.6 46.9 %collective-permute-start.13 = (bf16[512,768]{1,0:T(8,128)(2,1)}, bf16[512,768]{1,0:T(8,128)(2,1)}, u32[]{:S(2)}, u32[]{:S(2)}) collective-permute-start(bf16[512,768]{1,0:T(8,128)(2,1)} %select_convert_fusion.2), channel_id=1, source_target_pairs={{0,2},{1,3},{2,0},{3,1},{4,6},{5,7},{6,4},{7,5},{8,10},{9,11},{10,... | collective-permute-start | bytes 2359304 | tf_op jit(solution)/shard_map/ppermute | solution.py:682
  313.3 35.1 %copy-start.3 = (bf16[2048,768]{1,0:T(8,128)(2,1)S(1)}, bf16[2048,768]{1,0:T(8,128)(2,1)}, u32[]{:S(2)}) copy-start(bf16[2048,768]{1,0:T(8,128)(2,1)} %pad_maximum_fusion.3.gb_ref) | copy-start | bytes 9437188
  359.7 13.1 %copy-start.4 = (bf16[512,768]{1,0:T(8,128)(2,1)}, bf16[512,768]{1,0:T(8,128)(2,1)S(1)}, u32[]{:S(2)}) copy-start(bf16[512,768]{1,0:T(8,128)(2,1)S(1)} %get-tuple-element.165.rest_0_) | copy-start | bytes 2359300
  375.1 4.5 collective-permute-start.14
  380.3 19.5 %copy-start.46 = (bf16[512,768]{1,0:T(8,128)(2,1)S(1)}, bf16[512,768]{1,0:T(8,128)(2,1)}, u32[]{:S(2)}) copy-start(bf16[512,768]{1,0:T(8,128)(2,1)} %copy-done.45) | copy-start | bytes 2359300
  380.3 19.5 %collective-permute-start.15 = (bf16[512,768]{1,0:T(8,128)(2,1)S(1)}, bf16[512,768]{1,0:T(8,128)(2,1)S(1)}, u32[]{:S(2)}, u32[]{:S(2)}) collective-permute-start(bf16[512,768]{1,0:T(8,128)(2,1)S(1)} %select_convert_fusion.1), channel_id=1, source_target_pairs={{0,2},{1,3},{2,0},{3,1},{4,6},{5,7},{6,4},{7,5},{8,10},{9,11},{10,... | collective-permute-start | bytes 2359304 | tf_op jit(solution)/shard_map/ppermute | solution.py:682
  401.3 18.6 %copy-start.53 = (bf16[512,768]{1,0:T(8,128)(2,1)}, bf16[512,768]{1,0:T(8,128)(2,1)S(1)}, u32[]{:S(2)}) copy-start(bf16[512,768]{1,0:T(8,128)(2,1)S(1)} %get-tuple-element.127) | copy-start | bytes 2359300
  401.4 18.6 %collective-permute-start.16 = (bf16[512,768]{1,0:T(8,128)(2,1)S(1)}, bf16[512,768]{1,0:T(8,128)(2,1)S(1)}, u32[]{:S(2)}, u32[]{:S(2)}) collective-permute-start(bf16[512,768]{1,0:T(8,128)(2,1)S(1)} %get-tuple-element.127), channel_id=1, source_target_pairs={{0,2},{1,3},{2,0},{3,1},{4,6},{5,7},{6,4},{7,5},{8,10},{9,11},{10,... | collective-permute-start | bytes 2359304 | tf_op jit(solution)/shard_map/ppermute | solution.py:659
  404.9 277.7 %reduce-scatter.3.cloned.1.call-start = ((), (), s32[]{:S(2)}) async-start(), calls=%async_computation.4 | async-start | bytes 4423680 | tf_op jit(solution)/shard_map/reduce_scatter | solution.py:951
  422.3 7.1 %collective-permute-start.17 = (bf16[1024,768]{1,0:T(8,128)(2,1)}, bf16[1024,768]{1,0:T(8,128)(2,1)}, u32[]{:S(2)}, u32[]{:S(2)}) collective-permute-start(bf16[1024,768]{1,0:T(8,128)(2,1)} %pad_maximum_fusion.9), channel_id=1, source_target_pairs={{0,1},{1,0},{2,3},{3,2},{4,5},{5,4},{6,7},{7,6},{8,9},{9,8},{10,11... | collective-permute-start | bytes 4718600 | tf_op jit(solution)/shard_map/ppermute | solution.py:659
  453.0 32.7 %copy-start.7 = (f32[4,768]{1,0:T(4,128)S(1)}, f32[4,768]{1,0:T(4,128)}, u32[]{:S(2)}) copy-start(f32[4,768]{1,0:T(4,128)} %copy-done.6) | copy-start | bytes 36868
  453.0 32.7 %copy-start.12 = (f32[2048,128]{1,0:T(8,128)S(1)}, f32[2048,128]{1,0:T(8,128)}, u32[]{:S(2)}) copy-start(f32[2048,128]{1,0:T(8,128)} %constant.105.clone.c_ref) | copy-start | bytes 3145732
  453.0 32.7 %copy-start.16 = (f32[2048,128]{1,0:T(8,128)S(1)}, f32[2048,128]{1,0:T(8,128)}, u32[]{:S(2)}) copy-start(f32[2048,128]{1,0:T(8,128)} %constant.106.clone.s_ref) | copy-start | bytes 3145732
  503.0 6.4 collective-permute-start.18
  503.4 8.7 %collective-permute-start.24 = (f32[2,3840]{1,0:T(2,128)S(1)}, f32[2,3840]{1,0:T(2,128)S(1)}, u32[]{:S(2)}, u32[]{:S(2)}) collective-permute-start(f32[2,3840]{1,0:T(2,128)S(1)} %pad_maximum_fusion.11), channel_id=1, source_target_pairs={{0,1},{1,0},{2,3},{3,2},{4,5},{5,4},{6,7},{7,6},{8,9},{9,8},{10,11... | collective-permute-start | bytes 92168 | tf_op jit(solution)/shard_map/ppermute | solution.py:638
  511.5 20.2 %collective-permute-start.19 = (bf16[512,768]{1,0:T(8,128)(2,1)S(1)}, bf16[512,768]{1,0:T(8,128)(2,1)S(1)}, u32[]{:S(2)}, u32[]{:S(2)}) collective-permute-start(bf16[512,768]{1,0:T(8,128)(2,1)S(1)} %select_convert_fusion), channel_id=1, source_target_pairs={{0,2},{1,3},{2,0},{3,1},{4,6},{5,7},{6,4},{7,5},{8,10},{9,11},{10,... | collective-permute-start | bytes 2359304 | tf_op jit(solution)/shard_map/ppermute | solution.py:682
  512.1 19.5 %collective-permute-start.25 = (f32[2,3840]{1,0:T(2,128)S(1)}, f32[2,3840]{1,0:T(2,128)S(1)}, u32[]{:S(2)}, u32[]{:S(2)}) collective-permute-start(f32[2,3840]{1,0:T(2,128)S(1)} %fusion.33), channel_id=1, source_target_pairs={{0,2},{1,3},{2,0},{3,1},{4,6},{5,7},{6,4},{7,5},{8,10},{9,11},{10,... | collective-permute-start | bytes 92168 | tf_op jit(solution)/shard_map/ppermute | solution.py:638
  513.7 18.0 %copy-start.44 = (bf16[512,768]{1,0:T(8,128)(2,1)S(1)}, bf16[512,768]{1,0:T(8,128)(2,1)}, u32[]{:S(2)}) copy-start(bf16[512,768]{1,0:T(8,128)(2,1)} %copy-done.42) | copy-start | bytes 2359300
  513.7 18.0 %copy-start.74 = (f32[512]{0:T(512)S(1)}, f32[512]{0:T(512)}, u32[]{:S(2)}) copy-start(f32[512]{0:T(512)} %copy-done.73) | copy-start | bytes 6148
  535.0 4.6 collective-permute-start.26
  535.1 5.3 collective-permute-start.27
  536.2 5.8 collective-permute-start.28
  542.1 8.1 %collective-permute-start.29 = (f32[2,5184]{1,0:T(2,128)S(1)}, f32[2,5184]{1,0:T(2,128)S(1)}, u32[]{:S(2)}, u32[]{:S(2)}) collective-permute-start(f32[2,5184]{1,0:T(2,128)S(1)} %add_add_fusion), channel_id=1, source_target_pairs={{0,16},{16,0},{1,17},{17,1},{2,18},{18,2},{3,19},{19,3},{4,20},{20... | collective-permute-start | bytes 124424 | tf_op jit(solution)/shard_map/ppermute | solution.py:643
  543.9 26.5 %collective-permute-start.30 = (bf16[192,576]{0,1:T(8,128)(2,1)S(1)}, bf16[192,576]{0,1:T(8,128)(2,1)S(1)}, u32[]{:S(2)}, u32[]{:S(2)}) collective-permute-start(bf16[192,576]{0,1:T(8,128)(2,1)S(1)} %get-tuple-element.159), channel_id=1, source_target_pairs={{0,4},{4,0},{8,12},{12,8},{1,5},{5,1},{9,13},{13,9},{2,6},{6,2},{1... | collective-permute-start | bytes 663560 | tf_op jit(solution)/shard_map/ppermute | solution.py:587
  543.9 63.3 %collective-permute-start.31 = (bf16[192,576]{0,1:T(8,128)(2,1)S(1)}, bf16[192,576]{0,1:T(8,128)(2,1)S(1)}, u32[]{:S(2)}, u32[]{:S(2)}) collective-permute-start(bf16[192,576]{0,1:T(8,128)(2,1)S(1)} %get-tuple-element.161), channel_id=1, source_target_pairs={{0,8},{4,12},{8,0},{12,4},{1,9},{5,13},{9,1},{13,5},{2,10},{6,14},... | collective-permute-start | bytes 663560 | tf_op jit(solution)/shard_map/ppermute | solution.py:587
  547.1 62.0 %collective-permute-start.32 = (bf16[192,576]{0,1:T(8,128)(2,1)}, bf16[192,576]{0,1:T(8,128)(2,1)S(1)}, u32[]{:S(2)}, u32[]{:S(2)}) collective-permute-start(bf16[192,576]{0,1:T(8,128)(2,1)} %get-tuple-element.160), channel_id=1, source_target_pairs={{0,12},{4,8},{8,4},{12,0},{1,13},{5,9},{9,5},{13,1},{2,14},{6,10},... | collective-permute-start | bytes 663560 | tf_op jit(solution)/shard_map/ppermute | solution.py:587
  548.3 106.6 %collective-permute-start.20 = (bf16[512,768]{1,0:T(8,128)(2,1)S(1)}, bf16[512,768]{1,0:T(8,128)(2,1)}, u32[]{:S(2)}, u32[]{:S(2)}) collective-permute-start(bf16[512,768]{1,0:T(8,128)(2,1)S(1)} %broadcast_select_fusion.28), channel_id=1, source_target_pairs={{0,0},{16,16},{8,1},{24,17},{4,2},{20,18},{12,3},{28,19},{2,4},{18... | collective-permute-start | bytes 2359304 | tf_op jit(solution)/shard_map/ppermute | solution.py:564
  550.2 114.9 %collective-permute-start.21 = (bf16[512,768]{1,0:T(8,128)(2,1)S(1)}, bf16[512,768]{1,0:T(8,128)(2,1)}, u32[]{:S(2)}, u32[]{:S(2)}) collective-permute-start(bf16[512,768]{1,0:T(8,128)(2,1)S(1)} %get-tuple-element.128), channel_id=1, source_target_pairs={{0,16},{16,0},{8,17},{24,1},{4,18},{20,2},{12,19},{28,3},{2,20},{1... | collective-permute-start | bytes 2359304 | tf_op jit(solution)/shard_map/ppermute | solution.py:564
  554.7 145.9 %copy-start.75 = (f32[1,768]{1,0:T(1,128)}, f32[1,768]{1,0:T(1,128)S(1)}, u32[]{:S(2)}) copy-start(f32[1,768]{1,0:T(1,128)S(1)} %get-tuple-element.201) | copy-start | bytes 9220
  570.4 102.2 %collective-permute-start.22 = (bf16[512,768]{1,0:T(8,128)(2,1)}, bf16[512,768]{1,0:T(8,128)(2,1)}, u32[]{:S(2)}, u32[]{:S(2)}) collective-permute-start(bf16[512,768]{1,0:T(8,128)(2,1)} %get-tuple-element.148), channel_id=1, source_target_pairs={{0,0},{16,16},{8,1},{24,17},{4,2},{20,18},{12,3},{28,19},{2,4},{18... | collective-permute-start | bytes 2359304 | tf_op jit(solution)/shard_map/ppermute | solution.py:564
  607.2 73.9 %collective-permute-start.23 = (bf16[512,768]{1,0:T(8,128)(2,1)}, bf16[512,768]{1,0:T(8,128)(2,1)}, u32[]{:S(2)}, u32[]{:S(2)}) collective-permute-start(bf16[512,768]{1,0:T(8,128)(2,1)} %get-tuple-element.147), channel_id=1, source_target_pairs={{0,16},{16,0},{8,17},{24,1},{4,18},{20,2},{12,19},{28,3},{2,20},{1... | collective-permute-start | bytes 2359304 | tf_op jit(solution)/shard_map/ppermute | solution.py:564
  609.1 83.2 %collective-permute-start.36 = (bf16[96,1792]{1,0:T(8,128)(2,1)}, bf16[96,1792]{1,0:T(8,128)(2,1)}, u32[]{:S(2)}, u32[]{:S(2)}) collective-permute-start(bf16[96,1792]{1,0:T(8,128)(2,1)} %reduce-scatter.5.cloned.1.call-done), channel_id=1, source_target_pairs={{0,16},{1,17},{2,18},{3,19},{4,20},{5,21},{6,22},{7,23},{8,24},{9,... | collective-permute-start | bytes 1032200 | tf_op jit(solution)/shard_map/ppermute | solution.py:646
  654.9 35.1 %collective-permute-start.33 = (bf16[192,576]{0,1:T(8,128)(2,1)}, bf16[192,576]{0,1:T(8,128)(2,1)}, u32[]{:S(2)}, u32[]{:S(2)}) collective-permute-start(bf16[192,576]{0,1:T(8,128)(2,1)} %fusion.28), channel_id=1, source_target_pairs={{16,0},{17,1},{18,2},{19,3},{20,4},{21,5},{22,6},{23,7},{24,8},{25... | collective-permute-start | bytes 663560 | tf_op jit(solution)/shard_map/ppermute | solution.py:646
  683.5 5.9 collective-permute-start.34
  688.1 9.2 %collective-permute-start.35 = (bf16[96,1792]{1,0:T(8,128)(2,1)S(1)}, bf16[96,1792]{1,0:T(8,128)(2,1)}, u32[]{:S(2)}, u32[]{:S(2)}) collective-permute-start(bf16[96,1792]{1,0:T(8,128)(2,1)S(1)} %slice.323), channel_id=1, source_target_pairs={{16,0},{17,1},{18,2},{19,3},{20,4},{21,5},{22,6},{23,7},{24,8},{25... | collective-permute-start | bytes 1032200 | tf_op jit(solution)/shard_map/ppermute | solution.py:646
  (62 other events, 168.4 us)
Sparse Core Ops, SparseCore 0:
  23.3 88.0 all-gather.2
  135.6 78.5 all-gather.4
  405.0 69.3 reduce-scatter.4
  478.0 132.7 reduce-scatter.2

commit v4 on v3

--- a/solution.py
+++ b/solution.py
@@ -547,7 +547,7 @@
             chunks.append(piece)
         return chunks
 
-    def to_owner(self, chunks, cross, tokens):
+    def to_owner(self, chunks, planes, tokens):
         devices = self.wide * self.tp
         received = []
         for turn_index in range(self.chunks):
@@ -558,8 +558,7 @@
             pairs = []
             for owner, worker, _, chunk, part in self.units():
                 if (part + turn_index) % self.chunks == chunk:
-                    for plane in range(2):
-                        target = plane ^ cross
+                    for plane, target in planes:
                         pairs.append((plane * devices + worker, target * devices + owner))
             piece = lax.ppermute(piece, ("section", "wide", "tp"), pairs)
             received.append(hold(piece, *tokens))
@@ -576,10 +575,14 @@
             ordered.append(piece)
         return jnp.concatenate(ordered, 0)
 
+    def owned(self, chunks, layer, *tokens):
+        return jnp.stack([self.to_owner(chunks, [(micro, layer)], tokens) for micro in range(2)])
+
     def exchange(self, first, second, *tokens):
         mine = [pick(self.section, a, b) for a, b in zip(first, second)]
         other = [pick(self.section, b, a) for a, b in zip(first, second)]
-        same, cross = self.to_owner(mine, 0, tokens), self.to_owner(other, 1, tokens)
+        same = self.to_owner(mine, [(0, 0), (1, 1)], tokens)
+        cross = self.to_owner(other, [(0, 1), (1, 0)], tokens)
         return jnp.stack([pick(self.section, same, cross), pick(self.section, cross, same)])
 
     def wide_steps(self, value_at):
@@ -589,27 +592,6 @@
             )
             for step in range(1, self.wide)
         ]
-
-    def wide_gather(self, block):
-        if self.wide > 4:
-            return lax.all_gather(block, "wide", axis=0, tiled=True)
-        return self.wide_join(self.wide_pieces(block))
-
-    def wide_pieces(self, block):
-        if self.wide > 4:
-            return [lax.all_gather(block, "wide", axis=0, tiled=True)]
-        return [block] + self.wide_steps(lambda step: block)
-
-    def wide_join(self, pieces):
-        step = 1
-        while len(pieces) > 1:
-            here = (self.wide_index // step) % 2
-            pieces = [
-                pick(here, jnp.concatenate([a, b], 0), jnp.concatenate([b, a], 0))
-                for a, b in zip(pieces[::2], pieces[1::2])
-            ]
-            step *= 2
-        return pieces[0]
 
     def wide_scatter(self, block):
         if self.wide > 4:
@@ -817,7 +799,7 @@
         state.append(step_in(0, index, plan.gather(x), keys, values, ()))
         if index == 0:
             grads = jnp.where(section == 0, cotangent[0, 0], cotangent[1, 0])
-            grads = plan.to_work_whole(hold(grads, state[0]["q"]))
+            grads = plan.to_work_whole(hold(grads, weights_first))
         step_attend(index, state[index], ())
     for index in range(plan.chunks):
         parts.append(step_out(0, state[index], tuple(grads) if index == last else ()))
@@ -905,68 +887,65 @@
     order = list(reversed(range(plan.chunks)))
     second_grads = grads
     results, grad_mixed, pending, sums, carried = {}, {}, {}, 0.0, ((), ())
-    grad_up, waiting = {}, tuple(parts)
+    grad_up = {
+        index: feed_back(gathered[index], layers[1], kept[1][1][index]["d"]) for index in order
+    }
+    early = jnp.concatenate(early_terms(1, gathered, grad_up), 1)
+    held = [hold(item, kept[1][1][last]["q"]) for item in outputs[0]]
+    owned_first = plan.owned(held, 0, kept[1][1][last]["o"])
+    early_second = lax.psum_scatter(
+        early, ("wide", "section"), scatter_dimension=0, tiled=True
+    )
+    waiting = tuple(parts) + (early,)
     for index in order:
         results[index] = step_back(1, index, gathered[index], carried, waiting)
         carried = results[index][-1]
-        grad_up[index] = feed_back(gathered[index], layers[1], kept[1][1][index]["d"])
         if index == last:
             token = results[last][0]
             second_outputs = [
                 finished(other, pending_out[other], blocks, layers[1], token)
                 for other in range(plan.chunks)
             ]
-            tied = tuple(second_outputs)
+            tied = (owned_first, *second_outputs)
         else:
             tied = (pending[index + 1],)
         grad_mixed[index], e, part = step_leave(1, index, results[index], grad_up[index], tied)
         sums += part
         pending[index] = plan.scatter_first([e])
         waiting = (e,)
-    early = jnp.concatenate(early_terms(1, gathered, grad_up), 1)
-    early_second = lax.psum_scatter(
-        early, ("wide", "section"), scatter_dimension=0, tiled=True
-    )
     after = {}
     for index in order:
         if after:
             pending[index] = hold(pending[index], after[index + 1])
-        after[index] = hold(step_grad(1, index, pending[index]), early)
+        after[index] = step_grad(1, index, pending[index])
     small_second = jnp.concatenate([sums, bias_sum(grads)])
     second_qkv = qkv_terms(1, grad_mixed)
     input_second = [after[index] for index in range(plan.chunks)]
     grads = input_second
     gathered = {index: plan.gather(grads[index]) for index in order}
     results, grad_mixed, pending, sums, carried = {}, {}, {}, 0.0, ((), ())
-    grad_up, waiting = {}, ()
+    grad_up = {
+        index: feed_back(gathered[index], layers[0], kept[0][1][index]["d"]) for index in order
+    }
+    early = jnp.concatenate(early_terms(0, gathered, grad_up) + [second_qkv], 1)
+    early_sum = lax.psum_scatter(early, ("wide", "section"), scatter_dimension=0, tiled=True)
+    held = [hold(item, gathered[last]) for item in second_outputs]
+    waiting = (early,)
     for index in order:
         results[index] = step_back(0, index, gathered[index], carried, waiting)
         carried = results[index][-1]
-        if index == last:
-            for other in order:
-                grad_up[other] = feed_back(
-                    gathered[other], layers[0], kept[0][1][other]["d"]
-                )
-            early = jnp.concatenate(early_terms(0, gathered, grad_up) + [second_qkv], 1)
-            early_sum = lax.psum_scatter(
-                early, ("wide", "section"), scatter_dimension=0, tiled=True
-            )
-            token = results[last][0]
-            tied = (early,)
-        else:
-            tied = (pending[index + 1],)
+        tied = (early_second,) if index == last else (pending[index + 1],)
         grad_mixed[index], e, part = step_leave(0, index, results[index], grad_up[index], tied)
         sums += part
         pending[index] = plan.scatter_first([e])
         waiting = (e,)
     after = {index: step_grad(0, index, pending[index]) for index in order}
-    input_first = [after[index] for index in range(plan.chunks)]
+    input_first = [hold(after[index], early_sum) for index in range(plan.chunks)]
     all_grads = plan.exchange(input_first, input_second)
-    held = [hold(item, gathered[last]) for item in second_outputs]
-    section_outputs = plan.exchange(outputs[0], held, all_grads)
     qkv_shares = plan.wide_steps_of(
         hold(without_fill(qkv_terms(0, grad_mixed)), after[0])
     )
+    owned_second = plan.owned(held, 1, grad_mixed[0])
     total = jnp.stack([jnp.concatenate([sums, bias_sum(grads)]), small_second])
     at = 4 * width + 3 * local
     shared = jnp.concatenate([total[:, : 4 * width], total[:, at + hidden :]], 1)
@@ -998,7 +977,7 @@
     shared, own = total[: 5 * width], total[5 * width :]
     bias_grad = shared[4 * width :]
     return (
-        section_outputs[None, :, None],
+        pick(section, owned_first, owned_second)[None, :, None],
         all_grads.astype(f32)[None, :, None],
         shared[: 2 * width].reshape(1, 2, width),
         shared[2 * width : 4 * width].reshape(1, 2, width),

time: 714 us -> 714 us (level)
  waiting for transfers between devices: 314 us -> 292 us
  starting transfers between devices: 42.2 us -> 59.4 us
    ppermute x6, waiting for transfers between devices: 52.9 us -> 18 us  [wide_steps(): lax.ppermute(value_at(step), 'wide', [(index, index ^ step) for index in...]
    ppermute x8, waiting for transfers between devices: 55.4 us -> 86.3 us  [gather_bits(): lax.ppermute(block, 'tp', [(index, index ^ 1 << bit) for index in range(s...]
    reduce_scatter x2, waiting for transfers between devices: 0.02 us -> 20.9 us  [on_device(): lax.psum_scatter(early, ('wide', 'section'), scatter_dimension=0, tiled=T...]
    ppermute x4 -> x6, waiting for transfers between devices: 63.2 us -> 42.9 us  [to_owner(): piece = lax.ppermute(piece, ('section', 'wide', 'tp'), pairs)]
    ppermute x2, waiting for transfers between devices: 16.7 us -> 0.01 us  [sum_all(): value = value + lax.ppermute(value, axis, pairs)]
    ppermute x3, starting transfers between devices: 3.81 us -> 17.8 us  [swap(): return lax.ppermute(value, 'section', [(0, 1), (1, 0)])]
    ppermute x1, waiting for transfers between devices: 14 us -> 5.46 us  [to_work_whole(): received.append(lax.ppermute(piece, ('wide', 'tp'), pairs))]
    unnamed x181 -> x189, local copies, waits for them, and re-layouts: 35 us -> 31.4 us
  transfers between devices with their start and end apart: 41 -> 43, of which waited for: 24 -> 26; matrix products, arithmetic and copies ran while one was open for 12% -> 13% of each run, Pallas kernels for 21% -> 24%
where the time goes in v4:
time: 714 us; the launch traced here: 709 us
  waiting for transfers between devices  292 us (41%)
  Pallas kernels  196 us (27%)
  other arithmetic  68.5 us (10%)
  starting transfers between devices  59.4 us (8%)
  local copies, waits for them, and re-layouts  45 us (6%)
  matrix products  25.6 us (4%)
  between operations  22.3 us (3%)
    ppermute x8, waiting for transfers between devices, gather_bits(): lax.ppermute(block, 'tp', [(index, index ^ 1 << bit) for index in range(s...  86.3 us
    pallas_call x2, Pallas kernels, attend_back(): pl.pallas_call(functools.partial(attend_back_kernel, heads, key_block, le...  65.3 us
    pallas_call x2, Pallas kernels, attend(): pl.pallas_call(functools.partial(attend_kernel, heads, key_block, len(key...  48.2 us
    ppermute x6, waiting for transfers between devices, to_owner(): piece = lax.ppermute(piece, ('section', 'wide', 'tp'), pairs)  42.9 us
    ppermute x1, waiting for transfers between devices, to_work(): piece = lax.ppermute(piece, ('wide', 'tp'), pairs)  37.2 us
    ppermute x4, waiting for transfers between devices, scatter_rest(): lax.ppermute(sent, 'tp', [(index, index ^ 1 << bit) for index in range(se...  36.4 us
    unnamed x189, local copies, waits for them, and re-layouts  31.4 us
    pallas_call x2, Pallas kernels, feed(): pl.pallas_call(feed_kernel, grid=(tokens // rows,), in_specs=[rows_spec(r...  26.2 us
  transfers between devices with their start and end apart: 43, of which 26 were waited for; matrix products, arithmetic and copies ran while one was open for 13% of the time, Pallas kernels for 24%

profile of v4, /device:TPU:4, one launch (start us, length us, event | category | flops | bytes accessed | tf_op | source)
XLA Modules:
  0.0 708.7 jit_solution(14642382215590310988)
XLA Ops:
  10.7 11.5 %collective-permute-done.1 = bf16[96,2560]{1,0:T(8,128)(2,1)S(1)} collective-permute-done((bf16[96,2560]{1,0:T(8,128)(2,1)S(1)}, bf16[96,2560]{1,0:T(8,128)(2,1)S(1)}, u32[]{:S(2)}, u32[]{:S(2)}) %collective-permute-start.1) | collective-permute-done | bytes 491552 | tf_op jit(solution)/shard_map/ppermute | solution.py:625
  23.2 3.4 collective-permute-start
  28.5 2.3 collective-permute-done.2
  33.1 37.2 %collective-permute-done = bf16[512,768]{1,0:T(8,128)(2,1)S(1)} collective-permute-done((bf16[512,768]{1,0:T(8,128)(2,1)S(1)}, bf16[512,768]{1,0:T(8,128)(2,1)S(1)}, u32[]{:S(2)}, u32[]{:S(2)}) %collective-permute-start) | collective-permute-done | bytes 786464 | tf_op jit(solution)/shard_map/ppermute | solution.py:523
  70.5 15.2 %collective-permute-done.3 = bf16[512,768]{1,0:T(8,128)(2,1)} collective-permute-done((bf16[512,768]{1,0:T(8,128)(2,1)S(1)}, bf16[512,768]{1,0:T(8,128)(2,1)}, u32[]{:S(2)}, u32[]{:S(2)}) %collective-permute-start.3) | collective-permute-done | bytes 786464 | tf_op jit(solution)/shard_map/ppermute | solution.py:641
  88.7 3.3 collective-permute-done.4
  92.0 2.0 broadcast_select_fusion.11
  95.8 14.4 %all-gather.3.cloned.1.call-done.w_ref.wu_ref.wd_ref.wo_ref.wq_ref = bf16[768,2560]{1,0:T(8,128)(2,1)} async-done(((bf16[96,2560]{1,0:T(8,128)(2,1)}), bf16[768,2560]{1,0:T(8,128)(2,1)}) %all-gather.3.cloned.1.call-update) | async-done | bytes 3932176 | tf_op jit(solution)/shard_map/all_gather | solution.py:737
  112.2 2.3 select_bitcast_fusion.4
  114.5 3.0 collective-permute-start.5
  119.9 9.9 %project.2 = (bf16[2048,768]{1,0:T(8,128)(2,1)S(1)}, bf16[2048,768]{1,0:T(8,128)(2,1)}, bf16[2048,256]{1,0:T(8,128)(2,1)S(1)}, bf16[2048,256]{1,0:T(8,128)(2,1)S(1)}, bf16[2048,256]{1,0:T(8,128)(2,1)S(1)}) custom-call(bf16[2048,768]{1,0:T(8,128)(2,1)} %pad_maximum_fusion.1.x_ref, f32[4,768]{1,0:T(4,128)S(1)} %slice.233.gs_ref, ...), custom_call_target="tpu_custom_call" | custom-call | flops 9200000000 | bytes 9437184 | tf_op jit(solution)/shard_map/project/pallas_call | solution.py:133
  131.5 24.1 %attend.2 = (bf16[2048,256]{1,0:T(8,128)(2,1)S(1)}, f32[8,2048]{1,0:T(8,128)S(1)}) custom-call(s32[1]{0:T(128)} %constant.87.clone.1.start_ref, bf16[2048,256]{1,0:T(8,128)(2,1)S(1)} %get-tuple-element.49.q_ref, bf16[2048,256]{1,0:T(8,128)(2,1)S(1)} %get-tuple-element.50.rest_0_.rest_1_, bf16[2048,256]{1,0:T(8,128)(2,1)S(1)} %get-tuple-element.51.rest_1_.rest_2_), custom_call_target="tpu_custom_call" | custom-call | flops 32199999488 | bytes 3145728 | tf_op jit(solution)/shard_map/attend/pallas_call | solution.py:286
  155.6 5.5 collective-permute-done.5.rest_0_
  161.0 13.4 %feed.2 = (bf16[2048,768]{1,0:T(8,128)(2,1)S(1)}, bf16[2048,768]{1,0:T(8,128)(2,1)S(1)}, bf16[2048,768]{1,0:T(8,128)(2,1)}) custom-call(bf16[2048,768]{1,0:T(8,128)(2,1)} %get-tuple-element.48.a_ref, bf16[2048,256]{1,0:T(8,128)(2,1)S(1)} %get-tuple-element.52.o_ref, bf16[768,2560]{1,0:T(8,128)(2,1)} %all-gather.3.cloned.1.call-done.w_ref.wu_ref.wd_ref.wo_ref.wq_ref, ...), custom_call_target="tpu_custom_call" | custom-call | flops 11500000256 | bytes 9437184 | tf_op jit(solution)/shard_map/feed/pallas_call | solution.py:165
  176.1 3.2 broadcast_select_fusion.3
  179.4 3.4 collective-permute-done.6
  184.6 18.5 %collective-permute-done.7 = bf16[512,768]{1,0:T(8,128)(2,1)S(1)} collective-permute-done((bf16[512,768]{1,0:T(8,128)(2,1)S(1)}, bf16[512,768]{1,0:T(8,128)(2,1)S(1)}, u32[]{:S(2)}, u32[]{:S(2)}) %collective-permute-start.7) | collective-permute-done | bytes 786464 | tf_op jit(solution)/shard_map/ppermute | solution.py:664
  204.7 18.5 %collective-permute-done.8 = bf16[512,768]{1,0:T(8,128)(2,1)S(1)} collective-permute-done((bf16[512,768]{1,0:T(8,128)(2,1)S(1)}, bf16[512,768]{1,0:T(8,128)(2,1)S(1)}, u32[]{:S(2)}, u32[]{:S(2)}) %collective-permute-start.8) | collective-permute-done | bytes 786464 | tf_op jit(solution)/shard_map/ppermute | solution.py:641
  225.1 3.7 collective-permute-done.9
  228.8 2.4 broadcast_select_fusion.9
  234.4 9.9 %project.3 = (bf16[2048,768]{1,0:T(8,128)(2,1)S(1)}, bf16[2048,768]{1,0:T(8,128)(2,1)}, bf16[2048,256]{1,0:T(8,128)(2,1)S(1)}, bf16[2048,256]{1,0:T(8,128)(2,1)S(1)}, bf16[2048,256]{1,0:T(8,128)(2,1)S(1)}) custom-call(bf16[2048,768]{1,0:T(8,128)(2,1)} %pad_maximum_fusion.2.x_ref, f32[4,768]{1,0:T(4,128)S(1)} %slice.245.gs_ref, ...), custom_call_target="tpu_custom_call" | custom-call | flops 9200000000 | bytes 9437184 | tf_op jit(solution)/shard_map/project/pallas_call | solution.py:133
  251.1 24.1 %attend.3 = (bf16[2048,256]{1,0:T(8,128)(2,1)S(1)}, f32[8,2048]{1,0:T(8,128)S(1)}) custom-call(s32[1]{0:T(128)} %constant.87.clone.1.start_ref, bf16[2048,256]{1,0:T(8,128)(2,1)S(1)} %get-tuple-element.54.q_ref, bf16[2048,256]{1,0:T(8,128)(2,1)S(1)} %get-tuple-element.55.rest_0_.rest_1_, bf16[2048,256]{1,0:T(8,128)(2,1)S(1)} %get-tuple-element.56.rest_1_.rest_2_), custom_call_target="tpu_custom_call" | custom-call | flops 32199999488 | bytes 3145728 | tf_op jit(solution)/shard_map/attend/pallas_call | solution.py:286
  276.4 28.2 %collective-permute-done.12 = bf16[512,768]{1,0:T(8,128)(2,1)S(1)} collective-permute-done((bf16[512,768]{1,0:T(8,128)(2,1)S(1)}, bf16[512,768]{1,0:T(8,128)(2,1)S(1)}, u32[]{:S(2)}, u32[]{:S(2)}) %collective-permute-start.12) | collective-permute-done | bytes 786464 | tf_op jit(solution)/shard_map/ppermute | solution.py:641
  305.2 12.8 %feed.3 = (bf16[2048,768]{1,0:T(8,128)(2,1)S(1)}, bf16[2048,768]{1,0:T(8,128)(2,1)S(1)}, bf16[2048,768]{1,0:T(8,128)(2,1)}) custom-call(bf16[2048,768]{1,0:T(8,128)(2,1)} %get-tuple-element.59.a_ref, bf16[2048,256]{1,0:T(8,128)(2,1)S(1)} %get-tuple-element.57.o_ref, bf16[768,2560]{1,0:T(8,128)(2,1)} %all-gather.5.cloned.1.call-done.w_ref.wu_ref.wd_ref.wo_ref.wq_ref, ...), custom_call_target="tpu_custom_call" | custom-call | flops 11500000256 | bytes 9437184 | tf_op jit(solution)/shard_map/feed/pallas_call | solution.py:165
  318.0 3.2 broadcast_select_fusion.2
  325.4 6.1 feed_back.2.gu_ref
  331.5 3.6 convolution_convert_fusion.7
  335.1 2.7 convolution_convert_fusion.5
  337.8 2.7 convolution_convert_fusion.4
  351.9 32.6 %attend_back.2 = (f32[2048,256]{1,0:T(8,128)S(1)}, f32[2048,256]{1,0:T(8,128)S(1)}, f32[2048,256]{1,0:T(8,128)}) custom-call(s32[1]{0:T(128)} %constant.87.clone.1.start_ref, bf16[2048,768]{1,0:T(8,128)(2,1)} %copy-done.2, bf16[768,2560]{1,0:T(8,128)(2,1)} %all-gather.5.cloned.1.call-done.w_ref.wu_ref.wd_ref.wo_ref.wq_ref, bf16[2048,256]{1,0:T(8,128)(2,1)S(1)} %copy-done.8, ...), custom_call_target="tpu_custom_call" | custom-call | flops 57500000256 | bytes 6291456 | tf_op jit(solution)/shard_map/attend_back/pallas_call | solution.py:390
  388.5 12.9 %leave.2 = (bf16[2048,768]{1,0:T(8,128)(2,1)}, bf16[2048,768]{1,0:T(8,128)(2,1)}, f32[4,768]{1,0:T(4,128)S(1)}, f32[1,768]{1,0:T(1,128)S(1)}, f32[1,768]{1,0:T(1,128)S(1)}) custom-call(bf16[2048,768]{1,0:T(8,128)(2,1)} %pad_maximum_fusion.2.x_ref, f32[4,768]{1,0:T(4,128)S(1)} %slice.245.gs_ref, f32[2048,256]{1,0:T(8,128)S(1)} %get-tuple-element.63.dq_ref, ...), custom_call_target="tpu_custom_call" | custom-call | flops 15409999872 | bytes 9437184 | tf_op jit(solution)/shard_map/leave/pallas_call | solution.py:453
  401.4 2.0 broadcast_select_fusion.1
  403.9 3.2 collective-permute-done.16
  407.1 2.9 convert_add_fusion.1
  410.1 2.1 collective-permute-start.17
  412.2 17.9 %collective-permute-done.17 = bf16[512,768]{1,0:T(8,128)(2,1)S(1)} collective-permute-done((bf16[512,768]{1,0:T(8,128)(2,1)S(1)}, bf16[512,768]{1,0:T(8,128)(2,1)S(1)}, u32[]{:S(2)}, u32[]{:S(2)}) %collective-permute-start.17) | collective-permute-done | bytes 786464 | tf_op jit(solution)/shard_map/ppermute | solution.py:664
  433.4 17.5 %collective-permute-done.18 = bf16[512,768]{1,0:T(8,128)(2,1)S(1)} collective-permute-done((bf16[512,768]{1,0:T(8,128)(2,1)S(1)}, bf16[512,768]{1,0:T(8,128)(2,1)S(1)}, u32[]{:S(2)}, u32[]{:S(2)}) %collective-permute-start.18) | collective-permute-done | bytes 786464 | tf_op jit(solution)/shard_map/ppermute | solution.py:641
  453.1 6.6 convolution_convert_fusion.1
  459.8 13.3 %reduce-scatter.3.cloned.1.call-done.rest_0_ = bf16[96,1792]{1,0:T(8,128)(2,1)} async-done(((bf16[768,1792]{1,0:T(8,128)(2,1)}), bf16[96,1792]{1,0:T(8,128)(2,1)}) %reduce-scatter.3.cloned.1.call-update) | async-done | bytes 344080 | tf_op jit(solution)/shard_map/reduce_scatter | solution.py:896
  473.1 3.8 collective-permute-start.38
  476.9 2.0 broadcast_select_fusion.4
  481.8 2.0 copy-done.22
  483.7 2.7 convolution_convert_fusion.3
  486.4 5.6 feed_back.3.gu_ref
  492.0 2.7 convolution_convert_fusion.2
  494.7 2.1 pad_maximum_fusion.rest_3_
  500.6 32.7 %attend_back.3 = (f32[2048,256]{1,0:T(8,128)S(1)}, f32[2048,256]{1,0:T(8,128)S(1)}, f32[2048,256]{1,0:T(8,128)}) custom-call(s32[1]{0:T(128)} %constant.87.clone.1.start_ref, bf16[2048,768]{1,0:T(8,128)(2,1)} %copy-done.3, bf16[768,2560]{1,0:T(8,128)(2,1)} %all-gather.3.cloned.1.call-done.w_ref.wu_ref.wd_ref.wo_ref.wq_ref, bf16[2048,256]{1,0:T(8,128)(2,1)S(1)} %copy-done.30, ...), custom_call_target="tpu_custom_call" | custom-call | flops 57500000256 | bytes 6291456 | tf_op jit(solution)/shard_map/attend_back/pallas_call | solution.py:390
  536.0 12.2 %leave.3 = (bf16[2048,768]{1,0:T(8,128)(2,1)}, bf16[2048,768]{1,0:T(8,128)(2,1)}, f32[4,768]{1,0:T(4,128)S(1)}, f32[1,768]{1,0:T(1,128)S(1)}, f32[1,768]{1,0:T(1,128)S(1)}) custom-call(bf16[2048,768]{1,0:T(8,128)(2,1)} %pad_maximum_fusion.1.x_ref, f32[4,768]{1,0:T(4,128)S(1)} %copy-done.6, f32[2048,256]{1,0:T(8,128)S(1)} %get-tuple-element.72.dq_ref, ...), custom_call_target="tpu_custom_call" | custom-call | flops 15409999872 | bytes 9437184 | tf_op jit(solution)/shard_map/leave/pallas_call | solution.py:453
  548.2 2.0 broadcast_select_fusion
  555.0 3.0 convert_add_fusion
  559.7 3.7 convolution_convert_fusion
  565.2 16.6 %collective-permute-done.20 = bf16[512,768]{1,0:T(8,128)(2,1)S(1)} collective-permute-done((bf16[512,768]{1,0:T(8,128)(2,1)S(1)}, bf16[512,768]{1,0:T(8,128)(2,1)S(1)}, u32[]{:S(2)}, u32[]{:S(2)}) %collective-permute-start.20) | collective-permute-done | bytes 786464 | tf_op jit(solution)/shard_map/ppermute | solution.py:563
  585.8 7.6 %reduce-scatter.5.cloned.1.call-done = bf16[96,2560]{1,0:T(8,128)(2,1)} async-done(((bf16[768,2560]{1,0:T(8,128)(2,1)}), bf16[96,2560]{1,0:T(8,128)(2,1)}) %reduce-scatter.5.cloned.1.call-update) | async-done | bytes 491536 | tf_op jit(solution)/shard_map/reduce_scatter | solution.py:931
  595.3 2.4 broadcast_select_fusion.14
  598.9 5.1 collective-permute-start.28
  604.0 2.4 collective-permute-start.30
  610.0 14.7 %collective-permute-start.31 = (f32[2,5184]{1,0:T(2,128)S(1)}, f32[2,5184]{1,0:T(2,128)S(1)}, u32[]{:S(2)}, u32[]{:S(2)}) collective-permute-start(f32[2,5184]{1,0:T(2,128)S(1)} %add_add_fusion), channel_id=1, source_target_pairs={{0,16},{16,0},{1,17},{17,1},{2,18},{18,2},{3,19},{19,3},{4,20},{20... | collective-permute-start | bytes 124424 | tf_op jit(solution)/shard_map/ppermute | solution.py:625
  626.2 2.9 collective-permute-start.33
  629.2 2.9 collective-permute-done.31
  636.9 2.7 collective-permute-done.32
  639.6 14.2 %collective-permute-done.33 = bf16[192,576]{0,1:T(8,128)(2,1)} collective-permute-done((bf16[192,576]{0,1:T(8,128)(2,1)}, bf16[192,576]{0,1:T(8,128)(2,1)}, u32[]{:S(2)}, u32[]{:S(2)}) %collective-permute-start.33) | collective-permute-done | bytes 221216 | tf_op jit(solution)/shard_map/ppermute | solution.py:590
  662.2 7.0 collective-permute-done.35
  671.7 18.3 %collective-permute-done.25 = bf16[512,768]{1,0:T(8,128)(2,1)} collective-permute-done((bf16[512,768]{1,0:T(8,128)(2,1)}, bf16[512,768]{1,0:T(8,128)(2,1)}, u32[]{:S(2)}, u32[]{:S(2)}) %collective-permute-start.25) | collective-permute-done | bytes 786464 | tf_op jit(solution)/shard_map/ppermute | solution.py:563
  690.0 7.9 %collective-permute-done.24 = bf16[512,768]{1,0:T(8,128)(2,1)} collective-permute-done((bf16[512,768]{1,0:T(8,128)(2,1)}, bf16[512,768]{1,0:T(8,128)(2,1)}, u32[]{:S(2)}, u32[]{:S(2)}) %collective-permute-start.24) | collective-permute-done | bytes 786464 | tf_op jit(solution)/shard_map/ppermute | solution.py:563
  (372 shorter events, 106.0 us)
Async XLA Ops:
  7.2 81.1 %copy-start = (s32[2,4,2048]{2,1,0:T(4,128)S(1)}, s32[2,4,2048]{2,1,0:T(4,128)}, u32[]{:S(2)}) copy-start(s32[2,4,2048]{2,1,0:T(4,128)} %param.17) | copy-start | bytes 196612
  7.2 103.0 %all-gather.3.cloned.1.call-start = ((), (), s32[]{:S(2)}) async-start(), calls=%async_computation.2 | async-start | bytes 4423680 | tf_op jit(solution)/shard_map/all_gather | solution.py:737
  9.1 13.0 %collective-permute-start.1 = (bf16[96,2560]{1,0:T(8,128)(2,1)S(1)}, bf16[96,2560]{1,0:T(8,128)(2,1)S(1)}, u32[]{:S(2)}, u32[]{:S(2)}) collective-permute-start(bf16[96,2560]{1,0:T(8,128)(2,1)S(1)} %broadcast_select_fusion.29), channel_id=1, source_target_pairs={{0,16},{16,0},{1,17},{17,1},{2,18},{18,2},{3,19},{19,3},{4,20},{20... | collective-permute-start | bytes 1474568 | tf_op jit(solution)/shard_map/ppermute | solution.py:625
  23.1 210.1 %all-gather.5.cloned.1.call-start = ((), (), s32[]{:S(2)}) async-start(), calls=%async_computation.3 | async-start | bytes 4423680 | tf_op jit(solution)/shard_map/all_gather | solution.py:737
  23.2 47.2 %collective-permute-start = (bf16[512,768]{1,0:T(8,128)(2,1)S(1)}, bf16[512,768]{1,0:T(8,128)(2,1)S(1)}, u32[]{:S(2)}, u32[]{:S(2)}) collective-permute-start(bf16[512,768]{1,0:T(8,128)(2,1)S(1)} %select_bitcast_fusion.5), channel_id=1, source_target_pairs={{0,0},{1,8},{2,4},{3,12},{4,2},{5,10},{6,6},{7,14},{8,1},{9,9},{10... | collective-permute-start | bytes 2359304 | tf_op jit(solution)/shard_map/ppermute | solution.py:523
  26.9 3.9 collective-permute-start.2
  70.4 16.6 %copy-start.44 = (bf16[512,768]{1,0:T(8,128)(2,1)}, bf16[512,768]{1,0:T(8,128)(2,1)S(1)}, u32[]{:S(2)}) copy-start(bf16[512,768]{1,0:T(8,128)(2,1)S(1)} %collective-permute-done) | copy-start | bytes 2359300
  70.5 15.3 %collective-permute-start.3 = (bf16[512,768]{1,0:T(8,128)(2,1)S(1)}, bf16[512,768]{1,0:T(8,128)(2,1)}, u32[]{:S(2)}, u32[]{:S(2)}) collective-permute-start(bf16[512,768]{1,0:T(8,128)(2,1)S(1)} %select_select_fusion), channel_id=1, source_target_pairs={{0,2},{1,3},{2,0},{3,1},{4,6},{5,7},{6,4},{7,5},{8,10},{9,11},{10,... | collective-permute-start | bytes 2359304 | tf_op jit(solution)/shard_map/ppermute | solution.py:641
  88.2 3.8 collective-permute-start.4
  88.7 30.0 %copy-start.5 = (f32[4,768]{1,0:T(4,128)}, f32[4,768]{1,0:T(4,128)S(1)}, u32[]{:S(2)}) copy-start(f32[4,768]{1,0:T(4,128)S(1)} %slice.233.gs_ref) | copy-start | bytes 36868
  114.5 46.5 %collective-permute-start.5 = (bf16[512,768]{1,0:T(8,128)(2,1)}, bf16[512,768]{1,0:T(8,128)(2,1)S(1)}, u32[]{:S(2)}, u32[]{:S(2)}) collective-permute-start(bf16[512,768]{1,0:T(8,128)(2,1)} %select_bitcast_fusion.4), channel_id=1, source_target_pairs={{0,0},{1,8},{2,4},{3,12},{4,2},{5,10},{6,6},{7,14},{8,1},{9,9},{10... | collective-permute-start | bytes 2359304 | tf_op jit(solution)/shard_map/ppermute | solution.py:540
  118.4 354.7 %reduce-scatter.3.cloned.1.call-start = ((), (), s32[]{:S(2)}) async-start(), calls=%async_computation.4 | async-start | bytes 3096576 | tf_op jit(solution)/shard_map/reduce_scatter | solution.py:896
  131.4 24.1 %copy-start.29 = (bf16[2048,256]{1,0:T(8,128)(2,1)}, bf16[2048,256]{1,0:T(8,128)(2,1)S(1)}, u32[]{:S(2)}) copy-start(bf16[2048,256]{1,0:T(8,128)(2,1)S(1)} %get-tuple-element.49.q_ref) | copy-start | bytes 3145732
  131.4 24.1 %copy-start.31 = (bf16[2048,256]{1,0:T(8,128)(2,1)}, bf16[2048,256]{1,0:T(8,128)(2,1)S(1)}, u32[]{:S(2)}) copy-start(bf16[2048,256]{1,0:T(8,128)(2,1)S(1)} %get-tuple-element.50.rest_0_.rest_1_) | copy-start | bytes 3145732
  131.4 24.1 %copy-start.33 = (bf16[2048,256]{1,0:T(8,128)(2,1)}, bf16[2048,256]{1,0:T(8,128)(2,1)S(1)}, u32[]{:S(2)}) copy-start(bf16[2048,256]{1,0:T(8,128)(2,1)S(1)} %get-tuple-element.51.rest_1_.rest_2_) | copy-start | bytes 3145732
  155.6 18.8 %copy-start.27 = (bf16[2048,256]{1,0:T(8,128)(2,1)}, bf16[2048,256]{1,0:T(8,128)(2,1)S(1)}, u32[]{:S(2)}) copy-start(bf16[2048,256]{1,0:T(8,128)(2,1)S(1)} %get-tuple-element.52.o_ref) | copy-start | bytes 3145732
  179.3 3.5 collective-permute-start.6
  183.4 19.6 %collective-permute-start.7 = (bf16[512,768]{1,0:T(8,128)(2,1)S(1)}, bf16[512,768]{1,0:T(8,128)(2,1)S(1)}, u32[]{:S(2)}, u32[]{:S(2)}) collective-permute-start(bf16[512,768]{1,0:T(8,128)(2,1)S(1)} %select_convert_fusion.3), channel_id=1, source_target_pairs={{0,2},{1,3},{2,0},{3,1},{4,6},{5,7},{6,4},{7,5},{8,10},{9,11},{10,... | collective-permute-start | bytes 2359304 | tf_op jit(solution)/shard_map/ppermute | solution.py:664
  184.6 19.8 %copy-start.75 = (f32[512]{0:T(512)}, f32[512]{0:T(512)S(1)}, u32[]{:S(2)}) copy-start(f32[512]{0:T(512)S(1)} %broadcast_multiply_fusion.2) | copy-start | bytes 6148
  204.4 19.0 %copy-start.40 = (bf16[512,768]{1,0:T(8,128)(2,1)}, bf16[512,768]{1,0:T(8,128)(2,1)S(1)}, u32[]{:S(2)}) copy-start(bf16[512,768]{1,0:T(8,128)(2,1)S(1)} %get-tuple-element.133) | copy-start | bytes 2359300
  204.4 18.8 %collective-permute-start.8 = (bf16[512,768]{1,0:T(8,128)(2,1)S(1)}, bf16[512,768]{1,0:T(8,128)(2,1)S(1)}, u32[]{:S(2)}, u32[]{:S(2)}) collective-permute-start(bf16[512,768]{1,0:T(8,128)(2,1)S(1)} %get-tuple-element.133), channel_id=1, source_target_pairs={{0,2},{1,3},{2,0},{3,1},{4,6},{5,7},{6,4},{7,5},{8,10},{9,11},{10,... | collective-permute-start | bytes 2359304 | tf_op jit(solution)/shard_map/ppermute | solution.py:641
  225.1 3.8 collective-permute-start.9
  247.3 74.1 %collective-permute-start.10 = (bf16[512,768]{1,0:T(8,128)(2,1)S(1)}, bf16[512,768]{1,0:T(8,128)(2,1)S(1)}, u32[]{:S(2)}, u32[]{:S(2)}) collective-permute-start(bf16[512,768]{1,0:T(8,128)(2,1)S(1)} %broadcast_select_fusion.17), channel_id=1, source_target_pairs={{0,0},{8,1},{4,2},{12,3},{2,4},{10,5},{6,6},{14,7},{1,8},{9,9},{5,... | collective-permute-start | bytes 2359304 | tf_op jit(solution)/shard_map/ppermute | solution.py:563
  249.2 73.2 %collective-permute-start.11 = (bf16[512,768]{1,0:T(8,128)(2,1)S(1)}, bf16[512,768]{1,0:T(8,128)(2,1)S(1)}, u32[]{:S(2)}, u32[]{:S(2)}) collective-permute-start(bf16[512,768]{1,0:T(8,128)(2,1)S(1)} %broadcast_select_fusion.17), channel_id=1, source_target_pairs={{16,0},{24,1},{20,2},{28,3},{18,4},{26,5},{22,6},{30,7},{17,8},{25... | collective-permute-start | bytes 2359304 | tf_op jit(solution)/shard_map/ppermute | solution.py:563
  251.0 53.7 %collective-permute-start.12 = (bf16[512,768]{1,0:T(8,128)(2,1)S(1)}, bf16[512,768]{1,0:T(8,128)(2,1)S(1)}, u32[]{:S(2)}, u32[]{:S(2)}) collective-permute-start(bf16[512,768]{1,0:T(8,128)(2,1)S(1)} %broadcast_select_fusion.16), channel_id=1, source_target_pairs={{0,2},{1,3},{2,0},{3,1},{4,6},{5,7},{6,4},{7,5},{8,10},{9,11},{10,... | collective-permute-start | bytes 2359304 | tf_op jit(solution)/shard_map/ppermute | solution.py:641
  275.2 56.3 %copy-start.9 = (bf16[2048,256]{1,0:T(8,128)(2,1)}, bf16[2048,256]{1,0:T(8,128)(2,1)S(1)}, u32[]{:S(2)}) copy-start(bf16[2048,256]{1,0:T(8,128)(2,1)S(1)} %get-tuple-element.57.o_ref) | copy-start | bytes 3145732
  304.9 18.7 %collective-permute-start.13 = (bf16[1024,768]{1,0:T(8,128)(2,1)S(1)}, bf16[1024,768]{1,0:T(8,128)(2,1)S(1)}, u32[]{:S(2)}, u32[]{:S(2)}) collective-permute-start(bf16[1024,768]{1,0:T(8,128)(2,1)S(1)} %pad_maximum_fusion.8.rest_0_), channel_id=1, source_target_pairs={{0,1},{1,0},{2,3},{3,2},{4,5},{5,4},{6,7},{7,6},{8,9},{9,8},{10,11... | collective-permute-start | bytes 4718600 | tf_op jit(solution)/shard_map/ppermute | solution.py:641
  321.2 19.4 %collective-permute-start.14 = (bf16[1024,768]{1,0:T(8,128)(2,1)}, bf16[1024,768]{1,0:T(8,128)(2,1)}, u32[]{:S(2)}, u32[]{:S(2)}) collective-permute-start(bf16[1024,768]{1,0:T(8,128)(2,1)} %broadcast_select_fusion.2), channel_id=1, source_target_pairs={{0,1},{1,0},{2,3},{3,2},{4,5},{5,4},{6,7},{7,6},{8,9},{9,8},{10,11... | collective-permute-start | bytes 4718600 | tf_op jit(solution)/shard_map/ppermute | solution.py:653
  345.2 40.4 %collective-permute-start.15 = (bf16[512,768]{1,0:T(8,128)(2,1)}, bf16[512,768]{1,0:T(8,128)(2,1)S(1)}, u32[]{:S(2)}, u32[]{:S(2)}) collective-permute-start(bf16[512,768]{1,0:T(8,128)(2,1)} %select_convert_fusion.2), channel_id=1, source_target_pairs={{0,2},{1,3},{2,0},{3,1},{4,6},{5,7},{6,4},{7,5},{8,10},{9,11},{10,... | collective-permute-start | bytes 2359304 | tf_op jit(solution)/shard_map/ppermute | solution.py:664
  351.9 34.7 %copy-start.42 = (bf16[512,768]{1,0:T(8,128)(2,1)S(1)}, bf16[512,768]{1,0:T(8,128)(2,1)}, u32[]{:S(2)}) copy-start(bf16[512,768]{1,0:T(8,128)(2,1)} %copy-done.40) | copy-start | bytes 2359300
  351.9 34.7 %copy-start.48 = (f32[1024,768]{1,0:T(8,128)S(1)}, f32[1024,768]{1,0:T(8,128)}, u32[]{:S(2)}) copy-start(f32[1024,768]{1,0:T(8,128)} %copy-done.47) | copy-start | bytes 9437188
  403.5 3.6 collective-permute-start.16
  403.8 189.6 %reduce-scatter.5.cloned.1.call-start = ((), (), s32[]{:S(2)}) async-start(), calls=%async_computation.5 | async-start | bytes 4423680 | tf_op jit(solution)/shard_map/reduce_scatter | solution.py:931
  410.0 20.2 %copy-start.43 = (bf16[512,768]{1,0:T(8,128)(2,1)S(1)}, bf16[512,768]{1,0:T(8,128)(2,1)}, u32[]{:S(2)}) copy-start(bf16[512,768]{1,0:T(8,128)(2,1)} %copy-done.40) | copy-start | bytes 2359300
  410.1 20.0 %collective-permute-start.17 = (bf16[512,768]{1,0:T(8,128)(2,1)S(1)}, bf16[512,768]{1,0:T(8,128)(2,1)S(1)}, u32[]{:S(2)}, u32[]{:S(2)}) collective-permute-start(bf16[512,768]{1,0:T(8,128)(2,1)S(1)} %select_convert_fusion.1), channel_id=1, source_target_pairs={{0,2},{1,3},{2,0},{3,1},{4,6},{5,7},{6,4},{7,5},{8,10},{9,11},{10,... | collective-permute-start | bytes 2359304 | tf_op jit(solution)/shard_map/ppermute | solution.py:664
  431.6 19.5 %copy-start.51 = (bf16[512,768]{1,0:T(8,128)(2,1)}, bf16[512,768]{1,0:T(8,128)(2,1)S(1)}, u32[]{:S(2)}) copy-start(bf16[512,768]{1,0:T(8,128)(2,1)S(1)} %get-tuple-element.127) | copy-start | bytes 2359300
  431.6 19.3 %collective-permute-start.18 = (bf16[512,768]{1,0:T(8,128)(2,1)S(1)}, bf16[512,768]{1,0:T(8,128)(2,1)S(1)}, u32[]{:S(2)}, u32[]{:S(2)}) collective-permute-start(bf16[512,768]{1,0:T(8,128)(2,1)S(1)} %get-tuple-element.127), channel_id=1, source_target_pairs={{0,2},{1,3},{2,0},{3,1},{4,6},{5,7},{6,4},{7,5},{8,10},{9,11},{10,... | collective-permute-start | bytes 2359304 | tf_op jit(solution)/shard_map/ppermute | solution.py:641
  452.4 24.5 %collective-permute-start.19 = (bf16[1024,768]{1,0:T(8,128)(2,1)}, bf16[1024,768]{1,0:T(8,128)(2,1)}, u32[]{:S(2)}, u32[]{:S(2)}) collective-permute-start(bf16[1024,768]{1,0:T(8,128)(2,1)} %pad_maximum_fusion.10), channel_id=1, source_target_pairs={{0,1},{1,0},{2,3},{3,2},{4,5},{5,4},{6,7},{7,6},{8,9},{9,8},{10,11... | collective-permute-start | bytes 4718600 | tf_op jit(solution)/shard_map/ppermute | solution.py:641
  459.8 90.8 %copy-start.68 = (f32[1,5184]{1,0:T(1,128)}, f32[1,5184]{1,0:T(1,128)S(1)}, u32[]{:S(2)}) copy-start(f32[1,5184]{1,0:T(1,128)S(1)} %stack.55) | copy-start | bytes 62212
  473.1 185.9 %collective-permute-start.38 = (bf16[96,1792]{1,0:T(8,128)(2,1)}, bf16[96,1792]{1,0:T(8,128)(2,1)}, u32[]{:S(2)}, u32[]{:S(2)}) collective-permute-start(bf16[96,1792]{1,0:T(8,128)(2,1)} %reduce-scatter.3.cloned.1.call-done.rest_0_), channel_id=1, source_target_pairs={{0,16},{1,17},{2,18},{3,19},{4,20},{5,21},{6,22},{7,23},{8,24},{9,... | collective-permute-start | bytes 1032200 | tf_op jit(solution)/shard_map/ppermute | solution.py:628
  500.5 33.9 %copy-start.4 = (bf16[96,1792]{1,0:T(8,128)(2,1)S(1)}, bf16[96,1792]{1,0:T(8,128)(2,1)}, u32[]{:S(2)}) copy-start(bf16[96,1792]{1,0:T(8,128)(2,1)} %reduce-scatter.3.cloned.1.call-done.rest_0_) | copy-start | bytes 1032196
  500.6 33.9 %copy-start.6 = (f32[4,768]{1,0:T(4,128)S(1)}, f32[4,768]{1,0:T(4,128)}, u32[]{:S(2)}) copy-start(f32[4,768]{1,0:T(4,128)} %copy-done.5) | copy-start | bytes 36868
  500.6 33.9 %copy-start.13 = (f32[2048,128]{1,0:T(8,128)S(1)}, f32[2048,128]{1,0:T(8,128)}, u32[]{:S(2)}) copy-start(f32[2048,128]{1,0:T(8,128)} %constant.103.clone.c_ref) | copy-start | bytes 3145732
  500.6 33.9 %copy-start.17 = (f32[2048,128]{1,0:T(8,128)S(1)}, f32[2048,128]{1,0:T(8,128)}, u32[]{:S(2)}) copy-start(f32[2048,128]{1,0:T(8,128)} %constant.104.clone.s_ref) | copy-start | bytes 3145732
  550.2 4.7 collective-permute-start.22
  550.7 3.6 collective-permute-start.26
  552.0 29.8 %collective-permute-start.20 = (bf16[512,768]{1,0:T(8,128)(2,1)S(1)}, bf16[512,768]{1,0:T(8,128)(2,1)S(1)}, u32[]{:S(2)}, u32[]{:S(2)}) collective-permute-start(bf16[512,768]{1,0:T(8,128)(2,1)S(1)} %broadcast_select_fusion.15), channel_id=1, source_target_pairs={{0,16},{8,17},{4,18},{12,19},{2,20},{10,21},{6,22},{14,23},{1,24},... | collective-permute-start | bytes 2359304 | tf_op jit(solution)/shard_map/ppermute | solution.py:563
  553.3 28.5 %collective-permute-start.21 = (bf16[512,768]{1,0:T(8,128)(2,1)S(1)}, bf16[512,768]{1,0:T(8,128)(2,1)S(1)}, u32[]{:S(2)}, u32[]{:S(2)}) collective-permute-start(bf16[512,768]{1,0:T(8,128)(2,1)S(1)} %broadcast_select_fusion.15), channel_id=1, source_target_pairs={{16,16},{24,17},{20,18},{28,19},{18,20},{26,21},{22,22},{30,23},{1... | collective-permute-start | bytes 2359304 | tf_op jit(solution)/shard_map/ppermute | solution.py:563
  554.3 10.2 %collective-permute-start.27 = (f32[2,3840]{1,0:T(2,128)S(1)}, f32[2,3840]{1,0:T(2,128)S(1)}, u32[]{:S(2)}, u32[]{:S(2)}) collective-permute-start(f32[2,3840]{1,0:T(2,128)S(1)} %fusion.34), channel_id=1, source_target_pairs={{0,2},{1,3},{2,0},{3,1},{4,6},{5,7},{6,4},{7,5},{8,10},{9,11},{10,... | collective-permute-start | bytes 92168 | tf_op jit(solution)/shard_map/ppermute | solution.py:620
  558.1 26.4 %collective-permute-start.23 = (bf16[512,768]{1,0:T(8,128)(2,1)S(1)}, bf16[512,768]{1,0:T(8,128)(2,1)S(1)}, u32[]{:S(2)}, u32[]{:S(2)}) collective-permute-start(bf16[512,768]{1,0:T(8,128)(2,1)S(1)} %select_convert_fusion), channel_id=1, source_target_pairs={{0,2},{1,3},{2,0},{3,1},{4,6},{5,7},{6,4},{7,5},{8,10},{9,11},{10,... | collective-permute-start | bytes 2359304 | tf_op jit(solution)/shard_map/ppermute | solution.py:664
  598.9 9.9 %collective-permute-start.28 = (f32[2,5184]{1,0:T(2,128)S(1)}, f32[2,5184]{1,0:T(2,128)S(1)}, u32[]{:S(2)}, u32[]{:S(2)}) collective-permute-start(f32[2,5184]{1,0:T(2,128)S(1)} %fusion.31), channel_id=1, source_target_pairs={{0,4},{4,0},{8,12},{12,8},{1,5},{5,1},{9,13},{13,9},{2,6},{6,2},{1... | collective-permute-start | bytes 124424 | tf_op jit(solution)/shard_map/ppermute | solution.py:590
  604.0 5.2 collective-permute-start.29
  604.0 5.9 collective-permute-start.30
  607.5 18.5 %copy-start.63 = (bf16[96,1792]{1,0:T(8,128)(2,1)}, bf16[96,1792]{1,0:T(8,128)(2,1)S(1)}, u32[]{:S(2)}) copy-start(bf16[96,1792]{1,0:T(8,128)(2,1)S(1)} %slice.325) | copy-start | bytes 1032196
  607.5 51.6 %collective-permute-start.37 = (bf16[96,1792]{1,0:T(8,128)(2,1)S(1)}, bf16[96,1792]{1,0:T(8,128)(2,1)}, u32[]{:S(2)}, u32[]{:S(2)}) collective-permute-start(bf16[96,1792]{1,0:T(8,128)(2,1)S(1)} %slice.325), channel_id=1, source_target_pairs={{16,0},{17,1},{18,2},{19,3},{20,4},{21,5},{22,6},{23,7},{24,8},{25... | collective-permute-start | bytes 1032200 | tf_op jit(solution)/shard_map/ppermute | solution.py:628
  610.0 22.1 %collective-permute-start.31 = (f32[2,5184]{1,0:T(2,128)S(1)}, f32[2,5184]{1,0:T(2,128)S(1)}, u32[]{:S(2)}, u32[]{:S(2)}) collective-permute-start(f32[2,5184]{1,0:T(2,128)S(1)} %add_add_fusion), channel_id=1, source_target_pairs={{0,16},{16,0},{1,17},{17,1},{2,18},{18,2},{3,19},{19,3},{4,20},{20... | collective-permute-start | bytes 124424 | tf_op jit(solution)/shard_map/ppermute | solution.py:625
  626.0 13.7 %collective-permute-start.32 = (bf16[192,576]{0,1:T(8,128)(2,1)}, bf16[192,576]{0,1:T(8,128)(2,1)S(1)}, u32[]{:S(2)}, u32[]{:S(2)}) collective-permute-start(bf16[192,576]{0,1:T(8,128)(2,1)} %get-tuple-element.154), channel_id=1, source_target_pairs={{0,4},{4,0},{8,12},{12,8},{1,5},{5,1},{9,13},{13,9},{2,6},{6,2},{1... | collective-permute-start | bytes 663560 | tf_op jit(solution)/shard_map/ppermute | solution.py:590
  626.2 27.6 %collective-permute-start.33 = (bf16[192,576]{0,1:T(8,128)(2,1)}, bf16[192,576]{0,1:T(8,128)(2,1)}, u32[]{:S(2)}, u32[]{:S(2)}) collective-permute-start(bf16[192,576]{0,1:T(8,128)(2,1)} %get-tuple-element.156), channel_id=1, source_target_pairs={{0,8},{4,12},{8,0},{12,4},{1,9},{5,13},{9,1},{13,5},{2,10},{6,14},... | collective-permute-start | bytes 663560 | tf_op jit(solution)/shard_map/ppermute | solution.py:590
  632.1 4.1 collective-permute-start.36
  636.2 19.6 %collective-permute-start.34 = (bf16[192,576]{0,1:T(8,128)(2,1)}, bf16[192,576]{0,1:T(8,128)(2,1)}, u32[]{:S(2)}, u32[]{:S(2)}) collective-permute-start(bf16[192,576]{0,1:T(8,128)(2,1)} %get-tuple-element.155), channel_id=1, source_target_pairs={{0,12},{4,8},{8,4},{12,0},{1,13},{5,9},{9,5},{13,1},{2,14},{6,10},... | collective-permute-start | bytes 663560 | tf_op jit(solution)/shard_map/ppermute | solution.py:590
  636.9 22.1 %copy-start.64 = (bf16[96,1792]{1,0:T(8,128)(2,1)S(1)}, bf16[96,1792]{1,0:T(8,128)(2,1)}, u32[]{:S(2)}) copy-start(bf16[96,1792]{1,0:T(8,128)(2,1)} %copy-done.63) | copy-start | bytes 1032196
  639.6 50.3 %collective-permute-start.25 = (bf16[512,768]{1,0:T(8,128)(2,1)}, bf16[512,768]{1,0:T(8,128)(2,1)}, u32[]{:S(2)}, u32[]{:S(2)}) collective-permute-start(bf16[512,768]{1,0:T(8,128)(2,1)} %broadcast_select_fusion.13), channel_id=1, source_target_pairs={{0,16},{16,0},{8,17},{24,1},{4,18},{20,2},{12,19},{28,3},{2,20},{1... | collective-permute-start | bytes 2359304 | tf_op jit(solution)/shard_map/ppermute | solution.py:563
  653.8 44.1 %collective-permute-start.24 = (bf16[512,768]{1,0:T(8,128)(2,1)}, bf16[512,768]{1,0:T(8,128)(2,1)}, u32[]{:S(2)}, u32[]{:S(2)}) collective-permute-start(bf16[512,768]{1,0:T(8,128)(2,1)} %get-tuple-element.128), channel_id=1, source_target_pairs={{0,0},{16,16},{8,1},{24,17},{4,2},{20,18},{12,3},{28,19},{2,4},{18... | collective-permute-start | bytes 2359304 | tf_op jit(solution)/shard_map/ppermute | solution.py:563
  657.7 11.4 %collective-permute-start.35 = (bf16[192,576]{0,1:T(8,128)(2,1)}, bf16[192,576]{0,1:T(8,128)(2,1)}, u32[]{:S(2)}, u32[]{:S(2)}) collective-permute-start(bf16[192,576]{0,1:T(8,128)(2,1)} %fusion.29), channel_id=1, source_target_pairs={{16,0},{17,1},{18,2},{19,3},{20,4},{21,5},{22,6},{23,7},{24,8},{25... | collective-permute-start | bytes 663560 | tf_op jit(solution)/shard_map/ppermute | solution.py:628
  (68 other events, 241.7 us)
Sparse Core Ops, SparseCore 0:
  23.2 87.0 all-gather.2
  118.5 80.4 all-gather.4
  403.9 69.1 reduce-scatter.2
  497.0 96.3 reduce-scatter.4

commit v5 on v4

--- a/solution.py
+++ b/solution.py
@@ -892,7 +892,6 @@
     }
     early = jnp.concatenate(early_terms(1, gathered, grad_up), 1)
     held = [hold(item, kept[1][1][last]["q"]) for item in outputs[0]]
-    owned_first = plan.owned(held, 0, kept[1][1][last]["o"])
     early_second = lax.psum_scatter(
         early, ("wide", "section"), scatter_dimension=0, tiled=True
     )
@@ -906,6 +905,7 @@
                 finished(other, pending_out[other], blocks, layers[1], token)
                 for other in range(plan.chunks)
             ]
+            owned_first = plan.owned(held, 0, token)
             tied = (owned_first, *second_outputs)
         else:
             tied = (pending[index + 1],)
@@ -960,7 +960,7 @@
         total = terms[0]
     first_qkv_sum = sum(item.astype(f32) for item in qkv_shares)
     split = 2 * hidden + LANES
-    here = plan.send(early_second, 0)
+    here = plan.send(hold(early_second, grad_mixed[0]), 0)
     there, here_qkv = plan.send(early_sum[:, :split], 1), plan.send(early_sum[:, split:], 0)
     early = pick(
         section,

time: 714 us -> 741 us (1.038)
  waiting for transfers between devices: 292 us -> 328 us
  starting transfers between devices: 59.4 us -> 46.3 us
    reduce_scatter x2, waiting for transfers between devices: 20.9 us -> 45.5 us  [on_device(): lax.psum_scatter(early, ('wide', 'section'), scatter_dimension=0, tiled=T...]
    ppermute x8, waiting for transfers between devices: 86.3 us -> 106 us  [gather_bits(): lax.ppermute(block, 'tp', [(index, index ^ 1 << bit) for index in range(s...]
    ppermute x6, waiting for transfers between devices: 42.9 us -> 29.8 us  [to_owner(): piece = lax.ppermute(piece, ('section', 'wide', 'tp'), pairs)]
    ppermute x3, starting transfers between devices: 17.8 us -> 4.93 us  [swap(): return lax.ppermute(value, 'section', [(0, 1), (1, 0)])]
    ppermute x4, waiting for transfers between devices: 36.4 us -> 45.9 us  [scatter_rest(): lax.ppermute(sent, 'tp', [(index, index ^ 1 << bit) for index in range(se...]
    unnamed x189 -> x197, local copies, waits for them, and re-layouts: 31.4 us -> 33.4 us
where the time goes in v5:
time: 741 us; the launch traced here: 735 us
  waiting for transfers between devices  328 us (44%)
  Pallas kernels  196 us (26%)
  other arithmetic  70.5 us (10%)
  local copies, waits for them, and re-layouts  49.1 us (7%)
  starting transfers between devices  46.3 us (6%)
  matrix products  23 us (3%)
  between operations  21.9 us (3%)
    ppermute x8, waiting for transfers between devices, gather_bits(): lax.ppermute(block, 'tp', [(index, index ^ 1 << bit) for index in range(s...  106 us
    pallas_call x2, Pallas kernels, attend_back(): pl.pallas_call(functools.partial(attend_back_kernel, heads, key_block, le...  65.3 us
    pallas_call x2, Pallas kernels, attend(): pl.pallas_call(functools.partial(attend_kernel, heads, key_block, len(key...  48.2 us
    ppermute x4, waiting for transfers between devices, scatter_rest(): lax.ppermute(sent, 'tp', [(index, index ^ 1 << bit) for index in range(se...  45.9 us
    reduce_scatter x2, waiting for transfers between devices, on_device(): lax.psum_scatter(early, ('wide', 'section'), scatter_dimension=0, tiled=T...  45.5 us
    ppermute x1, waiting for transfers between devices, to_work(): piece = lax.ppermute(piece, ('wide', 'tp'), pairs)  37.2 us
    unnamed x197, local copies, waits for them, and re-layouts  33.4 us
    ppermute x6, waiting for transfers between devices, to_owner(): piece = lax.ppermute(piece, ('section', 'wide', 'tp'), pairs)  29.8 us
  transfers between devices with their start and end apart: 43, of which 26 were waited for; matrix products, arithmetic and copies ran while one was open for 13% of the time, Pallas kernels for 24%

profile of v5, /device:TPU:4, one launch (start us, length us, event | category | flops | bytes accessed | tf_op | source)
XLA Modules:
  0.0 735.2 jit_solution(13269774148565492365)
XLA Ops:
  10.7 11.5 %collective-permute-done.1 = bf16[96,2560]{1,0:T(8,128)(2,1)S(1)} collective-permute-done((bf16[96,2560]{1,0:T(8,128)(2,1)S(1)}, bf16[96,2560]{1,0:T(8,128)(2,1)S(1)}, u32[]{:S(2)}, u32[]{:S(2)}) %collective-permute-start.1) | collective-permute-done | bytes 491552 | tf_op jit(solution)/shard_map/ppermute | solution.py:625
  23.2 3.4 collective-permute-start
  28.5 2.3 collective-permute-done.2
  33.1 37.2 %collective-permute-done = bf16[512,768]{1,0:T(8,128)(2,1)S(1)} collective-permute-done((bf16[512,768]{1,0:T(8,128)(2,1)S(1)}, bf16[512,768]{1,0:T(8,128)(2,1)S(1)}, u32[]{:S(2)}, u32[]{:S(2)}) %collective-permute-start) | collective-permute-done | bytes 786464 | tf_op jit(solution)/shard_map/ppermute | solution.py:523
  70.5 15.2 %collective-permute-done.3 = bf16[512,768]{1,0:T(8,128)(2,1)} collective-permute-done((bf16[512,768]{1,0:T(8,128)(2,1)S(1)}, bf16[512,768]{1,0:T(8,128)(2,1)}, u32[]{:S(2)}, u32[]{:S(2)}) %collective-permute-start.3) | collective-permute-done | bytes 786464 | tf_op jit(solution)/shard_map/ppermute | solution.py:641
  88.7 3.3 collective-permute-done.4
  92.0 2.0 broadcast_select_fusion.11
  95.9 14.4 %all-gather.3.cloned.1.call-done.w_ref.wu_ref.wd_ref.wo_ref.wq_ref = bf16[768,2560]{1,0:T(8,128)(2,1)} async-done(((bf16[96,2560]{1,0:T(8,128)(2,1)}), bf16[768,2560]{1,0:T(8,128)(2,1)}) %all-gather.3.cloned.1.call-update) | async-done | bytes 3932176 | tf_op jit(solution)/shard_map/all_gather | solution.py:737
  113.2 3.0 collective-permute-start.5
  118.6 9.9 %project.2 = (bf16[2048,768]{1,0:T(8,128)(2,1)S(1)}, bf16[2048,768]{1,0:T(8,128)(2,1)}, bf16[2048,256]{1,0:T(8,128)(2,1)S(1)}, bf16[2048,256]{1,0:T(8,128)(2,1)S(1)}, bf16[2048,256]{1,0:T(8,128)(2,1)S(1)}) custom-call(bf16[2048,768]{1,0:T(8,128)(2,1)} %pad_maximum_fusion.1.x_ref, f32[4,768]{1,0:T(4,128)S(1)} %slice.232.gs_ref, ...), custom_call_target="tpu_custom_call" | custom-call | flops 9200000000 | bytes 9437184 | tf_op jit(solution)/shard_map/project/pallas_call | solution.py:133
  130.1 24.1 %attend.2 = (bf16[2048,256]{1,0:T(8,128)(2,1)S(1)}, f32[8,2048]{1,0:T(8,128)S(1)}) custom-call(s32[1]{0:T(128)} %constant.88.clone.1.start_ref, bf16[2048,256]{1,0:T(8,128)(2,1)S(1)} %get-tuple-element.49.q_ref, bf16[2048,256]{1,0:T(8,128)(2,1)S(1)} %get-tuple-element.50.rest_0_.rest_1_, bf16[2048,256]{1,0:T(8,128)(2,1)S(1)} %get-tuple-element.51.rest_1_.rest_2_), custom_call_target="tpu_custom_call" | custom-call | flops 32199999488 | bytes 3145728 | tf_op jit(solution)/shard_map/attend/pallas_call | solution.py:286
  154.2 5.4 collective-permute-done.5.rest_0_
  159.7 13.5 %feed.2 = (bf16[2048,768]{1,0:T(8,128)(2,1)S(1)}, bf16[2048,768]{1,0:T(8,128)(2,1)S(1)}, bf16[2048,768]{1,0:T(8,128)(2,1)}) custom-call(bf16[2048,768]{1,0:T(8,128)(2,1)} %get-tuple-element.48.a_ref, bf16[2048,256]{1,0:T(8,128)(2,1)S(1)} %get-tuple-element.52.o_ref, bf16[768,2560]{1,0:T(8,128)(2,1)} %all-gather.3.cloned.1.call-done.w_ref.wu_ref.wd_ref.wo_ref.wq_ref, ...), custom_call_target="tpu_custom_call" | custom-call | flops 11500000256 | bytes 9437184 | tf_op jit(solution)/shard_map/feed/pallas_call | solution.py:165
  174.8 3.2 broadcast_select_fusion.3
  178.2 3.4 collective-permute-done.6
  183.4 18.5 %collective-permute-done.7 = bf16[512,768]{1,0:T(8,128)(2,1)S(1)} collective-permute-done((bf16[512,768]{1,0:T(8,128)(2,1)S(1)}, bf16[512,768]{1,0:T(8,128)(2,1)S(1)}, u32[]{:S(2)}, u32[]{:S(2)}) %collective-permute-start.7) | collective-permute-done | bytes 786464 | tf_op jit(solution)/shard_map/ppermute | solution.py:664
  203.5 18.5 %collective-permute-done.8 = bf16[512,768]{1,0:T(8,128)(2,1)S(1)} collective-permute-done((bf16[512,768]{1,0:T(8,128)(2,1)S(1)}, bf16[512,768]{1,0:T(8,128)(2,1)S(1)}, u32[]{:S(2)}, u32[]{:S(2)}) %collective-permute-start.8) | collective-permute-done | bytes 786464 | tf_op jit(solution)/shard_map/ppermute | solution.py:641
  223.9 3.7 collective-permute-done.9
  227.6 2.4 broadcast_select_fusion.9
  230.0 1.9 pad_maximum_fusion.2.x_ref
  233.2 9.8 %project.3 = (bf16[2048,768]{1,0:T(8,128)(2,1)S(1)}, bf16[2048,768]{1,0:T(8,128)(2,1)}, bf16[2048,256]{1,0:T(8,128)(2,1)S(1)}, bf16[2048,256]{1,0:T(8,128)(2,1)S(1)}, bf16[2048,256]{1,0:T(8,128)(2,1)S(1)}) custom-call(bf16[2048,768]{1,0:T(8,128)(2,1)} %pad_maximum_fusion.2.x_ref, f32[4,768]{1,0:T(4,128)S(1)} %slice.244.gs_ref, ...), custom_call_target="tpu_custom_call" | custom-call | flops 9200000000 | bytes 9437184 | tf_op jit(solution)/shard_map/project/pallas_call | solution.py:133
  247.8 1.9 collective-permute-start.12
  251.5 48.1 %collective-permute-done.10 = bf16[512,768]{1,0:T(8,128)(2,1)S(1)} collective-permute-done((bf16[512,768]{1,0:T(8,128)(2,1)S(1)}, bf16[512,768]{1,0:T(8,128)(2,1)S(1)}, u32[]{:S(2)}, u32[]{:S(2)}) %collective-permute-start.10) | collective-permute-done | bytes 786464 | tf_op jit(solution)/shard_map/ppermute | solution.py:641
  299.9 24.1 %attend.3 = (bf16[2048,256]{1,0:T(8,128)(2,1)S(1)}, f32[8,2048]{1,0:T(8,128)S(1)}) custom-call(s32[1]{0:T(128)} %constant.88.clone.1.start_ref, bf16[2048,256]{1,0:T(8,128)(2,1)S(1)} %get-tuple-element.54.q_ref, bf16[2048,256]{1,0:T(8,128)(2,1)S(1)} %get-tuple-element.55.rest_0_.rest_1_, bf16[2048,256]{1,0:T(8,128)(2,1)S(1)} %get-tuple-element.56.rest_1_.rest_2_), custom_call_target="tpu_custom_call" | custom-call | flops 32199999488 | bytes 3145728 | tf_op jit(solution)/shard_map/attend/pallas_call | solution.py:286
  324.0 12.8 %feed.3 = (bf16[2048,768]{1,0:T(8,128)(2,1)S(1)}, bf16[2048,768]{1,0:T(8,128)(2,1)S(1)}, bf16[2048,768]{1,0:T(8,128)(2,1)}) custom-call(bf16[2048,768]{1,0:T(8,128)(2,1)} %get-tuple-element.59.a_ref, bf16[2048,256]{1,0:T(8,128)(2,1)S(1)} %get-tuple-element.57.o_ref, bf16[768,2560]{1,0:T(8,128)(2,1)} %all-gather.5.cloned.1.call-done.w_ref.wu_ref.wd_ref.wo_ref.wq_ref, ...), custom_call_target="tpu_custom_call" | custom-call | flops 11500000256 | bytes 9437184 | tf_op jit(solution)/shard_map/feed/pallas_call | solution.py:165
  336.8 2.0 broadcast_select_fusion.2
  340.3 6.2 feed_back.2.gu_ref
  347.5 2.7 convolution_convert_fusion.5
  350.3 2.7 convolution_convert_fusion.4
  360.0 32.6 %attend_back.2 = (f32[2048,256]{1,0:T(8,128)S(1)}, f32[2048,256]{1,0:T(8,128)S(1)}, f32[2048,256]{1,0:T(8,128)}) custom-call(s32[1]{0:T(128)} %constant.88.clone.1.start_ref, bf16[2048,768]{1,0:T(8,128)(2,1)} %copy-done.4, bf16[768,2560]{1,0:T(8,128)(2,1)} %all-gather.5.cloned.1.call-done.w_ref.wu_ref.wd_ref.wo_ref.wq_ref, bf16[2048,256]{1,0:T(8,128)(2,1)S(1)} %copy-done.11, ...), custom_call_target="tpu_custom_call" | custom-call | flops 57500000256 | bytes 6291456 | tf_op jit(solution)/shard_map/attend_back/pallas_call | solution.py:390
  393.8 2.1 fusion.24
  395.9 2.3 fusion.26
  399.3 1.9 fusion.15
  401.2 12.7 %leave.2 = (bf16[2048,768]{1,0:T(8,128)(2,1)}, bf16[2048,768]{1,0:T(8,128)(2,1)}, f32[4,768]{1,0:T(4,128)S(1)}, f32[1,768]{1,0:T(1,128)S(1)}, f32[1,768]{1,0:T(1,128)S(1)}) custom-call(bf16[2048,768]{1,0:T(8,128)(2,1)} %pad_maximum_fusion.2.x_ref, f32[4,768]{1,0:T(4,128)S(1)} %slice.244.gs_ref, f32[2048,256]{1,0:T(8,128)S(1)} %get-tuple-element.63.dq_ref, ...), custom_call_target="tpu_custom_call" | custom-call | flops 15409999872 | bytes 9437184 | tf_op jit(solution)/shard_map/leave/pallas_call | solution.py:453
  414.0 2.2 broadcast_select_fusion.1
  416.2 3.4 collective-permute-done.16
  421.6 18.3 %collective-permute-done.17 = bf16[512,768]{1,0:T(8,128)(2,1)S(1)} collective-permute-done((bf16[512,768]{1,0:T(8,128)(2,1)S(1)}, bf16[512,768]{1,0:T(8,128)(2,1)S(1)}, u32[]{:S(2)}, u32[]{:S(2)}) %collective-permute-start.17) | collective-permute-done | bytes 786464 | tf_op jit(solution)/shard_map/ppermute | solution.py:664
  443.3 17.5 %collective-permute-done.18 = bf16[512,768]{1,0:T(8,128)(2,1)} collective-permute-done((bf16[512,768]{1,0:T(8,128)(2,1)S(1)}, bf16[512,768]{1,0:T(8,128)(2,1)}, u32[]{:S(2)}, u32[]{:S(2)}) %collective-permute-start.18) | collective-permute-done | bytes 786464 | tf_op jit(solution)/shard_map/ppermute | solution.py:641
  464.0 6.6 convolution_convert_fusion.1
  471.3 2.1 broadcast_select_fusion.4
  475.5 2.4 collective-permute-start.20
  483.7 5.3 feed_back.3.gu_ref
  489.0 2.7 convolution_convert_fusion.3
  492.1 2.7 convolution_convert_fusion.2
  494.8 2.2 pad_maximum_fusion.rest_3_
  500.7 32.7 %attend_back.3 = (f32[2048,256]{1,0:T(8,128)S(1)}, f32[2048,256]{1,0:T(8,128)S(1)}, f32[2048,256]{1,0:T(8,128)}) custom-call(s32[1]{0:T(128)} %constant.88.clone.1.start_ref, bf16[2048,768]{1,0:T(8,128)(2,1)} %copy-done.5, bf16[768,2560]{1,0:T(8,128)(2,1)} %all-gather.3.cloned.1.call-done.w_ref.wu_ref.wd_ref.wo_ref.wq_ref, bf16[2048,256]{1,0:T(8,128)(2,1)S(1)} %copy-done.31, ...), custom_call_target="tpu_custom_call" | custom-call | flops 57500000256 | bytes 6291456 | tf_op jit(solution)/shard_map/attend_back/pallas_call | solution.py:390
  536.0 12.5 %reduce-scatter.3.cloned.1.call-done.rest_0_ = bf16[96,1792]{1,0:T(8,128)(2,1)} async-done(((bf16[768,1792]{1,0:T(8,128)(2,1)}), bf16[96,1792]{1,0:T(8,128)(2,1)}) %reduce-scatter.3.cloned.1.call-update) | async-done | bytes 344080 | tf_op jit(solution)/shard_map/reduce_scatter | solution.py:895
  554.2 12.1 %leave.3 = (bf16[2048,768]{1,0:T(8,128)(2,1)}, bf16[2048,768]{1,0:T(8,128)(2,1)}, f32[4,768]{1,0:T(4,128)S(1)}, f32[1,768]{1,0:T(1,128)S(1)}, f32[1,768]{1,0:T(1,128)S(1)}) custom-call(bf16[2048,768]{1,0:T(8,128)(2,1)} %pad_maximum_fusion.1.x_ref, f32[4,768]{1,0:T(4,128)S(1)} %copy-done.9, f32[2048,256]{1,0:T(8,128)S(1)} %copy-done.41, ...), custom_call_target="tpu_custom_call" | custom-call | flops 15409999872 | bytes 9437184 | tf_op jit(solution)/shard_map/leave/pallas_call | solution.py:453
  566.4 3.4 broadcast_select_fusion
  575.8 3.9 collective-permute-start.38
  580.4 2.1 convert_add_fusion
  584.2 3.7 convolution_convert_fusion
  592.6 9.1 %collective-permute-done.23 = bf16[512,768]{1,0:T(8,128)(2,1)S(1)} collective-permute-done((bf16[512,768]{1,0:T(8,128)(2,1)S(1)}, bf16[512,768]{1,0:T(8,128)(2,1)S(1)}, u32[]{:S(2)}, u32[]{:S(2)}) %collective-permute-start.23) | collective-permute-done | bytes 786464 | tf_op jit(solution)/shard_map/ppermute | solution.py:664
  602.3 33.1 %reduce-scatter.5.cloned.1.call-done = bf16[96,2560]{1,0:T(8,128)(2,1)} async-done(((bf16[768,2560]{1,0:T(8,128)(2,1)}), bf16[96,2560]{1,0:T(8,128)(2,1)}) %reduce-scatter.5.cloned.1.call-update) | async-done | bytes 491536 | tf_op jit(solution)/shard_map/reduce_scatter | solution.py:931
  652.6 1.9 collective-permute-start.33
  654.6 2.7 collective-permute-done.31
  661.4 2.5 collective-permute-start.34
  666.0 12.1 %collective-permute-done.33 = bf16[192,576]{0,1:T(8,128)(2,1)} collective-permute-done((bf16[192,576]{0,1:T(8,128)(2,1)}, bf16[192,576]{0,1:T(8,128)(2,1)}, u32[]{:S(2)}, u32[]{:S(2)}) %collective-permute-start.33) | collective-permute-done | bytes 221216 | tf_op jit(solution)/shard_map/ppermute | solution.py:590
  678.1 2.4 collective-permute-start.24
  680.5 2.0 fusion.29
  686.9 5.0 collective-permute-done.35
  694.4 21.3 %collective-permute-done.25 = bf16[512,768]{1,0:T(8,128)(2,1)} collective-permute-done((bf16[512,768]{1,0:T(8,128)(2,1)}, bf16[512,768]{1,0:T(8,128)(2,1)}, u32[]{:S(2)}, u32[]{:S(2)}) %collective-permute-start.25) | collective-permute-done | bytes 786464 | tf_op jit(solution)/shard_map/ppermute | solution.py:563
  715.7 8.6 %collective-permute-done.24 = bf16[512,768]{1,0:T(8,128)(2,1)} collective-permute-done((bf16[512,768]{1,0:T(8,128)(2,1)}, bf16[512,768]{1,0:T(8,128)(2,1)}, u32[]{:S(2)}, u32[]{:S(2)}) %collective-permute-start.24) | collective-permute-done | bytes 786464 | tf_op jit(solution)/shard_map/ppermute | solution.py:563
  725.7 1.9 maximum_convert_fusion
  (380 shorter events, 116.4 us)
Async XLA Ops:
  7.2 81.1 %copy-start = (s32[2,4,2048]{2,1,0:T(4,128)S(1)}, s32[2,4,2048]{2,1,0:T(4,128)}, u32[]{:S(2)}) copy-start(s32[2,4,2048]{2,1,0:T(4,128)} %param.17) | copy-start | bytes 196612
  7.2 103.0 %all-gather.3.cloned.1.call-start = ((), (), s32[]{:S(2)}) async-start(), calls=%async_computation.2 | async-start | bytes 4423680 | tf_op jit(solution)/shard_map/all_gather | solution.py:737
  9.1 13.0 %collective-permute-start.1 = (bf16[96,2560]{1,0:T(8,128)(2,1)S(1)}, bf16[96,2560]{1,0:T(8,128)(2,1)S(1)}, u32[]{:S(2)}, u32[]{:S(2)}) collective-permute-start(bf16[96,2560]{1,0:T(8,128)(2,1)S(1)} %broadcast_select_fusion.29), channel_id=1, source_target_pairs={{0,16},{16,0},{1,17},{17,1},{2,18},{18,2},{3,19},{19,3},{4,20},{20... | collective-permute-start | bytes 1474568 | tf_op jit(solution)/shard_map/ppermute | solution.py:625
  23.1 208.9 %all-gather.5.cloned.1.call-start = ((), (), s32[]{:S(2)}) async-start(), calls=%async_computation.3 | async-start | bytes 4423680 | tf_op jit(solution)/shard_map/all_gather | solution.py:737
  23.2 47.2 %collective-permute-start = (bf16[512,768]{1,0:T(8,128)(2,1)S(1)}, bf16[512,768]{1,0:T(8,128)(2,1)S(1)}, u32[]{:S(2)}, u32[]{:S(2)}) collective-permute-start(bf16[512,768]{1,0:T(8,128)(2,1)S(1)} %select_bitcast_fusion.5), channel_id=1, source_target_pairs={{0,0},{1,8},{2,4},{3,12},{4,2},{5,10},{6,6},{7,14},{8,1},{9,9},{10... | collective-permute-start | bytes 2359304 | tf_op jit(solution)/shard_map/ppermute | solution.py:523
  26.9 3.9 collective-permute-start.2
  70.4 16.6 %copy-start.48 = (bf16[512,768]{1,0:T(8,128)(2,1)}, bf16[512,768]{1,0:T(8,128)(2,1)S(1)}, u32[]{:S(2)}) copy-start(bf16[512,768]{1,0:T(8,128)(2,1)S(1)} %collective-permute-done) | copy-start | bytes 2359300
  70.5 15.3 %collective-permute-start.3 = (bf16[512,768]{1,0:T(8,128)(2,1)S(1)}, bf16[512,768]{1,0:T(8,128)(2,1)}, u32[]{:S(2)}, u32[]{:S(2)}) collective-permute-start(bf16[512,768]{1,0:T(8,128)(2,1)S(1)} %select_select_fusion), channel_id=1, source_target_pairs={{0,2},{1,3},{2,0},{3,1},{4,6},{5,7},{6,4},{7,5},{8,10},{9,11},{10,... | collective-permute-start | bytes 2359304 | tf_op jit(solution)/shard_map/ppermute | solution.py:641
  88.2 3.8 collective-permute-start.4
  88.7 28.6 %copy-start.8 = (f32[4,768]{1,0:T(4,128)}, f32[4,768]{1,0:T(4,128)S(1)}, u32[]{:S(2)}) copy-start(f32[4,768]{1,0:T(4,128)S(1)} %slice.232.gs_ref) | copy-start | bytes 36868
  94.0 18.2 %copy-start.66 = (bf16[2,1,512,768]{3,2,1,0:T(8,128)(2,1)S(1)}, bf16[2,1,512,768]{3,2,1,0:T(8,128)(2,1)}, u32[]{:S(2)}) copy-start(bf16[2,1,512,768]{3,2,1,0:T(8,128)(2,1)} %param.16) | copy-start | bytes 4718596
  113.2 46.5 %collective-permute-start.5 = (bf16[512,768]{1,0:T(8,128)(2,1)}, bf16[512,768]{1,0:T(8,128)(2,1)S(1)}, u32[]{:S(2)}, u32[]{:S(2)}) collective-permute-start(bf16[512,768]{1,0:T(8,128)(2,1)} %select_bitcast_fusion.4), channel_id=1, source_target_pairs={{0,0},{1,8},{2,4},{3,12},{4,2},{5,10},{6,6},{7,14},{8,1},{9,9},{10... | collective-permute-start | bytes 2359304 | tf_op jit(solution)/shard_map/ppermute | solution.py:540
  117.1 431.4 %reduce-scatter.3.cloned.1.call-start = ((), (), s32[]{:S(2)}) async-start(), calls=%async_computation.4 | async-start | bytes 3096576 | tf_op jit(solution)/shard_map/reduce_scatter | solution.py:895
  130.1 24.1 %copy-start.30 = (bf16[2048,256]{1,0:T(8,128)(2,1)}, bf16[2048,256]{1,0:T(8,128)(2,1)S(1)}, u32[]{:S(2)}) copy-start(bf16[2048,256]{1,0:T(8,128)(2,1)S(1)} %get-tuple-element.49.q_ref) | copy-start | bytes 3145732
  130.1 24.1 %copy-start.32 = (bf16[2048,256]{1,0:T(8,128)(2,1)}, bf16[2048,256]{1,0:T(8,128)(2,1)S(1)}, u32[]{:S(2)}) copy-start(bf16[2048,256]{1,0:T(8,128)(2,1)S(1)} %get-tuple-element.50.rest_0_.rest_1_) | copy-start | bytes 3145732
  130.1 24.1 %copy-start.34 = (bf16[2048,256]{1,0:T(8,128)(2,1)}, bf16[2048,256]{1,0:T(8,128)(2,1)S(1)}, u32[]{:S(2)}) copy-start(bf16[2048,256]{1,0:T(8,128)(2,1)S(1)} %get-tuple-element.51.rest_1_.rest_2_) | copy-start | bytes 3145732
  154.2 18.9 %copy-start.28 = (bf16[2048,256]{1,0:T(8,128)(2,1)}, bf16[2048,256]{1,0:T(8,128)(2,1)S(1)}, u32[]{:S(2)}) copy-start(bf16[2048,256]{1,0:T(8,128)(2,1)S(1)} %get-tuple-element.52.o_ref) | copy-start | bytes 3145732
  159.7 139.9 %copy-start.2 = (bf16[512,768]{1,0:T(8,128)(2,1)}, bf16[512,768]{1,0:T(8,128)(2,1)S(1)}, u32[]{:S(2)}) copy-start(bf16[512,768]{1,0:T(8,128)(2,1)S(1)} %collective-permute-done.5.rest_0_) | copy-start | bytes 2359300
  178.1 3.5 collective-permute-start.6
  182.2 19.6 %collective-permute-start.7 = (bf16[512,768]{1,0:T(8,128)(2,1)S(1)}, bf16[512,768]{1,0:T(8,128)(2,1)S(1)}, u32[]{:S(2)}, u32[]{:S(2)}) collective-permute-start(bf16[512,768]{1,0:T(8,128)(2,1)S(1)} %select_convert_fusion.3), channel_id=1, source_target_pairs={{0,2},{1,3},{2,0},{3,1},{4,6},{5,7},{6,4},{7,5},{8,10},{9,11},{10,... | collective-permute-start | bytes 2359304 | tf_op jit(solution)/shard_map/ppermute | solution.py:664
  183.4 19.8 %copy-start.79 = (f32[512]{0:T(512)}, f32[512]{0:T(512)S(1)}, u32[]{:S(2)}) copy-start(f32[512]{0:T(512)S(1)} %broadcast_multiply_fusion.2) | copy-start | bytes 6148
  203.2 19.0 %copy-start.45 = (bf16[512,768]{1,0:T(8,128)(2,1)}, bf16[512,768]{1,0:T(8,128)(2,1)S(1)}, u32[]{:S(2)}) copy-start(bf16[512,768]{1,0:T(8,128)(2,1)S(1)} %get-tuple-element.133) | copy-start | bytes 2359300
  203.2 18.8 %collective-permute-start.8 = (bf16[512,768]{1,0:T(8,128)(2,1)S(1)}, bf16[512,768]{1,0:T(8,128)(2,1)S(1)}, u32[]{:S(2)}, u32[]{:S(2)}) collective-permute-start(bf16[512,768]{1,0:T(8,128)(2,1)S(1)} %get-tuple-element.133), channel_id=1, source_target_pairs={{0,2},{1,3},{2,0},{3,1},{4,6},{5,7},{6,4},{7,5},{8,10},{9,11},{10,... | collective-permute-start | bytes 2359304 | tf_op jit(solution)/shard_map/ppermute | solution.py:641
  223.9 3.8 collective-permute-start.9
  244.6 55.2 %copy-start.10 = (bf16[2048,256]{1,0:T(8,128)(2,1)}, bf16[2048,256]{1,0:T(8,128)(2,1)S(1)}, u32[]{:S(2)}) copy-start(bf16[2048,256]{1,0:T(8,128)(2,1)S(1)} %get-tuple-element.54.q_ref) | copy-start | bytes 3145732
  244.7 55.2 %copy-start.36 = (bf16[2048,256]{1,0:T(8,128)(2,1)}, bf16[2048,256]{1,0:T(8,128)(2,1)S(1)}, u32[]{:S(2)}) copy-start(bf16[2048,256]{1,0:T(8,128)(2,1)S(1)} %get-tuple-element.55.rest_0_.rest_1_) | copy-start | bytes 3145732
  244.7 55.2 %copy-start.38 = (bf16[2048,256]{1,0:T(8,128)(2,1)}, bf16[2048,256]{1,0:T(8,128)(2,1)S(1)}, u32[]{:S(2)}) copy-start(bf16[2048,256]{1,0:T(8,128)(2,1)S(1)} %get-tuple-element.56.rest_1_.rest_2_) | copy-start | bytes 3145732
  246.2 53.4 %collective-permute-start.10 = (bf16[512,768]{1,0:T(8,128)(2,1)S(1)}, bf16[512,768]{1,0:T(8,128)(2,1)S(1)}, u32[]{:S(2)}, u32[]{:S(2)}) collective-permute-start(bf16[512,768]{1,0:T(8,128)(2,1)S(1)} %broadcast_select_fusion.19), channel_id=1, source_target_pairs={{0,2},{1,3},{2,0},{3,1},{4,6},{5,7},{6,4},{7,5},{8,10},{9,11},{10,... | collective-permute-start | bytes 2359304 | tf_op jit(solution)/shard_map/ppermute | solution.py:641
  247.8 145.9 %collective-permute-start.12 = (bf16[512,768]{1,0:T(8,128)(2,1)}, bf16[512,768]{1,0:T(8,128)(2,1)}, u32[]{:S(2)}, u32[]{:S(2)}) collective-permute-start(bf16[512,768]{1,0:T(8,128)(2,1)} %broadcast_select_fusion.18), channel_id=1, source_target_pairs={{0,0},{8,1},{4,2},{12,3},{2,4},{10,5},{6,6},{14,7},{1,8},{9,9},{5,... | collective-permute-start | bytes 2359304 | tf_op jit(solution)/shard_map/ppermute | solution.py:563
  249.8 146.2 %collective-permute-start.13 = (bf16[512,768]{1,0:T(8,128)(2,1)}, bf16[512,768]{1,0:T(8,128)(2,1)}, u32[]{:S(2)}, u32[]{:S(2)}) collective-permute-start(bf16[512,768]{1,0:T(8,128)(2,1)} %broadcast_select_fusion.18), channel_id=1, source_target_pairs={{16,0},{24,1},{20,2},{28,3},{18,4},{26,5},{22,6},{30,7},{17,8},{25... | collective-permute-start | bytes 2359304 | tf_op jit(solution)/shard_map/ppermute | solution.py:563
  299.8 39.6 %collective-permute-start.11 = (bf16[1024,768]{1,0:T(8,128)(2,1)S(1)}, bf16[1024,768]{1,0:T(8,128)(2,1)S(1)}, u32[]{:S(2)}, u32[]{:S(2)}) collective-permute-start(bf16[1024,768]{1,0:T(8,128)(2,1)S(1)} %pad_maximum_fusion.8.rest_0_), channel_id=1, source_target_pairs={{0,1},{1,0},{2,3},{3,2},{4,5},{5,4},{6,7},{7,6},{8,9},{9,8},{10,11... | collective-permute-start | bytes 4718600 | tf_op jit(solution)/shard_map/ppermute | solution.py:641
  338.9 14.1 %collective-permute-start.14 = (bf16[1024,768]{1,0:T(8,128)(2,1)S(1)}, bf16[1024,768]{1,0:T(8,128)(2,1)S(1)}, u32[]{:S(2)}, u32[]{:S(2)}) collective-permute-start(bf16[1024,768]{1,0:T(8,128)(2,1)S(1)} %broadcast_select_fusion.2), channel_id=1, source_target_pairs={{0,1},{1,0},{2,3},{3,2},{4,5},{5,4},{6,7},{7,6},{8,9},{9,8},{10,11... | collective-permute-start | bytes 4718600 | tf_op jit(solution)/shard_map/ppermute | solution.py:653
  356.2 42.1 %collective-permute-start.15 = (bf16[512,768]{1,0:T(8,128)(2,1)}, bf16[512,768]{1,0:T(8,128)(2,1)}, u32[]{:S(2)}, u32[]{:S(2)}) collective-permute-start(bf16[512,768]{1,0:T(8,128)(2,1)} %select_convert_fusion.2), channel_id=1, source_target_pairs={{0,2},{1,3},{2,0},{3,1},{4,6},{5,7},{6,4},{7,5},{8,10},{9,11},{10,... | collective-permute-start | bytes 2359304 | tf_op jit(solution)/shard_map/ppermute | solution.py:664
  416.2 3.5 collective-permute-start.16
  420.3 19.6 %collective-permute-start.17 = (bf16[512,768]{1,0:T(8,128)(2,1)S(1)}, bf16[512,768]{1,0:T(8,128)(2,1)S(1)}, u32[]{:S(2)}, u32[]{:S(2)}) collective-permute-start(bf16[512,768]{1,0:T(8,128)(2,1)S(1)} %select_convert_fusion.1), channel_id=1, source_target_pairs={{0,2},{1,3},{2,0},{3,1},{4,6},{5,7},{6,4},{7,5},{8,10},{9,11},{10,... | collective-permute-start | bytes 2359304 | tf_op jit(solution)/shard_map/ppermute | solution.py:664
  421.6 19.0 %copy-start.3 = (bf16[512,768]{1,0:T(8,128)(2,1)S(1)}, bf16[512,768]{1,0:T(8,128)(2,1)}, u32[]{:S(2)}) copy-start(bf16[512,768]{1,0:T(8,128)(2,1)} %copy-done.2) | copy-start | bytes 2359300
  441.9 20.1 %copy-start.57 = (bf16[512,768]{1,0:T(8,128)(2,1)}, bf16[512,768]{1,0:T(8,128)(2,1)S(1)}, u32[]{:S(2)}) copy-start(bf16[512,768]{1,0:T(8,128)(2,1)S(1)} %get-tuple-element.127) | copy-start | bytes 2359300
  441.9 18.9 %collective-permute-start.18 = (bf16[512,768]{1,0:T(8,128)(2,1)S(1)}, bf16[512,768]{1,0:T(8,128)(2,1)}, u32[]{:S(2)}, u32[]{:S(2)}) collective-permute-start(bf16[512,768]{1,0:T(8,128)(2,1)S(1)} %get-tuple-element.127), channel_id=1, source_target_pairs={{0,2},{1,3},{2,0},{3,1},{4,6},{5,7},{6,4},{7,5},{8,10},{9,11},{10,... | collective-permute-start | bytes 2359304 | tf_op jit(solution)/shard_map/ppermute | solution.py:641
  443.2 192.2 %reduce-scatter.5.cloned.1.call-start = ((), (), s32[]{:S(2)}) async-start(), calls=%async_computation.5 | async-start | bytes 4423680 | tf_op jit(solution)/shard_map/reduce_scatter | solution.py:931
  463.3 8.0 %collective-permute-start.19 = (bf16[1024,768]{1,0:T(8,128)(2,1)}, bf16[1024,768]{1,0:T(8,128)(2,1)}, u32[]{:S(2)}, u32[]{:S(2)}) collective-permute-start(bf16[1024,768]{1,0:T(8,128)(2,1)} %pad_maximum_fusion.10), channel_id=1, source_target_pairs={{0,1},{1,0},{2,3},{3,2},{4,5},{5,4},{6,7},{7,6},{8,9},{9,8},{10,11... | collective-permute-start | bytes 4718600 | tf_op jit(solution)/shard_map/ppermute | solution.py:641
  475.5 113.0 %collective-permute-start.20 = (bf16[512,768]{1,0:T(8,128)(2,1)}, bf16[512,768]{1,0:T(8,128)(2,1)}, u32[]{:S(2)}, u32[]{:S(2)}) collective-permute-start(bf16[512,768]{1,0:T(8,128)(2,1)} %broadcast_select_fusion.15), channel_id=1, source_target_pairs={{0,16},{8,17},{4,18},{12,19},{2,20},{10,21},{6,22},{14,23},{1,24},... | collective-permute-start | bytes 2359304 | tf_op jit(solution)/shard_map/ppermute | solution.py:563
  477.9 112.0 %collective-permute-start.21 = (bf16[512,768]{1,0:T(8,128)(2,1)}, bf16[512,768]{1,0:T(8,128)(2,1)}, u32[]{:S(2)}, u32[]{:S(2)}) collective-permute-start(bf16[512,768]{1,0:T(8,128)(2,1)} %broadcast_select_fusion.15), channel_id=1, source_target_pairs={{16,16},{24,17},{20,18},{28,19},{18,20},{26,21},{22,22},{30,23},{1... | collective-permute-start | bytes 2359304 | tf_op jit(solution)/shard_map/ppermute | solution.py:563
  500.7 47.8 %copy-start.9 = (f32[4,768]{1,0:T(4,128)S(1)}, f32[4,768]{1,0:T(4,128)}, u32[]{:S(2)}) copy-start(f32[4,768]{1,0:T(4,128)} %copy-done.8) | copy-start | bytes 36868
  500.7 47.8 %copy-start.14 = (f32[2048,128]{1,0:T(8,128)S(1)}, f32[2048,128]{1,0:T(8,128)}, u32[]{:S(2)}) copy-start(f32[2048,128]{1,0:T(8,128)} %constant.104.clone.c_ref) | copy-start | bytes 3145732
  500.7 47.8 %copy-start.18 = (f32[2048,128]{1,0:T(8,128)S(1)}, f32[2048,128]{1,0:T(8,128)}, u32[]{:S(2)}) copy-start(f32[2048,128]{1,0:T(8,128)} %constant.105.clone.s_ref) | copy-start | bytes 3145732
  569.7 10.7 %collective-permute-start.22 = (bf16[1024,768]{1,0:T(8,128)(2,1)}, bf16[1024,768]{1,0:T(8,128)(2,1)}, u32[]{:S(2)}, u32[]{:S(2)}) collective-permute-start(bf16[1024,768]{1,0:T(8,128)(2,1)} %broadcast_select_fusion), channel_id=1, source_target_pairs={{0,1},{1,0},{2,3},{3,2},{4,5},{5,4},{6,7},{7,6},{8,9},{9,8},{10,11... | collective-permute-start | bytes 4718600 | tf_op jit(solution)/shard_map/ppermute | solution.py:653
  574.5 5.3 collective-permute-start.26
  575.8 107.9 %collective-permute-start.38 = (bf16[96,1792]{1,0:T(8,128)(2,1)}, bf16[96,1792]{1,0:T(8,128)(2,1)}, u32[]{:S(2)}, u32[]{:S(2)}) collective-permute-start(bf16[96,1792]{1,0:T(8,128)(2,1)} %broadcast_select_fusion.30), channel_id=1, source_target_pairs={{0,16},{1,17},{2,18},{3,19},{4,20},{5,21},{6,22},{7,23},{8,24},{9,... | collective-permute-start | bytes 1032200 | tf_op jit(solution)/shard_map/ppermute | solution.py:628
  579.8 8.1 %collective-permute-start.27 = (f32[2,3840]{1,0:T(2,128)S(1)}, f32[2,3840]{1,0:T(2,128)S(1)}, u32[]{:S(2)}, u32[]{:S(2)}) collective-permute-start(f32[2,3840]{1,0:T(2,128)S(1)} %fusion.34), channel_id=1, source_target_pairs={{0,2},{1,3},{2,0},{3,1},{4,6},{5,7},{6,4},{7,5},{8,10},{9,11},{10,... | collective-permute-start | bytes 92168 | tf_op jit(solution)/shard_map/ppermute | solution.py:620
  582.7 19.0 %collective-permute-start.23 = (bf16[512,768]{1,0:T(8,128)(2,1)S(1)}, bf16[512,768]{1,0:T(8,128)(2,1)S(1)}, u32[]{:S(2)}, u32[]{:S(2)}) collective-permute-start(bf16[512,768]{1,0:T(8,128)(2,1)S(1)} %select_convert_fusion), channel_id=1, source_target_pairs={{0,2},{1,3},{2,0},{3,1},{4,6},{5,7},{6,4},{7,5},{8,10},{9,11},{10,... | collective-permute-start | bytes 2359304 | tf_op jit(solution)/shard_map/ppermute | solution.py:664
  592.6 44.7 %copy-start.58 = (bf16[512,768]{1,0:T(8,128)(2,1)S(1)}, bf16[512,768]{1,0:T(8,128)(2,1)}, u32[]{:S(2)}) copy-start(bf16[512,768]{1,0:T(8,128)(2,1)} %copy-done.57) | copy-start | bytes 2359300
  640.2 6.9 collective-permute-start.28
  641.9 5.6 collective-permute-start.29
  642.9 5.8 collective-permute-start.30
  645.7 38.1 %collective-permute-start.37 = (bf16[96,1792]{1,0:T(8,128)(2,1)S(1)}, bf16[96,1792]{1,0:T(8,128)(2,1)}, u32[]{:S(2)}, u32[]{:S(2)}) collective-permute-start(bf16[96,1792]{1,0:T(8,128)(2,1)S(1)} %slice.323), channel_id=1, source_target_pairs={{16,0},{17,1},{18,2},{19,3},{20,4},{21,5},{22,6},{23,7},{24,8},{25... | collective-permute-start | bytes 1032200 | tf_op jit(solution)/shard_map/ppermute | solution.py:628
  648.8 8.5 %collective-permute-start.31 = (f32[2,5184]{1,0:T(2,128)S(1)}, f32[2,5184]{1,0:T(2,128)S(1)}, u32[]{:S(2)}, u32[]{:S(2)}) collective-permute-start(f32[2,5184]{1,0:T(2,128)S(1)} %add_add_fusion), channel_id=1, source_target_pairs={{0,16},{16,0},{1,17},{17,1},{2,18},{18,2},{3,19},{19,3},{4,20},{20... | collective-permute-start | bytes 124424 | tf_op jit(solution)/shard_map/ppermute | solution.py:625
  651.9 14.1 %collective-permute-start.32 = (bf16[192,576]{0,1:T(8,128)(2,1)}, bf16[192,576]{0,1:T(8,128)(2,1)S(1)}, u32[]{:S(2)}, u32[]{:S(2)}) collective-permute-start(bf16[192,576]{0,1:T(8,128)(2,1)} %get-tuple-element.154), channel_id=1, source_target_pairs={{0,4},{4,0},{8,12},{12,8},{1,5},{5,1},{9,13},{13,9},{2,6},{6,2},{1... | collective-permute-start | bytes 663560 | tf_op jit(solution)/shard_map/ppermute | solution.py:590
  652.6 25.5 %collective-permute-start.33 = (bf16[192,576]{0,1:T(8,128)(2,1)}, bf16[192,576]{0,1:T(8,128)(2,1)}, u32[]{:S(2)}, u32[]{:S(2)}) collective-permute-start(bf16[192,576]{0,1:T(8,128)(2,1)} %get-tuple-element.156), channel_id=1, source_target_pairs={{0,8},{4,12},{8,0},{12,4},{1,9},{5,13},{9,1},{13,5},{2,10},{6,14},... | collective-permute-start | bytes 663560 | tf_op jit(solution)/shard_map/ppermute | solution.py:590
  657.3 4.1 collective-permute-start.36
  661.4 19.1 %collective-permute-start.34 = (bf16[192,576]{0,1:T(8,128)(2,1)}, bf16[192,576]{0,1:T(8,128)(2,1)}, u32[]{:S(2)}, u32[]{:S(2)}) collective-permute-start(bf16[192,576]{0,1:T(8,128)(2,1)} %get-tuple-element.155), channel_id=1, source_target_pairs={{0,12},{4,8},{8,4},{12,0},{1,13},{5,9},{9,5},{13,1},{2,14},{6,10},... | collective-permute-start | bytes 663560 | tf_op jit(solution)/shard_map/ppermute | solution.py:590
  664.3 19.5 %copy-start.68 = (bf16[96,1792]{1,0:T(8,128)(2,1)S(1)}, bf16[96,1792]{1,0:T(8,128)(2,1)}, u32[]{:S(2)}) copy-start(bf16[96,1792]{1,0:T(8,128)(2,1)} %copy-done.67) | copy-start | bytes 1032196
  666.0 49.7 %collective-permute-start.25 = (bf16[512,768]{1,0:T(8,128)(2,1)}, bf16[512,768]{1,0:T(8,128)(2,1)}, u32[]{:S(2)}, u32[]{:S(2)}) collective-permute-start(bf16[512,768]{1,0:T(8,128)(2,1)} %broadcast_select_fusion.13), channel_id=1, source_target_pairs={{0,16},{16,0},{8,17},{24,1},{4,18},{20,2},{12,19},{28,3},{2,20},{1... | collective-permute-start | bytes 2359304 | tf_op jit(solution)/shard_map/ppermute | solution.py:563
  678.1 46.2 %collective-permute-start.24 = (bf16[512,768]{1,0:T(8,128)(2,1)}, bf16[512,768]{1,0:T(8,128)(2,1)}, u32[]{:S(2)}, u32[]{:S(2)}) collective-permute-start(bf16[512,768]{1,0:T(8,128)(2,1)} %get-tuple-element.128), channel_id=1, source_target_pairs={{0,0},{16,16},{8,1},{24,17},{4,2},{20,18},{12,3},{28,19},{2,4},{18... | collective-permute-start | bytes 2359304 | tf_op jit(solution)/shard_map/ppermute | solution.py:563
  682.5 9.5 %collective-permute-start.35 = (bf16[192,576]{0,1:T(8,128)(2,1)}, bf16[192,576]{0,1:T(8,128)(2,1)}, u32[]{:S(2)}, u32[]{:S(2)}) collective-permute-start(bf16[192,576]{0,1:T(8,128)(2,1)} %fusion.29), channel_id=1, source_target_pairs={{16,0},{17,1},{18,2},{19,3},{20,4},{21,5},{22,6},{23,7},{24,8},{25... | collective-permute-start | bytes 663560 | tf_op jit(solution)/shard_map/ppermute | solution.py:628
  (72 other events, 260.7 us)
Sparse Core Ops, SparseCore 0:
  23.2 87.0 all-gather.2
  117.2 80.4 all-gather.4
  443.3 105.0 reduce-scatter.2
  552.0 83.3 reduce-scatter.4
